TPU v7x, 32 devices: a whole 2x2x4 slice. The times are simulated.
32 devices in a mesh: dp: 2 (over x), ctx: 16 (over z, y, core).
Axes of the slice: x: 2, y: 2, z: 4, core: 2. Of those that a mesh axis runs over, the one named last changes fastest.
Arguments:
- tokens: bfloat16 [2, 2048, 4096], P('dp', 'ctx'), may hold values from -6 to 6
- proj_weight: bfloat16 [4096, 512], P('dp'), may hold values from -0.09375 to 0.09375
- values: bfloat16 [2, 2048, 2048], P('dp', 'ctx'), may hold values from -60 to 60
- grad_out: bfloat16 [2, 2048, 2048], P('dp', 'ctx'), may hold values from -6 to 6
Outputs:
- attended: bfloat16 [2, 2048, 2048], P('dp', 'ctx')
- grad_tokens: bfloat16 [2, 2048, 4096], P('dp', 'ctx')
- grad_values: bfloat16 [2, 2048, 2048], P('dp', 'ctx')
- grad_proj: float32 [4096, 512], P(('dp', 'ctx'))
All inputs are finite; a program needn't handle non-finite values.
Results may differ from a plain program's by a relative error of at most 0.0049.
Values may be sent and summed in bfloat16 or wider, within the bound.
No kernel may reach another device: no remote copies, remote signals or barrier semaphores. Data moves between devices by JAX's collectives and lax.ppermute only.
A program may use at most 192 MiB of HBM per device.

v0:
```python
import functools

import jax
import jax.numpy as jnp
from jax import lax
from jax.experimental import pallas as pl
from jax.experimental.pallas import tpu as pltpu
from jax.sharding import PartitionSpec as P

H = 16
F = 16
DH = 128
EPSILON = 1e-05
GROUP = 8
TILE = 256
PSI = 9 * F + 2 * F
PSI_SCALE = (0.5,) + (1.0,) * 7 + (0.5,)

f32 = jnp.float32
bf16 = jnp.bfloat16

NN = (((1,), (0,)), ((), ()))
NT = (((1,), (1,)), ((), ()))


def dot(a, b, dims=NN):
    return lax.dot_general(a, b, dims, preferred_element_type=f32)


def split(x):
    high = x.astype(bf16)
    return high, (x - high.astype(f32)).astype(bf16)


def dot3(a, b, dims=NN):
    a_high, a_low = split(a)
    b_high, b_low = split(b)
    return dot(a_high, b_high, dims) + (dot(a_high, b_low, dims) + dot(a_low, b_high, dims))


def turned(x, r):
    return x if r == 0 else jnp.concatenate([x[r:], x[:r]], axis=0)


def psi(x, weights):
    parts = []
    for r in range(9):
        part = x * turned(x, r)
        parts.append(part * PSI_SCALE[r] if weights and PSI_SCALE[r] != 1.0 else part)
    row = lax.broadcasted_iota(jnp.int32, x.shape, 0)
    return jnp.concatenate(parts + [x, jnp.where(row == 0, 1.0, 0.0)], axis=0)


def pull_psi(x, upstream, weights):
    total = upstream[9 * F : 10 * F]
    for r in range(9):
        part = upstream[r * F : (r + 1) * F]
        if weights and PSI_SCALE[r] != 1.0:
            part = part * PSI_SCALE[r]
        total = total + part * turned(x, r) + turned(part * x, (F - r) % F)
    return total


def feature_major(qk_ref, which, head):
    return jnp.concatenate([qk_ref[src, which, head] for src in range(qk_ref.shape[0])], axis=1)


def rows_of(ref, which, head, start, stop):
    tok = ref.shape[2]
    return jnp.concatenate(
        [
            ref[src, which, :, head * DH : (head + 1) * DH]
            for src in range(start // tok, stop // tok)
        ],
        axis=0,
    )


def score_sides(q, k):
    q_high, q_low = split(q)
    k_high, k_low = split(k)
    left = jnp.concatenate([q_high, q_high, q_low, q_low], axis=0)
    right = jnp.concatenate([k_high, k_low, k_high, k_low], axis=0)
    return left.T, right


def causal_mask(tile, width):
    row = lax.broadcasted_iota(jnp.int32, (tile, width), 0) + (width - tile)
    return row >= lax.broadcasted_iota(jnp.int32, (tile, width), 1)


def state_kernel(qk_ref, vg_ref, state_ref):
    heads = qk_ref.shape[2]
    length = qk_ref.shape[0] * qk_ref.shape[4]
    for head in range(heads):
        high, low = split(psi(feature_major(qk_ref, 1, head), False))
        v = rows_of(vg_ref, 0, head, 0, length)
        state_ref[head] = dot(high, v) + dot(low, v)


def numerator_kernel(qk_ref, vg_ref, num_ref):
    heads = qk_ref.shape[2]
    length = qk_ref.shape[0] * qk_ref.shape[4]
    tile = min(TILE, length)
    for head in range(heads):
        q = feature_major(qk_ref, 0, head) * 0.25
        k = feature_major(qk_ref, 1, head)
        left, right = score_sides(q, k)
        for at in range(0, length, tile):
            width = at + tile
            scores = dot(left[at:width], right[:, :width])
            kernel = jnp.where(
                causal_mask(tile, width), 1.0 + scores * (1.0 + 0.5 * scores), 0.0
            )
            high, low = split(kernel)
            v = rows_of(vg_ref, 0, head, 0, width)
            num_ref[at:width, head * DH : (head + 1) * DH] = dot(high, v) + dot(low, v)


def normalize_kernel(with_state, qk_ref, vg_ref, num_ref, *rest):
    if with_state:
        prefix_ref, attended_ref, grad_ref, carried_ref = rest
    else:
        attended_ref, grad_ref = rest
    heads = qk_ref.shape[2]
    blocks, tok = qk_ref.shape[0], qk_ref.shape[4]
    length = blocks * tok
    for head in range(heads):
        cols = slice(head * DH, (head + 1) * DH)
        numerator = num_ref[:, cols]
        if with_state:
            feat = psi(feature_major(qk_ref, 0, head) * 0.25, True)
            numerator = numerator + dot3(feat.T, prefix_ref[head])
        inv_rms = lax.rsqrt(jnp.mean(numerator * numerator, axis=-1, keepdims=True) + EPSILON)
        normed = numerator * inv_rms
        upstream = rows_of(vg_ref, 1, head, 0, length).astype(f32)
        grad = inv_rms * (
            upstream - normed * jnp.mean(normed * upstream, axis=-1, keepdims=True)
        )
        attended = normed.astype(bf16)
        for src in range(blocks):
            attended_ref[src, :, cols] = attended[src * tok : (src + 1) * tok]
        grad_ref[:, cols] = grad
        if with_state:
            carried_ref[head] = dot3(feat, grad)


def backward_kernel(with_state, qk_ref, vg_ref, grad_ref, *rest):
    if with_state:
        prefix_ref, grad_qk_ref, grad_v_ref = rest
    else:
        grad_qk_ref, grad_v_ref = rest
    heads = qk_ref.shape[2]
    length = qk_ref.shape[0] * qk_ref.shape[4]
    tile = min(TILE, length)
    for head in range(heads):
        cols = slice(head * DH, (head + 1) * DH)
        q = feature_major(qk_ref, 0, head) * 0.25
        k = feature_major(qk_ref, 1, head)
        left, right = score_sides(q, k)
        q_both = jnp.concatenate(split(q), axis=0)
        k_both = jnp.concatenate(split(k), axis=0)
        grad = grad_ref[:, cols]
        grad_t = grad.T
        if with_state:
            grad_q = pull_psi(q, dot3(prefix_ref[head], grad_t), True)
        for at in reversed(range(0, length, tile)):
            width = at + tile
            scores = dot(left[at:width], right[:, :width])
            causal = causal_mask(tile, width)
            v = rows_of(vg_ref, 0, head, 0, width)
            high, low = split(grad[at:width])
            mixing = dot(
                jnp.concatenate([high, low], axis=1), jnp.concatenate([v, v], axis=1), NT
            )
            more = 1.0 + scores
            slope = jnp.where(causal, mixing * more, 0.0).astype(bf16)
            kernel = jnp.where(causal, more + 0.5 * scores * scores, 0.0).astype(bf16)
            both = dot(k_both[:, :width], slope, NT)
            piece = both[:F] + both[F:]
            if with_state:
                piece = piece + grad_q[:, at:width]
            grad_qk_ref[0, head, :, at:width] = piece * 0.25
            both = dot(q_both[:, at:width], slope)
            piece_k = both[:F] + both[F:]
            both = dot(jnp.concatenate(split(grad_t[:, at:width]), axis=0), kernel)
            piece_v = both[:DH] + both[DH:]
            if width == length:
                grad_qk_ref[1, head] = piece_k
                grad_v_ref[head] = piece_v
            else:
                grad_qk_ref[1, head, :, :width] += piece_k
                grad_v_ref[head, :, :width] += piece_v


def finish_kernel(with_state, qk_ref, vg_ref, grad_qk_ref, grad_v_ref, *rest):
    if with_state:
        suffix_ref, rows_ref, out_ref = rest
    else:
        rows_ref, out_ref = rest
    heads = qk_ref.shape[2]
    blocks, tok = qk_ref.shape[0], qk_ref.shape[4]
    length = blocks * tok
    for head in range(heads):
        grad_k = grad_qk_ref[1, head]
        grad_v = grad_v_ref[head]
        if with_state:
            k = feature_major(qk_ref, 1, head)
            v = rows_of(vg_ref, 0, head, 0, length)
            suffix = suffix_ref[head]
            high, low = split(suffix)
            grad_k = grad_k + pull_psi(k, dot(high, v, NT) + dot(low, v, NT), False)
            grad_v = grad_v + dot3(suffix.T, psi(k, False))
        rows_ref[0, head] = grad_qk_ref[0, head].astype(bf16)
        rows_ref[1, head] = grad_k.astype(bf16)
        grad_v = grad_v.T.astype(bf16)
        for src in range(blocks):
            out_ref[src, :, head * DH : (head + 1) * DH] = grad_v[src * tok : (src + 1) * tok]


def call(body, out_shapes, flops, *operands):
    return pl.pallas_call(
        body,
        out_shape=[jax.ShapeDtypeStruct(shape, kind) for shape, kind in out_shapes],
        in_specs=[pl.BlockSpec(memory_space=pltpu.VMEM)] * len(operands),
        out_specs=[pl.BlockSpec(memory_space=pltpu.VMEM)] * len(out_shapes),
        compiler_params=pltpu.CompilerParams(vmem_limit_bytes=48 * 1024 * 1024),
        cost_estimate=pl.CostEstimate(flops=flops, bytes_accessed=4 << 20, transcendentals=0),
    )(*operands)


def local(dp_size, ctx_size, tokens, proj_weight, values, grad_out):
    group = min(GROUP, ctx_size, H)
    runs = ctx_size // group
    heads = H // group
    tok, width = tokens.shape[1:]
    length = group * tok
    cols = proj_weight.shape[1]
    share = width // dp_size
    depth = share // ctx_size
    with_state = runs > 1
    groups = [[run * group + i for i in range(group)] for run in range(runs)]
    dp_at, ctx_at = lax.axis_index("dp"), lax.axis_index("ctx")
    run_at, member = ctx_at // group, ctx_at % group

    def exchange(x):
        return lax.all_to_all(
            x, "ctx", split_axis=0, concat_axis=0, tiled=True, axis_index_groups=groups
        )

    def to_dp(x, shift):
        return lax.ppermute(x, "dp", [(i, (i + shift) % dp_size) for i in range(dp_size)])

    def to_run(x, shift, wrap):
        pairs = [
            (i, (i + shift * group) % ctx_size)
            for i in range(ctx_size)
            if wrap or 0 <= i + shift * group < ctx_size
        ]
        return lax.ppermute(x, "ctx", pairs)

    token_rows = tokens[0]

    def token_part(owner):
        return lax.dynamic_slice_in_dim(token_rows, owner * share, share, axis=1)

    def project(part):
        return lax.dot_general(
            proj_weight, part, (((0,), (1,)), ((), ())), preferred_element_type=f32
        )

    with jax.named_scope("projection"):
        arrived = [
            to_dp(token_part((dp_at + shift) % dp_size), shift) for shift in range(1, dp_size)
        ]
        projected = project(token_part(dp_at))
        for shift in range(1, dp_size):
            projected = projected + to_dp(project(arrived[shift - 1]), -shift)
    with jax.named_scope("to_heads"):
        both = jnp.stack([values[0], grad_out[0]]).reshape(2, tok, group, heads * DH)
        vg = exchange(both.transpose(2, 0, 1, 3))
        qk = exchange(
            projected.reshape(2, group, heads, F, tok).transpose(1, 0, 2, 3, 4)
        )
    with jax.named_scope("weight"):
        pair = 2 if ctx_size % 2 == 0 else 1
        piece = share // pair
        mine = lax.dynamic_slice_in_dim(proj_weight, (ctx_at % pair) * piece, piece, axis=0)
        weights = [proj_weight]
        for shift in range(1, dp_size):
            half = to_dp(mine, shift)
            if pair == 2:
                other = lax.ppermute(half, "ctx", [(i, i ^ 1) for i in range(ctx_size)])
                first = ctx_at % 2 == 0
                half = jnp.concatenate(
                    [jnp.where(first, half, other), jnp.where(first, other, half)], axis=0
                )
            weights.append(half)
    with jax.named_scope("token_columns"):
        token_cols = exchange(
            token_rows.reshape(tok, dp_size * runs, group, depth).transpose(2, 0, 1, 3)
        ).reshape(length, dp_size * runs * depth)

    pairs = heads * length * (length + TILE) // 2
    state_flops = 4 * heads * length * PSI * DH
    state_shape = ((heads, PSI, DH), f32)
    rows_shape = ((length, heads * DH), f32)
    blocks_shape = ((group, tok, heads * DH), bf16)
    prefix, suffix = (), ()
    if with_state:
        (state,) = call(state_kernel, [state_shape], state_flops, qk, vg)
        prefix = (sum(to_run(state, shift, False) for shift in range(1, runs)),)
    (numerator,) = call(numerator_kernel, [rows_shape], pairs * 2 * 512, qk, vg)
    result = call(
        functools.partial(normalize_kernel, with_state),
        [blocks_shape, rows_shape] + [state_shape] * with_state,
        2 * state_flops,
        qk,
        vg,
        numerator,
        *prefix,
    )
    attended, grad_num = result[:2]
    if with_state:
        suffix = (sum(to_run(result[2], -shift, False) for shift in range(1, runs)),)
    grad_qk, grad_v = call(
        functools.partial(backward_kernel, with_state),
        [((2, heads, F, length), f32), ((heads, DH, length), f32)],
        pairs * 2 * 1024,
        qk,
        vg,
        grad_num,
        *prefix,
    )
    rows, grad_v = call(
        functools.partial(finish_kernel, with_state),
        [((2, heads, F, length), bf16), blocks_shape],
        state_flops,
        qk,
        vg,
        grad_qk,
        grad_v,
        *suffix,
    )
    with jax.named_scope("rows"):
        gathered = exchange(jnp.broadcast_to(rows[None], (group,) + rows.shape))
        gathered = gathered.transpose(1, 0, 2, 3, 4).reshape(cols, length)
    with jax.named_scope("from_heads"):
        attended = exchange(attended).transpose(1, 0, 2).reshape(1, tok, H * DH)
        grad_values = exchange(grad_v).transpose(1, 0, 2).reshape(1, tok, H * DH)
    with jax.named_scope("grad_proj"):
        product = lax.dot_general(
            token_cols, gathered, (((0,), (1,)), ((), ())), preferred_element_type=f32
        ).reshape(dp_size, runs, depth, cols)
        total = lax.dynamic_index_in_dim(product, dp_at, 0, keepdims=False)
        for shift in range(1, dp_size):
            part = lax.dynamic_index_in_dim(
                product, (dp_at + shift) % dp_size, 0, keepdims=False
            )
            total = total + to_dp(part.astype(bf16), shift).astype(f32)
        grad_proj = lax.dynamic_index_in_dim(total, run_at, 0, keepdims=False)
        for shift in range(1, runs):
            part = lax.dynamic_index_in_dim(total, (run_at + shift) % runs, 0, keepdims=False)
            grad_proj = grad_proj + to_run(part.astype(bf16), shift, True).astype(f32)
    with jax.named_scope("grad_tokens"):
        own_rows = lax.dynamic_slice_in_dim(gathered, member * tok, tok, axis=1)
        grad_tokens = jnp.zeros((tok, width), bf16)
        for shift in range(dp_size):
            part = lax.dot_general(
                own_rows, weights[shift], (((0,), (1,)), ((), ())), preferred_element_type=f32
            ).astype(bf16)
            grad_tokens = lax.dynamic_update_slice_in_dim(
                grad_tokens, part, ((dp_at - shift) % dp_size) * share, axis=1
            )
    return (attended, grad_tokens[None], grad_values, grad_proj)


def solution(mesh):
    return jax.shard_map(
        functools.partial(local, mesh.shape["dp"], mesh.shape["ctx"]),
        mesh=mesh,
        in_specs=(P("dp", "ctx", None), P("dp", None), P("dp", "ctx", None), P("dp", "ctx", None)),
        out_specs=(
            P("dp", "ctx", None),
            P("dp", "ctx", None),
            P("dp", "ctx", None),
            P(("dp", "ctx"), None),
        ),
        check_vma=False,
    )
```

profile of v0, /device:TPU:0, one launch (start us, length us, event | category | flops | bytes accessed | tf_op | source)
XLA Modules:
  0.0 162.7 jit_solution(10775891798637450529)
XLA Ops:
  0.7 2.0 %dynamic-slice_bitcast_fusion = bf16[128,2048]{1,0:T(8,128)(2,1)} fusion(bf16[1,128,4096]{2,1,0:T(8,128)(2,1)} %param.4, s32[]{:T(128)S(6)} %select_n.81), kind=kLoop, calls=%fused_computation.20 | loop fusion | bytes 1048580 | tf_op jit(solution)/shard_map/projection/dynamic_slice | solution.py:265
  2.7 2.9 %collective-permute-start = (bf16[128,2048]{1,0:T(8,128)(2,1)}, bf16[128,2048]{1,0:T(8,128)(2,1)}, u32[]{:S(2)}, u32[]{:S(2)}) collective-permute-start(bf16[128,2048]{1,0:T(8,128)(2,1)} %dynamic-slice_bitcast_fusion), channel_id=1, source_target_pairs={{0,16},{16,0},{1,17},{17,1},{2,18},{18,2},{3,19},{19,3},{4,20},{20... | collective-permute-start | bytes 1572872 | tf_op jit(solution)/shard_map/projection/ppermute | solution.py:252
  5.7 12.2 %collective-permute-done = bf16[128,2048]{1,0:T(8,128)(2,1)} collective-permute-done((bf16[128,2048]{1,0:T(8,128)(2,1)}, bf16[128,2048]{1,0:T(8,128)(2,1)}, u32[]{:S(2)}, u32[]{:S(2)}) %collective-permute-start) | collective-permute-done | bytes 524320 | tf_op jit(solution)/shard_map/projection/ppermute | solution.py:252
  21.7 5.3 %collective-permute-done.1 = f32[512,128]{0,1:T(8,128)S(1)} collective-permute-done((f32[512,128]{0,1:T(8,128)S(1)}, f32[512,128]{0,1:T(8,128)S(1)}, u32[]{:S(2)}, u32[]{:S(2)}) %collective-permute-start.1) | collective-permute-done | bytes 262176 | tf_op jit(solution)/shard_map/projection/ppermute | solution.py:252
  27.8 3.7 %all-to-all-start = ((f32[8,2,2,16,128]{4,3,2,1,0:T(8,128)}), f32[8,2,2,16,128]{4,3,2,1,0:T(8,128)S(1)}, u32[]{:S(2)}, u32[]{:S(2)}) async-start(f32[8,2,2,16,128]{4,3,2,1,0:T(8,128)} %bitcast.55), calls=%async_computation | async-start | bytes 524288 | tf_op jit(solution)/shard_map/to_heads/all_to_all | solution.py:247
  31.6 2.0 %copy.32 = bf16[1,128,2048]{1,2,0:T(8,128)(2,1)} copy(bf16[1,128,2048]{2,1,0:T(8,128)(2,1)} %param.7) | data formatting | bytes 1048576 | tf_op args[3]
  37.6 3.8 %all-to-all-start.1 = ((bf16[8,2,128,256]{3,2,1,0:T(8,128)(2,1)}), bf16[8,2,128,256]{3,2,1,0:T(8,128)(2,1)S(1)}, u32[]{:S(2)}, u32[]{:S(2)}) async-start(bf16[8,2,128,256]{3,2,1,0:T(8,128)(2,1)} %bitcast.56), calls=%async_computation.1 | async-start | bytes 2097152 | tf_op jit(solution)/shard_map/to_heads/all_to_all | solution.py:247
  41.4 2.3 %copy.37 = bf16[1,128,4096]{1,2,0:T(8,128)(2,1)} copy(bf16[1,128,4096]{2,1,0:T(8,128)(2,1)} %param.4) | data formatting | bytes 2097152 | tf_op args[0]
  43.7 2.3 %copy.38 = bf16[8,128,4,128]{1,3,2,0:T(8,128)(2,1)} copy(bf16[8,128,4,128]{1,3,0,2:T(8,128)(2,1)} %bitcast.58) | data formatting | bytes 2097152 | tf_op jit(solution)/shard_map/token_columns/transpose | solution.py:301
  46.0 9.9 %all-to-all-done.1.vg_ref = bf16[8,2,128,256]{3,2,1,0:T(8,128)(2,1)S(1)} async-done(((bf16[8,2,128,256]{3,2,1,0:T(8,128)(2,1)}), bf16[8,2,128,256]{3,2,1,0:T(8,128)(2,1)S(1)}, u32[]{:S(2)}, u32[]{:S(2)}) %all-to-all-start.1) | async-done | bytes 1048608 | tf_op jit(solution)/shard_map/to_heads/all_to_all | solution.py:247
  55.9 4.2 %all-to-all-start.5 = ((bf16[8,128,4,128]{1,3,2,0:T(8,128)(2,1)}), bf16[8,128,4,128]{1,3,2,0:T(8,128)(2,1)}, u32[]{:S(2)}, u32[]{:S(2)}) async-start(bf16[8,128,4,128]{1,3,2,0:T(8,128)(2,1)} %copy.38), calls=%async_computation.5 | async-start | bytes 2097152 | tf_op jit(solution)/shard_map/token_columns/all_to_all | solution.py:247
  60.7 4.5 %collective-permute-start.2 = (f32[2,176,128]{2,1,0:T(8,128)S(1)}, f32[2,176,128]{2,1,0:T(8,128)S(1)}, u32[]{:S(2)}, u32[]{:S(2)}) collective-permute-start(f32[2,176,128]{2,1,0:T(8,128)S(1)} %shard_map.76), channel_id=1, source_target_pairs={{0,8},{1,9},{2,10},{3,11},{4,12},{5,13},{6,14},{7,15},{16,24},{17,... | collective-permute-start | bytes 540680 | tf_op jit(solution)/shard_map/ppermute | solution.py:260
  65.2 3.1 %shard_map.75.num_ref = f32[1024,256]{1,0:T(8,128)S(1)} custom-call(f32[8,2,2,16,128]{4,3,2,1,0:T(8,128)S(1)} %all-to-all-done.qk_ref, bf16[8,2,128,256]{3,2,1,0:T(8,128)(2,1)S(1)} %all-to-all-done.1.vg_ref), custom_call_target="tpu_custom_call" | custom-call | flops 1342177280 | bytes 4194304 | tf_op jit(solution)/shard_map/pallas_call | solution.py:222
  68.3 7.9 %collective-permute-done.2.rest_0_ = f32[2,176,128]{2,1,0:T(8,128)S(1)} collective-permute-done((f32[2,176,128]{2,1,0:T(8,128)S(1)}, f32[2,176,128]{2,1,0:T(8,128)S(1)}, u32[]{:S(2)}, u32[]{:S(2)}) %collective-permute-start.2) | collective-permute-done | bytes 180256 | tf_op jit(solution)/shard_map/ppermute | solution.py:260
  76.3 2.5 %shard_map.77 = (bf16[8,128,256]{2,1,0:T(8,128)(2,1)S(1)}, f32[1024,256]{1,0:T(8,128)S(1)}, f32[2,176,128]{2,1,0:T(8,128)S(1)}) custom-call(f32[8,2,2,16,128]{4,3,2,1,0:T(8,128)S(1)} %all-to-all-done.qk_ref, bf16[8,2,128,256]{3,2,1,0:T(8,128)(2,1)S(1)} %all-to-all-done.1.vg_ref, f32[1024,256]{1,0:T(8,128)S(1)} %shard_map.75.num_ref, ...), custom_call_target="tpu_custom_call" | custom-call | flops 369098752 | bytes 4194304 | tf_op jit(solution)/shard_map/pallas_call | solution.py:222
  81.9 4.1 %all-to-all-start.2 = ((bf16[8,128,256]{2,1,0:T(8,128)(2,1)}), bf16[8,128,256]{2,1,0:T(8,128)(2,1)}, u32[]{:S(2)}, u32[]{:S(2)}) async-start(bf16[8,128,256]{2,1,0:T(8,128)(2,1)} %copy-done.1), calls=%async_computation.2 | async-start | bytes 1048576 | tf_op jit(solution)/shard_map/from_heads/all_to_all | solution.py:247
  89.7 4.6 %shard_map.78 = (f32[2,2,16,1024]{3,2,1,0:T(8,128)S(1)}, f32[2,128,1024]{2,1,0:T(8,128)S(1)}) custom-call(f32[8,2,2,16,128]{4,3,2,1,0:T(8,128)S(1)} %all-to-all-done.qk_ref, bf16[8,2,128,256]{3,2,1,0:T(8,128)(2,1)S(1)} %all-to-all-done.1.vg_ref, f32[1024,256]{1,0:T(8,128)S(1)} %copy-done.5, f32[2,176,128]{2,1,0:T(8,128)S(1)} %copy-done.3), custom_call_target="tpu_custom_call" | custom-call | flops 2684354560 | bytes 4194304 | tf_op jit(solution)/shard_map/pallas_call | solution.py:222
  96.1 2.0 %shard_map.79 = (bf16[2,2,16,1024]{3,2,1,0:T(8,128)(2,1)S(1)}, bf16[8,128,256]{2,1,0:T(8,128)(2,1)}) custom-call(f32[8,2,2,16,128]{4,3,2,1,0:T(8,128)S(1)} %all-to-all-done.qk_ref, bf16[8,2,128,256]{3,2,1,0:T(8,128)(2,1)S(1)} %all-to-all-done.1.vg_ref, f32[2,2,16,1024]{3,2,1,0:T(8,128)S(1)} %get-tuple-element.13.grad_qk_ref, ...), custom_call_target="tpu_custom_call" | custom-call | flops 184549376 | bytes 4194304 | tf_op jit(solution)/shard_map/pallas_call | solution.py:222
  99.8 7.5 %all-to-all-start.3 = ((bf16[8,2,2,16,1024]{4,3,2,1,0:T(8,128)(2,1)}), bf16[8,2,2,16,1024]{4,3,2,1,0:T(8,128)(2,1)S(1)}, u32[]{:S(2)}, u32[]{:S(2)}) async-start(bf16[8,2,2,16,1024]{4,3,2,1,0:T(8,128)(2,1)} %broadcast_in_dim.15), calls=%async_computation.3 | async-start | bytes 2097152 | tf_op jit(solution)/shard_map/rows/all_to_all | solution.py:247
  108.9 24.2 %collective-permute-done.4 = bf16[1024,512]{1,0:T(8,128)(2,1)} collective-permute-done((bf16[1024,512]{1,0:T(8,128)(2,1)S(1)}, bf16[1024,512]{1,0:T(8,128)(2,1)}, u32[]{:S(2)}, u32[]{:S(2)}) %collective-permute-start.4) | collective-permute-done | bytes 1048608 | tf_op jit(solution)/shard_map/weight/ppermute | solution.py:252
  133.1 4.2 %all-to-all-start.4 = ((bf16[8,128,256]{2,1,0:T(8,128)(2,1)}), bf16[8,128,256]{2,1,0:T(8,128)(2,1)}, u32[]{:S(2)}, u32[]{:S(2)}) async-start(bf16[8,128,256]{2,1,0:T(8,128)(2,1)} %get-tuple-element.17), calls=%async_computation.4 | async-start | bytes 1048576 | tf_op jit(solution)/shard_map/from_heads/all_to_all | solution.py:247
  137.4 1.9 %copy.39 = bf16[8,128,4,128]{1,0,3,2:T(8,128)(2,1)S(1)} copy(bf16[8,128,4,128]{1,3,2,0:T(8,128)(2,1)} %all-to-all-done.5) | data formatting | bytes 2097152 | tf_op jit(solution)/shard_map/token_columns/all_to_all | solution.py:247
  143.7 3.0 %broadcast_select_fusion.1 = (bf16[1024,512]{1,0:T(8,128)(2,1)}, bf16[1024,512]{1,0:T(8,128)(2,1)}) fusion(bf16[1024,512]{1,0:T(8,128)(2,1)} %collective-permute-done.4, bf16[1024,512]{1,0:T(8,128)(2,1)} %collective-permute-done.5, pred[]{:T(512)S(6)} %eq.12), kind=kLoop, calls=%fused_computation.16 | loop fusion | flops 1048576 | bytes 4194305 | tf_op jit(solution)/shard_map/weight/jit(_where)/select_n | solution.py:296
  156.4 5.5 %collective-permute-done.7 = bf16[128,512]{1,0:T(8,128)(2,1)S(1)} collective-permute-done((bf16[128,512]{1,0:T(8,128)(2,1)S(1)}, bf16[128,512]{1,0:T(8,128)(2,1)S(1)}, u32[]{:S(2)}, u32[]{:S(2)}) %collective-permute-start.7) | collective-permute-done | bytes 131104 | tf_op jit(solution)/shard_map/grad_proj/ppermute | solution.py:260
  (66 shorter events, 35.8 us)
Async XLA Ops:
  0.6 17.3 %copy-start = (bf16[2048,512]{1,0:T(8,128)(2,1)S(1)}, bf16[2048,512]{1,0:T(8,128)(2,1)}, u32[]{:S(2)}) copy-start(bf16[2048,512]{1,0:T(8,128)(2,1)} %param.5) | copy-start | bytes 6291460
  0.6 20.6 %copy-start.7 = (bf16[1,128,4096]{2,1,0:T(8,128)(2,1)S(1)}, bf16[1,128,4096]{2,1,0:T(8,128)(2,1)}, u32[]{:S(2)}) copy-start(bf16[1,128,4096]{2,1,0:T(8,128)(2,1)} %param.4) | copy-start | bytes 3145732
  2.7 15.2 %collective-permute-start = (bf16[128,2048]{1,0:T(8,128)(2,1)}, bf16[128,2048]{1,0:T(8,128)(2,1)}, u32[]{:S(2)}, u32[]{:S(2)}) collective-permute-start(bf16[128,2048]{1,0:T(8,128)(2,1)} %dynamic-slice_bitcast_fusion), channel_id=1, source_target_pairs={{0,16},{16,0},{1,17},{17,1},{2,18},{18,2},{3,19},{19,3},{4,20},{20... | collective-permute-start | bytes 1572872 | tf_op jit(solution)/shard_map/projection/ppermute | solution.py:252
  19.4 7.6 %collective-permute-start.1 = (f32[512,128]{0,1:T(8,128)S(1)}, f32[512,128]{0,1:T(8,128)S(1)}, u32[]{:S(2)}, u32[]{:S(2)}) collective-permute-start(f32[512,128]{0,1:T(8,128)S(1)} %convolution_bitcast_fusion), channel_id=1, source_target_pairs={{0,16},{16,0},{1,17},{17,1},{2,18},{18,2},{3,19},{19,3},{4,20},{20... | collective-permute-start | bytes 786440 | tf_op jit(solution)/shard_map/projection/ppermute | solution.py:252
  21.6 12.0 %copy-start.13 = (bf16[1,128,2048]{2,1,0:T(8,128)(2,1)S(1)}, bf16[1,128,2048]{2,1,0:T(8,128)(2,1)}, u32[]{:S(2)}) copy-start(bf16[1,128,2048]{2,1,0:T(8,128)(2,1)} %param.6) | copy-start | bytes 1572868
  27.8 9.8 %all-to-all-start = ((f32[8,2,2,16,128]{4,3,2,1,0:T(8,128)}), f32[8,2,2,16,128]{4,3,2,1,0:T(8,128)S(1)}, u32[]{:S(2)}, u32[]{:S(2)}) async-start(f32[8,2,2,16,128]{4,3,2,1,0:T(8,128)} %bitcast.55), calls=%async_computation | async-start | bytes 524288 | tf_op jit(solution)/shard_map/to_heads/all_to_all | solution.py:247
  37.6 18.3 %all-to-all-start.1 = ((bf16[8,2,128,256]{3,2,1,0:T(8,128)(2,1)}), bf16[8,2,128,256]{3,2,1,0:T(8,128)(2,1)S(1)}, u32[]{:S(2)}, u32[]{:S(2)}) async-start(bf16[8,2,128,256]{3,2,1,0:T(8,128)(2,1)} %bitcast.56), calls=%async_computation.1 | async-start | bytes 2097152 | tf_op jit(solution)/shard_map/to_heads/all_to_all | solution.py:247
  55.9 26.0 %all-to-all-start.5 = ((bf16[8,128,4,128]{1,3,2,0:T(8,128)(2,1)}), bf16[8,128,4,128]{1,3,2,0:T(8,128)(2,1)}, u32[]{:S(2)}, u32[]{:S(2)}) async-start(bf16[8,128,4,128]{1,3,2,0:T(8,128)(2,1)} %copy.38), calls=%async_computation.5 | async-start | bytes 2097152 | tf_op jit(solution)/shard_map/token_columns/all_to_all | solution.py:247
  60.7 15.6 %collective-permute-start.2 = (f32[2,176,128]{2,1,0:T(8,128)S(1)}, f32[2,176,128]{2,1,0:T(8,128)S(1)}, u32[]{:S(2)}, u32[]{:S(2)}) collective-permute-start(f32[2,176,128]{2,1,0:T(8,128)S(1)} %shard_map.76), channel_id=1, source_target_pairs={{0,8},{1,9},{2,10},{3,11},{4,12},{5,13},{6,14},{7,15},{16,24},{17,... | collective-permute-start | bytes 540680 | tf_op jit(solution)/shard_map/ppermute | solution.py:260
  80.2 1.0 copy-start.4
  81.9 16.9 %all-to-all-start.2 = ((bf16[8,128,256]{2,1,0:T(8,128)(2,1)}), bf16[8,128,256]{2,1,0:T(8,128)(2,1)}, u32[]{:S(2)}, u32[]{:S(2)}) async-start(bf16[8,128,256]{2,1,0:T(8,128)(2,1)} %copy-done.1), calls=%async_computation.2 | async-start | bytes 1048576 | tf_op jit(solution)/shard_map/from_heads/all_to_all | solution.py:247
  86.0 10.0 %collective-permute-start.3 = (f32[2,176,128]{2,1,0:T(8,128)}, f32[2,176,128]{2,1,0:T(8,128)S(1)}, u32[]{:S(2)}, u32[]{:S(2)}) collective-permute-start(f32[2,176,128]{2,1,0:T(8,128)} %copy-done.6), channel_id=1, source_target_pairs={{8,0},{9,1},{10,2},{11,3},{12,4},{13,5},{14,6},{15,7},{24,16},{25,... | collective-permute-start | bytes 540680 | tf_op jit(solution)/shard_map/ppermute | solution.py:260
  88.4 1.2 copy-start.5
  99.8 33.3 %all-to-all-start.3 = ((bf16[8,2,2,16,1024]{4,3,2,1,0:T(8,128)(2,1)}), bf16[8,2,2,16,1024]{4,3,2,1,0:T(8,128)(2,1)S(1)}, u32[]{:S(2)}, u32[]{:S(2)}) async-start(bf16[8,2,2,16,1024]{4,3,2,1,0:T(8,128)(2,1)} %broadcast_in_dim.15), calls=%async_computation.3 | async-start | bytes 2097152 | tf_op jit(solution)/shard_map/rows/all_to_all | solution.py:247
  107.4 25.7 %collective-permute-start.4 = (bf16[1024,512]{1,0:T(8,128)(2,1)S(1)}, bf16[1024,512]{1,0:T(8,128)(2,1)}, u32[]{:S(2)}, u32[]{:S(2)}) collective-permute-start(bf16[1024,512]{1,0:T(8,128)(2,1)S(1)} %constant_dynamic-slice_fusion), channel_id=1, source_target_pairs={{0,16},{16,0},{1,17},{17,1},{2,18},{18,2},{3,19},{19,3},{4,20},{20... | collective-permute-start | bytes 3145736 | tf_op jit(solution)/shard_map/weight/ppermute | solution.py:252
  133.1 10.6 %collective-permute-start.5 = (bf16[1024,512]{1,0:T(8,128)(2,1)}, bf16[1024,512]{1,0:T(8,128)(2,1)}, u32[]{:S(2)}, u32[]{:S(2)}) collective-permute-start(bf16[1024,512]{1,0:T(8,128)(2,1)} %collective-permute-done.4), channel_id=1, source_target_pairs={{0,1},{1,0},{2,3},{3,2},{4,5},{5,4},{6,7},{7,6},{8,9},{9,8},{10,11... | collective-permute-start | bytes 3145736 | tf_op jit(solution)/shard_map/weight/ppermute | solution.py:293
  133.1 16.0 %all-to-all-start.4 = ((bf16[8,128,256]{2,1,0:T(8,128)(2,1)}), bf16[8,128,256]{2,1,0:T(8,128)(2,1)}, u32[]{:S(2)}, u32[]{:S(2)}) async-start(bf16[8,128,256]{2,1,0:T(8,128)(2,1)} %get-tuple-element.17), calls=%async_computation.4 | async-start | bytes 1048576 | tf_op jit(solution)/shard_map/from_heads/all_to_all | solution.py:247
  139.4 1.0 copy-start.8
  141.1 1.0 copy-start.12
  142.2 9.3 %collective-permute-start.6 = (bf16[2,128,512]{2,1,0:T(8,128)(2,1)S(1)}, bf16[2,128,512]{2,1,0:T(8,128)(2,1)S(1)}, u32[]{:S(2)}, u32[]{:S(2)}) collective-permute-start(bf16[2,128,512]{2,1,0:T(8,128)(2,1)S(1)} %fusion.12), channel_id=1, source_target_pairs={{0,16},{16,0},{1,17},{17,1},{2,18},{18,2},{3,19},{19,3},{4,20},{20... | collective-permute-start | bytes 786440 | tf_op jit(solution)/shard_map/grad_proj/ppermute | solution.py:252
  152.6 2.1 %copy-start.9 = (bf16[1024,512]{1,0:T(8,128)(2,1)S(1)}, bf16[1024,512]{1,0:T(8,128)(2,1)}, u32[]{:S(2)}) copy-start(bf16[1024,512]{1,0:T(8,128)(2,1)} %get-tuple-element.30) | copy-start | bytes 3145732
  152.6 2.1 %copy-start.10 = (bf16[1024,512]{1,0:T(8,128)(2,1)S(1)}, bf16[1024,512]{1,0:T(8,128)(2,1)}, u32[]{:S(2)}) copy-start(bf16[1024,512]{1,0:T(8,128)(2,1)} %get-tuple-element.31) | copy-start | bytes 3145732
  152.6 9.3 %collective-permute-start.7 = (bf16[128,512]{1,0:T(8,128)(2,1)S(1)}, bf16[128,512]{1,0:T(8,128)(2,1)S(1)}, u32[]{:S(2)}, u32[]{:S(2)}) collective-permute-start(bf16[128,512]{1,0:T(8,128)(2,1)S(1)} %fusion.13), channel_id=1, source_target_pairs={{0,8},{1,9},{2,10},{3,11},{4,12},{5,13},{6,14},{7,15},{8,0},{9,1},... | collective-permute-start | bytes 393224 | tf_op jit(solution)/shard_map/grad_proj/ppermute | solution.py:260
  156.4 6.3 %copy-start.11 = (bf16[1,128,4096]{2,1,0:T(8,128)(2,1)}, bf16[1,128,4096]{2,1,0:T(8,128)(2,1)S(1)}, u32[]{:S(2)}) copy-start(bf16[1,128,4096]{2,1,0:T(8,128)(2,1)S(1)} %fusion.3) | copy-start | bytes 3145732
  (4 other events, 3.1 us)
where the time goes:
time: 164 us; the launch traced here: 163 us
  waiting for transfers between devices  67.9 us (41%)
  starting transfers between devices  41.5 us (25%)
  local copies, waits for them, and re-layouts  27 us (16%)
  Pallas kernels  12.8 us (8%)
  matrix products  6.26 us (4%)
  other arithmetic  6.21 us (4%)
    ppermute x4, waiting for transfers between devices, to_dp(): lax.ppermute(x, 'dp', [(i, (i + shift) % dp_size) for i in range(dp_size)])  41.7 us
    all_to_all x6, starting transfers between devices, exchange(): lax.all_to_all(x, 'ctx', split_axis=0, concat_axis=0, tiled=True, axis_in...  27.6 us
    ppermute x3, waiting for transfers between devices, to_run(): return lax.ppermute(x, 'ctx', pairs)  15.2 us
    unnamed x33, local copies, waits for them, and re-layouts  14.6 us
    pallas_call x5, Pallas kernels, call(): pl.pallas_call(body, out_shape=[jax.ShapeDtypeStruct(shape, kind) for sha...  12.8 us
    all_to_all x6, waiting for transfers between devices, exchange(): lax.all_to_all(x, 'ctx', split_axis=0, concat_axis=0, tiled=True, axis_in...  10.9 us
    ppermute x4, starting transfers between devices, to_dp(): lax.ppermute(x, 'dp', [(i, (i + shift) % dp_size) for i in range(dp_size)])  7.87 us
    ppermute x3, starting transfers between devices, to_run(): return lax.ppermute(x, 'ctx', pairs)  6.06 us
  transfers between devices with their start and end apart: 14, of which 9 were waited for; matrix products, arithmetic and copies ran while one was open for 15% of the time, Pallas kernels for 8%

commit v1 on v0

v1 whole, which is shorter than its diff:
```python
import functools

import jax
import jax.numpy as jnp
from jax import lax
from jax.experimental import pallas as pl
from jax.experimental.pallas import tpu as pltpu
from jax.sharding import PartitionSpec as P

H = 16
F = 16
DH = 128
EPSILON = 1e-05
GROUP = 8
TILE = 256
PSI = 9 * F + 2 * F
PSI_SCALE = (0.5,) + (1.0,) * 7 + (0.5,)

f32 = jnp.float32
bf16 = jnp.bfloat16

NN = (((1,), (0,)), ((), ()))
NT = (((1,), (1,)), ((), ()))


def dot(a, b, dims=NN):
    return lax.dot_general(a, b, dims, preferred_element_type=f32)


def split(x):
    high = x.astype(bf16)
    return high, (x - high.astype(f32)).astype(bf16)


def dot3(a, b, dims=NN):
    a_high, a_low = split(a)
    b_high, b_low = split(b)
    return dot(a_high, b_high, dims) + (dot(a_high, b_low, dims) + dot(a_low, b_high, dims))


def turned(x, r):
    return x if r == 0 else jnp.concatenate([x[r:], x[:r]], axis=0)


def psi(x, weights):
    parts = []
    for r in range(9):
        part = x * turned(x, r)
        parts.append(part * PSI_SCALE[r] if weights and PSI_SCALE[r] != 1.0 else part)
    row = lax.broadcasted_iota(jnp.int32, x.shape, 0)
    return jnp.concatenate(parts + [x, jnp.where(row == 0, 1.0, 0.0)], axis=0)


def pull_psi(x, upstream, weights):
    total = upstream[9 * F : 10 * F]
    for r in range(9):
        part = upstream[r * F : (r + 1) * F]
        if weights and PSI_SCALE[r] != 1.0:
            part = part * PSI_SCALE[r]
        total = total + part * turned(x, r) + turned(part * x, (F - r) % F)
    return total


def feature_major(qk_ref, which, head):
    return jnp.concatenate([qk_ref[src, which, head] for src in range(qk_ref.shape[0])], axis=1)


def rows_of(ref, which, head, start, stop):
    tok = ref.shape[2]
    return jnp.concatenate(
        [
            ref[src, which, :, head * DH : (head + 1) * DH]
            for src in range(start // tok, stop // tok)
        ],
        axis=0,
    )


def score_sides(q, k):
    q_high, q_low = split(q)
    k_high, k_low = split(k)
    left = jnp.concatenate([q_high, q_high, q_low, q_low], axis=0)
    right = jnp.concatenate([k_high, k_low, k_high, k_low], axis=0)
    return left.T, right


def causal_mask(tile, width):
    row = lax.broadcasted_iota(jnp.int32, (tile, width), 0) + (width - tile)
    return row >= lax.broadcasted_iota(jnp.int32, (tile, width), 1)


def token_parts_kernel(at_ref, tokens_ref, *out_refs):
    count = len(out_refs)
    share = out_refs[0].shape[1]
    for shift, out_ref in enumerate(out_refs):
        owner = lax.rem(at_ref[0] + shift, count)
        out_ref[...] = tokens_ref[0, :, pl.ds(pl.multiple_of(owner * share, share), share)]


def pack_heads_kernel(values_ref, grad_ref, out_ref):
    group, width = out_ref.shape[0], out_ref.shape[3]
    for member in range(group):
        cols = slice(member * width, (member + 1) * width)
        out_ref[member, 0] = values_ref[0, :, cols]
        out_ref[member, 1] = grad_ref[0, :, cols]


def pack_tokens_kernel(depth, tokens_ref, out_ref):
    group, rows = out_ref.shape[:2]
    for member in range(group):
        for part in range(rows // depth):
            first = (part * group + member) * depth
            out_ref[member, part * depth : (part + 1) * depth] = tokens_ref[
                0, :, first : first + depth
            ].T


def projected_blocks(part, weight, out_ref):
    projected = dot(part, weight).T
    group, _, heads, feat, _ = out_ref.shape
    for member in range(group):
        for which in range(2):
            for head in range(heads):
                first = ((which * group + member) * heads + head) * feat
                out_ref[member, which, head] = projected[first : first + feat]


def project_kernel(part_ref, weight_ref, out_ref):
    projected_blocks(part_ref[...], weight_ref[...], out_ref)


def project_rest_kernel(at_ref, own_ref, weight_ref, *rest):
    *part_refs, out_ref = rest
    count = len(part_refs) + 1
    at = at_ref[0]
    out_ref[at] = own_ref[...]
    for shift, part_ref in enumerate(part_refs, 1):
        owner = lax.rem(at + count - shift, count)
        projected_blocks(part_ref[...], weight_ref[...], out_ref.at[owner])


def weight_piece_kernel(at_ref, weight_ref, out_ref):
    size = out_ref.shape[0]
    out_ref[...] = weight_ref[pl.ds(pl.multiple_of(at_ref[0] * size, size), size), :]


def state_kernel(with_state, parts_ref, vg_ref, qk_ref, *state_refs):
    count, blocks, _, heads, _, tok = parts_ref.shape
    for head in range(heads):
        for which in range(2):
            for src in range(blocks):
                total = parts_ref[0, src, which, head]
                for part in range(1, count):
                    total = total + parts_ref[part, src, which, head]
                qk_ref[src, which, head] = total
        if with_state:
            high, low = split(psi(feature_major(qk_ref, 1, head), False))
            v = rows_of(vg_ref, 0, head, 0, blocks * tok)
            state_refs[0][head] = dot(high, v) + dot(low, v)


def numerator_kernel(qk_ref, vg_ref, num_ref):
    heads = qk_ref.shape[2]
    length = qk_ref.shape[0] * qk_ref.shape[4]
    tile = min(TILE, length)
    for head in range(heads):
        q = feature_major(qk_ref, 0, head) * 0.25
        k = feature_major(qk_ref, 1, head)
        left, right = score_sides(q, k)
        for at in range(0, length, tile):
            width = at + tile
            scores = dot(left[at:width], right[:, :width])
            kernel = jnp.where(
                causal_mask(tile, width), 1.0 + scores * (1.0 + 0.5 * scores), 0.0
            )
            high, low = split(kernel)
            v = rows_of(vg_ref, 0, head, 0, width)
            num_ref[at:width, head * DH : (head + 1) * DH] = dot(high, v) + dot(low, v)


def normalize_kernel(with_state, qk_ref, vg_ref, num_ref, *rest):
    if with_state:
        prefix_ref, attended_ref, grad_ref, carried_ref = rest
    else:
        attended_ref, grad_ref = rest
    heads = qk_ref.shape[2]
    blocks, tok = qk_ref.shape[0], qk_ref.shape[4]
    length = blocks * tok
    for head in range(heads):
        cols = slice(head * DH, (head + 1) * DH)
        numerator = num_ref[:, cols]
        if with_state:
            feat = psi(feature_major(qk_ref, 0, head) * 0.25, True)
            numerator = numerator + dot3(feat.T, prefix_ref[head])
        inv_rms = lax.rsqrt(jnp.mean(numerator * numerator, axis=-1, keepdims=True) + EPSILON)
        normed = numerator * inv_rms
        upstream = rows_of(vg_ref, 1, head, 0, length).astype(f32)
        grad = inv_rms * (
            upstream - normed * jnp.mean(normed * upstream, axis=-1, keepdims=True)
        )
        attended = normed.astype(bf16)
        for src in range(blocks):
            attended_ref[src, :, cols] = attended[src * tok : (src + 1) * tok]
        grad_ref[:, cols] = grad
        if with_state:
            carried_ref[head] = dot3(feat, grad)


def backward_kernel(with_state, first, qk_ref, vg_ref, grad_ref, *rest):
    rest = list(rest)
    prefix_ref = rest.pop(0) if with_state else None
    if first == 0:
        attended_in_ref = rest.pop(0)
        attended_ref = rest.pop()
        attended_ref[...] = attended_in_ref[...]
    grad_qk_ref, grad_v_ref = rest[-2:]
    length = qk_ref.shape[0] * qk_ref.shape[4]
    tile = min(TILE, length)
    for at_head in range(grad_v_ref.shape[0]):
        head = first + at_head
        cols = slice(head * DH, (head + 1) * DH)
        q = feature_major(qk_ref, 0, head) * 0.25
        k = feature_major(qk_ref, 1, head)
        left, right = score_sides(q, k)
        q_both = jnp.concatenate(split(q), axis=0)
        k_both = jnp.concatenate(split(k), axis=0)
        grad = grad_ref[:, cols]
        grad_t = grad.T
        if with_state:
            grad_q = pull_psi(q, dot3(prefix_ref[head], grad_t), True)
        for at in reversed(range(0, length, tile)):
            width = at + tile
            scores = dot(left[at:width], right[:, :width])
            causal = causal_mask(tile, width)
            v = rows_of(vg_ref, 0, head, 0, width)
            high, low = split(grad[at:width])
            mixing = dot(
                jnp.concatenate([high, low], axis=1), jnp.concatenate([v, v], axis=1), NT
            )
            more = 1.0 + scores
            slope = jnp.where(causal, mixing * more, 0.0).astype(bf16)
            kernel = jnp.where(causal, more + 0.5 * scores * scores, 0.0).astype(bf16)
            both = dot(k_both[:, :width], slope, NT)
            piece = both[:F] + both[F:]
            if with_state:
                piece = piece + grad_q[:, at:width]
            grad_qk_ref[0, at_head, :, at:width] = piece * 0.25
            both = dot(q_both[:, at:width], slope)
            piece_k = both[:F] + both[F:]
            both = dot(jnp.concatenate(split(grad_t[:, at:width]), axis=0), kernel)
            piece_v = both[:DH] + both[DH:]
            if width == length:
                grad_qk_ref[1, at_head] = piece_k
                grad_v_ref[at_head] = piece_v
            else:
                grad_qk_ref[1, at_head, :, :width] += piece_k
                grad_v_ref[at_head, :, :width] += piece_v


def rows_kernel(with_state, halves, qk_ref, vg_ref, *rest):
    rest = list(rest)
    suffix_ref = rest.pop(0) if with_state else None
    rows_ref = rest[-1]
    blocks, tok = qk_ref.shape[0], qk_ref.shape[4]
    head = 0
    for grad_ref in rest[:halves]:
        for at_head in range(grad_ref.shape[1]):
            grad_k = grad_ref[1, at_head]
            if with_state:
                k = feature_major(qk_ref, 1, head)
                v = rows_of(vg_ref, 0, head, 0, blocks * tok)
                high, low = split(suffix_ref[head])
                grad_k = grad_k + pull_psi(k, dot(high, v, NT) + dot(low, v, NT), False)
            grad_q, grad_k = grad_ref[0, at_head].astype(bf16), grad_k.astype(bf16)
            for member in range(rows_ref.shape[0]):
                rows_ref[member, 0, head] = grad_q
                rows_ref[member, 1, head] = grad_k
            head += 1


def grad_values_kernel(with_state, halves, qk_ref, *rest):
    rest = list(rest)
    suffix_ref = rest.pop(0) if with_state else None
    out_ref = rest[-1]
    blocks, tok = qk_ref.shape[0], qk_ref.shape[4]
    head = 0
    for grad_ref in rest[:halves]:
        for at_head in range(grad_ref.shape[0]):
            grad_v = grad_ref[at_head]
            if with_state:
                feat = psi(feature_major(qk_ref, 1, head), False)
                grad_v = grad_v + dot3(suffix_ref[head].T, feat)
            grad_v = grad_v.T.astype(bf16)
            for src in range(blocks):
                out_ref[src, :, head * DH : (head + 1) * DH] = grad_v[src * tok : (src + 1) * tok]
            head += 1


def unpack_heads_kernel(in_ref, out_ref):
    group, _, width = in_ref.shape
    for member in range(group):
        out_ref[0, :, member * width : (member + 1) * width] = in_ref[member]


def all_rows(rows_ref, cols):
    group, _, heads = rows_ref.shape[:3]
    return jnp.concatenate(
        [
            rows_ref[src, which, head, :, cols]
            for which in range(2)
            for src in range(group)
            for head in range(heads)
        ],
        axis=0,
    )


def product_kernel(at_ref, rows_ref, tokens_ref, *rest):
    *part_refs, total_ref = rest
    tokens = jnp.concatenate([tokens_ref[src] for src in range(tokens_ref.shape[0])], axis=1)
    total_ref[...] = dot(tokens, all_rows(rows_ref, slice(None)), NT)
    count = len(part_refs)
    size = part_refs[0].shape[0]
    for shift, part_ref in enumerate(part_refs):
        owner = lax.rem(at_ref[0] + shift, count)
        part = total_ref[pl.ds(pl.multiple_of(owner * size, size), size), :]
        part_ref[...] = part.astype(part_ref.dtype)


def run_sum_kernel(arrived, at_ref, *rest):
    own_ref, *rest = rest
    total_ref = rest[-1]
    total = own_ref[...]
    for ref in rest[:arrived]:
        total = total + ref[...].astype(f32)
    total_ref[...] = total
    part_refs = rest[arrived:-1]
    size = part_refs[0].shape[0]
    for shift, part_ref in enumerate(part_refs):
        owner = lax.rem(at_ref[0] + shift, len(part_refs))
        part = total_ref[pl.ds(pl.multiple_of(owner * size, size), size), :]
        part_ref[...] = part.astype(part_ref.dtype)


def grad_tokens_kernel(at_ref, rows_ref, *rest):
    *weight_refs, out_ref = rest
    tok = out_ref.shape[1]
    start = pl.multiple_of(at_ref[0] * tok, tok)
    rows = all_rows(rows_ref, pl.ds(start, tok)).T
    for i, weight_ref in enumerate(weight_refs):
        size = weight_ref.shape[0]
        first = pl.multiple_of(at_ref[1 + i], size)
        out_ref[0, :, pl.ds(first, size)] = dot(rows, weight_ref[...], NT).astype(bf16)


VMEM = pl.BlockSpec(memory_space=pltpu.VMEM)
SMEM = pl.BlockSpec(memory_space=pltpu.SMEM)
ANYWHERE = pl.BlockSpec(memory_space=pl.ANY)


def call(body, out_shapes, flops, *operands, scalars=(), after=(), scratch=()):
    at = [jnp.stack([jnp.int32(s) for s in scalars])] if scalars else []
    count = len(at) + len(operands)

    def kernel(*refs):
        body(*refs[:count], *refs[count + len(after) :])

    return pl.pallas_call(
        kernel,
        out_shape=[jax.ShapeDtypeStruct(shape, kind) for shape, kind in out_shapes],
        in_specs=[SMEM] * len(at) + [VMEM] * len(operands) + [ANYWHERE] * len(after),
        out_specs=[VMEM] * len(out_shapes),
        scratch_shapes=scratch,
        compiler_params=pltpu.CompilerParams(vmem_limit_bytes=24 * 1024 * 1024),
        cost_estimate=pl.CostEstimate(flops=flops, bytes_accessed=4 << 20, transcendentals=0),
    )(*at, *operands, *after)


def local(dp_size, ctx_size, tokens, proj_weight, values, grad_out):
    group = min(GROUP, ctx_size, H)
    runs = ctx_size // group
    heads = H // group
    tok, width = tokens.shape[1:]
    length = group * tok
    cols = proj_weight.shape[1]
    share = width // dp_size
    depth = share // ctx_size
    with_state = runs > 1
    groups = [[run * group + i for i in range(group)] for run in range(runs)]
    wide_groups = [
        [dp * ctx_size + i for dp in range(dp_size) for i in members] for members in groups
    ]
    dp_at, ctx_at = lax.axis_index("dp"), lax.axis_index("ctx")
    run_at, member = ctx_at // group, ctx_at % group

    def exchange(x):
        return lax.all_to_all(
            x, "ctx", split_axis=0, concat_axis=0, tiled=True, axis_index_groups=groups
        )

    def to_dp(x, shift):
        return lax.ppermute(x, "dp", [(i, (i + shift) % dp_size) for i in range(dp_size)])

    def to_run(x, shift, wrap):
        pairs = [
            (i, (i + shift * group) % ctx_size)
            for i in range(ctx_size)
            if wrap or 0 <= i + shift * group < ctx_size
        ]
        return lax.ppermute(x, "ctx", pairs)

    qk_shape = ((group, 2, heads, F, tok), f32)
    pairs = length * (length + TILE) // 2
    state_flops = 4 * heads * length * PSI * DH
    state_shape = ((heads, PSI, DH), f32)
    blocks_shape = ((group, tok, heads * DH), bf16)
    project_flops = 2 * tok * share * cols

    own, *parts = call(
        token_parts_kernel, [((tok, share), bf16)] * dp_size, 0, tokens, scalars=(dp_at,)
    )
    arrived = [to_dp(part, shift) for shift, part in enumerate(parts, 1)]
    (vg,) = call(
        pack_heads_kernel,
        [((group, 2, tok, heads * DH), bf16)],
        0,
        values,
        grad_out,
        after=parts[:1],
    )
    vg = exchange(vg)
    (projected,) = call(project_kernel, [qk_shape], project_flops, own, proj_weight)
    (projected,) = call(
        project_rest_kernel,
        [((dp_size,) + qk_shape[0], f32)],
        project_flops,
        projected,
        proj_weight,
        *arrived,
        scalars=(dp_at,),
        after=(vg,),
    )
    qk_parts = lax.all_to_all(
        projected.reshape((dp_size * group,) + qk_shape[0][1:]),
        ("dp", "ctx"),
        split_axis=0,
        concat_axis=0,
        tiled=True,
        axis_index_groups=wide_groups,
    ).reshape(projected.shape)

    pair = 2 if ctx_size % 2 == 0 else 1
    parity = ctx_at % pair
    piece = share // pair
    (mine,) = call(
        weight_piece_kernel,
        [((piece, cols), bf16)],
        0,
        proj_weight,
        scalars=(parity,),
        after=(projected,),
    )
    fetched = [to_dp(mine, shift) for shift in range(1, dp_size)]
    weights, firsts = [proj_weight], [dp_at * share]
    for shift, half in enumerate(fetched, 1):
        base = (dp_at + dp_size - shift) % dp_size * share
        weights.append(half)
        firsts.append(base + parity * piece)
        if pair == 2:
            weights.append(lax.ppermute(half, "ctx", [(i, i ^ 1) for i in range(ctx_size)]))
            firsts.append(base + (1 - parity) * piece)

    qk, *state = call(
        functools.partial(state_kernel, with_state),
        [qk_shape] + [state_shape] * with_state,
        state_flops,
        qk_parts,
        vg,
    )
    if depth % 128 == 0:
        (token_cols,) = call(
            functools.partial(pack_tokens_kernel, depth),
            [((group, dp_size * runs * depth, tok), bf16)],
            0,
            tokens,
            after=(qk,),
        )
    else:
        token_cols = (
            tokens[0]
            .reshape(tok, dp_size * runs, group, depth)
            .transpose(2, 1, 3, 0)
            .reshape(group, dp_size * runs * depth, tok)
        )
    token_cols = exchange(token_cols)

    prefix, suffix = (), ()
    if with_state:
        prefix = (sum(to_run(state[0], shift, False) for shift in range(1, runs)),)
    (numerator,) = call(
        numerator_kernel, [((length, heads * DH), f32)], heads * pairs * 2 * 512, qk, vg
    )
    attended, grad_num, *carried = call(
        functools.partial(normalize_kernel, with_state),
        [blocks_shape, ((length, heads * DH), f32)] + [state_shape] * with_state,
        2 * state_flops,
        qk,
        vg,
        numerator,
        *prefix,
    )
    if with_state:
        suffix = (sum(to_run(carried[0], -shift, False) for shift in range(1, runs)),)
    grad_qks, grad_vs = [], []
    for first in range(0, heads, max(1, heads // 2)):
        count = max(1, heads // 2)
        result = call(
            functools.partial(backward_kernel, with_state, first),
            [((2, count, F, length), f32), ((count, DH, length), f32)]
            + [blocks_shape] * (first == 0),
            count * pairs * 2 * 1024,
            qk,
            vg,
            grad_num,
            *prefix,
            *([attended] if first == 0 else []),
            after=[] if first == 0 else [grad_qks[0], *fetched],
        )
        grad_qks.append(result[0])
        grad_vs.append(result[1])
        if first == 0:
            attended = exchange(result[2])
    (rows,) = call(
        functools.partial(rows_kernel, with_state, len(grad_qks)),
        [((group, 2, heads, F, length), bf16)],
        state_flops,
        qk,
        vg,
        *suffix,
        *grad_qks,
    )
    rows = exchange(rows)

    own, *parts = call(
        product_kernel,
        [((runs * depth, cols), f32)] + [((runs * depth, cols), bf16)] * (dp_size - 1),
        2 * dp_size * runs * depth * length * cols,
        rows,
        token_cols,
        scalars=(dp_at,),
        after=weights[1:] + [attended],
        scratch=[pltpu.VMEM((dp_size * runs * depth, cols), f32)],
    )
    parts = [to_dp(part, shift) for shift, part in enumerate(parts, 1)]
    (grad_values,) = call(
        functools.partial(grad_values_kernel, with_state, len(grad_vs)),
        [blocks_shape],
        state_flops,
        qk,
        *suffix,
        *grad_vs,
        after=(own,),
    )
    grad_values = exchange(grad_values)
    (grad_tokens,) = call(
        grad_tokens_kernel,
        [((1, tok, width), bf16)],
        2 * tok * width * cols,
        rows,
        *weights,
        scalars=(member, *firsts),
        after=(own,),
    )
    grad_proj, *parts = call(
        functools.partial(run_sum_kernel, len(parts)),
        [((depth, cols), f32)] + [((depth, cols), bf16)] * (runs - 1),
        0,
        own,
        *parts,
        scalars=(run_at,),
        scratch=[pltpu.VMEM((runs * depth, cols), f32)],
    )
    for shift, part in enumerate(parts, 1):
        grad_proj = grad_proj + to_run(part, shift, True).astype(f32)
    attended, grad_values = [
        call(unpack_heads_kernel, [((1, tok, H * DH), bf16)], 0, blocks)[0]
        for blocks in (attended, grad_values)
    ]
    return (attended, grad_tokens, grad_values, grad_proj)


def solution(mesh):
    return jax.shard_map(
        functools.partial(local, mesh.shape["dp"], mesh.shape["ctx"]),
        mesh=mesh,
        in_specs=(P("dp", "ctx", None), P("dp", None), P("dp", "ctx", None), P("dp", "ctx", None)),
        out_specs=(
            P("dp", "ctx", None),
            P("dp", "ctx", None),
            P("dp", "ctx", None),
            P(("dp", "ctx"), None),
        ),
        check_vma=False,
    )
```

time: 164 us -> 164 us (level)
  blocking collectives: 0 us -> 15.2 us
  Pallas kernels: 12.8 us -> 22.8 us
  matrix products: 6.26 us -> 0 us
  waiting for transfers between devices: 67.9 us -> 62.4 us
  other arithmetic: 6.21 us -> 0.81 us
  starting transfers between devices: 41.5 us -> 36.5 us
  local copies, waits for them, and re-layouts: 27 us -> 24.2 us
    all_to_all x0 -> x1, blocking collectives: none -> 15.2 us  [local(): lax.all_to_all(projected.reshape((dp_size * group,) + qk_shape[0][1:]), (...]
    ppermute x3, waiting for transfers between devices: 15.2 us -> 0.22 us  [to_run(): return lax.ppermute(x, 'ctx', pairs)]
    pallas_call x5 -> x18, Pallas kernels: 12.8 us -> 22.8 us  [call(): pl.pallas_call(kernel, out_shape=[jax.ShapeDtypeStruct(shape, kind) for s...]
    unnamed x33 -> x78, local copies, waits for them, and re-layouts: 14.6 us -> 24.2 us
    dot_general x5 -> x0, matrix products: 6.26 us -> none  [the longest x2 3.6 us: local(): lax.dot_general(own_rows, weights[shift], (((0,), (1,)), ((), ())), prefe...]
    all_to_all x6 -> x5, waiting for transfers between devices: 10.9 us -> 16.9 us  [exchange(): lax.all_to_all(x, 'ctx', split_axis=0, concat_axis=0, tiled=True, axis_in...]
    ppermute x4 -> x3, starting transfers between devices: 7.87 us -> 2.89 us  [to_dp(): lax.ppermute(x, 'dp', [(i, (i + shift) % dp_size) for i in range(dp_size)])]
    transpose x3 -> x0, local copies, waits for them, and re-layouts: 4.93 us -> none  [the longest x1 2.3 us: local(): token_rows.reshape(tok, dp_size * runs, group, depth).transpose(2, 0, 1, 3)]
  transfers between devices with their start and end apart: 14 -> 12, of which waited for: 9 -> 7; matrix products, arithmetic and copies ran while one was open for 15% -> 0% of each run, Pallas kernels for 8% -> 7%
where the time goes in v1:
time: 164 us; the launch traced here: 163 us
  waiting for transfers between devices  62.4 us (38%)
  starting transfers between devices  36.5 us (22%)
  local copies, waits for them, and re-layouts  24.2 us (15%)
  Pallas kernels  22.8 us (14%)
  blocking collectives  15.2 us (9%)
    ppermute x3, waiting for transfers between devices, to_dp(): lax.ppermute(x, 'dp', [(i, (i + shift) % dp_size) for i in range(dp_size)])  42.7 us
    unnamed x78, local copies, waits for them, and re-layouts  24.2 us
    all_to_all x5, starting transfers between devices, exchange(): lax.all_to_all(x, 'ctx', split_axis=0, concat_axis=0, tiled=True, axis_in...  23.7 us
    pallas_call x18, Pallas kernels, call(): pl.pallas_call(kernel, out_shape=[jax.ShapeDtypeStruct(shape, kind) for s...  22.8 us
    all_to_all x5, waiting for transfers between devices, exchange(): lax.all_to_all(x, 'ctx', split_axis=0, concat_axis=0, tiled=True, axis_in...  16.9 us
    all_to_all x1, blocking collectives, local(): lax.all_to_all(projected.reshape((dp_size * group,) + qk_shape[0][1:]), (...  15.2 us
    ppermute x3, starting transfers between devices, to_run(): return lax.ppermute(x, 'ctx', pairs)  9.42 us
  transfers between devices with their start and end apart: 12, of which 7 were waited for; matrix products, arithmetic and copies ran while one was open for 0% of the time, Pallas kernels for 7%

profile of v1, /device:TPU:0, one launch (start us, length us, event | category | flops | bytes accessed | tf_op | source)
XLA Modules:
  0.0 162.8 jit_solution(18008432880705996627)
XLA Ops:
  6.7 5.3 %all-to-all-start = ((bf16[8,2,128,256]{3,2,1,0:T(8,128)(2,1)}), bf16[8,2,128,256]{3,2,1,0:T(8,128)(2,1)S(1)}, u32[]{:S(2)}, u32[]{:S(2)}) async-start(bf16[8,2,128,256]{3,2,1,0:T(8,128)(2,1)} %copy-done.16), calls=%async_computation | async-start | bytes 2097152 | tf_op jit(solution)/shard_map/all_to_all | solution.py:397
  11.9 1.5 collective-permute-start
  15.0 11.5 %collective-permute-done.refs_3_ = bf16[128,2048]{1,0:T(8,128)(2,1)S(1)} collective-permute-done((bf16[128,2048]{1,0:T(8,128)(2,1)}, bf16[128,2048]{1,0:T(8,128)(2,1)S(1)}, u32[]{:S(2)}, u32[]{:S(2)}) %collective-permute-start) | collective-permute-done | bytes 524320 | tf_op jit(solution)/shard_map/ppermute | solution.py:402
  28.9 15.2 %all_to_all.30 = f32[16,2,2,16,128]{4,3,2,1,0:T(8,128)S(1)} all-to-all(f32[16,2,2,16,128]{4,3,2,1,0:T(8,128)S(1)} %bitcast.9), channel_id=1, replica_groups={{0,1,2,3,4,5,6,7,16,17,18,19,20,21,22,23},{8,9,10,11,12,13,14,15,24,25,..., dimensions={0} | all-to-all | bytes 1048576 | tf_op jit(solution)/shard_map/all_to_all | solution.py:443
  44.7 4.5 %collective-permute-start.1 = (f32[2,176,128]{2,1,0:T(8,128)S(1)}, f32[2,176,128]{2,1,0:T(8,128)S(1)}, u32[]{:S(2)}, u32[]{:S(2)}) collective-permute-start(f32[2,176,128]{2,1,0:T(8,128)S(1)} %get-tuple-element.23), channel_id=1, source_target_pairs={{0,8},{1,9},{2,10},{3,11},{4,12},{5,13},{6,14},{7,15},{16,24},{17,... | collective-permute-start | bytes 540680 | tf_op jit(solution)/shard_map/ppermute | solution.py:410
  49.2 3.1 %shard_map.80.refs_2_ = f32[1024,256]{1,0:T(8,128)S(1)} custom-call(f32[8,2,2,16,128]{4,3,2,1,0:T(8,128)S(1)} %get-tuple-element.22.refs_0_.refs_1_, bf16[8,2,128,256]{3,2,1,0:T(8,128)(2,1)S(1)} %all-to-all-done.refs_4_.refs_1_), custom_call_target="tpu_custom_call" | custom-call | flops 1342177280 | bytes 4194304 | tf_op jit(solution)/shard_map/pallas_call | solution.py:368
  52.5 2.5 %shard_map.81 = (bf16[8,128,256]{2,1,0:T(8,128)(2,1)S(1)}, f32[1024,256]{1,0:T(8,128)S(1)}, f32[2,176,128]{2,1,0:T(8,128)S(1)}) custom-call(f32[8,2,2,16,128]{4,3,2,1,0:T(8,128)S(1)} %get-tuple-element.22.refs_0_.refs_1_, bf16[8,2,128,256]{3,2,1,0:T(8,128)(2,1)S(1)} %all-to-all-done.refs_4_.refs_1_, f32[1024,256]{1,0:T(8,128)S(1)} %shard_map.80.refs_2_, ...), custom_call_target="tpu_custom_call" | custom-call | flops 369098752 | bytes 4194304 | tf_op jit(solution)/shard_map/pallas_call | solution.py:368
  55.0 2.3 %shard_map.82 = (f32[2,1,16,1024]{3,2,1,0:T(8,128)S(1)}, f32[1,128,1024]{2,1,0:T(8,128)S(1)}, bf16[8,128,256]{2,1,0:T(8,128)(2,1)S(1)}) custom-call(f32[8,2,2,16,128]{4,3,2,1,0:T(8,128)S(1)} %get-tuple-element.22.refs_0_.refs_1_, bf16[8,2,128,256]{3,2,1,0:T(8,128)(2,1)S(1)} %all-to-all-done.refs_4_.refs_1_, f32[1024,256]{1,0:T(8,128)S(1)} %get-tuple-element.24.refs_2_, ...), custom_call_target="tpu_custom_call" | custom-call | flops 1342177280 | bytes 4194304 | tf_op jit(solution)/shard_map/pallas_call | solution.py:368
  59.0 6.1 %all-to-all-start.2 = ((bf16[8,128,256]{2,1,0:T(8,128)(2,1)}), bf16[8,128,256]{2,1,0:T(8,128)(2,1)}, u32[]{:S(2)}, u32[]{:S(2)}) async-start(bf16[8,128,256]{2,1,0:T(8,128)(2,1)} %copy-done.29), calls=%async_computation.2 | async-start | bytes 1048576 | tf_op jit(solution)/shard_map/all_to_all | solution.py:397
  67.6 6.4 %all-to-all-done.2.refs_0_.refs_5_ = bf16[8,128,256]{2,1,0:T(8,128)(2,1)} async-done(((bf16[8,128,256]{2,1,0:T(8,128)(2,1)}), bf16[8,128,256]{2,1,0:T(8,128)(2,1)}, u32[]{:S(2)}, u32[]{:S(2)}) %all-to-all-start.2) | async-done | bytes 524320 | tf_op jit(solution)/shard_map/all_to_all | solution.py:397
  74.1 4.3 %all-to-all-start.4 = ((bf16[8,512,128]{2,1,0:T(8,128)(2,1)}), bf16[8,512,128]{2,1,0:T(8,128)(2,1)}, u32[]{:S(2)}, u32[]{:S(2)}) async-start(bf16[8,512,128]{2,1,0:T(8,128)(2,1)} %copy-done.14), calls=%async_computation.4 | async-start | bytes 2097152 | tf_op jit(solution)/shard_map/all_to_all | solution.py:397
  80.3 1.5 collective-permute-start.2
  81.8 23.2 %collective-permute-done.3.refs_5_.refs_3_ = bf16[1024,512]{1,0:T(8,128)(2,1)S(1)} collective-permute-done((bf16[1024,512]{1,0:T(8,128)(2,1)S(1)}, bf16[1024,512]{1,0:T(8,128)(2,1)S(1)}, u32[]{:S(2)}, u32[]{:S(2)}) %collective-permute-start.3) | collective-permute-done | bytes 1048608 | tf_op jit(solution)/shard_map/ppermute | solution.py:402
  105.0 2.3 %shard_map.85 = (f32[2,1,16,1024]{3,2,1,0:T(8,128)S(1)}, f32[1,128,1024]{2,1,0:T(8,128)S(1)}) custom-call(f32[8,2,2,16,128]{4,3,2,1,0:T(8,128)S(1)} %get-tuple-element.22.refs_0_.refs_1_, bf16[8,2,128,256]{3,2,1,0:T(8,128)(2,1)S(1)} %all-to-all-done.refs_4_.refs_1_, f32[1024,256]{1,0:T(8,128)S(1)} %copy-done.35, f32[2,176,128]{2,1,0:T(8,128)S(1)} %copy-done.33, ...), custom_call_target="tpu_custom_call" | custom-call | flops 1342177280 | bytes 4194304 | tf_op jit(solution)/shard_map/pallas_call | solution.py:368
  110.4 3.9 %all-to-all-start.3 = ((bf16[8,2,2,16,1024]{4,3,2,1,0:T(8,128)(2,1)}), bf16[8,2,2,16,1024]{4,3,2,1,0:T(8,128)(2,1)S(1)}, u32[]{:S(2)}, u32[]{:S(2)}) async-start(bf16[8,2,2,16,1024]{4,3,2,1,0:T(8,128)(2,1)} %copy-done.15), calls=%async_computation.3 | async-start | bytes 2097152 | tf_op jit(solution)/shard_map/all_to_all | solution.py:397
  114.8 2.5 %collective-permute-done.4.refs_4_ = bf16[1024,512]{1,0:T(8,128)(2,1)S(1)} collective-permute-done((bf16[1024,512]{1,0:T(8,128)(2,1)}, bf16[1024,512]{1,0:T(8,128)(2,1)S(1)}, u32[]{:S(2)}, u32[]{:S(2)}) %collective-permute-start.4) | collective-permute-done | bytes 1048608 | tf_op jit(solution)/shard_map/ppermute | solution.py:470
  118.3 10.4 %all-to-all-done.3.refs_1_ = bf16[8,2,2,16,1024]{4,3,2,1,0:T(8,128)(2,1)S(1)} async-done(((bf16[8,2,2,16,1024]{4,3,2,1,0:T(8,128)(2,1)}), bf16[8,2,2,16,1024]{4,3,2,1,0:T(8,128)(2,1)S(1)}, u32[]{:S(2)}, u32[]{:S(2)}) %all-to-all-start.3) | async-done | bytes 1048608 | tf_op jit(solution)/shard_map/all_to_all | solution.py:397
  131.2 2.2 %shard_map.88 = (f32[256,512]{1,0:T(8,128)S(1)}, bf16[256,512]{1,0:T(8,128)(2,1)S(1)}) custom-call(s32[1]{0:T(128)} %bitcast.refs_0_, bf16[8,2,2,16,1024]{4,3,2,1,0:T(8,128)(2,1)S(1)} %all-to-all-done.3.refs_1_, bf16[8,512,128]{2,1,0:T(8,128)(2,1)} %all-to-all-done.4.refs_2_, bf16[1024,512]{1,0:T(8,128)(2,1)S(1)} %copy-done.9, ...), custom_call_target="tpu_custom_call" | custom-call | flops 536870912 | bytes 4194304 | tf_op jit(solution)/shard_map/pallas_call | solution.py:368
  136.4 4.1 %all-to-all-start.5 = ((bf16[8,128,256]{2,1,0:T(8,128)(2,1)}), bf16[8,128,256]{2,1,0:T(8,128)(2,1)}, u32[]{:S(2)}, u32[]{:S(2)}) async-start(bf16[8,128,256]{2,1,0:T(8,128)(2,1)} %copy-done.17), calls=%async_computation.5 | async-start | bytes 1048576 | tf_op jit(solution)/shard_map/all_to_all | solution.py:397
  141.3 8.1 %collective-permute-done.5.refs_2_ = bf16[256,512]{1,0:T(8,128)(2,1)S(1)} collective-permute-done((bf16[256,512]{1,0:T(8,128)(2,1)}, bf16[256,512]{1,0:T(8,128)(2,1)S(1)}, u32[]{:S(2)}, u32[]{:S(2)}) %collective-permute-start.5) | collective-permute-done | bytes 262176 | tf_op jit(solution)/shard_map/ppermute | solution.py:402
  150.5 3.5 %collective-permute-start.6 = (bf16[128,512]{1,0:T(8,128)(2,1)S(1)}, bf16[128,512]{1,0:T(8,128)(2,1)S(1)}, u32[]{:S(2)}, u32[]{:S(2)}) collective-permute-start(bf16[128,512]{1,0:T(8,128)(2,1)S(1)} %get-tuple-element.35), channel_id=1, source_target_pairs={{0,8},{1,9},{2,10},{3,11},{4,12},{5,13},{6,14},{7,15},{8,0},{9,1},... | collective-permute-start | bytes 393224 | tf_op jit(solution)/shard_map/ppermute | solution.py:410
  154.1 1.9 %shard_map.83 = bf16[1,128,2048]{2,1,0:T(8,128)(2,1)} custom-call(bf16[8,128,256]{2,1,0:T(8,128)(2,1)} %all-to-all-done.2.refs_0_.refs_5_), custom_call_target="tpu_custom_call" | custom-call | bytes 4194304 | tf_op jit(solution)/shard_map/pallas_call | solution.py:368
  157.2 3.0 %shard_map.89 = bf16[1,128,4096]{2,1,0:T(8,128)(2,1)} custom-call(s32[4]{0:T(128)S(1)} %pad_add_fusion.refs_0_, bf16[8,2,2,16,1024]{4,3,2,1,0:T(8,128)(2,1)S(1)} %all-to-all-done.3.refs_1_, bf16[2048,512]{1,0:T(8,128)(2,1)S(1)} %copy-done, bf16[1024,512]{1,0:T(8,128)(2,1)S(1)} %copy-done.10, bf16[1024,512]{1,0:T(8,128)(2,1)S(1)} %copy-done.13, ...), custom_call_target="tpu_custom_call" | custom-call | flops 536870912 | bytes 4194304 | tf_op jit(solution)/shard_map/pallas_call | solution.py:368
  160.9 1.9 %shard_map.91 = bf16[1,128,2048]{2,1,0:T(8,128)(2,1)} custom-call(bf16[8,128,256]{2,1,0:T(8,128)(2,1)} %all-to-all-done.5.refs_0_), custom_call_target="tpu_custom_call" | custom-call | bytes 4194304 | tf_op jit(solution)/shard_map/pallas_call | solution.py:368
  (99 shorter events, 30.8 us)
Async XLA Ops:
  4.8 8.6 %copy-start = (bf16[2048,512]{1,0:T(8,128)(2,1)S(1)}, bf16[2048,512]{1,0:T(8,128)(2,1)}, u32[]{:S(2)}) copy-start(bf16[2048,512]{1,0:T(8,128)(2,1)} %refs_2_.3) | copy-start | bytes 6291460
  6.7 20.6 %all-to-all-start = ((bf16[8,2,128,256]{3,2,1,0:T(8,128)(2,1)}), bf16[8,2,128,256]{3,2,1,0:T(8,128)(2,1)S(1)}, u32[]{:S(2)}, u32[]{:S(2)}) async-start(bf16[8,2,128,256]{3,2,1,0:T(8,128)(2,1)} %copy-done.16), calls=%async_computation | async-start | bytes 2097152 | tf_op jit(solution)/shard_map/all_to_all | solution.py:397
  11.9 14.5 %collective-permute-start = (bf16[128,2048]{1,0:T(8,128)(2,1)}, bf16[128,2048]{1,0:T(8,128)(2,1)S(1)}, u32[]{:S(2)}, u32[]{:S(2)}) collective-permute-start(bf16[128,2048]{1,0:T(8,128)(2,1)} %copy-done.26), channel_id=1, source_target_pairs={{0,16},{16,0},{1,17},{17,1},{2,18},{18,2},{3,19},{19,3},{4,20},{20... | collective-permute-start | bytes 1572872 | tf_op jit(solution)/shard_map/ppermute | solution.py:402
  28.9 23.4 %copy-start.1 = (f32[2,8,2,2,16,128]{5,4,3,2,1,0:T(8,128)}, f32[2,8,2,2,16,128]{5,4,3,2,1,0:T(8,128)S(1)}, u32[]{:S(2)}) copy-start(f32[2,8,2,2,16,128]{5,4,3,2,1,0:T(8,128)S(1)} %shard_map.78.refs_2_) | copy-start | bytes 1572868
  44.7 7.8 %collective-permute-start.1 = (f32[2,176,128]{2,1,0:T(8,128)S(1)}, f32[2,176,128]{2,1,0:T(8,128)S(1)}, u32[]{:S(2)}, u32[]{:S(2)}) collective-permute-start(f32[2,176,128]{2,1,0:T(8,128)S(1)} %get-tuple-element.23), channel_id=1, source_target_pairs={{0,8},{1,9},{2,10},{3,11},{4,12},{5,13},{6,14},{7,15},{16,24},{17,... | collective-permute-start | bytes 540680 | tf_op jit(solution)/shard_map/ppermute | solution.py:410
  52.5 4.8 %copy-start.32 = (f32[2,176,128]{2,1,0:T(8,128)}, f32[2,176,128]{2,1,0:T(8,128)S(1)}, u32[]{:S(2)}) copy-start(f32[2,176,128]{2,1,0:T(8,128)S(1)} %collective-permute-done.1.refs_3_) | copy-start | bytes 540676
  55.0 2.3 %copy-start.34 = (f32[1024,256]{1,0:T(8,128)}, f32[1024,256]{1,0:T(8,128)S(1)}, u32[]{:S(2)}) copy-start(f32[1024,256]{1,0:T(8,128)S(1)} %get-tuple-element.24.refs_2_) | copy-start | bytes 3145732
  55.0 2.3 %copy-start.37 = (f32[2,176,128]{2,1,0:T(8,128)}, f32[2,176,128]{2,1,0:T(8,128)S(1)}, u32[]{:S(2)}) copy-start(f32[2,176,128]{2,1,0:T(8,128)S(1)} %get-tuple-element.27) | copy-start | bytes 540676
  59.0 15.1 %all-to-all-start.2 = ((bf16[8,128,256]{2,1,0:T(8,128)(2,1)}), bf16[8,128,256]{2,1,0:T(8,128)(2,1)}, u32[]{:S(2)}, u32[]{:S(2)}) async-start(bf16[8,128,256]{2,1,0:T(8,128)(2,1)} %copy-done.29), calls=%async_computation.2 | async-start | bytes 1048576 | tf_op jit(solution)/shard_map/all_to_all | solution.py:397
  74.1 36.3 %all-to-all-start.4 = ((bf16[8,512,128]{2,1,0:T(8,128)(2,1)}), bf16[8,512,128]{2,1,0:T(8,128)(2,1)}, u32[]{:S(2)}, u32[]{:S(2)}) async-start(bf16[8,512,128]{2,1,0:T(8,128)(2,1)} %copy-done.14), calls=%async_computation.4 | async-start | bytes 2097152 | tf_op jit(solution)/shard_map/all_to_all | solution.py:397
  79.4 25.6 %copy-start.33 = (f32[2,176,128]{2,1,0:T(8,128)S(1)}, f32[2,176,128]{2,1,0:T(8,128)}, u32[]{:S(2)}) copy-start(f32[2,176,128]{2,1,0:T(8,128)} %copy-done.32) | copy-start | bytes 540676
  79.4 25.6 %copy-start.35 = (f32[1024,256]{1,0:T(8,128)S(1)}, f32[1024,256]{1,0:T(8,128)}, u32[]{:S(2)}) copy-start(f32[1024,256]{1,0:T(8,128)} %copy-done.34) | copy-start | bytes 3145732
  79.5 25.5 %collective-permute-start.3 = (bf16[1024,512]{1,0:T(8,128)(2,1)S(1)}, bf16[1024,512]{1,0:T(8,128)(2,1)S(1)}, u32[]{:S(2)}, u32[]{:S(2)}) collective-permute-start(bf16[1024,512]{1,0:T(8,128)(2,1)S(1)} %shard_map.84), channel_id=1, source_target_pairs={{0,16},{16,0},{1,17},{17,1},{2,18},{18,2},{3,19},{19,3},{4,20},{20... | collective-permute-start | bytes 3145736 | tf_op jit(solution)/shard_map/ppermute | solution.py:402
  80.3 27.8 %collective-permute-start.2 = (f32[2,176,128]{2,1,0:T(8,128)S(1)}, f32[2,176,128]{2,1,0:T(8,128)S(1)}, u32[]{:S(2)}, u32[]{:S(2)}) collective-permute-start(f32[2,176,128]{2,1,0:T(8,128)S(1)} %copy-done.38), channel_id=1, source_target_pairs={{8,0},{9,1},{10,2},{11,3},{12,4},{13,5},{14,6},{15,7},{24,16},{25,... | collective-permute-start | bytes 540680 | tf_op jit(solution)/shard_map/ppermute | solution.py:410
  110.4 18.3 %all-to-all-start.3 = ((bf16[8,2,2,16,1024]{4,3,2,1,0:T(8,128)(2,1)}), bf16[8,2,2,16,1024]{4,3,2,1,0:T(8,128)(2,1)S(1)}, u32[]{:S(2)}, u32[]{:S(2)}) async-start(bf16[8,2,2,16,1024]{4,3,2,1,0:T(8,128)(2,1)} %copy-done.15), calls=%async_computation.3 | async-start | bytes 2097152 | tf_op jit(solution)/shard_map/all_to_all | solution.py:397
  114.3 3.0 %collective-permute-start.4 = (bf16[1024,512]{1,0:T(8,128)(2,1)}, bf16[1024,512]{1,0:T(8,128)(2,1)S(1)}, u32[]{:S(2)}, u32[]{:S(2)}) collective-permute-start(bf16[1024,512]{1,0:T(8,128)(2,1)} %copy-done.8), channel_id=1, source_target_pairs={{0,1},{1,0},{2,3},{3,2},{4,5},{5,4},{6,7},{7,6},{8,9},{9,8},{10,11... | collective-permute-start | bytes 3145736 | tf_op jit(solution)/shard_map/ppermute | solution.py:470
  131.2 2.9 %copy-start.19 = (f32[2,176,128]{2,1,0:T(8,128)S(1)}, f32[2,176,128]{2,1,0:T(8,128)}, u32[]{:S(2)}) copy-start(f32[2,176,128]{2,1,0:T(8,128)} %copy-done.18) | copy-start | bytes 540676
  131.2 2.9 %copy-start.23 = (f32[1,128,1024]{2,1,0:T(8,128)S(1)}, f32[1,128,1024]{2,1,0:T(8,128)}, u32[]{:S(2)}) copy-start(f32[1,128,1024]{2,1,0:T(8,128)} %copy-done.22) | copy-start | bytes 1572868
  131.2 2.9 %copy-start.25 = (f32[1,128,1024]{2,1,0:T(8,128)S(1)}, f32[1,128,1024]{2,1,0:T(8,128)}, u32[]{:S(2)}) copy-start(f32[1,128,1024]{2,1,0:T(8,128)} %copy-done.24) | copy-start | bytes 1572868
  136.4 24.5 %all-to-all-start.5 = ((bf16[8,128,256]{2,1,0:T(8,128)(2,1)}), bf16[8,128,256]{2,1,0:T(8,128)(2,1)}, u32[]{:S(2)}, u32[]{:S(2)}) async-start(bf16[8,128,256]{2,1,0:T(8,128)(2,1)} %copy-done.17), calls=%async_computation.5 | async-start | bytes 1048576 | tf_op jit(solution)/shard_map/all_to_all | solution.py:397
  140.6 8.8 %collective-permute-start.5 = (bf16[256,512]{1,0:T(8,128)(2,1)}, bf16[256,512]{1,0:T(8,128)(2,1)S(1)}, u32[]{:S(2)}, u32[]{:S(2)}) collective-permute-start(bf16[256,512]{1,0:T(8,128)(2,1)} %copy-done.36), channel_id=1, source_target_pairs={{0,16},{16,0},{1,17},{17,1},{2,18},{18,2},{3,19},{19,3},{4,20},{20... | collective-permute-start | bytes 786440 | tf_op jit(solution)/shard_map/ppermute | solution.py:402
  150.4 5.5 %copy-start.5 = (f32[256,512]{1,0:T(8,128)S(1)}, f32[256,512]{1,0:T(8,128)}, u32[]{:S(2)}) copy-start(f32[256,512]{1,0:T(8,128)} %copy-done.3) | copy-start | bytes 1572868
  150.4 5.5 %copy-start.10 = (bf16[1024,512]{1,0:T(8,128)(2,1)S(1)}, bf16[1024,512]{1,0:T(8,128)(2,1)}, u32[]{:S(2)}) copy-start(bf16[1024,512]{1,0:T(8,128)(2,1)} %copy-done.8) | copy-start | bytes 3145732
  150.5 9.7 %collective-permute-start.6 = (bf16[128,512]{1,0:T(8,128)(2,1)S(1)}, bf16[128,512]{1,0:T(8,128)(2,1)S(1)}, u32[]{:S(2)}, u32[]{:S(2)}) collective-permute-start(bf16[128,512]{1,0:T(8,128)(2,1)S(1)} %get-tuple-element.35), channel_id=1, source_target_pairs={{0,8},{1,9},{2,10},{3,11},{4,12},{5,13},{6,14},{7,15},{8,0},{9,1},... | collective-permute-start | bytes 393224 | tf_op jit(solution)/shard_map/ppermute | solution.py:410
  (27 other events, 27.3 us)

commit v2 on v1

--- a/solution.py
+++ b/solution.py
@@ -13,6 +13,7 @@
 EPSILON = 1e-05
 GROUP = 8
 TILE = 256
+VMEM_LIMIT = 16 * 1024 * 1024
 PSI = 9 * F + 2 * F
 PSI_SCALE = (0.5,) + (1.0,) * 7 + (0.5,)
 
@@ -89,30 +90,73 @@
     return row >= lax.broadcasted_iota(jnp.int32, (tile, width), 1)
 
 
-def token_parts_kernel(at_ref, tokens_ref, *out_refs):
-    count = len(out_refs)
-    share = out_refs[0].shape[1]
+def run_copies(sems, pairs):
+    copies = [
+        pltpu.make_async_copy(source, target, sems.at[i])
+        for i, (source, target) in enumerate(pairs)
+    ]
+    for copy in copies:
+        copy.start()
+    for copy in copies:
+        copy.wait()
+
+
+def aligned(at, size):
+    return pl.ds(pl.multiple_of(at * size, size), size)
+
+
+def token_parts_kernel(at_ref, tokens_ref, *rest):
+    *out_refs, sems = rest
+    count, share = len(out_refs) + 1, out_refs[0].shape[1]
+    run_copies(
+        sems,
+        [
+            (tokens_ref.at[0, :, aligned(lax.rem(at_ref[0] + shift, count), share)], out_ref)
+            for shift, out_ref in enumerate(out_refs, 1)
+        ],
+    )
+
+
+def pack_heads_kernel(at_ref, values_ref, grad_ref, *rest):
+    *out_refs, sems = rest
+    width = out_refs[0].shape[2]
+    pairs = []
     for shift, out_ref in enumerate(out_refs):
-        owner = lax.rem(at_ref[0] + shift, count)
-        out_ref[...] = tokens_ref[0, :, pl.ds(pl.multiple_of(owner * share, share), share)]
-
-
-def pack_heads_kernel(values_ref, grad_ref, out_ref):
-    group, width = out_ref.shape[0], out_ref.shape[3]
-    for member in range(group):
-        cols = slice(member * width, (member + 1) * width)
-        out_ref[member, 0] = values_ref[0, :, cols]
-        out_ref[member, 1] = grad_ref[0, :, cols]
-
-
-def pack_tokens_kernel(depth, tokens_ref, out_ref):
-    group, rows = out_ref.shape[:2]
-    for member in range(group):
-        for part in range(rows // depth):
-            first = (part * group + member) * depth
-            out_ref[member, part * depth : (part + 1) * depth] = tokens_ref[
-                0, :, first : first + depth
-            ].T
+        cols = aligned(lax.rem(at_ref[0] + shift, len(out_refs)), width)
+        pairs.append((values_ref.at[0, :, cols], out_ref.at[0]))
+        pairs.append((grad_ref.at[0, :, cols], out_ref.at[1]))
+    run_copies(sems, pairs)
+
+
+def collect_heads_kernel(at_ref, *rest):
+    *part_refs, out_ref = rest
+    group = len(part_refs)
+    for shift, part_ref in enumerate(part_refs):
+        out_ref[lax.rem(at_ref[0] + group - shift, group)] = part_ref[...]
+
+
+def pack_tokens_kernel(depth, at_ref, tokens_ref, *rest):
+    *out_refs, sems = rest
+    group = len(out_refs)
+    pairs = []
+    for shift, out_ref in enumerate(out_refs):
+        member = lax.rem(at_ref[0] + shift, group)
+        for part in range(out_ref.shape[1] // depth):
+            pairs.append(
+                (
+                    tokens_ref.at[0, :, aligned(part * group + member, depth)],
+                    out_ref.at[:, part * depth : (part + 1) * depth],
+                )
+            )
+    run_copies(sems, pairs)
+
+
+def collect_tokens_kernel(at_ref, *rest):
+    *part_refs, out_ref = rest
+    group, tok = len(part_refs), part_refs[0].shape[0]
+    for shift, part_ref in enumerate(part_refs):
+        src = lax.rem(at_ref[0] + group - shift, group)
+        out_ref[:, aligned(src, tok)] = part_ref[...].T
 
 
 def projected_blocks(part, weight, out_ref):
@@ -125,7 +169,9 @@
                 out_ref[member, which, head] = projected[first : first + feat]
 
 
-def project_kernel(part_ref, weight_ref, out_ref):
+def project_kernel(at_ref, tokens_ref, weight_ref, out_ref, part_ref, sem):
+    share = part_ref.shape[1]
+    run_copies(sem, [(tokens_ref.at[0, :, aligned(at_ref[0], share)], part_ref)])
     projected_blocks(part_ref[...], weight_ref[...], out_ref)
 
 
@@ -139,9 +185,8 @@
         projected_blocks(part_ref[...], weight_ref[...], out_ref.at[owner])
 
 
-def weight_piece_kernel(at_ref, weight_ref, out_ref):
-    size = out_ref.shape[0]
-    out_ref[...] = weight_ref[pl.ds(pl.multiple_of(at_ref[0] * size, size), size), :]
+def weight_piece_kernel(at_ref, weight_ref, out_ref, sems):
+    run_copies(sems, [(weight_ref.at[aligned(at_ref[0], out_ref.shape[0])], out_ref)])
 
 
 def state_kernel(with_state, parts_ref, vg_ref, qk_ref, *state_refs):
@@ -260,40 +305,46 @@
 def rows_kernel(with_state, halves, qk_ref, vg_ref, *rest):
     rest = list(rest)
     suffix_ref = rest.pop(0) if with_state else None
-    rows_ref = rest[-1]
+    out_ref = rest[-1]
     blocks, tok = qk_ref.shape[0], qk_ref.shape[4]
+    heads = qk_ref.shape[2]
+    feats = 2 * heads * F
+    fold = blocks * tok // (heads * DH)
+    step = tok // fold
     head = 0
-    for grad_ref in rest[:halves]:
-        for at_head in range(grad_ref.shape[1]):
+    for grad_ref, grad_v_ref in zip(rest[:halves], rest[halves : 2 * halves]):
+        for at_head in range(grad_v_ref.shape[0]):
             grad_k = grad_ref[1, at_head]
+            grad_v = grad_v_ref[at_head]
             if with_state:
                 k = feature_major(qk_ref, 1, head)
                 v = rows_of(vg_ref, 0, head, 0, blocks * tok)
                 high, low = split(suffix_ref[head])
                 grad_k = grad_k + pull_psi(k, dot(high, v, NT) + dot(low, v, NT), False)
+                grad_v = grad_v + dot3(suffix_ref[head].T, psi(k, False))
             grad_q, grad_k = grad_ref[0, at_head].astype(bf16), grad_k.astype(bf16)
-            for member in range(rows_ref.shape[0]):
-                rows_ref[member, 0, head] = grad_q
-                rows_ref[member, 1, head] = grad_k
+            grad_v = grad_v.T.astype(bf16)
+            for member in range(blocks):
+                out_ref[member, head * F : (head + 1) * F] = grad_q
+                out_ref[member, (heads + head) * F : (heads + head + 1) * F] = grad_k
+                for i in range(fold):
+                    first = (i * heads + head) * DH
+                    row = member * tok + i * step
+                    out_ref[member, feats:, first : first + DH] = grad_v[row : row + step]
             head += 1
 
 
-def grad_values_kernel(with_state, halves, qk_ref, *rest):
-    rest = list(rest)
-    suffix_ref = rest.pop(0) if with_state else None
-    out_ref = rest[-1]
-    blocks, tok = qk_ref.shape[0], qk_ref.shape[4]
-    head = 0
-    for grad_ref in rest[:halves]:
-        for at_head in range(grad_ref.shape[0]):
-            grad_v = grad_ref[at_head]
-            if with_state:
-                feat = psi(feature_major(qk_ref, 1, head), False)
-                grad_v = grad_v + dot3(suffix_ref[head].T, feat)
-            grad_v = grad_v.T.astype(bf16)
-            for src in range(blocks):
-                out_ref[src, :, head * DH : (head + 1) * DH] = grad_v[src * tok : (src + 1) * tok]
-            head += 1
+def unpack_values_kernel(in_ref, out_ref):
+    group, rows, length = in_ref.shape
+    width = out_ref.shape[2] // group
+    tok = out_ref.shape[1]
+    fold = length // width
+    step = tok // fold
+    for member in range(group):
+        for i in range(fold):
+            out_ref[0, i * step : (i + 1) * step, member * width : (member + 1) * width] = in_ref[
+                member, rows - step :, i * width : (i + 1) * width
+            ]
 
 
 def unpack_heads_kernel(in_ref, out_ref):
@@ -302,14 +353,13 @@
         out_ref[0, :, member * width : (member + 1) * width] = in_ref[member]
 
 
-def all_rows(rows_ref, cols):
-    group, _, heads = rows_ref.shape[:3]
+def all_rows(rows_ref, count, cols):
+    half = count // rows_ref.shape[0] // 2
     return jnp.concatenate(
         [
-            rows_ref[src, which, head, :, cols]
+            rows_ref[src, which * half : (which + 1) * half, cols]
             for which in range(2)
-            for src in range(group)
-            for head in range(heads)
+            for src in range(rows_ref.shape[0])
         ],
         axis=0,
     )
@@ -317,8 +367,8 @@
 
 def product_kernel(at_ref, rows_ref, tokens_ref, *rest):
     *part_refs, total_ref = rest
-    tokens = jnp.concatenate([tokens_ref[src] for src in range(tokens_ref.shape[0])], axis=1)
-    total_ref[...] = dot(tokens, all_rows(rows_ref, slice(None)), NT)
+    count = total_ref.shape[1]
+    total_ref[...] = dot(tokens_ref[...], all_rows(rows_ref, count, slice(None)), NT)
     count = len(part_refs)
     size = part_refs[0].shape[0]
     for shift, part_ref in enumerate(part_refs):
@@ -346,7 +396,7 @@
     *weight_refs, out_ref = rest
     tok = out_ref.shape[1]
     start = pl.multiple_of(at_ref[0] * tok, tok)
-    rows = all_rows(rows_ref, pl.ds(start, tok)).T
+    rows = all_rows(rows_ref, weight_refs[0].shape[1], pl.ds(start, tok)).T
     for i, weight_ref in enumerate(weight_refs):
         size = weight_ref.shape[0]
         first = pl.multiple_of(at_ref[1 + i], size)
@@ -358,22 +408,30 @@
 ANYWHERE = pl.BlockSpec(memory_space=pl.ANY)
 
 
-def call(body, out_shapes, flops, *operands, scalars=(), after=(), scratch=()):
+def call(
+    body, outs, *operands, scalars=(), after=(), scratch=(), far_in=0, far_out=False, copies=0
+):
     at = [jnp.stack([jnp.int32(s) for s in scalars])] if scalars else []
     count = len(at) + len(operands)
 
     def kernel(*refs):
-        body(*refs[:count], *refs[count + len(after) :])
-
-    return pl.pallas_call(
+        ins, rest = refs[:count], refs[count + len(after) :]
+        body(*ins, *rest[: len(outs)], *rest[len(outs) + 1 :])
+        rest[len(outs)][...] = jnp.zeros((8, 128), f32)
+
+    *results, token = pl.pallas_call(
         kernel,
-        out_shape=[jax.ShapeDtypeStruct(shape, kind) for shape, kind in out_shapes],
-        in_specs=[SMEM] * len(at) + [VMEM] * len(operands) + [ANYWHERE] * len(after),
-        out_specs=[VMEM] * len(out_shapes),
-        scratch_shapes=scratch,
-        compiler_params=pltpu.CompilerParams(vmem_limit_bytes=24 * 1024 * 1024),
-        cost_estimate=pl.CostEstimate(flops=flops, bytes_accessed=4 << 20, transcendentals=0),
+        out_shape=[jax.ShapeDtypeStruct(shape, kind) for shape, kind in [*outs, ((8, 128), f32)]],
+        in_specs=[SMEM] * len(at)
+        + [ANYWHERE] * far_in
+        + [VMEM] * (len(operands) - far_in)
+        + [ANYWHERE] * len(after),
+        out_specs=[ANYWHERE if far_out else VMEM] * len(outs) + [VMEM],
+        scratch_shapes=[*scratch] + [pltpu.SemaphoreType.DMA((copies,))] * (copies > 0),
+        compiler_params=pltpu.CompilerParams(vmem_limit_bytes=VMEM_LIMIT),
+        cost_estimate=pl.CostEstimate(flops=0, bytes_accessed=0, transcendentals=0),
     )(*at, *operands, *after)
+    return results, token
 
 
 def local(dp_size, ctx_size, tokens, proj_weight, values, grad_out):
@@ -401,6 +459,10 @@
     def to_dp(x, shift):
         return lax.ppermute(x, "dp", [(i, (i + shift) % dp_size) for i in range(dp_size)])
 
+    def to_member(x, shift):
+        pairs = [(i, i - i % group + (i + shift) % group) for i in range(ctx_size)]
+        return lax.ppermute(x, "ctx", pairs)
+
     def to_run(x, shift, wrap):
         pairs = [
             (i, (i + shift * group) % ctx_size)
@@ -410,35 +472,79 @@
         return lax.ppermute(x, "ctx", pairs)
 
     qk_shape = ((group, 2, heads, F, tok), f32)
-    pairs = length * (length + TILE) // 2
-    state_flops = 4 * heads * length * PSI * DH
     state_shape = ((heads, PSI, DH), f32)
     blocks_shape = ((group, tok, heads * DH), bf16)
-    project_flops = 2 * tok * share * cols
-
-    own, *parts = call(
-        token_parts_kernel, [((tok, share), bf16)] * dp_size, 0, tokens, scalars=(dp_at,)
+    rows_shape = ((length, heads * DH), f32)
+
+    parts, token = call(
+        token_parts_kernel,
+        [((tok, share), bf16)] * (dp_size - 1),
+        tokens,
+        scalars=(dp_at,),
+        far_in=1,
+        far_out=True,
+        copies=dp_size - 1,
     )
     arrived = [to_dp(part, shift) for shift, part in enumerate(parts, 1)]
-    (vg,) = call(
+    parts, token = call(
         pack_heads_kernel,
-        [((group, 2, tok, heads * DH), bf16)],
-        0,
+        [((2, tok, heads * DH), bf16)] * group,
         values,
         grad_out,
-        after=parts[:1],
-    )
-    vg = exchange(vg)
-    (projected,) = call(project_kernel, [qk_shape], project_flops, own, proj_weight)
-    (projected,) = call(
+        scalars=(member,),
+        after=(token,),
+        far_in=2,
+        far_out=True,
+        copies=2 * group,
+    )
+    parts = parts[:1] + [to_member(part, shift) for shift, part in enumerate(parts[1:], 1)]
+    (vg,), vg_token = call(
+        collect_heads_kernel,
+        [((group, 2, tok, heads * DH), bf16)],
+        *parts,
+        scalars=(member,),
+    )
+    (projected,), token = call(
+        project_kernel,
+        [qk_shape],
+        tokens,
+        proj_weight,
+        scalars=(dp_at,),
+        after=(token,),
+        far_in=1,
+        copies=1,
+        scratch=[pltpu.VMEM((tok, share), bf16)],
+    )
+    part_shape = (tok, dp_size * runs * depth)
+    if depth % 128 == 0:
+        parts, token = call(
+            functools.partial(pack_tokens_kernel, depth),
+            [(part_shape, bf16)] * group,
+            tokens,
+            scalars=(member,),
+            after=(token,),
+            far_in=1,
+            far_out=True,
+            copies=group * dp_size * runs,
+        )
+    else:
+        blocks = tokens[0].reshape(tok, dp_size * runs, group, depth).transpose(2, 0, 1, 3)
+        parts = [
+            lax.dynamic_index_in_dim(blocks, (member + shift) % group, 0, keepdims=False).reshape(
+                part_shape
+            )
+            for shift in range(group)
+        ]
+    token_parts = parts[:1] + [to_member(part, shift) for shift, part in enumerate(parts[1:], 1)]
+
+    (projected,), token = call(
         project_rest_kernel,
         [((dp_size,) + qk_shape[0], f32)],
-        project_flops,
         projected,
         proj_weight,
         *arrived,
         scalars=(dp_at,),
-        after=(vg,),
+        after=(vg_token,),
     )
     qk_parts = lax.all_to_all(
         projected.reshape((dp_size * group,) + qk_shape[0][1:]),
@@ -452,13 +558,15 @@
     pair = 2 if ctx_size % 2 == 0 else 1
     parity = ctx_at % pair
     piece = share // pair
-    (mine,) = call(
+    (mine,), token = call(
         weight_piece_kernel,
         [((piece, cols), bf16)],
-        0,
         proj_weight,
         scalars=(parity,),
-        after=(projected,),
+        after=(token,),
+        far_in=1,
+        far_out=True,
+        copies=1,
     )
     fetched = [to_dp(mine, shift) for shift in range(1, dp_size)]
     weights, firsts = [proj_weight], [dp_at * share]
@@ -470,122 +578,99 @@
             weights.append(lax.ppermute(half, "ctx", [(i, i ^ 1) for i in range(ctx_size)]))
             firsts.append(base + (1 - parity) * piece)
 
-    qk, *state = call(
+    (qk, *state), token = call(
         functools.partial(state_kernel, with_state),
         [qk_shape] + [state_shape] * with_state,
-        state_flops,
         qk_parts,
         vg,
     )
-    if depth % 128 == 0:
-        (token_cols,) = call(
-            functools.partial(pack_tokens_kernel, depth),
-            [((group, dp_size * runs * depth, tok), bf16)],
-            0,
-            tokens,
-            after=(qk,),
-        )
-    else:
-        token_cols = (
-            tokens[0]
-            .reshape(tok, dp_size * runs, group, depth)
-            .transpose(2, 1, 3, 0)
-            .reshape(group, dp_size * runs * depth, tok)
-        )
-    token_cols = exchange(token_cols)
+    (token_cols,), tokens_token = call(
+        collect_tokens_kernel,
+        [(part_shape[1:] + (length,), bf16)],
+        *token_parts,
+        scalars=(member,),
+        after=(token,),
+    )
 
     prefix, suffix = (), ()
     if with_state:
         prefix = (sum(to_run(state[0], shift, False) for shift in range(1, runs)),)
-    (numerator,) = call(
-        numerator_kernel, [((length, heads * DH), f32)], heads * pairs * 2 * 512, qk, vg
-    )
-    attended, grad_num, *carried = call(
+    (numerator,), token = call(numerator_kernel, [rows_shape], qk, vg)
+    (attended, grad_num, *carried), token = call(
         functools.partial(normalize_kernel, with_state),
-        [blocks_shape, ((length, heads * DH), f32)] + [state_shape] * with_state,
-        2 * state_flops,
+        [blocks_shape, rows_shape] + [state_shape] * with_state,
         qk,
         vg,
         numerator,
         *prefix,
+        after=(tokens_token,),
     )
     if with_state:
         suffix = (sum(to_run(carried[0], -shift, False) for shift in range(1, runs)),)
     grad_qks, grad_vs = [], []
     for first in range(0, heads, max(1, heads // 2)):
         count = max(1, heads // 2)
-        result = call(
+        result, token = call(
             functools.partial(backward_kernel, with_state, first),
             [((2, count, F, length), f32), ((count, DH, length), f32)]
             + [blocks_shape] * (first == 0),
-            count * pairs * 2 * 1024,
             qk,
             vg,
             grad_num,
             *prefix,
             *([attended] if first == 0 else []),
-            after=[] if first == 0 else [grad_qks[0], *fetched],
+            after=[half[:8, :128] for half in fetched] if first == 0 else [token],
         )
         grad_qks.append(result[0])
         grad_vs.append(result[1])
         if first == 0:
             attended = exchange(result[2])
-    (rows,) = call(
+    (rows,), token = call(
         functools.partial(rows_kernel, with_state, len(grad_qks)),
-        [((group, 2, heads, F, length), bf16)],
-        state_flops,
+        [((group, 2 * heads * F + tok * heads * DH // length, length), bf16)],
         qk,
         vg,
         *suffix,
         *grad_qks,
+        *grad_vs,
     )
     rows = exchange(rows)
-
-    own, *parts = call(
+    (attended,), attended_token = call(
+        unpack_heads_kernel, [((1, tok, H * DH), bf16)], attended, after=(token,)
+    )
+
+    (own, *parts), token = call(
         product_kernel,
         [((runs * depth, cols), f32)] + [((runs * depth, cols), bf16)] * (dp_size - 1),
-        2 * dp_size * runs * depth * length * cols,
         rows,
         token_cols,
         scalars=(dp_at,),
-        after=weights[1:] + [attended],
+        after=(attended_token,),
         scratch=[pltpu.VMEM((dp_size * runs * depth, cols), f32)],
     )
     parts = [to_dp(part, shift) for shift, part in enumerate(parts, 1)]
-    (grad_values,) = call(
-        functools.partial(grad_values_kernel, with_state, len(grad_vs)),
-        [blocks_shape],
-        state_flops,
-        qk,
-        *suffix,
-        *grad_vs,
-        after=(own,),
-    )
-    grad_values = exchange(grad_values)
-    (grad_tokens,) = call(
+    (grad_tokens,), tokens_token = call(
         grad_tokens_kernel,
         [((1, tok, width), bf16)],
-        2 * tok * width * cols,
         rows,
         *weights,
         scalars=(member, *firsts),
-        after=(own,),
-    )
-    grad_proj, *parts = call(
+        after=(token,),
+    )
+    (grad_proj, *parts), token = call(
         functools.partial(run_sum_kernel, len(parts)),
         [((depth, cols), f32)] + [((depth, cols), bf16)] * (runs - 1),
-        0,
         own,
         *parts,
         scalars=(run_at,),
+        after=(tokens_token,),
         scratch=[pltpu.VMEM((runs * depth, cols), f32)],
+    )
+    (grad_values,), token = call(
+        unpack_values_kernel, [((1, tok, H * DH), bf16)], rows, after=(token,)
     )
     for shift, part in enumerate(parts, 1):
         grad_proj = grad_proj + to_run(part, shift, True).astype(f32)
-    attended, grad_values = [
-        call(unpack_heads_kernel, [((1, tok, H * DH), bf16)], 0, blocks)[0]
-        for blocks in (attended, grad_values)
-    ]
     return (attended, grad_tokens, grad_values, grad_proj)
 
 

time: 164 us -> 135 us (0.82)
  waiting for transfers between devices: 62.4 us -> 37.1 us
  blocking collectives: 15.2 us -> 0 us
  Pallas kernels: 22.8 us -> 33.3 us
  starting transfers between devices: 36.5 us -> 45.7 us
  local copies, waits for them, and re-layouts: 24.2 us -> 16.4 us
    ppermute x3, waiting for transfers between devices: 42.7 us -> 3.3 us  [to_dp(): lax.ppermute(x, 'dp', [(i, (i + shift) % dp_size) for i in range(dp_size)])]
    ppermute x0 -> x14, starting transfers between devices: none -> 17.2 us  [to_member(): return lax.ppermute(x, 'ctx', pairs)]
    all_to_all x1 -> x0, blocking collectives: 15.2 us -> none  [local(): lax.all_to_all(projected.reshape((dp_size * group,) + qk_shape[0][1:]), (...]
    all_to_all x5 -> x2, starting transfers between devices: 23.7 us -> 12.4 us  [exchange(): lax.all_to_all(x, 'ctx', split_axis=0, concat_axis=0, tiled=True, axis_in...]
    pallas_call x18 -> x19, Pallas kernels: 22.8 us -> 33.3 us  [call(): pl.pallas_call(kernel, out_shape=[jax.ShapeDtypeStruct(shape, kind) for s...]
    ppermute x3, waiting for transfers between devices: 0.22 us -> 9.01 us  [to_run(): return lax.ppermute(x, 'ctx', pairs)]
    unnamed x78 -> x52, local copies, waits for them, and re-layouts: 24.2 us -> 15.7 us
    ppermute x0 -> x14, waiting for transfers between devices: none -> 7.01 us  [to_member(): return lax.ppermute(x, 'ctx', pairs)]
  transfers between devices with their start and end apart: 12 -> 24, of which waited for: 7 -> 12; matrix products, arithmetic and copies ran while one was open for 0% -> 1% of each run, Pallas kernels for 7% -> 19%
where the time goes in v2:
time: 135 us; the launch traced here: 134 us
  starting transfers between devices  45.7 us (34%)
  waiting for transfers between devices  37.1 us (27%)
  Pallas kernels  33.3 us (25%)
  local copies, waits for them, and re-layouts  16.4 us (12%)
    pallas_call x19, Pallas kernels, call(): pl.pallas_call(kernel, out_shape=[jax.ShapeDtypeStruct(shape, kind) for s...  33.3 us
    all_to_all x2, waiting for transfers between devices, exchange(): lax.all_to_all(x, 'ctx', split_axis=0, concat_axis=0, tiled=True, axis_in...  17.8 us
    ppermute x14, starting transfers between devices, to_member(): return lax.ppermute(x, 'ctx', pairs)  17.2 us
    unnamed x52, local copies, waits for them, and re-layouts  15.7 us
    all_to_all x2, starting transfers between devices, exchange(): lax.all_to_all(x, 'ctx', split_axis=0, concat_axis=0, tiled=True, axis_in...  12.4 us
    ppermute x3, waiting for transfers between devices, to_run(): return lax.ppermute(x, 'ctx', pairs)  9.01 us
    ppermute x14, waiting for transfers between devices, to_member(): return lax.ppermute(x, 'ctx', pairs)  7.01 us
    ppermute x3, starting transfers between devices, to_run(): return lax.ppermute(x, 'ctx', pairs)  5.86 us
  transfers between devices with their start and end apart: 24, of which 12 were waited for; matrix products, arithmetic and copies ran while one was open for 1% of the time, Pallas kernels for 19%

profile of v2, /device:TPU:0, one launch (start us, length us, event | category | flops | bytes accessed | tf_op | source)
XLA Modules:
  0.0 134.3 jit_solution(9297804795849052663)
XLA Ops:
  2.8 3.0 %collective-permute-start = (bf16[128,2048]{1,0:T(8,128)(2,1)}, bf16[128,2048]{1,0:T(8,128)(2,1)}, u32[]{:S(2)}, u32[]{:S(2)}) collective-permute-start(bf16[128,2048]{1,0:T(8,128)(2,1)} %get-tuple-element.61), channel_id=1, source_target_pairs={{0,16},{16,0},{1,17},{17,1},{2,18},{18,2},{3,19},{19,3},{4,20},{20... | collective-permute-start | bytes 1572872 | tf_op jit(solution)/shard_map/ppermute | solution.py:460
  9.9 2.4 %collective-permute-start.3 = (bf16[2,128,256]{2,1,0:T(8,128)(2,1)S(1)}, bf16[2,128,256]{2,1,0:T(8,128)(2,1)S(1)}, u32[]{:S(2)}, u32[]{:S(2)}) collective-permute-start(bf16[2,128,256]{2,1,0:T(8,128)(2,1)S(1)} %get-tuple-element.65), channel_id=1, source_target_pairs={{0,3},{1,4},{2,5},{3,6},{4,7},{5,0},{6,1},{7,2},{8,11},{9,12},{10,... | collective-permute-start | bytes 393224 | tf_op jit(solution)/shard_map/ppermute | solution.py:464
  17.2 2.2 %collective-permute-start.7 = (bf16[2,128,256]{2,1,0:T(8,128)(2,1)S(1)}, bf16[2,128,256]{2,1,0:T(8,128)(2,1)S(1)}, u32[]{:S(2)}, u32[]{:S(2)}) collective-permute-start(bf16[2,128,256]{2,1,0:T(8,128)(2,1)S(1)} %get-tuple-element.69), channel_id=1, source_target_pairs={{0,7},{1,0},{2,1},{3,2},{4,3},{5,4},{6,5},{7,6},{8,15},{9,8},{10,9... | collective-permute-start | bytes 393224 | tf_op jit(solution)/shard_map/ppermute | solution.py:464
  25.7 4.2 %all-to-all-start = ((f32[16,2,2,16,128]{4,3,2,1,0:T(8,128)}), f32[16,2,2,16,128]{4,3,2,1,0:T(8,128)}, u32[]{:S(2)}, u32[]{:S(2)}) async-start(f32[16,2,2,16,128]{4,3,2,1,0:T(8,128)} %bitcast.9), calls=%async_computation | async-start | bytes 1048576 | tf_op jit(solution)/shard_map/all_to_all | solution.py:549
  31.6 1.9 %collective-permute-start.16 = (bf16[1024,512]{1,0:T(8,128)(2,1)}, bf16[1024,512]{1,0:T(8,128)(2,1)}, u32[]{:S(2)}, u32[]{:S(2)}) collective-permute-start(bf16[1024,512]{1,0:T(8,128)(2,1)} %get-tuple-element.90), channel_id=1, source_target_pairs={{0,16},{16,0},{1,17},{17,1},{2,18},{18,2},{3,19},{19,3},{4,20},{20... | collective-permute-start | bytes 3145736 | tf_op jit(solution)/shard_map/ppermute | solution.py:460
  33.5 1.7 %shard_map.82 = (bf16[128,512]{1,0:T(8,128)(2,1)S(1)}, bf16[128,512]{1,0:T(8,128)(2,1)}, bf16[128,512]{1,0:T(8,128)(2,1)}, bf16[128,512]{1,0:T(8,128)(2,1)}, bf1...) custom-call(s32[1]{0:T(128)} %bitcast.1.refs_0_, ...), custom_call_target="tpu_custom_call" | custom-call | tf_op jit(solution)/shard_map/pallas_call | solution.py:422
  38.7 2.3 %collective-permute-start.11 = (bf16[128,512]{1,0:T(8,128)(2,1)}, bf16[128,512]{1,0:T(8,128)(2,1)}, u32[]{:S(2)}, u32[]{:S(2)}) collective-permute-start(bf16[128,512]{1,0:T(8,128)(2,1)} %get-tuple-element.80), channel_id=1, source_target_pairs={{0,3},{1,4},{2,5},{3,6},{4,7},{5,0},{6,1},{7,2},{8,11},{9,12},{10,... | collective-permute-start | bytes 393224 | tf_op jit(solution)/shard_map/ppermute | solution.py:464
  43.6 4.5 %collective-permute-start.8 = (f32[2,176,128]{2,1,0:T(8,128)S(1)}, f32[2,176,128]{2,1,0:T(8,128)S(1)}, u32[]{:S(2)}, u32[]{:S(2)}) collective-permute-start(f32[2,176,128]{2,1,0:T(8,128)S(1)} %get-tuple-element.75), channel_id=1, source_target_pairs={{0,8},{1,9},{2,10},{3,11},{4,12},{5,13},{6,14},{7,15},{16,24},{17,... | collective-permute-start | bytes 540680 | tf_op jit(solution)/shard_map/ppermute | solution.py:472
  48.2 2.5 %collective-permute-start.14 = (bf16[128,512]{1,0:T(8,128)(2,1)S(1)}, bf16[128,512]{1,0:T(8,128)(2,1)S(1)}, u32[]{:S(2)}, u32[]{:S(2)}) collective-permute-start(bf16[128,512]{1,0:T(8,128)(2,1)S(1)} %copy-done.23), channel_id=1, source_target_pairs={{0,6},{1,7},{2,0},{3,1},{4,2},{5,3},{6,4},{7,5},{8,14},{9,15},{10,... | collective-permute-start | bytes 393224 | tf_op jit(solution)/shard_map/ppermute | solution.py:464
  50.7 2.0 %collective-permute-start.15 = (bf16[128,512]{1,0:T(8,128)(2,1)S(1)}, bf16[128,512]{1,0:T(8,128)(2,1)S(1)}, u32[]{:S(2)}, u32[]{:S(2)}) collective-permute-start(bf16[128,512]{1,0:T(8,128)(2,1)S(1)} %copy-done.21), channel_id=1, source_target_pairs={{0,7},{1,0},{2,1},{3,2},{4,3},{5,4},{6,5},{7,6},{8,15},{9,8},{10,9... | collective-permute-start | bytes 393224 | tf_op jit(solution)/shard_map/ppermute | solution.py:464
  52.7 3.6 %shard_map.81 = (f32[1024,256]{1,0:T(8,128)S(1)}, f32[8,128]{1,0:T(8,128)}) custom-call(f32[8,2,2,16,128]{4,3,2,1,0:T(8,128)S(1)} %get-tuple-element.73.refs_0_, bf16[8,2,128,256]{3,2,1,0:T(8,128)(2,1)S(1)} %get-tuple-element.72.refs_1_), custom_call_target="tpu_custom_call" | custom-call | tf_op jit(solution)/shard_map/pallas_call | solution.py:422
  61.9 2.5 %shard_map.84 = (bf16[8,128,256]{2,1,0:T(8,128)(2,1)S(1)}, f32[1024,256]{1,0:T(8,128)S(1)}, f32[2,176,128]{2,1,0:T(8,128)S(1)}, f32[8,128]{1,0:T(8,128)}) custom-call(f32[8,2,2,16,128]{4,3,2,1,0:T(8,128)S(1)} %get-tuple-element.73.refs_0_, bf16[8,2,128,256]{3,2,1,0:T(8,128)(2,1)S(1)} %get-tuple-element.72.refs_1_, ...), custom_call_target="tpu_custom_call" | custom-call | tf_op jit(solution)/shard_map/pallas_call | solution.py:422
  65.1 2.3 %shard_map.86 = (f32[2,1,16,1024]{3,2,1,0:T(8,128)S(1)}, f32[1,128,1024]{2,1,0:T(8,128)S(1)}, bf16[8,128,256]{2,1,0:T(8,128)(2,1)S(1)}, f32[8,128]{1,0:T(8,128)S(1)}) custom-call(f32[8,2,2,16,128]{4,3,2,1,0:T(8,128)S(1)} %get-tuple-element.73.refs_0_, bf16[8,2,128,256]{3,2,1,0:T(8,128)(2,1)S(1)} %get-tuple-element.72.refs_1_, ...), custom_call_target="tpu_custom_call" | custom-call | tf_op jit(solution)/shard_map/pallas_call | solution.py:422
  69.9 4.1 %all-to-all-start.1 = ((bf16[8,128,256]{2,1,0:T(8,128)(2,1)}), bf16[8,128,256]{2,1,0:T(8,128)(2,1)}, u32[]{:S(2)}, u32[]{:S(2)}) async-start(bf16[8,128,256]{2,1,0:T(8,128)(2,1)} %copy-done.14), calls=%async_computation.1 | async-start | bytes 1048576 | tf_op jit(solution)/shard_map/all_to_all | solution.py:455
  77.5 2.7 %shard_map.87 = (f32[2,1,16,1024]{3,2,1,0:T(8,128)S(1)}, f32[1,128,1024]{2,1,0:T(8,128)S(1)}, f32[8,128]{1,0:T(8,128)}) custom-call(f32[8,2,2,16,128]{4,3,2,1,0:T(8,128)S(1)} %get-tuple-element.73.refs_0_, bf16[8,2,128,256]{3,2,1,0:T(8,128)(2,1)S(1)} %get-tuple-element.72.refs_1_, f32[1024,256]{1,0:T(8,128)S(1)} %copy-done.5, f32[2,176,128]{2,1,0:T(8,128)S(1)} %copy-done.7, ...), custom_call_target="tpu_custom_call" | custom-call | tf_op jit(solution)/shard_map/pallas_call | solution.py:422
  80.3 4.0 %collective-permute-done.17.refs_2_ = f32[2,176,128]{2,1,0:T(8,128)S(1)} collective-permute-done((f32[2,176,128]{2,1,0:T(8,128)}, f32[2,176,128]{2,1,0:T(8,128)S(1)}, u32[]{:S(2)}, u32[]{:S(2)}) %collective-permute-start.17) | collective-permute-done | bytes 180256 | tf_op jit(solution)/shard_map/ppermute | solution.py:472
  86.8 8.2 %all-to-all-start.2 = ((bf16[8,96,1024]{2,1,0:T(8,128)(2,1)}), bf16[8,96,1024]{2,1,0:T(8,128)(2,1)}, u32[]{:S(2)}, u32[]{:S(2)}) async-start(bf16[8,96,1024]{2,1,0:T(8,128)(2,1)} %copy-done.8), calls=%async_computation.2 | async-start | bytes 3145728 | tf_op jit(solution)/shard_map/all_to_all | solution.py:455
  95.5 1.9 %shard_map.89 = (bf16[1,128,2048]{2,1,0:T(8,128)(2,1)}, f32[8,128]{1,0:T(8,128)S(1)}) custom-call(bf16[8,128,256]{2,1,0:T(8,128)(2,1)} %all-to-all-done.1.refs_0_, f32[8,128]{1,0:T(8,128)S(1)} %get-tuple-element.98.refs_1_), custom_call_target="tpu_custom_call" | custom-call | tf_op jit(solution)/shard_map/pallas_call | solution.py:422
  97.4 17.8 %all-to-all-done.2.refs_1_.refs_0_ = bf16[8,96,1024]{2,1,0:T(8,128)(2,1)} async-done(((bf16[8,96,1024]{2,1,0:T(8,128)(2,1)}), bf16[8,96,1024]{2,1,0:T(8,128)(2,1)}, u32[]{:S(2)}, u32[]{:S(2)}) %all-to-all-start.2) | async-done | bytes 1572896 | tf_op jit(solution)/shard_map/all_to_all | solution.py:455
  115.2 2.3 %shard_map.90 = (f32[256,512]{1,0:T(8,128)S(1)}, bf16[256,512]{1,0:T(8,128)(2,1)S(1)}, f32[8,128]{1,0:T(8,128)S(1)}) custom-call(s32[1]{0:T(128)} %bitcast.refs_0_, bf16[8,96,1024]{2,1,0:T(8,128)(2,1)} %all-to-all-done.2.refs_1_.refs_0_, bf16[512,1024]{1,0:T(8,128)(2,1)S(1)} %copy-done.10, f32[8,128]{1,0:T(8,128)S(1)} %get-tuple-element.102.refs_3_), custom_call_target="tpu_custom_call" | custom-call | tf_op jit(solution)/shard_map/pallas_call | solution.py:422
  118.9 4.5 %shard_map.91 = (bf16[1,128,4096]{2,1,0:T(8,128)(2,1)}, f32[8,128]{1,0:T(8,128)S(1)}) custom-call(s32[4]{0:T(128)S(1)} %pad_add_fusion.refs_0_, bf16[8,96,1024]{2,1,0:T(8,128)(2,1)} %all-to-all-done.2.refs_1_.refs_0_, bf16[2048,512]{1,0:T(8,128)(2,1)S(1)} %copy-done, bf16[1024,512]{1,0:T(8,128)(2,1)} %collective-permute-done.16.refs_3_, ...), custom_call_target="tpu_custom_call" | custom-call | tf_op jit(solution)/shard_map/pallas_call | solution.py:422
  123.5 2.7 %collective-permute-done.19.refs_2_ = bf16[256,512]{1,0:T(8,128)(2,1)S(1)} collective-permute-done((bf16[256,512]{1,0:T(8,128)(2,1)S(1)}, bf16[256,512]{1,0:T(8,128)(2,1)S(1)}, u32[]{:S(2)}, u32[]{:S(2)}) %collective-permute-start.19) | collective-permute-done | bytes 262176 | tf_op jit(solution)/shard_map/ppermute | solution.py:460
  126.3 2.3 %shard_map.93 = (bf16[1,128,2048]{2,1,0:T(8,128)(2,1)}, f32[8,128]{1,0:T(8,128)}) custom-call(bf16[8,96,1024]{2,1,0:T(8,128)(2,1)} %all-to-all-done.2.refs_1_.refs_0_, f32[8,128]{1,0:T(8,128)S(1)} %get-tuple-element.108.refs_1_), custom_call_target="tpu_custom_call" | custom-call | tf_op jit(solution)/shard_map/pallas_call | solution.py:422
  128.6 5.0 %collective-permute-done.20 = bf16[128,512]{1,0:T(8,128)(2,1)S(1)} collective-permute-done((bf16[128,512]{1,0:T(8,128)(2,1)S(1)}, bf16[128,512]{1,0:T(8,128)(2,1)S(1)}, u32[]{:S(2)}, u32[]{:S(2)}) %collective-permute-start.20) | collective-permute-done | bytes 131104 | tf_op jit(solution)/shard_map/ppermute | solution.py:472
  (98 shorter events, 42.6 us)
Async XLA Ops:
  2.8 20.5 %collective-permute-start = (bf16[128,2048]{1,0:T(8,128)(2,1)}, bf16[128,2048]{1,0:T(8,128)(2,1)}, u32[]{:S(2)}, u32[]{:S(2)}) collective-permute-start(bf16[128,2048]{1,0:T(8,128)(2,1)} %get-tuple-element.61), channel_id=1, source_target_pairs={{0,16},{16,0},{1,17},{17,1},{2,18},{18,2},{3,19},{19,3},{4,20},{20... | collective-permute-start | bytes 1572872 | tf_op jit(solution)/shard_map/ppermute | solution.py:460
  8.3 6.2 %collective-permute-start.1 = (bf16[2,128,256]{2,1,0:T(8,128)(2,1)S(1)}, bf16[2,128,256]{2,1,0:T(8,128)(2,1)S(1)}, u32[]{:S(2)}, u32[]{:S(2)}) collective-permute-start(bf16[2,128,256]{2,1,0:T(8,128)(2,1)S(1)} %get-tuple-element.63), channel_id=1, source_target_pairs={{0,1},{1,2},{2,3},{3,4},{4,5},{5,6},{6,7},{7,0},{8,9},{9,10},{10,1... | collective-permute-start | bytes 393224 | tf_op jit(solution)/shard_map/ppermute | solution.py:464
  8.3 7.3 %collective-permute-start.2 = (bf16[2,128,256]{2,1,0:T(8,128)(2,1)S(1)}, bf16[2,128,256]{2,1,0:T(8,128)(2,1)S(1)}, u32[]{:S(2)}, u32[]{:S(2)}) collective-permute-start(bf16[2,128,256]{2,1,0:T(8,128)(2,1)S(1)} %get-tuple-element.64), channel_id=1, source_target_pairs={{0,2},{1,3},{2,4},{3,5},{4,6},{5,7},{6,0},{7,1},{8,10},{9,11},{10,... | collective-permute-start | bytes 393224 | tf_op jit(solution)/shard_map/ppermute | solution.py:464
  9.9 7.3 %collective-permute-start.3 = (bf16[2,128,256]{2,1,0:T(8,128)(2,1)S(1)}, bf16[2,128,256]{2,1,0:T(8,128)(2,1)S(1)}, u32[]{:S(2)}, u32[]{:S(2)}) collective-permute-start(bf16[2,128,256]{2,1,0:T(8,128)(2,1)S(1)} %get-tuple-element.65), channel_id=1, source_target_pairs={{0,3},{1,4},{2,5},{3,6},{4,7},{5,0},{6,1},{7,2},{8,11},{9,12},{10,... | collective-permute-start | bytes 393224 | tf_op jit(solution)/shard_map/ppermute | solution.py:464
  12.3 8.9 %collective-permute-start.4 = (bf16[2,128,256]{2,1,0:T(8,128)(2,1)S(1)}, bf16[2,128,256]{2,1,0:T(8,128)(2,1)S(1)}, u32[]{:S(2)}, u32[]{:S(2)}) collective-permute-start(bf16[2,128,256]{2,1,0:T(8,128)(2,1)S(1)} %get-tuple-element.66), channel_id=1, source_target_pairs={{0,4},{1,5},{2,6},{3,7},{4,0},{5,1},{6,2},{7,3},{8,12},{9,13},{10,... | collective-permute-start | bytes 393224 | tf_op jit(solution)/shard_map/ppermute | solution.py:464
  14.4 6.8 %collective-permute-start.5 = (bf16[2,128,256]{2,1,0:T(8,128)(2,1)S(1)}, bf16[2,128,256]{2,1,0:T(8,128)(2,1)S(1)}, u32[]{:S(2)}, u32[]{:S(2)}) collective-permute-start(bf16[2,128,256]{2,1,0:T(8,128)(2,1)S(1)} %get-tuple-element.67), channel_id=1, source_target_pairs={{0,5},{1,6},{2,7},{3,0},{4,1},{5,2},{6,3},{7,4},{8,13},{9,14},{10,... | collective-permute-start | bytes 393224 | tf_op jit(solution)/shard_map/ppermute | solution.py:464
  15.6 6.2 %collective-permute-start.6 = (bf16[2,128,256]{2,1,0:T(8,128)(2,1)S(1)}, bf16[2,128,256]{2,1,0:T(8,128)(2,1)S(1)}, u32[]{:S(2)}, u32[]{:S(2)}) collective-permute-start(bf16[2,128,256]{2,1,0:T(8,128)(2,1)S(1)} %get-tuple-element.68), channel_id=1, source_target_pairs={{0,6},{1,7},{2,0},{3,1},{4,2},{5,3},{6,4},{7,5},{8,14},{9,15},{10,... | collective-permute-start | bytes 393224 | tf_op jit(solution)/shard_map/ppermute | solution.py:464
  17.2 6.0 %collective-permute-start.7 = (bf16[2,128,256]{2,1,0:T(8,128)(2,1)S(1)}, bf16[2,128,256]{2,1,0:T(8,128)(2,1)S(1)}, u32[]{:S(2)}, u32[]{:S(2)}) collective-permute-start(bf16[2,128,256]{2,1,0:T(8,128)(2,1)S(1)} %get-tuple-element.69), channel_id=1, source_target_pairs={{0,7},{1,0},{2,1},{3,2},{4,3},{5,4},{6,5},{7,6},{8,15},{9,8},{10,9... | collective-permute-start | bytes 393224 | tf_op jit(solution)/shard_map/ppermute | solution.py:464
  25.7 15.9 %all-to-all-start = ((f32[16,2,2,16,128]{4,3,2,1,0:T(8,128)}), f32[16,2,2,16,128]{4,3,2,1,0:T(8,128)}, u32[]{:S(2)}, u32[]{:S(2)}) async-start(f32[16,2,2,16,128]{4,3,2,1,0:T(8,128)} %bitcast.9), calls=%async_computation | async-start | bytes 1048576 | tf_op jit(solution)/shard_map/all_to_all | solution.py:549
  31.6 29.7 %collective-permute-start.16 = (bf16[1024,512]{1,0:T(8,128)(2,1)}, bf16[1024,512]{1,0:T(8,128)(2,1)}, u32[]{:S(2)}, u32[]{:S(2)}) collective-permute-start(bf16[1024,512]{1,0:T(8,128)(2,1)} %get-tuple-element.90), channel_id=1, source_target_pairs={{0,16},{16,0},{1,17},{17,1},{2,18},{18,2},{3,19},{19,3},{4,20},{20... | collective-permute-start | bytes 3145736 | tf_op jit(solution)/shard_map/ppermute | solution.py:460
  37.2 6.5 %collective-permute-start.9 = (bf16[128,512]{1,0:T(8,128)(2,1)}, bf16[128,512]{1,0:T(8,128)(2,1)}, u32[]{:S(2)}, u32[]{:S(2)}) collective-permute-start(bf16[128,512]{1,0:T(8,128)(2,1)} %get-tuple-element.78), channel_id=1, source_target_pairs={{0,1},{1,2},{2,3},{3,4},{4,5},{5,6},{6,7},{7,0},{8,9},{9,10},{10,1... | collective-permute-start | bytes 393224 | tf_op jit(solution)/shard_map/ppermute | solution.py:464
  37.2 11.0 %collective-permute-start.10 = (bf16[128,512]{1,0:T(8,128)(2,1)}, bf16[128,512]{1,0:T(8,128)(2,1)}, u32[]{:S(2)}, u32[]{:S(2)}) collective-permute-start(bf16[128,512]{1,0:T(8,128)(2,1)} %get-tuple-element.79), channel_id=1, source_target_pairs={{0,2},{1,3},{2,4},{3,5},{4,6},{5,7},{6,0},{7,1},{8,10},{9,11},{10,... | collective-permute-start | bytes 393224 | tf_op jit(solution)/shard_map/ppermute | solution.py:464
  38.7 9.6 %collective-permute-start.11 = (bf16[128,512]{1,0:T(8,128)(2,1)}, bf16[128,512]{1,0:T(8,128)(2,1)}, u32[]{:S(2)}, u32[]{:S(2)}) collective-permute-start(bf16[128,512]{1,0:T(8,128)(2,1)} %get-tuple-element.80), channel_id=1, source_target_pairs={{0,3},{1,4},{2,5},{3,6},{4,7},{5,0},{6,1},{7,2},{8,11},{9,12},{10,... | collective-permute-start | bytes 393224 | tf_op jit(solution)/shard_map/ppermute | solution.py:464
  41.0 9.7 %collective-permute-start.12 = (bf16[128,512]{1,0:T(8,128)(2,1)}, bf16[128,512]{1,0:T(8,128)(2,1)}, u32[]{:S(2)}, u32[]{:S(2)}) collective-permute-start(bf16[128,512]{1,0:T(8,128)(2,1)} %get-tuple-element.81), channel_id=1, source_target_pairs={{0,4},{1,5},{2,6},{3,7},{4,0},{5,1},{6,2},{7,3},{8,12},{9,13},{10,... | collective-permute-start | bytes 393224 | tf_op jit(solution)/shard_map/ppermute | solution.py:464
  43.6 18.3 %collective-permute-start.8 = (f32[2,176,128]{2,1,0:T(8,128)S(1)}, f32[2,176,128]{2,1,0:T(8,128)S(1)}, u32[]{:S(2)}, u32[]{:S(2)}) collective-permute-start(f32[2,176,128]{2,1,0:T(8,128)S(1)} %get-tuple-element.75), channel_id=1, source_target_pairs={{0,8},{1,9},{2,10},{3,11},{4,12},{5,13},{6,14},{7,15},{16,24},{17,... | collective-permute-start | bytes 540680 | tf_op jit(solution)/shard_map/ppermute | solution.py:472
  48.2 8.2 %collective-permute-start.13 = (bf16[128,512]{1,0:T(8,128)(2,1)S(1)}, bf16[128,512]{1,0:T(8,128)(2,1)S(1)}, u32[]{:S(2)}, u32[]{:S(2)}) collective-permute-start(bf16[128,512]{1,0:T(8,128)(2,1)S(1)} %copy-done.25), channel_id=1, source_target_pairs={{0,5},{1,6},{2,7},{3,0},{4,1},{5,2},{6,3},{7,4},{8,13},{9,14},{10,... | collective-permute-start | bytes 393224 | tf_op jit(solution)/shard_map/ppermute | solution.py:464
  48.2 8.5 %collective-permute-start.14 = (bf16[128,512]{1,0:T(8,128)(2,1)S(1)}, bf16[128,512]{1,0:T(8,128)(2,1)S(1)}, u32[]{:S(2)}, u32[]{:S(2)}) collective-permute-start(bf16[128,512]{1,0:T(8,128)(2,1)S(1)} %copy-done.23), channel_id=1, source_target_pairs={{0,6},{1,7},{2,0},{3,1},{4,2},{5,3},{6,4},{7,5},{8,14},{9,15},{10,... | collective-permute-start | bytes 393224 | tf_op jit(solution)/shard_map/ppermute | solution.py:464
  50.7 7.4 %collective-permute-start.15 = (bf16[128,512]{1,0:T(8,128)(2,1)S(1)}, bf16[128,512]{1,0:T(8,128)(2,1)S(1)}, u32[]{:S(2)}, u32[]{:S(2)}) collective-permute-start(bf16[128,512]{1,0:T(8,128)(2,1)S(1)} %copy-done.21), channel_id=1, source_target_pairs={{0,7},{1,0},{2,1},{3,2},{4,3},{5,4},{6,5},{7,6},{8,15},{9,8},{10,9... | collective-permute-start | bytes 393224 | tf_op jit(solution)/shard_map/ppermute | solution.py:464
  69.9 16.9 %all-to-all-start.1 = ((bf16[8,128,256]{2,1,0:T(8,128)(2,1)}), bf16[8,128,256]{2,1,0:T(8,128)(2,1)}, u32[]{:S(2)}, u32[]{:S(2)}) async-start(bf16[8,128,256]{2,1,0:T(8,128)(2,1)} %copy-done.14), calls=%async_computation.1 | async-start | bytes 1048576 | tf_op jit(solution)/shard_map/all_to_all | solution.py:455
  74.1 10.2 %collective-permute-start.17 = (f32[2,176,128]{2,1,0:T(8,128)}, f32[2,176,128]{2,1,0:T(8,128)S(1)}, u32[]{:S(2)}, u32[]{:S(2)}) collective-permute-start(f32[2,176,128]{2,1,0:T(8,128)} %copy-done.19), channel_id=1, source_target_pairs={{8,0},{9,1},{10,2},{11,3},{12,4},{13,5},{14,6},{15,7},{24,16},{25,... | collective-permute-start | bytes 540680 | tf_op jit(solution)/shard_map/ppermute | solution.py:472
  86.8 28.4 %all-to-all-start.2 = ((bf16[8,96,1024]{2,1,0:T(8,128)(2,1)}), bf16[8,96,1024]{2,1,0:T(8,128)(2,1)}, u32[]{:S(2)}, u32[]{:S(2)}) async-start(bf16[8,96,1024]{2,1,0:T(8,128)(2,1)} %copy-done.8), calls=%async_computation.2 | async-start | bytes 3145728 | tf_op jit(solution)/shard_map/all_to_all | solution.py:455
  95.0 23.9 %collective-permute-start.18 = (bf16[1024,512]{1,0:T(8,128)(2,1)}, bf16[1024,512]{1,0:T(8,128)(2,1)}, u32[]{:S(2)}, u32[]{:S(2)}) collective-permute-start(bf16[1024,512]{1,0:T(8,128)(2,1)} %collective-permute-done.16.refs_3_), channel_id=1, source_target_pairs={{0,1},{1,0},{2,3},{3,2},{4,5},{5,4},{6,7},{7,6},{8,9},{9,8},{10,11... | collective-permute-start | bytes 3145736 | tf_op jit(solution)/shard_map/ppermute | solution.py:578
  118.3 7.8 %collective-permute-start.19 = (bf16[256,512]{1,0:T(8,128)(2,1)S(1)}, bf16[256,512]{1,0:T(8,128)(2,1)S(1)}, u32[]{:S(2)}, u32[]{:S(2)}) collective-permute-start(bf16[256,512]{1,0:T(8,128)(2,1)S(1)} %get-tuple-element.106), channel_id=1, source_target_pairs={{0,16},{16,0},{1,17},{17,1},{2,18},{18,2},{3,19},{19,3},{4,20},{20... | collective-permute-start | bytes 786440 | tf_op jit(solution)/shard_map/ppermute | solution.py:460
  126.2 7.3 %collective-permute-start.20 = (bf16[128,512]{1,0:T(8,128)(2,1)S(1)}, bf16[128,512]{1,0:T(8,128)(2,1)S(1)}, u32[]{:S(2)}, u32[]{:S(2)}) collective-permute-start(bf16[128,512]{1,0:T(8,128)(2,1)S(1)} %get-tuple-element.111), channel_id=1, source_target_pairs={{0,8},{1,9},{2,10},{3,11},{4,12},{5,13},{6,14},{7,15},{8,0},{9,1},... | collective-permute-start | bytes 393224 | tf_op jit(solution)/shard_map/ppermute | solution.py:472
  (26 other events, 108.3 us)

commit v3 on v2

--- a/solution.py
+++ b/solution.py
@@ -159,8 +159,7 @@
         out_ref[:, aligned(src, tok)] = part_ref[...].T
 
 
-def projected_blocks(part, weight, out_ref):
-    projected = dot(part, weight).T
+def write_blocks(projected, out_ref):
     group, _, heads, feat, _ = out_ref.shape
     for member in range(group):
         for which in range(2):
@@ -172,17 +171,38 @@
 def project_kernel(at_ref, tokens_ref, weight_ref, out_ref, part_ref, sem):
     share = part_ref.shape[1]
     run_copies(sem, [(tokens_ref.at[0, :, aligned(at_ref[0], share)], part_ref)])
-    projected_blocks(part_ref[...], weight_ref[...], out_ref)
+    write_blocks(dot(part_ref[...], weight_ref[...]).T, out_ref)
 
 
 def project_rest_kernel(at_ref, own_ref, weight_ref, *rest):
-    *part_refs, out_ref = rest
+    *part_refs, out_ref, slots_ref, held_ref, sems, out_sems = rest
     count = len(part_refs) + 1
     at = at_ref[0]
-    out_ref[at] = own_ref[...]
+    pieces, size = held_ref.shape[:2]
+    loads = [
+        pltpu.make_async_copy(
+            weight_ref.at[i * size : (i + 1) * size], held_ref.at[i], sems.at[i]
+        )
+        for i in range(pieces)
+    ]
+    for load in loads:
+        load.start()
+    copies = [pltpu.make_async_copy(own_ref, out_ref.at[at], out_sems.at[0])]
+    copies[0].start()
     for shift, part_ref in enumerate(part_refs, 1):
+        total = 0.0
+        for i, load in enumerate(loads):
+            if shift == 1:
+                load.wait()
+            total = total + dot(part_ref[:, i * size : (i + 1) * size], held_ref[i])
+        write_blocks(total.T, slots_ref.at[shift - 1])
         owner = lax.rem(at + count - shift, count)
-        projected_blocks(part_ref[...], weight_ref[...], out_ref.at[owner])
+        copies.append(
+            pltpu.make_async_copy(slots_ref.at[shift - 1], out_ref.at[owner], out_sems.at[shift])
+        )
+        copies[-1].start()
+    for copy in copies:
+        copy.wait()
 
 
 def weight_piece_kernel(at_ref, weight_ref, out_ref, sems):
@@ -243,26 +263,32 @@
         grad = inv_rms * (
             upstream - normed * jnp.mean(normed * upstream, axis=-1, keepdims=True)
         )
-        attended = normed.astype(bf16)
-        for src in range(blocks):
-            attended_ref[src, :, cols] = attended[src * tok : (src + 1) * tok]
+        attended_ref[:, cols] = normed.astype(bf16)
         grad_ref[:, cols] = grad
         if with_state:
             carried_ref[head] = dot3(feat, grad)
 
 
-def backward_kernel(with_state, first, qk_ref, vg_ref, grad_ref, *rest):
-    rest = list(rest)
-    prefix_ref = rest.pop(0) if with_state else None
-    if first == 0:
-        attended_in_ref = rest.pop(0)
-        attended_ref = rest.pop()
-        attended_ref[...] = attended_in_ref[...]
-    grad_qk_ref, grad_v_ref = rest[-2:]
+def split_rows_kernel(at_ref, in_ref, *rest):
+    *out_refs, sems = rest
+    group, tok = len(out_refs), out_refs[0].shape[0]
+    run_copies(
+        sems,
+        [
+            (in_ref.at[aligned(lax.rem(at_ref[0] + shift, group), tok)], out_ref)
+            for shift, out_ref in enumerate(out_refs)
+        ],
+    )
+
+
+def backward_kernel(with_state, qk_ref, vg_ref, grad_ref, *rest):
+    if with_state:
+        prefix_ref, grad_qk_ref, grad_v_ref = rest
+    else:
+        grad_qk_ref, grad_v_ref = rest
     length = qk_ref.shape[0] * qk_ref.shape[4]
     tile = min(TILE, length)
-    for at_head in range(grad_v_ref.shape[0]):
-        head = first + at_head
+    for head in range(grad_v_ref.shape[0]):
         cols = slice(head * DH, (head + 1) * DH)
         q = feature_major(qk_ref, 0, head) * 0.25
         k = feature_major(qk_ref, 1, head)
@@ -289,86 +315,71 @@
             piece = both[:F] + both[F:]
             if with_state:
                 piece = piece + grad_q[:, at:width]
-            grad_qk_ref[0, at_head, :, at:width] = piece * 0.25
+            grad_qk_ref[0, head, :, at:width] = piece * 0.25
             both = dot(q_both[:, at:width], slope)
             piece_k = both[:F] + both[F:]
             both = dot(jnp.concatenate(split(grad_t[:, at:width]), axis=0), kernel)
             piece_v = both[:DH] + both[DH:]
             if width == length:
-                grad_qk_ref[1, at_head] = piece_k
-                grad_v_ref[at_head] = piece_v
+                grad_qk_ref[1, head] = piece_k
+                grad_v_ref[head] = piece_v
             else:
-                grad_qk_ref[1, at_head, :, :width] += piece_k
-                grad_v_ref[at_head, :, :width] += piece_v
-
-
-def rows_kernel(with_state, halves, qk_ref, vg_ref, *rest):
-    rest = list(rest)
-    suffix_ref = rest.pop(0) if with_state else None
-    out_ref = rest[-1]
-    blocks, tok = qk_ref.shape[0], qk_ref.shape[4]
+                grad_qk_ref[1, head, :, :width] += piece_k
+                grad_v_ref[head, :, :width] += piece_v
+
+
+def rows_kernel(with_state, qk_ref, vg_ref, grad_qk_ref, *rest):
+    *suffix_refs, out_ref, held_ref, sems = rest
     heads = qk_ref.shape[2]
-    feats = 2 * heads * F
-    fold = blocks * tok // (heads * DH)
-    step = tok // fold
-    head = 0
-    for grad_ref, grad_v_ref in zip(rest[:halves], rest[halves : 2 * halves]):
-        for at_head in range(grad_v_ref.shape[0]):
-            grad_k = grad_ref[1, at_head]
-            grad_v = grad_v_ref[at_head]
-            if with_state:
-                k = feature_major(qk_ref, 1, head)
-                v = rows_of(vg_ref, 0, head, 0, blocks * tok)
-                high, low = split(suffix_ref[head])
-                grad_k = grad_k + pull_psi(k, dot(high, v, NT) + dot(low, v, NT), False)
-                grad_v = grad_v + dot3(suffix_ref[head].T, psi(k, False))
-            grad_q, grad_k = grad_ref[0, at_head].astype(bf16), grad_k.astype(bf16)
-            grad_v = grad_v.T.astype(bf16)
-            for member in range(blocks):
-                out_ref[member, head * F : (head + 1) * F] = grad_q
-                out_ref[member, (heads + head) * F : (heads + head + 1) * F] = grad_k
-                for i in range(fold):
-                    first = (i * heads + head) * DH
-                    row = member * tok + i * step
-                    out_ref[member, feats:, first : first + DH] = grad_v[row : row + step]
-            head += 1
-
-
-def unpack_values_kernel(in_ref, out_ref):
-    group, rows, length = in_ref.shape
-    width = out_ref.shape[2] // group
-    tok = out_ref.shape[1]
-    fold = length // width
-    step = tok // fold
-    for member in range(group):
-        for i in range(fold):
-            out_ref[0, i * step : (i + 1) * step, member * width : (member + 1) * width] = in_ref[
-                member, rows - step :, i * width : (i + 1) * width
-            ]
-
-
-def unpack_heads_kernel(in_ref, out_ref):
-    group, _, width = in_ref.shape
-    for member in range(group):
-        out_ref[0, :, member * width : (member + 1) * width] = in_ref[member]
-
-
-def all_rows(rows_ref, count, cols):
-    half = count // rows_ref.shape[0] // 2
-    return jnp.concatenate(
-        [
-            rows_ref[src, which * half : (which + 1) * half, cols]
-            for which in range(2)
-            for src in range(rows_ref.shape[0])
-        ],
-        axis=0,
-    )
-
-
-def product_kernel(at_ref, rows_ref, tokens_ref, *rest):
-    *part_refs, total_ref = rest
-    count = total_ref.shape[1]
-    total_ref[...] = dot(tokens_ref[...], all_rows(rows_ref, count, slice(None)), NT)
+    length = qk_ref.shape[0] * qk_ref.shape[4]
+    for head in range(heads):
+        grad_k = grad_qk_ref[1, head]
+        if with_state:
+            k = feature_major(qk_ref, 1, head)
+            v = rows_of(vg_ref, 0, head, 0, length)
+            high, low = split(suffix_refs[0][head])
+            grad_k = grad_k + pull_psi(k, dot(high, v, NT) + dot(low, v, NT), False)
+        held_ref[head * F : (head + 1) * F] = grad_qk_ref[0, head].astype(bf16)
+        held_ref[(heads + head) * F : (heads + head + 1) * F] = grad_k.astype(bf16)
+    run_copies(sems, [(held_ref, out_ref)])
+
+
+def grad_values_kernel(with_state, at_ref, qk_ref, grad_v_ref, *rest):
+    heads = qk_ref.shape[2]
+    group, tok = qk_ref.shape[0], qk_ref.shape[4]
+    suffix_refs, out_refs = rest[: -group - 2], rest[-group - 2 : -2]
+    held_ref, sems = rest[-2:]
+    for head in range(heads):
+        grad_v = grad_v_ref[head]
+        if with_state:
+            feat = psi(feature_major(qk_ref, 1, head), False)
+            grad_v = grad_v + dot3(suffix_refs[0][head].T, feat)
+        held_ref[:, head * DH : (head + 1) * DH] = grad_v.T.astype(bf16)
+    split_rows_kernel(at_ref, held_ref, *out_refs, sems)
+
+
+def unpack_heads_kernel(at_ref, *rest):
+    *part_refs, out_ref = rest
+    group, width = len(part_refs), part_refs[0].shape[1]
+    for shift, part_ref in enumerate(part_refs):
+        src = lax.rem(at_ref[0] + group - shift, group)
+        out_ref[0, :, aligned(src, width)] = part_ref[...]
+
+
+def place_rows(at, part_refs, cols, held_ref):
+    group, half = len(part_refs), part_refs[0].shape[0] // 2
+    for shift, part_ref in enumerate(part_refs):
+        src = lax.rem(at + group - shift, group)
+        for which in range(2):
+            rows = aligned(which * group + src, half)
+            held_ref[rows, :] = part_ref[which * half : (which + 1) * half, cols]
+
+
+def product_kernel(group, at_ref, *rest):
+    rows_refs, rest = rest[:group], rest[group:]
+    tokens_ref, *part_refs, total_ref, held_ref = rest
+    place_rows(at_ref[1], rows_refs, slice(None), held_ref)
+    total_ref[...] = dot(tokens_ref[...], held_ref[...], NT)
     count = len(part_refs)
     size = part_refs[0].shape[0]
     for shift, part_ref in enumerate(part_refs):
@@ -392,11 +403,11 @@
         part_ref[...] = part.astype(part_ref.dtype)
 
 
-def grad_tokens_kernel(at_ref, rows_ref, *rest):
-    *weight_refs, out_ref = rest
-    tok = out_ref.shape[1]
-    start = pl.multiple_of(at_ref[0] * tok, tok)
-    rows = all_rows(rows_ref, weight_refs[0].shape[1], pl.ds(start, tok)).T
+def grad_tokens_kernel(group, at_ref, *rest):
+    rows_refs, rest = rest[:group], rest[group:]
+    *weight_refs, out_ref, held_ref = rest
+    place_rows(at_ref[0], rows_refs, aligned(at_ref[0], out_ref.shape[1]), held_ref)
+    rows = held_ref[...].T
     for i, weight_ref in enumerate(weight_refs):
         size = weight_ref.shape[0]
         first = pl.multiple_of(at_ref[1 + i], size)
@@ -405,17 +416,27 @@
 
 VMEM = pl.BlockSpec(memory_space=pltpu.VMEM)
 SMEM = pl.BlockSpec(memory_space=pltpu.SMEM)
+FAR = pl.BlockSpec(memory_space=pltpu.HBM)
 ANYWHERE = pl.BlockSpec(memory_space=pl.ANY)
 
 
 def call(
-    body, outs, *operands, scalars=(), after=(), scratch=(), far_in=0, far_out=False, copies=0
+    body,
+    outs,
+    *operands,
+    scalars=(),
+    after=(),
+    after_far=(),
+    scratch=(),
+    far_in=(),
+    far_out=False,
+    copies=(),
 ):
     at = [jnp.stack([jnp.int32(s) for s in scalars])] if scalars else []
     count = len(at) + len(operands)
 
     def kernel(*refs):
-        ins, rest = refs[:count], refs[count + len(after) :]
+        ins, rest = refs[:count], refs[count + len(after) + len(after_far) :]
         body(*ins, *rest[: len(outs)], *rest[len(outs) + 1 :])
         rest[len(outs)][...] = jnp.zeros((8, 128), f32)
 
@@ -423,14 +444,14 @@
         kernel,
         out_shape=[jax.ShapeDtypeStruct(shape, kind) for shape, kind in [*outs, ((8, 128), f32)]],
         in_specs=[SMEM] * len(at)
-        + [ANYWHERE] * far_in
-        + [VMEM] * (len(operands) - far_in)
-        + [ANYWHERE] * len(after),
-        out_specs=[ANYWHERE if far_out else VMEM] * len(outs) + [VMEM],
-        scratch_shapes=[*scratch] + [pltpu.SemaphoreType.DMA((copies,))] * (copies > 0),
+        + [FAR if i in far_in else VMEM for i in range(len(operands))]
+        + [ANYWHERE] * len(after)
+        + [FAR] * len(after_far),
+        out_specs=[FAR if far_out else VMEM] * len(outs) + [VMEM],
+        scratch_shapes=[*scratch] + [pltpu.SemaphoreType.DMA((n,)) for n in copies],
         compiler_params=pltpu.CompilerParams(vmem_limit_bytes=VMEM_LIMIT),
         cost_estimate=pl.CostEstimate(flops=0, bytes_accessed=0, transcendentals=0),
-    )(*at, *operands, *after)
+    )(*at, *operands, *after, *after_far)
     return results, token
 
 
@@ -463,6 +484,9 @@
         pairs = [(i, i - i % group + (i + shift) % group) for i in range(ctx_size)]
         return lax.ppermute(x, "ctx", pairs)
 
+    def to_members(parts):
+        return [part if not shift else to_member(part, shift) for shift, part in enumerate(parts)]
+
     def to_run(x, shift, wrap):
         pairs = [
             (i, (i + shift * group) % ctx_size)
@@ -473,7 +497,7 @@
 
     qk_shape = ((group, 2, heads, F, tok), f32)
     state_shape = ((heads, PSI, DH), f32)
-    blocks_shape = ((group, tok, heads * DH), bf16)
+    blocks_shape = ((tok, heads * DH), bf16)
     rows_shape = ((length, heads * DH), f32)
 
     parts, token = call(
@@ -481,9 +505,9 @@
         [((tok, share), bf16)] * (dp_size - 1),
         tokens,
         scalars=(dp_at,),
-        far_in=1,
+        far_in=(0,),
         far_out=True,
-        copies=dp_size - 1,
+        copies=(dp_size - 1,),
     )
     arrived = [to_dp(part, shift) for shift, part in enumerate(parts, 1)]
     parts, token = call(
@@ -493,11 +517,11 @@
         grad_out,
         scalars=(member,),
         after=(token,),
-        far_in=2,
+        far_in=(0, 1),
         far_out=True,
-        copies=2 * group,
-    )
-    parts = parts[:1] + [to_member(part, shift) for shift, part in enumerate(parts[1:], 1)]
+        copies=(2 * group,),
+    )
+    parts = to_members(parts)
     (vg,), vg_token = call(
         collect_heads_kernel,
         [((group, 2, tok, heads * DH), bf16)],
@@ -511,8 +535,8 @@
         proj_weight,
         scalars=(dp_at,),
         after=(token,),
-        far_in=1,
-        copies=1,
+        far_in=(0,),
+        copies=(1,),
         scratch=[pltpu.VMEM((tok, share), bf16)],
     )
     part_shape = (tok, dp_size * runs * depth)
@@ -523,9 +547,9 @@
             tokens,
             scalars=(member,),
             after=(token,),
-            far_in=1,
+            far_in=(0,),
             far_out=True,
-            copies=group * dp_size * runs,
+            copies=(group * dp_size * runs,),
         )
     else:
         blocks = tokens[0].reshape(tok, dp_size * runs, group, depth).transpose(2, 0, 1, 3)
@@ -535,7 +559,7 @@
             )
             for shift in range(group)
         ]
-    token_parts = parts[:1] + [to_member(part, shift) for shift, part in enumerate(parts[1:], 1)]
+    token_parts = to_members(parts)
 
     (projected,), token = call(
         project_rest_kernel,
@@ -545,6 +569,13 @@
         *arrived,
         scalars=(dp_at,),
         after=(vg_token,),
+        far_in=(1,),
+        far_out=True,
+        scratch=[
+            pltpu.VMEM((dp_size - 1,) + qk_shape[0], f32),
+            pltpu.VMEM((4, share // 4, cols), bf16),
+        ],
+        copies=(4, dp_size),
     )
     qk_parts = lax.all_to_all(
         projected.reshape((dp_size * group,) + qk_shape[0][1:]),
@@ -564,9 +595,9 @@
         proj_weight,
         scalars=(parity,),
         after=(token,),
-        far_in=1,
+        far_in=(0,),
         far_out=True,
-        copies=1,
+        copies=(1,),
     )
     fetched = [to_dp(mine, shift) for shift in range(1, dp_size)]
     weights, firsts = [proj_weight], [dp_at * share]
@@ -584,6 +615,51 @@
         qk_parts,
         vg,
     )
+    prefix, suffix = (), ()
+    if with_state:
+        prefix = (sum(to_run(state[0], shift, False) for shift in range(1, runs)),)
+    (numerator,), token = call(numerator_kernel, [rows_shape], qk, vg)
+    (attended, grad_num, *carried), token = call(
+        functools.partial(normalize_kernel, with_state),
+        [((length, heads * DH), bf16), rows_shape] + [state_shape] * with_state,
+        qk,
+        vg,
+        numerator,
+        *prefix,
+        after_far=token_parts[1:],
+    )
+    if with_state:
+        suffix = (sum(to_run(carried[0], -shift, False) for shift in range(1, runs)),)
+    (grad_qk, grad_v), token = call(
+        functools.partial(backward_kernel, with_state),
+        [((2, heads, F, length), f32), ((heads, DH, length), f32)],
+        qk,
+        vg,
+        grad_num,
+        *prefix,
+        after_far=fetched,
+    )
+    attended, attended_token = call(
+        split_rows_kernel,
+        [blocks_shape] * group,
+        attended,
+        scalars=(member,),
+        after=(token,),
+        far_out=True,
+        copies=(group,),
+    )
+    (rows,), token = call(
+        functools.partial(rows_kernel, with_state),
+        [((2 * heads * F, length), bf16)],
+        qk,
+        vg,
+        grad_qk,
+        *suffix,
+        far_out=True,
+        scratch=[pltpu.VMEM((2 * heads * F, length), bf16)],
+        copies=(1,),
+    )
+    rows = [rows] + [to_member(rows, shift) for shift in range(1, group)]
     (token_cols,), tokens_token = call(
         collect_tokens_kernel,
         [(part_shape[1:] + (length,), bf16)],
@@ -591,70 +667,39 @@
         scalars=(member,),
         after=(token,),
     )
-
-    prefix, suffix = (), ()
-    if with_state:
-        prefix = (sum(to_run(state[0], shift, False) for shift in range(1, runs)),)
-    (numerator,), token = call(numerator_kernel, [rows_shape], qk, vg)
-    (attended, grad_num, *carried), token = call(
-        functools.partial(normalize_kernel, with_state),
-        [blocks_shape, rows_shape] + [state_shape] * with_state,
+    grad_values, token = call(
+        functools.partial(grad_values_kernel, with_state),
+        [blocks_shape] * group,
         qk,
-        vg,
-        numerator,
-        *prefix,
-        after=(tokens_token,),
-    )
-    if with_state:
-        suffix = (sum(to_run(carried[0], -shift, False) for shift in range(1, runs)),)
-    grad_qks, grad_vs = [], []
-    for first in range(0, heads, max(1, heads // 2)):
-        count = max(1, heads // 2)
-        result, token = call(
-            functools.partial(backward_kernel, with_state, first),
-            [((2, count, F, length), f32), ((count, DH, length), f32)]
-            + [blocks_shape] * (first == 0),
-            qk,
-            vg,
-            grad_num,
-            *prefix,
-            *([attended] if first == 0 else []),
-            after=[half[:8, :128] for half in fetched] if first == 0 else [token],
-        )
-        grad_qks.append(result[0])
-        grad_vs.append(result[1])
-        if first == 0:
-            attended = exchange(result[2])
-    (rows,), token = call(
-        functools.partial(rows_kernel, with_state, len(grad_qks)),
-        [((group, 2 * heads * F + tok * heads * DH // length, length), bf16)],
-        qk,
-        vg,
+        grad_v,
         *suffix,
-        *grad_qks,
-        *grad_vs,
-    )
-    rows = exchange(rows)
+        scalars=(member,),
+        after=(token,),
+        far_out=True,
+        scratch=[pltpu.VMEM((length, heads * DH), bf16)],
+        copies=(group,),
+    )
+    attended, grad_values = to_members(attended), to_members(grad_values)
     (attended,), attended_token = call(
-        unpack_heads_kernel, [((1, tok, H * DH), bf16)], attended, after=(token,)
-    )
-
+        unpack_heads_kernel, [((1, tok, H * DH), bf16)], *attended, scalars=(member,)
+    )
+
+    held = pltpu.VMEM((cols, length), bf16)
     (own, *parts), token = call(
-        product_kernel,
+        functools.partial(product_kernel, group),
         [((runs * depth, cols), f32)] + [((runs * depth, cols), bf16)] * (dp_size - 1),
-        rows,
+        *rows,
         token_cols,
-        scalars=(dp_at,),
+        scalars=(dp_at, member),
         after=(attended_token,),
-        scratch=[pltpu.VMEM((dp_size * runs * depth, cols), f32)],
+        scratch=[pltpu.VMEM((dp_size * runs * depth, cols), f32), held],
     )
     parts = [to_dp(part, shift) for shift, part in enumerate(parts, 1)]
-    (grad_tokens,), tokens_token = call(
-        grad_tokens_kernel,
-        [((1, tok, width), bf16)],
-        rows,
-        *weights,
-        scalars=(member, *firsts),
+    (grad_values,), values_token = call(
+        unpack_heads_kernel,
+        [((1, tok, H * DH), bf16)],
+        *grad_values,
+        scalars=(member,),
         after=(token,),
     )
     (grad_proj, *parts), token = call(
@@ -663,11 +708,17 @@
         own,
         *parts,
         scalars=(run_at,),
-        after=(tokens_token,),
+        after=(values_token,),
         scratch=[pltpu.VMEM((runs * depth, cols), f32)],
     )
-    (grad_values,), token = call(
-        unpack_values_kernel, [((1, tok, H * DH), bf16)], rows, after=(token,)
+    (grad_tokens,), _ = call(
+        functools.partial(grad_tokens_kernel, group),
+        [((1, tok, width), bf16)],
+        *rows,
+        *weights,
+        scalars=(member, *firsts),
+        after=(token,),
+        scratch=[pltpu.VMEM((cols, tok), bf16)],
     )
     for shift, part in enumerate(parts, 1):
         grad_proj = grad_proj + to_run(part, shift, True).astype(f32)

time: 135 us -> 143 us (1.059)
  starting transfers between devices: 45.7 us -> 56.3 us
  waiting for transfers between devices: 37.1 us -> 33.7 us
  local copies, waits for them, and re-layouts: 16.4 us -> 13.2 us
  Pallas kernels: 33.3 us -> 35.7 us
    ppermute x14 -> x35, starting transfers between devices: 17.2 us -> 37.9 us  [to_member(): return lax.ppermute(x, 'ctx', pairs)]
    ppermute x14 -> x35, waiting for transfers between devices: 7.01 us -> 25.7 us  [to_member(): return lax.ppermute(x, 'ctx', pairs)]
    all_to_all x2 -> x0, waiting for transfers between devices: 17.8 us -> none  [exchange(): lax.all_to_all(x, 'ctx', split_axis=0, concat_axis=0, tiled=True, axis_in...]
    all_to_all x2 -> x0, starting transfers between devices: 12.4 us -> none  [exchange(): lax.all_to_all(x, 'ctx', split_axis=0, concat_axis=0, tiled=True, axis_in...]
    ppermute x3, waiting for transfers between devices: 3.3 us -> 0.01 us  [to_dp(): lax.ppermute(x, 'dp', [(i, (i + shift) % dp_size) for i in range(dp_size)])]
    ppermute x3, starting transfers between devices: 5.86 us -> 9.09 us  [to_run(): return lax.ppermute(x, 'ctx', pairs)]
    unnamed x52 -> x48, local copies, waits for them, and re-layouts: 15.7 us -> 13.2 us
    pallas_call x19 -> x20, Pallas kernels: 33.3 us -> 35.7 us  [call(): pl.pallas_call(kernel, out_shape=[jax.ShapeDtypeStruct(shape, kind) for s...]
  transfers between devices with their start and end apart: 24 -> 43, of which waited for: 12 -> 19; matrix products, arithmetic and copies ran while one was open for 1% -> 1% of each run, Pallas kernels for 19% -> 20%
where the time goes in v3:
time: 143 us; the launch traced here: 142 us
  starting transfers between devices  56.3 us (39%)
  Pallas kernels  35.7 us (25%)
  waiting for transfers between devices  33.7 us (24%)
  local copies, waits for them, and re-layouts  13.2 us (9%)
  other arithmetic  1.79 us (1%)
    ppermute x35, starting transfers between devices, to_member(): return lax.ppermute(x, 'ctx', pairs)  37.9 us
    pallas_call x20, Pallas kernels, call(): pl.pallas_call(kernel, out_shape=[jax.ShapeDtypeStruct(shape, kind) for s...  35.7 us
    ppermute x35, waiting for transfers between devices, to_member(): return lax.ppermute(x, 'ctx', pairs)  25.7 us
    unnamed x48, local copies, waits for them, and re-layouts  13.2 us
    ppermute x3, starting transfers between devices, to_run(): return lax.ppermute(x, 'ctx', pairs)  9.09 us
    ppermute x3, waiting for transfers between devices, to_run(): return lax.ppermute(x, 'ctx', pairs)  6.86 us
    ppermute x3, starting transfers between devices, to_dp(): lax.ppermute(x, 'dp', [(i, (i + shift) % dp_size) for i in range(dp_size)])  5 us
    all_to_all x1, starting transfers between devices, local(): lax.all_to_all(projected.reshape((dp_size * group,) + qk_shape[0][1:]), (...  4.25 us
  transfers between devices with their start and end apart: 43, of which 19 were waited for; matrix products, arithmetic and copies ran while one was open for 1% of the time, Pallas kernels for 20%

profile of v3, /device:TPU:0, one launch (start us, length us, event | category | flops | bytes accessed | tf_op | source)
XLA Modules:
  0.0 141.8 jit_solution(2626600931108701917)
XLA Ops:
  2.8 3.0 %collective-permute-start = (bf16[128,2048]{1,0:T(8,128)(2,1)}, bf16[128,2048]{1,0:T(8,128)(2,1)}, u32[]{:S(2)}, u32[]{:S(2)}) collective-permute-start(bf16[128,2048]{1,0:T(8,128)(2,1)} %get-tuple-element.72), channel_id=1, source_target_pairs={{0,16},{16,0},{1,17},{17,1},{2,18},{18,2},{3,19},{19,3},{4,20},{20... | collective-permute-start | bytes 1572872 | tf_op jit(solution)/shard_map/ppermute | solution.py:481
  9.9 2.4 %collective-permute-start.3 = (bf16[2,128,256]{2,1,0:T(8,128)(2,1)S(1)}, bf16[2,128,256]{2,1,0:T(8,128)(2,1)S(1)}, u32[]{:S(2)}, u32[]{:S(2)}) collective-permute-start(bf16[2,128,256]{2,1,0:T(8,128)(2,1)S(1)} %get-tuple-element.76), channel_id=1, source_target_pairs={{0,3},{1,4},{2,5},{3,6},{4,7},{5,0},{6,1},{7,2},{8,11},{9,12},{10,... | collective-permute-start | bytes 393224 | tf_op jit(solution)/shard_map/ppermute | solution.py:485
  17.2 2.2 %collective-permute-start.7 = (bf16[2,128,256]{2,1,0:T(8,128)(2,1)S(1)}, bf16[2,128,256]{2,1,0:T(8,128)(2,1)S(1)}, u32[]{:S(2)}, u32[]{:S(2)}) collective-permute-start(bf16[2,128,256]{2,1,0:T(8,128)(2,1)S(1)} %get-tuple-element.80), channel_id=1, source_target_pairs={{0,7},{1,0},{2,1},{3,2},{4,3},{5,4},{6,5},{7,6},{8,15},{9,8},{10,9... | collective-permute-start | bytes 393224 | tf_op jit(solution)/shard_map/ppermute | solution.py:485
  23.3 2.0 %shard_map.79 = (f32[2,8,2,2,16,128]{5,4,3,2,1,0:T(8,128)S(1)}, f32[8,128]{1,0:T(8,128)S(1)}) custom-call(s32[1]{0:T(128)} %bitcast.1.refs_0_, f32[8,2,2,16,128]{4,3,2,1,0:T(8,128)S(1)} %get-tuple-element.71.refs_1_, bf16[2048,512]{1,0:T(8,128)(2,1)S(1)} %copy-done, bf16[128,2048]{1,0:T(8,128)(2,1)} %collective-permute-done.refs_3_, ...), custom_call_target="tpu_custom_call" | custom-call | tf_op jit(solution)/shard_map/pallas_call | solution.py:443
  26.1 4.2 %all-to-all-start = ((f32[16,2,2,16,128]{4,3,2,1,0:T(8,128)}), f32[16,2,2,16,128]{4,3,2,1,0:T(8,128)}, u32[]{:S(2)}, u32[]{:S(2)}) async-start(f32[16,2,2,16,128]{4,3,2,1,0:T(8,128)} %bitcast.9), calls=%async_computation | async-start | bytes 1048576 | tf_op jit(solution)/shard_map/all_to_all | solution.py:580
  37.8 2.3 %collective-permute-start.11 = (bf16[128,512]{1,0:T(8,128)(2,1)}, bf16[128,512]{1,0:T(8,128)(2,1)S(1)}, u32[]{:S(2)}, u32[]{:S(2)}) collective-permute-start(bf16[128,512]{1,0:T(8,128)(2,1)} %get-tuple-element.90), channel_id=1, source_target_pairs={{0,3},{1,4},{2,5},{3,6},{4,7},{5,0},{6,1},{7,2},{8,11},{9,12},{10,... | collective-permute-start | bytes 393224 | tf_op jit(solution)/shard_map/ppermute | solution.py:485
  43.7 4.5 %collective-permute-start.8 = (f32[2,176,128]{2,1,0:T(8,128)S(1)}, f32[2,176,128]{2,1,0:T(8,128)S(1)}, u32[]{:S(2)}, u32[]{:S(2)}) collective-permute-start(f32[2,176,128]{2,1,0:T(8,128)S(1)} %get-tuple-element.86), channel_id=1, source_target_pairs={{0,8},{1,9},{2,10},{3,11},{4,12},{5,13},{6,14},{7,15},{16,24},{17,... | collective-permute-start | bytes 540680 | tf_op jit(solution)/shard_map/ppermute | solution.py:496
  51.5 3.6 %shard_map.81 = (f32[1024,256]{1,0:T(8,128)S(1)}, f32[8,128]{1,0:T(8,128)}) custom-call(f32[8,2,2,16,128]{4,3,2,1,0:T(8,128)S(1)} %get-tuple-element.84.refs_0_.refs_1_, bf16[8,2,128,256]{3,2,1,0:T(8,128)(2,1)S(1)} %get-tuple-element.83.refs_1_), custom_call_target="tpu_custom_call" | custom-call | tf_op jit(solution)/shard_map/pallas_call | solution.py:443
  58.3 2.5 %shard_map.83 = (bf16[1024,256]{1,0:T(8,128)(2,1)S(1)}, f32[1024,256]{1,0:T(8,128)S(1)}, f32[2,176,128]{2,1,0:T(8,128)S(1)}, f32[8,128]{1,0:T(8,128)}) custom-call(f32[8,2,2,16,128]{4,3,2,1,0:T(8,128)S(1)} %get-tuple-element.84.refs_0_.refs_1_, bf16[8,2,128,256]{3,2,1,0:T(8,128)(2,1)S(1)} %get-tuple-element.83.refs_1_, ...), custom_call_target="tpu_custom_call" | custom-call | tf_op jit(solution)/shard_map/pallas_call | solution.py:443
  62.4 4.6 %shard_map.85 = (f32[2,2,16,1024]{3,2,1,0:T(8,128)S(1)}, f32[2,128,1024]{2,1,0:T(8,128)S(1)}, f32[8,128]{1,0:T(8,128)S(1)}) custom-call(f32[8,2,2,16,128]{4,3,2,1,0:T(8,128)S(1)} %get-tuple-element.84.refs_0_.refs_1_, bf16[8,2,128,256]{3,2,1,0:T(8,128)(2,1)S(1)} %get-tuple-element.83.refs_1_, f32[1024,256]{1,0:T(8,128)S(1)} %get-tuple-element.96.refs_2_, ...), custom_call_target="tpu_custom_call" | custom-call | tf_op jit(solution)/shard_map/pallas_call | solution.py:443
  69.7 3.4 %collective-permute-start.19 = (bf16[128,256]{1,0:T(8,128)(2,1)S(1)}, bf16[128,256]{1,0:T(8,128)(2,1)S(1)}, u32[]{:S(2)}, u32[]{:S(2)}) collective-permute-start(bf16[128,256]{1,0:T(8,128)(2,1)S(1)} %get-tuple-element.103), channel_id=1, source_target_pairs={{0,3},{1,4},{2,5},{3,6},{4,7},{5,0},{6,1},{7,2},{8,11},{9,12},{10,... | collective-permute-start | bytes 196616 | tf_op jit(solution)/shard_map/ppermute | solution.py:485
  80.8 2.1 %collective-permute-start.23 = (bf16[128,256]{1,0:T(8,128)(2,1)S(1)}, bf16[128,256]{1,0:T(8,128)(2,1)S(1)}, u32[]{:S(2)}, u32[]{:S(2)}) collective-permute-start(bf16[128,256]{1,0:T(8,128)(2,1)S(1)} %get-tuple-element.107), channel_id=1, source_target_pairs={{0,7},{1,0},{2,1},{3,2},{4,3},{5,4},{6,5},{7,6},{8,15},{9,8},{10,9... | collective-permute-start | bytes 196616 | tf_op jit(solution)/shard_map/ppermute | solution.py:485
  82.9 4.7 %collective-permute-done.23.refs_8_ = bf16[128,256]{1,0:T(8,128)(2,1)S(1)} collective-permute-done((bf16[128,256]{1,0:T(8,128)(2,1)S(1)}, bf16[128,256]{1,0:T(8,128)(2,1)S(1)}, u32[]{:S(2)}, u32[]{:S(2)}) %collective-permute-start.23) | collective-permute-done | bytes 65568 | tf_op jit(solution)/shard_map/ppermute | solution.py:485
  88.7 2.0 %collective-permute-start.27 = (bf16[64,1024]{1,0:T(8,128)(2,1)S(1)}, bf16[64,1024]{1,0:T(8,128)(2,1)S(1)}, u32[]{:S(2)}, u32[]{:S(2)}) collective-permute-start(bf16[64,1024]{1,0:T(8,128)(2,1)S(1)} %get-tuple-element.111.refs_1_), channel_id=1, source_target_pairs={{0,3},{1,4},{2,5},{3,6},{4,7},{5,0},{6,1},{7,2},{8,11},{9,12},{10,... | collective-permute-start | bytes 393224 | tf_op jit(solution)/shard_map/ppermute | solution.py:485
  94.3 3.7 %collective-permute-done.26.refs_3_ = bf16[64,1024]{1,0:T(8,128)(2,1)S(1)} collective-permute-done((bf16[64,1024]{1,0:T(8,128)(2,1)S(1)}, bf16[64,1024]{1,0:T(8,128)(2,1)S(1)}, u32[]{:S(2)}, u32[]{:S(2)}) %collective-permute-start.26) | collective-permute-done | bytes 131104 | tf_op jit(solution)/shard_map/ppermute | solution.py:485
  98.1 2.5 %collective-permute-done.25.refs_2_ = bf16[64,1024]{1,0:T(8,128)(2,1)S(1)} collective-permute-done((bf16[64,1024]{1,0:T(8,128)(2,1)S(1)}, bf16[64,1024]{1,0:T(8,128)(2,1)S(1)}, u32[]{:S(2)}, u32[]{:S(2)}) %collective-permute-start.25) | collective-permute-done | bytes 131104 | tf_op jit(solution)/shard_map/ppermute | solution.py:485
  100.6 2.2 %shard_map.90 = (f32[256,512]{1,0:T(8,128)S(1)}, bf16[256,512]{1,0:T(8,128)(2,1)}, f32[8,128]{1,0:T(8,128)S(1)}) custom-call(s32[2]{0:T(128)S(1)} %pad_add_fusion.1.refs_0_, bf16[64,1024]{1,0:T(8,128)(2,1)S(1)} %get-tuple-element.111.refs_1_, bf16[64,1024]{1,0:T(8,128)(2,1)S(1)} %collective-permute-done.25.refs_2_, ...), custom_call_target="tpu_custom_call" | custom-call | tf_op jit(solution)/shard_map/pallas_call | solution.py:443
  102.8 2.5 %shard_map.91 = (bf16[128,256]{1,0:T(8,128)(2,1)S(1)}, bf16[128,256]{1,0:T(8,128)(2,1)S(1)}, bf16[128,256]{1,0:T(8,128)(2,1)S(1)}, bf16[128,256]{1,0:T(8,128)(2,...) custom-call(s32[1]{0:T(128)} %bitcast.refs_0_, ...), custom_call_target="tpu_custom_call" | custom-call | tf_op jit(solution)/shard_map/pallas_call | solution.py:443
  105.5 2.5 %collective-permute-start.36 = (bf16[128,256]{1,0:T(8,128)(2,1)S(1)}, bf16[128,256]{1,0:T(8,128)(2,1)S(1)}, u32[]{:S(2)}, u32[]{:S(2)}) collective-permute-start(bf16[128,256]{1,0:T(8,128)(2,1)S(1)} %get-tuple-element.122), channel_id=1, source_target_pairs={{0,3},{1,4},{2,5},{3,6},{4,7},{5,0},{6,1},{7,2},{8,11},{9,12},{10,... | collective-permute-start | bytes 196616 | tf_op jit(solution)/shard_map/ppermute | solution.py:485
  107.9 2.2 %collective-permute-done.34.refs_2_ = bf16[128,256]{1,0:T(8,128)(2,1)S(1)} collective-permute-done((bf16[128,256]{1,0:T(8,128)(2,1)S(1)}, bf16[128,256]{1,0:T(8,128)(2,1)S(1)}, u32[]{:S(2)}, u32[]{:S(2)}) %collective-permute-start.34) | collective-permute-done | bytes 65568 | tf_op jit(solution)/shard_map/ppermute | solution.py:485
  116.1 2.1 %collective-permute-done.39.refs_7_ = bf16[128,256]{1,0:T(8,128)(2,1)} collective-permute-done((bf16[128,256]{1,0:T(8,128)(2,1)}, bf16[128,256]{1,0:T(8,128)(2,1)}, u32[]{:S(2)}, u32[]{:S(2)}) %collective-permute-start.39) | collective-permute-done | bytes 65568 | tf_op jit(solution)/shard_map/ppermute | solution.py:485
  126.1 3.1 %collective-permute-start.41 = (bf16[128,512]{1,0:T(8,128)(2,1)}, bf16[128,512]{1,0:T(8,128)(2,1)}, u32[]{:S(2)}, u32[]{:S(2)}) collective-permute-start(bf16[128,512]{1,0:T(8,128)(2,1)} %get-tuple-element.133), channel_id=1, source_target_pairs={{0,8},{1,9},{2,10},{3,11},{4,12},{5,13},{6,14},{7,15},{8,0},{9,1},... | collective-permute-start | bytes 393224 | tf_op jit(solution)/shard_map/ppermute | solution.py:496
  129.3 6.9 %collective-permute-done.41 = bf16[128,512]{1,0:T(8,128)(2,1)} collective-permute-done((bf16[128,512]{1,0:T(8,128)(2,1)}, bf16[128,512]{1,0:T(8,128)(2,1)}, u32[]{:S(2)}, u32[]{:S(2)}) %collective-permute-start.41) | collective-permute-done | bytes 131104 | tf_op jit(solution)/shard_map/ppermute | solution.py:496
  137.8 4.0 %shard_map.94 = (bf16[1,128,4096]{2,1,0:T(8,128)(2,1)}, f32[8,128]{1,0:T(8,128)}) custom-call(s32[4]{0:T(128)S(1)} %pad_add_fusion.refs_0_, bf16[64,1024]{1,0:T(8,128)(2,1)S(1)} %get-tuple-element.111.refs_1_, bf16[64,1024]{1,0:T(8,128)(2,1)S(1)} %collective-permute-done.25.refs_2_, bf16[64,1024]{1,0:T(8,128)(2,1)S(1)} %collective-permute-done.26.refs_3_, ...), custom_call_target="tpu_custom_call" | custom-call | tf_op jit(solution)/shard_map/pallas_call | solution.py:443
  (133 shorter events, 65.6 us)
Async XLA Ops:
  2.8 20.5 %collective-permute-start = (bf16[128,2048]{1,0:T(8,128)(2,1)}, bf16[128,2048]{1,0:T(8,128)(2,1)}, u32[]{:S(2)}, u32[]{:S(2)}) collective-permute-start(bf16[128,2048]{1,0:T(8,128)(2,1)} %get-tuple-element.72), channel_id=1, source_target_pairs={{0,16},{16,0},{1,17},{17,1},{2,18},{18,2},{3,19},{19,3},{4,20},{20... | collective-permute-start | bytes 1572872 | tf_op jit(solution)/shard_map/ppermute | solution.py:481
  9.9 7.3 %collective-permute-start.3 = (bf16[2,128,256]{2,1,0:T(8,128)(2,1)S(1)}, bf16[2,128,256]{2,1,0:T(8,128)(2,1)S(1)}, u32[]{:S(2)}, u32[]{:S(2)}) collective-permute-start(bf16[2,128,256]{2,1,0:T(8,128)(2,1)S(1)} %get-tuple-element.76), channel_id=1, source_target_pairs={{0,3},{1,4},{2,5},{3,6},{4,7},{5,0},{6,1},{7,2},{8,11},{9,12},{10,... | collective-permute-start | bytes 393224 | tf_op jit(solution)/shard_map/ppermute | solution.py:485
  12.3 8.9 %collective-permute-start.4 = (bf16[2,128,256]{2,1,0:T(8,128)(2,1)S(1)}, bf16[2,128,256]{2,1,0:T(8,128)(2,1)S(1)}, u32[]{:S(2)}, u32[]{:S(2)}) collective-permute-start(bf16[2,128,256]{2,1,0:T(8,128)(2,1)S(1)} %get-tuple-element.77), channel_id=1, source_target_pairs={{0,4},{1,5},{2,6},{3,7},{4,0},{5,1},{6,2},{7,3},{8,12},{9,13},{10,... | collective-permute-start | bytes 393224 | tf_op jit(solution)/shard_map/ppermute | solution.py:485
  26.1 15.7 %all-to-all-start = ((f32[16,2,2,16,128]{4,3,2,1,0:T(8,128)}), f32[16,2,2,16,128]{4,3,2,1,0:T(8,128)}, u32[]{:S(2)}, u32[]{:S(2)}) async-start(f32[16,2,2,16,128]{4,3,2,1,0:T(8,128)} %bitcast.9), calls=%async_computation | async-start | bytes 1048576 | tf_op jit(solution)/shard_map/all_to_all | solution.py:580
  32.0 30.4 %collective-permute-start.16 = (bf16[1024,512]{1,0:T(8,128)(2,1)}, bf16[1024,512]{1,0:T(8,128)(2,1)}, u32[]{:S(2)}, u32[]{:S(2)}) collective-permute-start(bf16[1024,512]{1,0:T(8,128)(2,1)} %get-tuple-element.98), channel_id=1, source_target_pairs={{0,16},{16,0},{1,17},{17,1},{2,18},{18,2},{3,19},{19,3},{4,20},{20... | collective-permute-start | bytes 3145736 | tf_op jit(solution)/shard_map/ppermute | solution.py:481
  36.2 7.5 %collective-permute-start.9 = (bf16[128,512]{1,0:T(8,128)(2,1)}, bf16[128,512]{1,0:T(8,128)(2,1)S(1)}, u32[]{:S(2)}, u32[]{:S(2)}) collective-permute-start(bf16[128,512]{1,0:T(8,128)(2,1)} %get-tuple-element.88), channel_id=1, source_target_pairs={{0,1},{1,2},{2,3},{3,4},{4,5},{5,6},{6,7},{7,0},{8,9},{9,10},{10,1... | collective-permute-start | bytes 393224 | tf_op jit(solution)/shard_map/ppermute | solution.py:485
  36.2 12.0 %collective-permute-start.10 = (bf16[128,512]{1,0:T(8,128)(2,1)}, bf16[128,512]{1,0:T(8,128)(2,1)S(1)}, u32[]{:S(2)}, u32[]{:S(2)}) collective-permute-start(bf16[128,512]{1,0:T(8,128)(2,1)} %get-tuple-element.89), channel_id=1, source_target_pairs={{0,2},{1,3},{2,4},{3,5},{4,6},{5,7},{6,0},{7,1},{8,10},{9,11},{10,... | collective-permute-start | bytes 393224 | tf_op jit(solution)/shard_map/ppermute | solution.py:485
  37.8 10.6 %collective-permute-start.11 = (bf16[128,512]{1,0:T(8,128)(2,1)}, bf16[128,512]{1,0:T(8,128)(2,1)S(1)}, u32[]{:S(2)}, u32[]{:S(2)}) collective-permute-start(bf16[128,512]{1,0:T(8,128)(2,1)} %get-tuple-element.90), channel_id=1, source_target_pairs={{0,3},{1,4},{2,5},{3,6},{4,7},{5,0},{6,1},{7,2},{8,11},{9,12},{10,... | collective-permute-start | bytes 393224 | tf_op jit(solution)/shard_map/ppermute | solution.py:485
  40.1 9.6 %collective-permute-start.12 = (bf16[128,512]{1,0:T(8,128)(2,1)}, bf16[128,512]{1,0:T(8,128)(2,1)}, u32[]{:S(2)}, u32[]{:S(2)}) collective-permute-start(bf16[128,512]{1,0:T(8,128)(2,1)} %get-tuple-element.91), channel_id=1, source_target_pairs={{0,4},{1,5},{2,6},{3,7},{4,0},{5,1},{6,2},{7,3},{8,12},{9,13},{10,... | collective-permute-start | bytes 393224 | tf_op jit(solution)/shard_map/ppermute | solution.py:485
  43.7 14.6 %collective-permute-start.8 = (f32[2,176,128]{2,1,0:T(8,128)S(1)}, f32[2,176,128]{2,1,0:T(8,128)S(1)}, u32[]{:S(2)}, u32[]{:S(2)}) collective-permute-start(f32[2,176,128]{2,1,0:T(8,128)S(1)} %get-tuple-element.86), channel_id=1, source_target_pairs={{0,8},{1,9},{2,10},{3,11},{4,12},{5,13},{6,14},{7,15},{16,24},{17,... | collective-permute-start | bytes 540680 | tf_op jit(solution)/shard_map/ppermute | solution.py:496
  48.2 7.3 %collective-permute-start.13 = (bf16[128,512]{1,0:T(8,128)(2,1)}, bf16[128,512]{1,0:T(8,128)(2,1)S(1)}, u32[]{:S(2)}, u32[]{:S(2)}) collective-permute-start(bf16[128,512]{1,0:T(8,128)(2,1)} %copy-done.23), channel_id=1, source_target_pairs={{0,5},{1,6},{2,7},{3,0},{4,1},{5,2},{6,3},{7,4},{8,13},{9,14},{10,... | collective-permute-start | bytes 393224 | tf_op jit(solution)/shard_map/ppermute | solution.py:485
  48.3 8.6 %collective-permute-start.14 = (bf16[128,512]{1,0:T(8,128)(2,1)}, bf16[128,512]{1,0:T(8,128)(2,1)S(1)}, u32[]{:S(2)}, u32[]{:S(2)}) collective-permute-start(bf16[128,512]{1,0:T(8,128)(2,1)} %copy-done.22), channel_id=1, source_target_pairs={{0,6},{1,7},{2,0},{3,1},{4,2},{5,3},{6,4},{7,5},{8,14},{9,15},{10,... | collective-permute-start | bytes 393224 | tf_op jit(solution)/shard_map/ppermute | solution.py:485
  49.6 8.7 %collective-permute-start.15 = (bf16[128,512]{1,0:T(8,128)(2,1)}, bf16[128,512]{1,0:T(8,128)(2,1)S(1)}, u32[]{:S(2)}, u32[]{:S(2)}) collective-permute-start(bf16[128,512]{1,0:T(8,128)(2,1)} %copy-done.21), channel_id=1, source_target_pairs={{0,7},{1,0},{2,1},{3,2},{4,3},{5,4},{6,5},{7,6},{8,15},{9,8},{10,9... | collective-permute-start | bytes 393224 | tf_op jit(solution)/shard_map/ppermute | solution.py:485
  60.8 15.2 %collective-permute-start.24 = (f32[2,176,128]{2,1,0:T(8,128)S(1)}, f32[2,176,128]{2,1,0:T(8,128)S(1)}, u32[]{:S(2)}, u32[]{:S(2)}) collective-permute-start(f32[2,176,128]{2,1,0:T(8,128)S(1)} %get-tuple-element.110), channel_id=1, source_target_pairs={{8,0},{9,1},{10,2},{11,3},{12,4},{13,5},{14,6},{15,7},{24,16},{25,... | collective-permute-start | bytes 540680 | tf_op jit(solution)/shard_map/ppermute | solution.py:496
  62.3 75.4 %collective-permute-start.32 = (bf16[1024,512]{1,0:T(8,128)(2,1)}, bf16[1024,512]{1,0:T(8,128)(2,1)}, u32[]{:S(2)}, u32[]{:S(2)}) collective-permute-start(bf16[1024,512]{1,0:T(8,128)(2,1)} %collective-permute-done.16.refs_4_.refs_10_), channel_id=1, source_target_pairs={{0,1},{1,0},{2,3},{3,2},{4,5},{5,4},{6,7},{7,6},{8,9},{9,8},{10,11... | collective-permute-start | bytes 3145736 | tf_op jit(solution)/shard_map/ppermute | solution.py:609
  69.7 7.7 %collective-permute-start.19 = (bf16[128,256]{1,0:T(8,128)(2,1)S(1)}, bf16[128,256]{1,0:T(8,128)(2,1)S(1)}, u32[]{:S(2)}, u32[]{:S(2)}) collective-permute-start(bf16[128,256]{1,0:T(8,128)(2,1)S(1)} %get-tuple-element.103), channel_id=1, source_target_pairs={{0,3},{1,4},{2,5},{3,6},{4,7},{5,0},{6,1},{7,2},{8,11},{9,12},{10,... | collective-permute-start | bytes 196616 | tf_op jit(solution)/shard_map/ppermute | solution.py:485
  77.4 11.3 %collective-permute-start.31 = (bf16[64,1024]{1,0:T(8,128)(2,1)S(1)}, bf16[64,1024]{1,0:T(8,128)(2,1)S(1)}, u32[]{:S(2)}, u32[]{:S(2)}) collective-permute-start(bf16[64,1024]{1,0:T(8,128)(2,1)S(1)} %get-tuple-element.111.refs_1_), channel_id=1, source_target_pairs={{0,7},{1,0},{2,1},{3,2},{4,3},{5,4},{6,5},{7,6},{8,15},{9,8},{10,9... | collective-permute-start | bytes 393224 | tf_op jit(solution)/shard_map/ppermute | solution.py:485
  79.2 11.5 %collective-permute-start.30 = (bf16[64,1024]{1,0:T(8,128)(2,1)S(1)}, bf16[64,1024]{1,0:T(8,128)(2,1)S(1)}, u32[]{:S(2)}, u32[]{:S(2)}) collective-permute-start(bf16[64,1024]{1,0:T(8,128)(2,1)S(1)} %get-tuple-element.111.refs_1_), channel_id=1, source_target_pairs={{0,6},{1,7},{2,0},{3,1},{4,2},{5,3},{6,4},{7,5},{8,14},{9,15},{10,... | collective-permute-start | bytes 393224 | tf_op jit(solution)/shard_map/ppermute | solution.py:485
  80.1 10.6 %collective-permute-start.29 = (bf16[64,1024]{1,0:T(8,128)(2,1)S(1)}, bf16[64,1024]{1,0:T(8,128)(2,1)S(1)}, u32[]{:S(2)}, u32[]{:S(2)}) collective-permute-start(bf16[64,1024]{1,0:T(8,128)(2,1)S(1)} %get-tuple-element.111.refs_1_), channel_id=1, source_target_pairs={{0,5},{1,6},{2,7},{3,0},{4,1},{5,2},{6,3},{7,4},{8,13},{9,14},{10,... | collective-permute-start | bytes 393224 | tf_op jit(solution)/shard_map/ppermute | solution.py:485
  90.7 7.3 %collective-permute-start.26 = (bf16[64,1024]{1,0:T(8,128)(2,1)S(1)}, bf16[64,1024]{1,0:T(8,128)(2,1)S(1)}, u32[]{:S(2)}, u32[]{:S(2)}) collective-permute-start(bf16[64,1024]{1,0:T(8,128)(2,1)S(1)} %get-tuple-element.111.refs_1_), channel_id=1, source_target_pairs={{0,2},{1,3},{2,4},{3,5},{4,6},{5,7},{6,0},{7,1},{8,10},{9,11},{10,... | collective-permute-start | bytes 393224 | tf_op jit(solution)/shard_map/ppermute | solution.py:485
  90.7 9.9 %collective-permute-start.25 = (bf16[64,1024]{1,0:T(8,128)(2,1)S(1)}, bf16[64,1024]{1,0:T(8,128)(2,1)S(1)}, u32[]{:S(2)}, u32[]{:S(2)}) collective-permute-start(bf16[64,1024]{1,0:T(8,128)(2,1)S(1)} %get-tuple-element.111.refs_1_), channel_id=1, source_target_pairs={{0,1},{1,2},{2,3},{3,4},{4,5},{5,6},{6,7},{7,0},{8,9},{9,10},{10,1... | collective-permute-start | bytes 393224 | tf_op jit(solution)/shard_map/ppermute | solution.py:485
  102.8 19.9 %collective-permute-start.33 = (bf16[256,512]{1,0:T(8,128)(2,1)}, bf16[256,512]{1,0:T(8,128)(2,1)S(1)}, u32[]{:S(2)}, u32[]{:S(2)}) collective-permute-start(bf16[256,512]{1,0:T(8,128)(2,1)} %get-tuple-element.117), channel_id=1, source_target_pairs={{0,16},{16,0},{1,17},{17,1},{2,18},{18,2},{3,19},{19,3},{4,20},{20... | collective-permute-start | bytes 786440 | tf_op jit(solution)/shard_map/ppermute | solution.py:481
  105.5 7.5 %collective-permute-start.36 = (bf16[128,256]{1,0:T(8,128)(2,1)S(1)}, bf16[128,256]{1,0:T(8,128)(2,1)S(1)}, u32[]{:S(2)}, u32[]{:S(2)}) collective-permute-start(bf16[128,256]{1,0:T(8,128)(2,1)S(1)} %get-tuple-element.122), channel_id=1, source_target_pairs={{0,3},{1,4},{2,5},{3,6},{4,7},{5,0},{6,1},{7,2},{8,11},{9,12},{10,... | collective-permute-start | bytes 196616 | tf_op jit(solution)/shard_map/ppermute | solution.py:485
  126.1 10.1 %collective-permute-start.41 = (bf16[128,512]{1,0:T(8,128)(2,1)}, bf16[128,512]{1,0:T(8,128)(2,1)}, u32[]{:S(2)}, u32[]{:S(2)}) collective-permute-start(bf16[128,512]{1,0:T(8,128)(2,1)} %get-tuple-element.133), channel_id=1, source_target_pairs={{0,8},{1,9},{2,10},{3,11},{4,12},{5,13},{6,14},{7,15},{8,0},{9,1},... | collective-permute-start | bytes 393224 | tf_op jit(solution)/shard_map/ppermute | solution.py:496
  (43 other events, 211.6 us)

commit v4 on v3

--- a/solution.py
+++ b/solution.py
@@ -14,6 +14,7 @@
 GROUP = 8
 TILE = 256
 VMEM_LIMIT = 16 * 1024 * 1024
+VMEM_MOST = 60 * 1024 * 1024
 PSI = 9 * F + 2 * F
 PSI_SCALE = (0.5,) + (1.0,) * 7 + (0.5,)
 
@@ -269,15 +270,10 @@
             carried_ref[head] = dot3(feat, grad)
 
 
-def split_rows_kernel(at_ref, in_ref, *rest):
-    *out_refs, sems = rest
-    group, tok = len(out_refs), out_refs[0].shape[0]
+def leave_kernel(in_ref, out_ref, sems):
+    group, tok = out_ref.shape[:2]
     run_copies(
-        sems,
-        [
-            (in_ref.at[aligned(lax.rem(at_ref[0] + shift, group), tok)], out_ref)
-            for shift, out_ref in enumerate(out_refs)
-        ],
+        sems, [(in_ref.at[i * tok : (i + 1) * tok], out_ref.at[i]) for i in range(group)]
     )
 
 
@@ -344,26 +340,22 @@
     run_copies(sems, [(held_ref, out_ref)])
 
 
-def grad_values_kernel(with_state, at_ref, qk_ref, grad_v_ref, *rest):
+def grad_values_kernel(with_state, qk_ref, grad_v_ref, *rest):
+    *suffix_refs, out_ref, held_ref, sems = rest
     heads = qk_ref.shape[2]
-    group, tok = qk_ref.shape[0], qk_ref.shape[4]
-    suffix_refs, out_refs = rest[: -group - 2], rest[-group - 2 : -2]
-    held_ref, sems = rest[-2:]
     for head in range(heads):
         grad_v = grad_v_ref[head]
         if with_state:
             feat = psi(feature_major(qk_ref, 1, head), False)
             grad_v = grad_v + dot3(suffix_refs[0][head].T, feat)
         held_ref[:, head * DH : (head + 1) * DH] = grad_v.T.astype(bf16)
-    split_rows_kernel(at_ref, held_ref, *out_refs, sems)
-
-
-def unpack_heads_kernel(at_ref, *rest):
-    *part_refs, out_ref = rest
-    group, width = len(part_refs), part_refs[0].shape[1]
-    for shift, part_ref in enumerate(part_refs):
-        src = lax.rem(at_ref[0] + group - shift, group)
-        out_ref[0, :, aligned(src, width)] = part_ref[...]
+    leave_kernel(held_ref, out_ref, sems)
+
+
+def unpack_heads_kernel(in_ref, out_ref):
+    group, _, width = in_ref.shape
+    for member in range(group):
+        out_ref[0, :, member * width : (member + 1) * width] = in_ref[member]
 
 
 def place_rows(at, part_refs, cols, held_ref):
@@ -414,6 +406,14 @@
         out_ref[0, :, pl.ds(first, size)] = dot(rows, weight_ref[...], NT).astype(bf16)
 
 
+def final_sum_kernel(own_ref, *rest):
+    *part_refs, out_ref = rest
+    total = own_ref[...]
+    for part_ref in part_refs:
+        total = total + part_ref[...].astype(f32)
+    out_ref[...] = total
+
+
 VMEM = pl.BlockSpec(memory_space=pltpu.VMEM)
 SMEM = pl.BlockSpec(memory_space=pltpu.SMEM)
 FAR = pl.BlockSpec(memory_space=pltpu.HBM)
@@ -431,6 +431,7 @@
     far_in=(),
     far_out=False,
     copies=(),
+    limit=VMEM_LIMIT,
 ):
     at = [jnp.stack([jnp.int32(s) for s in scalars])] if scalars else []
     count = len(at) + len(operands)
@@ -449,7 +450,7 @@
         + [FAR] * len(after_far),
         out_specs=[FAR if far_out else VMEM] * len(outs) + [VMEM],
         scratch_shapes=[*scratch] + [pltpu.SemaphoreType.DMA((n,)) for n in copies],
-        compiler_params=pltpu.CompilerParams(vmem_limit_bytes=VMEM_LIMIT),
+        compiler_params=pltpu.CompilerParams(vmem_limit_bytes=limit),
         cost_estimate=pl.CostEstimate(flops=0, bytes_accessed=0, transcendentals=0),
     )(*at, *operands, *after, *after_far)
     return results, token
@@ -497,7 +498,7 @@
 
     qk_shape = ((group, 2, heads, F, tok), f32)
     state_shape = ((heads, PSI, DH), f32)
-    blocks_shape = ((tok, heads * DH), bf16)
+    blocks_shape = ((group, tok, heads * DH), bf16)
     rows_shape = ((length, heads * DH), f32)
 
     parts, token = call(
@@ -508,6 +509,7 @@
         far_in=(0,),
         far_out=True,
         copies=(dp_size - 1,),
+        limit=VMEM_MOST,
     )
     arrived = [to_dp(part, shift) for shift, part in enumerate(parts, 1)]
     parts, token = call(
@@ -520,6 +522,7 @@
         far_in=(0, 1),
         far_out=True,
         copies=(2 * group,),
+        limit=VMEM_MOST,
     )
     parts = to_members(parts)
     (vg,), vg_token = call(
@@ -550,6 +553,7 @@
             far_in=(0,),
             far_out=True,
             copies=(group * dp_size * runs,),
+            limit=VMEM_MOST,
         )
     else:
         blocks = tokens[0].reshape(tok, dp_size * runs, group, depth).transpose(2, 0, 1, 3)
@@ -568,7 +572,7 @@
         proj_weight,
         *arrived,
         scalars=(dp_at,),
-        after=(vg_token,),
+        after=(vg_token, token),
         far_in=(1,),
         far_out=True,
         scratch=[
@@ -598,6 +602,7 @@
         far_in=(0,),
         far_out=True,
         copies=(1,),
+        limit=VMEM_MOST,
     )
     fetched = [to_dp(mine, shift) for shift in range(1, dp_size)]
     weights, firsts = [proj_weight], [dp_at * share]
@@ -639,15 +644,15 @@
         *prefix,
         after_far=fetched,
     )
-    attended, attended_token = call(
-        split_rows_kernel,
-        [blocks_shape] * group,
+    (attended,), attended_token = call(
+        leave_kernel,
+        [blocks_shape],
         attended,
-        scalars=(member,),
         after=(token,),
         far_out=True,
         copies=(group,),
     )
+    attended = exchange(attended)
     (rows,), token = call(
         functools.partial(rows_kernel, with_state),
         [((2 * heads * F, length), bf16)],
@@ -667,21 +672,20 @@
         scalars=(member,),
         after=(token,),
     )
-    grad_values, token = call(
+    (grad_values,), token = call(
         functools.partial(grad_values_kernel, with_state),
-        [blocks_shape] * group,
+        [blocks_shape],
         qk,
         grad_v,
         *suffix,
-        scalars=(member,),
         after=(token,),
         far_out=True,
         scratch=[pltpu.VMEM((length, heads * DH), bf16)],
         copies=(group,),
     )
-    attended, grad_values = to_members(attended), to_members(grad_values)
+    grad_values = exchange(grad_values)
     (attended,), attended_token = call(
-        unpack_heads_kernel, [((1, tok, H * DH), bf16)], *attended, scalars=(member,)
+        unpack_heads_kernel, [((1, tok, H * DH), bf16)], attended
     )
 
     held = pltpu.VMEM((cols, length), bf16)
@@ -691,15 +695,14 @@
         *rows,
         token_cols,
         scalars=(dp_at, member),
-        after=(attended_token,),
+        after=(attended_token, token),
         scratch=[pltpu.VMEM((dp_size * runs * depth, cols), f32), held],
     )
     parts = [to_dp(part, shift) for shift, part in enumerate(parts, 1)]
     (grad_values,), values_token = call(
         unpack_heads_kernel,
         [((1, tok, H * DH), bf16)],
-        *grad_values,
-        scalars=(member,),
+        grad_values,
         after=(token,),
     )
     (grad_proj, *parts), token = call(
@@ -711,7 +714,7 @@
         after=(values_token,),
         scratch=[pltpu.VMEM((runs * depth, cols), f32)],
     )
-    (grad_tokens,), _ = call(
+    (grad_tokens,), token = call(
         functools.partial(grad_tokens_kernel, group),
         [((1, tok, width), bf16)],
         *rows,
@@ -720,8 +723,13 @@
         after=(token,),
         scratch=[pltpu.VMEM((cols, tok), bf16)],
     )
-    for shift, part in enumerate(parts, 1):
-        grad_proj = grad_proj + to_run(part, shift, True).astype(f32)
+    (grad_proj,), _ = call(
+        final_sum_kernel,
+        [((depth, cols), f32)],
+        grad_proj,
+        *[to_run(part, shift, True) for shift, part in enumerate(parts, 1)],
+        after=(token,),
+    )
     return (attended, grad_tokens, grad_values, grad_proj)
 
 

time: 143 us -> 256 us (1.79)
  Pallas kernels: 35.7 us -> 147 us
  local copies, waits for them, and re-layouts: 13.2 us -> 18.5 us
    pallas_call x20 -> x21, Pallas kernels: 35.7 us -> 147 us  [call(): pl.pallas_call(kernel, out_shape=[jax.ShapeDtypeStruct(shape, kind) for s...]
    ppermute x35 -> x21, waiting for transfers between devices: 25.7 us -> 11.3 us  [to_member(): return lax.ppermute(x, 'ctx', pairs)]
    all_to_all x0 -> x2, starting transfers between devices: none -> 12.2 us  [exchange(): lax.all_to_all(x, 'ctx', split_axis=0, concat_axis=0, tiled=True, axis_in...]
    ppermute x35 -> x21, starting transfers between devices: 37.9 us -> 29.2 us  [to_member(): return lax.ppermute(x, 'ctx', pairs)]
    ppermute x3, waiting for transfers between devices: 0.01 us -> 7.8 us  [to_dp(): lax.ppermute(x, 'dp', [(i, (i + shift) % dp_size) for i in range(dp_size)])]
    ppermute x3, waiting for transfers between devices: 6.86 us -> 12.4 us  [to_run(): return lax.ppermute(x, 'ctx', pairs)]
    unnamed x48 -> x86, local copies, waits for them, and re-layouts: 13.2 us -> 18.5 us
    ppermute x3, starting transfers between devices: 9.09 us -> 5.84 us  [to_run(): return lax.ppermute(x, 'ctx', pairs)]
  transfers between devices with their start and end apart: 43 -> 31, of which waited for: 19 -> 10; matrix products, arithmetic and copies ran while one was open for 1% -> 0% of each run, Pallas kernels for 20% -> 47%
where the time goes in v4:
time: 256 us; the launch traced here: 255 us
  Pallas kernels  147 us (57%)
  starting transfers between devices  57.1 us (22%)
  waiting for transfers between devices  31.5 us (12%)
  local copies, waits for them, and re-layouts  18.5 us (7%)
    pallas_call x21, Pallas kernels, call(): pl.pallas_call(kernel, out_shape=[jax.ShapeDtypeStruct(shape, kind) for s...  147 us
    ppermute x21, starting transfers between devices, to_member(): return lax.ppermute(x, 'ctx', pairs)  29.2 us
    unnamed x86, local copies, waits for them, and re-layouts  18.5 us
    ppermute x3, waiting for transfers between devices, to_run(): return lax.ppermute(x, 'ctx', pairs)  12.4 us
    all_to_all x2, starting transfers between devices, exchange(): lax.all_to_all(x, 'ctx', split_axis=0, concat_axis=0, tiled=True, axis_in...  12.2 us
    ppermute x21, waiting for transfers between devices, to_member(): return lax.ppermute(x, 'ctx', pairs)  11.3 us
    ppermute x3, waiting for transfers between devices, to_dp(): lax.ppermute(x, 'dp', [(i, (i + shift) % dp_size) for i in range(dp_size)])  7.8 us
    ppermute x3, starting transfers between devices, to_run(): return lax.ppermute(x, 'ctx', pairs)  5.84 us
  transfers between devices with their start and end apart: 31, of which 10 were waited for; matrix products, arithmetic and copies ran while one was open for 0% of the time, Pallas kernels for 47%

profile of v4, /device:TPU:0, one launch (start us, length us, event | category | flops | bytes accessed | tf_op | source)
XLA Modules:
  0.0 255.1 jit_solution(18386474590371409888)
XLA Ops:
  0.6 17.6 %shard_map.75 = (bf16[128,2048]{1,0:T(8,128)(2,1)}, f32[8,128]{1,0:T(8,128)}) custom-call(s32[1]{0:T(128)} %bitcast.refs_0_, bf16[1,128,4096]{2,1,0:T(8,128)(2,1)} %refs_1_.8), custom_call_target="tpu_custom_call" | custom-call | tf_op jit(solution)/shard_map/pallas_call | solution.py:444
  18.2 3.0 %collective-permute-start = (bf16[128,2048]{1,0:T(8,128)(2,1)}, bf16[128,2048]{1,0:T(8,128)(2,1)}, u32[]{:S(2)}, u32[]{:S(2)}) collective-permute-start(bf16[128,2048]{1,0:T(8,128)(2,1)} %get-tuple-element.62), channel_id=1, source_target_pairs={{0,16},{16,0},{1,17},{17,1},{2,18},{18,2},{3,19},{19,3},{4,20},{20... | collective-permute-start | bytes 1572872 | tf_op jit(solution)/shard_map/ppermute | solution.py:482
  21.2 33.6 %shard_map.76 = (bf16[2,128,256]{2,1,0:T(8,128)(2,1)}, bf16[2,128,256]{2,1,0:T(8,128)(2,1)}, bf16[2,128,256]{2,1,0:T(8,128)(2,1)}, bf16[2,128,256]{2,1,0:T(8,128...) custom-call(s32[1]{0:T(128)} %bitcast.1.refs_0_, ...), custom_call_target="tpu_custom_call" | custom-call | tf_op jit(solution)/shard_map/pallas_call | solution.py:444
  56.5 2.4 collective-permute-start.3
  64.0 2.2 collective-permute-start.7
  69.3 33.7 %shard_map.79 = (bf16[128,512]{1,0:T(8,128)(2,1)}, bf16[128,512]{1,0:T(8,128)(2,1)}, bf16[128,512]{1,0:T(8,128)(2,1)}, bf16[128,512]{1,0:T(8,128)(2,1)}, bf16[12...) custom-call(s32[1]{0:T(128)} %bitcast.1.refs_0_, ...), custom_call_target="tpu_custom_call" | custom-call | tf_op jit(solution)/shard_map/pallas_call | solution.py:444
  111.9 3.8 %all-to-all-start = ((f32[16,2,2,16,128]{4,3,2,1,0:T(8,128)}), f32[16,2,2,16,128]{4,3,2,1,0:T(8,128)S(1)}, u32[]{:S(2)}, u32[]{:S(2)}) async-start(f32[16,2,2,16,128]{4,3,2,1,0:T(8,128)} %bitcast.10), calls=%async_computation | async-start | bytes 1048576 | tf_op jit(solution)/shard_map/all_to_all | solution.py:584
  115.8 33.5 %shard_map.84 = (bf16[1024,512]{1,0:T(8,128)(2,1)}, f32[8,128]{1,0:T(8,128)}) custom-call(s32[1]{0:T(128)} %bitcast.4.refs_0_, bf16[2048,512]{1,0:T(8,128)(2,1)} %refs_9_.1, f32[8,128]{1,0:T(8,128)} %copy-done.34), custom_call_target="tpu_custom_call" | custom-call | tf_op jit(solution)/shard_map/pallas_call | solution.py:444
  152.8 2.3 collective-permute-start.11
  157.4 4.5 %collective-permute-start.8 = (f32[2,176,128]{2,1,0:T(8,128)S(1)}, f32[2,176,128]{2,1,0:T(8,128)S(1)}, u32[]{:S(2)}, u32[]{:S(2)}) collective-permute-start(f32[2,176,128]{2,1,0:T(8,128)S(1)} %get-tuple-element.78), channel_id=1, source_target_pairs={{0,8},{1,9},{2,10},{3,11},{4,12},{5,13},{6,14},{7,15},{16,24},{17,... | collective-permute-start | bytes 540680 | tf_op jit(solution)/shard_map/ppermute | solution.py:497
  162.0 2.5 collective-permute-start.14
  164.4 2.6 %collective-permute-start.15 = (bf16[128,512]{1,0:T(8,128)(2,1)S(1)}, bf16[128,512]{1,0:T(8,128)(2,1)S(1)}, u32[]{:S(2)}, u32[]{:S(2)}) collective-permute-start(bf16[128,512]{1,0:T(8,128)(2,1)S(1)} %copy-done.36), channel_id=1, source_target_pairs={{0,7},{1,0},{2,1},{3,2},{4,3},{5,4},{6,5},{7,6},{8,15},{9,8},{10,9... | collective-permute-start | bytes 393224 | tf_op jit(solution)/shard_map/ppermute | solution.py:486
  167.1 3.6 %shard_map.82 = (f32[1024,256]{1,0:T(8,128)S(1)}, f32[8,128]{1,0:T(8,128)}) custom-call(f32[8,2,2,16,128]{4,3,2,1,0:T(8,128)S(1)} %get-tuple-element.76.refs_0_, bf16[8,2,128,256]{3,2,1,0:T(8,128)(2,1)S(1)} %get-tuple-element.75.refs_1_), custom_call_target="tpu_custom_call" | custom-call | tf_op jit(solution)/shard_map/pallas_call | solution.py:444
  171.9 2.5 shard_map.83
  175.1 4.6 %shard_map.85 = (f32[2,2,16,1024]{3,2,1,0:T(8,128)S(1)}, f32[2,128,1024]{2,1,0:T(8,128)S(1)}, f32[8,128]{1,0:T(8,128)S(1)}) custom-call(f32[8,2,2,16,128]{4,3,2,1,0:T(8,128)S(1)} %get-tuple-element.76.refs_0_, bf16[8,2,128,256]{3,2,1,0:T(8,128)(2,1)S(1)} %get-tuple-element.75.refs_1_, f32[1024,256]{1,0:T(8,128)S(1)} %get-tuple-element.87.refs_2_, ...), custom_call_target="tpu_custom_call" | custom-call | tf_op jit(solution)/shard_map/pallas_call | solution.py:444
  181.2 3.8 %all-to-all-start.1 = ((bf16[8,128,256]{2,1,0:T(8,128)(2,1)}), bf16[8,128,256]{2,1,0:T(8,128)(2,1)S(1)}, u32[]{:S(2)}, u32[]{:S(2)}) async-start(bf16[8,128,256]{2,1,0:T(8,128)(2,1)} %get-tuple-element.91), calls=%async_computation.1 | async-start | bytes 1048576 | tf_op jit(solution)/shard_map/all_to_all | solution.py:477
  186.3 9.5 %collective-permute-done.17.refs_3_.refs_2_ = f32[2,176,128]{2,1,0:T(8,128)S(1)} collective-permute-done((f32[2,176,128]{2,1,0:T(8,128)S(1)}, f32[2,176,128]{2,1,0:T(8,128)S(1)}, u32[]{:S(2)}, u32[]{:S(2)}) %collective-permute-start.17) | collective-permute-done | bytes 180256 | tf_op jit(solution)/shard_map/ppermute | solution.py:497
  198.2 8.3 %all-to-all-start.2 = ((bf16[8,128,256]{2,1,0:T(8,128)(2,1)}), bf16[8,128,256]{2,1,0:T(8,128)(2,1)S(1)}, u32[]{:S(2)}, u32[]{:S(2)}) async-start(bf16[8,128,256]{2,1,0:T(8,128)(2,1)} %get-tuple-element.104), calls=%async_computation.2 | async-start | bytes 1048576 | tf_op jit(solution)/shard_map/all_to_all | solution.py:477
  207.1 2.5 collective-permute-start.24
  211.5 4.9 %collective-permute-done.24.refs_8_ = bf16[64,1024]{1,0:T(8,128)(2,1)S(1)} collective-permute-done((bf16[64,1024]{1,0:T(8,128)(2,1)S(1)}, bf16[64,1024]{1,0:T(8,128)(2,1)S(1)}, u32[]{:S(2)}, u32[]{:S(2)}) %collective-permute-start.24) | collective-permute-done | bytes 131104 | tf_op jit(solution)/shard_map/ppermute | solution.py:486
  216.4 3.5 %collective-permute-start.20 = (bf16[64,1024]{1,0:T(8,128)(2,1)S(1)}, bf16[64,1024]{1,0:T(8,128)(2,1)S(1)}, u32[]{:S(2)}, u32[]{:S(2)}) collective-permute-start(bf16[64,1024]{1,0:T(8,128)(2,1)S(1)} %get-tuple-element.95.refs_1_), channel_id=1, source_target_pairs={{0,3},{1,4},{2,5},{3,6},{4,7},{5,0},{6,1},{7,2},{8,11},{9,12},{10,... | collective-permute-start | bytes 393224 | tf_op jit(solution)/shard_map/ppermute | solution.py:486
  237.1 7.1 %collective-permute-done.26.refs_2_ = bf16[256,512]{1,0:T(8,128)(2,1)} collective-permute-done((bf16[256,512]{1,0:T(8,128)(2,1)}, bf16[256,512]{1,0:T(8,128)(2,1)}, u32[]{:S(2)}, u32[]{:S(2)}) %collective-permute-start.26) | collective-permute-done | bytes 262176 | tf_op jit(solution)/shard_map/ppermute | solution.py:482
  247.4 4.0 %shard_map.94 = (bf16[1,128,4096]{2,1,0:T(8,128)(2,1)}, f32[8,128]{1,0:T(8,128)S(1)}) custom-call(s32[4]{0:T(128)S(1)} %pad_add_fusion.refs_0_, bf16[64,1024]{1,0:T(8,128)(2,1)S(1)} %get-tuple-element.95.refs_1_, bf16[64,1024]{1,0:T(8,128)(2,1)S(1)} %copy-done.6, bf16[64,1024]{1,0:T(8,128)(2,1)S(1)} %collective-permute-done.19.refs_3_, ...), custom_call_target="tpu_custom_call" | custom-call | tf_op jit(solution)/shard_map/pallas_call | solution.py:444
  251.5 2.9 %collective-permute-done.27.refs_1_ = bf16[128,512]{1,0:T(8,128)(2,1)S(1)} collective-permute-done((bf16[128,512]{1,0:T(8,128)(2,1)S(1)}, bf16[128,512]{1,0:T(8,128)(2,1)S(1)}, u32[]{:S(2)}, u32[]{:S(2)}) %collective-permute-start.27) | collective-permute-done | bytes 131104 | tf_op jit(solution)/shard_map/ppermute | solution.py:497
  (147 shorter events, 54.9 us)
Async XLA Ops:
  18.2 89.6 %collective-permute-start = (bf16[128,2048]{1,0:T(8,128)(2,1)}, bf16[128,2048]{1,0:T(8,128)(2,1)}, u32[]{:S(2)}, u32[]{:S(2)}) collective-permute-start(bf16[128,2048]{1,0:T(8,128)(2,1)} %get-tuple-element.62), channel_id=1, source_target_pairs={{0,16},{16,0},{1,17},{17,1},{2,18},{18,2},{3,19},{19,3},{4,20},{20... | collective-permute-start | bytes 1572872 | tf_op jit(solution)/shard_map/ppermute | solution.py:482
  58.9 44.2 %collective-permute-start.4 = (bf16[2,128,256]{2,1,0:T(8,128)(2,1)}, bf16[2,128,256]{2,1,0:T(8,128)(2,1)S(1)}, u32[]{:S(2)}, u32[]{:S(2)}) collective-permute-start(bf16[2,128,256]{2,1,0:T(8,128)(2,1)} %get-tuple-element.67), channel_id=1, source_target_pairs={{0,4},{1,5},{2,6},{3,7},{4,0},{5,1},{6,2},{7,3},{8,12},{9,13},{10,... | collective-permute-start | bytes 393224 | tf_op jit(solution)/shard_map/ppermute | solution.py:486
  61.2 41.8 %collective-permute-start.5 = (bf16[2,128,256]{2,1,0:T(8,128)(2,1)}, bf16[2,128,256]{2,1,0:T(8,128)(2,1)S(1)}, u32[]{:S(2)}, u32[]{:S(2)}) collective-permute-start(bf16[2,128,256]{2,1,0:T(8,128)(2,1)} %get-tuple-element.68), channel_id=1, source_target_pairs={{0,5},{1,6},{2,7},{3,0},{4,1},{5,2},{6,3},{7,4},{8,13},{9,14},{10,... | collective-permute-start | bytes 393224 | tf_op jit(solution)/shard_map/ppermute | solution.py:486
  62.4 41.3 %collective-permute-start.6 = (bf16[2,128,256]{2,1,0:T(8,128)(2,1)}, bf16[2,128,256]{2,1,0:T(8,128)(2,1)S(1)}, u32[]{:S(2)}, u32[]{:S(2)}) collective-permute-start(bf16[2,128,256]{2,1,0:T(8,128)(2,1)} %get-tuple-element.69), channel_id=1, source_target_pairs={{0,6},{1,7},{2,0},{3,1},{4,2},{5,3},{6,4},{7,5},{8,14},{9,15},{10,... | collective-permute-start | bytes 393224 | tf_op jit(solution)/shard_map/ppermute | solution.py:486
  64.0 40.4 %collective-permute-start.7 = (bf16[2,128,256]{2,1,0:T(8,128)(2,1)}, bf16[2,128,256]{2,1,0:T(8,128)(2,1)S(1)}, u32[]{:S(2)}, u32[]{:S(2)}) collective-permute-start(bf16[2,128,256]{2,1,0:T(8,128)(2,1)} %get-tuple-element.70), channel_id=1, source_target_pairs={{0,7},{1,0},{2,1},{3,2},{4,3},{5,4},{6,5},{7,6},{8,15},{9,8},{10,9... | collective-permute-start | bytes 393224 | tf_op jit(solution)/shard_map/ppermute | solution.py:486
  111.9 43.8 %all-to-all-start = ((f32[16,2,2,16,128]{4,3,2,1,0:T(8,128)}), f32[16,2,2,16,128]{4,3,2,1,0:T(8,128)S(1)}, u32[]{:S(2)}, u32[]{:S(2)}) async-start(f32[16,2,2,16,128]{4,3,2,1,0:T(8,128)} %bitcast.10), calls=%async_computation | async-start | bytes 1048576 | tf_op jit(solution)/shard_map/all_to_all | solution.py:584
  149.2 25.9 %collective-permute-start.16 = (bf16[1024,512]{1,0:T(8,128)(2,1)}, bf16[1024,512]{1,0:T(8,128)(2,1)}, u32[]{:S(2)}, u32[]{:S(2)}) collective-permute-start(bf16[1024,512]{1,0:T(8,128)(2,1)} %get-tuple-element.89), channel_id=1, source_target_pairs={{0,16},{16,0},{1,17},{17,1},{2,18},{18,2},{3,19},{19,3},{4,20},{20... | collective-permute-start | bytes 3145736 | tf_op jit(solution)/shard_map/ppermute | solution.py:482
  151.2 10.6 %collective-permute-start.10 = (bf16[128,512]{1,0:T(8,128)(2,1)S(1)}, bf16[128,512]{1,0:T(8,128)(2,1)S(1)}, u32[]{:S(2)}, u32[]{:S(2)}) collective-permute-start(bf16[128,512]{1,0:T(8,128)(2,1)S(1)} %copy-done.41), channel_id=1, source_target_pairs={{0,2},{1,3},{2,4},{3,5},{4,6},{5,7},{6,0},{7,1},{8,10},{9,11},{10,... | collective-permute-start | bytes 393224 | tf_op jit(solution)/shard_map/ppermute | solution.py:486
  152.8 9.2 %collective-permute-start.11 = (bf16[128,512]{1,0:T(8,128)(2,1)S(1)}, bf16[128,512]{1,0:T(8,128)(2,1)S(1)}, u32[]{:S(2)}, u32[]{:S(2)}) collective-permute-start(bf16[128,512]{1,0:T(8,128)(2,1)S(1)} %copy-done.40), channel_id=1, source_target_pairs={{0,3},{1,4},{2,5},{3,6},{4,7},{5,0},{6,1},{7,2},{8,11},{9,12},{10,... | collective-permute-start | bytes 393224 | tf_op jit(solution)/shard_map/ppermute | solution.py:486
  155.1 9.4 %collective-permute-start.12 = (bf16[128,512]{1,0:T(8,128)(2,1)S(1)}, bf16[128,512]{1,0:T(8,128)(2,1)S(1)}, u32[]{:S(2)}, u32[]{:S(2)}) collective-permute-start(bf16[128,512]{1,0:T(8,128)(2,1)S(1)} %copy-done.39), channel_id=1, source_target_pairs={{0,4},{1,5},{2,6},{3,7},{4,0},{5,1},{6,2},{7,3},{8,12},{9,13},{10,... | collective-permute-start | bytes 393224 | tf_op jit(solution)/shard_map/ppermute | solution.py:486
  157.4 14.6 %collective-permute-start.8 = (f32[2,176,128]{2,1,0:T(8,128)S(1)}, f32[2,176,128]{2,1,0:T(8,128)S(1)}, u32[]{:S(2)}, u32[]{:S(2)}) collective-permute-start(f32[2,176,128]{2,1,0:T(8,128)S(1)} %get-tuple-element.78), channel_id=1, source_target_pairs={{0,8},{1,9},{2,10},{3,11},{4,12},{5,13},{6,14},{7,15},{16,24},{17,... | collective-permute-start | bytes 540680 | tf_op jit(solution)/shard_map/ppermute | solution.py:497
  161.9 8.8 %collective-permute-start.13 = (bf16[128,512]{1,0:T(8,128)(2,1)S(1)}, bf16[128,512]{1,0:T(8,128)(2,1)S(1)}, u32[]{:S(2)}, u32[]{:S(2)}) collective-permute-start(bf16[128,512]{1,0:T(8,128)(2,1)S(1)} %copy-done.38), channel_id=1, source_target_pairs={{0,5},{1,6},{2,7},{3,0},{4,1},{5,2},{6,3},{7,4},{8,13},{9,14},{10,... | collective-permute-start | bytes 393224 | tf_op jit(solution)/shard_map/ppermute | solution.py:486
  162.0 8.7 %collective-permute-start.14 = (bf16[128,512]{1,0:T(8,128)(2,1)S(1)}, bf16[128,512]{1,0:T(8,128)(2,1)S(1)}, u32[]{:S(2)}, u32[]{:S(2)}) collective-permute-start(bf16[128,512]{1,0:T(8,128)(2,1)S(1)} %copy-done.37), channel_id=1, source_target_pairs={{0,6},{1,7},{2,0},{3,1},{4,2},{5,3},{6,4},{7,5},{8,14},{9,15},{10,... | collective-permute-start | bytes 393224 | tf_op jit(solution)/shard_map/ppermute | solution.py:486
  181.2 17.0 %all-to-all-start.1 = ((bf16[8,128,256]{2,1,0:T(8,128)(2,1)}), bf16[8,128,256]{2,1,0:T(8,128)(2,1)S(1)}, u32[]{:S(2)}, u32[]{:S(2)}) async-start(bf16[8,128,256]{2,1,0:T(8,128)(2,1)} %get-tuple-element.91), calls=%async_computation.1 | async-start | bytes 1048576 | tf_op jit(solution)/shard_map/all_to_all | solution.py:477
  185.0 10.8 %collective-permute-start.17 = (f32[2,176,128]{2,1,0:T(8,128)S(1)}, f32[2,176,128]{2,1,0:T(8,128)S(1)}, u32[]{:S(2)}, u32[]{:S(2)}) collective-permute-start(f32[2,176,128]{2,1,0:T(8,128)S(1)} %get-tuple-element.94), channel_id=1, source_target_pairs={{8,0},{9,1},{10,2},{11,3},{12,4},{13,5},{14,6},{15,7},{24,16},{25,... | collective-permute-start | bytes 540680 | tf_op jit(solution)/shard_map/ppermute | solution.py:497
  198.2 38.1 %all-to-all-start.2 = ((bf16[8,128,256]{2,1,0:T(8,128)(2,1)}), bf16[8,128,256]{2,1,0:T(8,128)(2,1)S(1)}, u32[]{:S(2)}, u32[]{:S(2)}) async-start(bf16[8,128,256]{2,1,0:T(8,128)(2,1)} %get-tuple-element.104), calls=%async_computation.2 | async-start | bytes 1048576 | tf_op jit(solution)/shard_map/all_to_all | solution.py:477
  206.6 39.9 %collective-permute-start.25 = (bf16[1024,512]{1,0:T(8,128)(2,1)}, bf16[1024,512]{1,0:T(8,128)(2,1)}, u32[]{:S(2)}, u32[]{:S(2)}) collective-permute-start(bf16[1024,512]{1,0:T(8,128)(2,1)} %collective-permute-done.16.refs_4_.refs_10_), channel_id=1, source_target_pairs={{0,1},{1,0},{2,3},{3,2},{4,5},{5,4},{6,7},{7,6},{8,9},{9,8},{10,11... | collective-permute-start | bytes 3145736 | tf_op jit(solution)/shard_map/ppermute | solution.py:614
  207.1 9.3 %collective-permute-start.24 = (bf16[64,1024]{1,0:T(8,128)(2,1)S(1)}, bf16[64,1024]{1,0:T(8,128)(2,1)S(1)}, u32[]{:S(2)}, u32[]{:S(2)}) collective-permute-start(bf16[64,1024]{1,0:T(8,128)(2,1)S(1)} %get-tuple-element.95.refs_1_), channel_id=1, source_target_pairs={{0,7},{1,0},{2,1},{3,2},{4,3},{5,4},{6,5},{7,6},{8,15},{9,8},{10,9... | collective-permute-start | bytes 393224 | tf_op jit(solution)/shard_map/ppermute | solution.py:486
  209.6 11.4 %collective-permute-start.23 = (bf16[64,1024]{1,0:T(8,128)(2,1)S(1)}, bf16[64,1024]{1,0:T(8,128)(2,1)S(1)}, u32[]{:S(2)}, u32[]{:S(2)}) collective-permute-start(bf16[64,1024]{1,0:T(8,128)(2,1)S(1)} %get-tuple-element.95.refs_1_), channel_id=1, source_target_pairs={{0,6},{1,7},{2,0},{3,1},{4,2},{5,3},{6,4},{7,5},{8,14},{9,15},{10,... | collective-permute-start | bytes 393224 | tf_op jit(solution)/shard_map/ppermute | solution.py:486
  210.2 12.8 %collective-permute-start.22 = (bf16[64,1024]{1,0:T(8,128)(2,1)S(1)}, bf16[64,1024]{1,0:T(8,128)(2,1)S(1)}, u32[]{:S(2)}, u32[]{:S(2)}) collective-permute-start(bf16[64,1024]{1,0:T(8,128)(2,1)S(1)} %get-tuple-element.95.refs_1_), channel_id=1, source_target_pairs={{0,5},{1,6},{2,7},{3,0},{4,1},{5,2},{6,3},{7,4},{8,13},{9,14},{10,... | collective-permute-start | bytes 393224 | tf_op jit(solution)/shard_map/ppermute | solution.py:486
  210.2 22.5 %collective-permute-start.21 = (bf16[64,1024]{1,0:T(8,128)(2,1)S(1)}, bf16[64,1024]{1,0:T(8,128)(2,1)S(1)}, u32[]{:S(2)}, u32[]{:S(2)}) collective-permute-start(bf16[64,1024]{1,0:T(8,128)(2,1)S(1)} %get-tuple-element.95.refs_1_), channel_id=1, source_target_pairs={{0,4},{1,5},{2,6},{3,7},{4,0},{5,1},{6,2},{7,3},{8,12},{9,13},{10,... | collective-permute-start | bytes 393224 | tf_op jit(solution)/shard_map/ppermute | solution.py:486
  216.4 16.3 %collective-permute-start.20 = (bf16[64,1024]{1,0:T(8,128)(2,1)S(1)}, bf16[64,1024]{1,0:T(8,128)(2,1)S(1)}, u32[]{:S(2)}, u32[]{:S(2)}) collective-permute-start(bf16[64,1024]{1,0:T(8,128)(2,1)S(1)} %get-tuple-element.95.refs_1_), channel_id=1, source_target_pairs={{0,3},{1,4},{2,5},{3,6},{4,7},{5,0},{6,1},{7,2},{8,11},{9,12},{10,... | collective-permute-start | bytes 393224 | tf_op jit(solution)/shard_map/ppermute | solution.py:486
  221.0 11.7 %collective-permute-start.19 = (bf16[64,1024]{1,0:T(8,128)(2,1)S(1)}, bf16[64,1024]{1,0:T(8,128)(2,1)S(1)}, u32[]{:S(2)}, u32[]{:S(2)}) collective-permute-start(bf16[64,1024]{1,0:T(8,128)(2,1)S(1)} %get-tuple-element.95.refs_1_), channel_id=1, source_target_pairs={{0,2},{1,3},{2,4},{3,5},{4,6},{5,7},{6,0},{7,1},{8,10},{9,11},{10,... | collective-permute-start | bytes 393224 | tf_op jit(solution)/shard_map/ppermute | solution.py:486
  223.0 9.7 %collective-permute-start.18 = (bf16[64,1024]{1,0:T(8,128)(2,1)S(1)}, bf16[64,1024]{1,0:T(8,128)(2,1)S(1)}, u32[]{:S(2)}, u32[]{:S(2)}) collective-permute-start(bf16[64,1024]{1,0:T(8,128)(2,1)S(1)} %get-tuple-element.95.refs_1_), channel_id=1, source_target_pairs={{0,1},{1,2},{2,3},{3,4},{4,5},{5,6},{6,7},{7,0},{8,9},{9,10},{10,1... | collective-permute-start | bytes 393224 | tf_op jit(solution)/shard_map/ppermute | solution.py:486
  (50 other events, 653.3 us)

commit v5 on v4

--- a/solution.py
+++ b/solution.py
@@ -102,14 +102,29 @@
         copy.wait()
 
 
+def relay(held_ref, sems, pairs):
+    loads, stores = [], []
+    for i, (source, target) in enumerate(pairs):
+        held = held_ref.at[i]
+        loads.append(pltpu.make_async_copy(source, held, sems.at[2 * i]))
+        stores.append(pltpu.make_async_copy(held, target, sems.at[2 * i + 1]))
+        loads[-1].start()
+    for load, store in zip(loads, stores):
+        load.wait()
+        store.start()
+    for store in stores:
+        store.wait()
+
+
 def aligned(at, size):
     return pl.ds(pl.multiple_of(at * size, size), size)
 
 
 def token_parts_kernel(at_ref, tokens_ref, *rest):
-    *out_refs, sems = rest
+    *out_refs, held_ref, sems = rest
     count, share = len(out_refs) + 1, out_refs[0].shape[1]
-    run_copies(
+    relay(
+        held_ref,
         sems,
         [
             (tokens_ref.at[0, :, aligned(lax.rem(at_ref[0] + shift, count), share)], out_ref)
@@ -119,14 +134,14 @@
 
 
 def pack_heads_kernel(at_ref, values_ref, grad_ref, *rest):
-    *out_refs, sems = rest
+    *out_refs, held_ref, sems = rest
     width = out_refs[0].shape[2]
     pairs = []
     for shift, out_ref in enumerate(out_refs):
         cols = aligned(lax.rem(at_ref[0] + shift, len(out_refs)), width)
         pairs.append((values_ref.at[0, :, cols], out_ref.at[0]))
         pairs.append((grad_ref.at[0, :, cols], out_ref.at[1]))
-    run_copies(sems, pairs)
+    relay(held_ref, sems, pairs)
 
 
 def collect_heads_kernel(at_ref, *rest):
@@ -169,45 +184,32 @@
                 out_ref[member, which, head] = projected[first : first + feat]
 
 
-def project_kernel(at_ref, tokens_ref, weight_ref, out_ref, part_ref, sem):
+def project_kernel(at_ref, tokens_ref, weight_ref, out_ref, weight_out_ref, part_ref, sem):
     share = part_ref.shape[1]
     run_copies(sem, [(tokens_ref.at[0, :, aligned(at_ref[0], share)], part_ref)])
+    weight_out_ref[...] = weight_ref[...]
     write_blocks(dot(part_ref[...], weight_ref[...]).T, out_ref)
 
 
 def project_rest_kernel(at_ref, own_ref, weight_ref, *rest):
-    *part_refs, out_ref, slots_ref, held_ref, sems, out_sems = rest
+    *part_refs, out_ref = rest
     count = len(part_refs) + 1
     at = at_ref[0]
-    pieces, size = held_ref.shape[:2]
-    loads = [
-        pltpu.make_async_copy(
-            weight_ref.at[i * size : (i + 1) * size], held_ref.at[i], sems.at[i]
-        )
-        for i in range(pieces)
-    ]
-    for load in loads:
-        load.start()
-    copies = [pltpu.make_async_copy(own_ref, out_ref.at[at], out_sems.at[0])]
-    copies[0].start()
+    out_ref[at] = own_ref[...]
     for shift, part_ref in enumerate(part_refs, 1):
-        total = 0.0
-        for i, load in enumerate(loads):
-            if shift == 1:
-                load.wait()
-            total = total + dot(part_ref[:, i * size : (i + 1) * size], held_ref[i])
-        write_blocks(total.T, slots_ref.at[shift - 1])
         owner = lax.rem(at + count - shift, count)
-        copies.append(
-            pltpu.make_async_copy(slots_ref.at[shift - 1], out_ref.at[owner], out_sems.at[shift])
-        )
-        copies[-1].start()
-    for copy in copies:
-        copy.wait()
+        write_blocks(dot(part_ref[...], weight_ref[...]).T, out_ref.at[owner])
 
 
 def weight_piece_kernel(at_ref, weight_ref, out_ref, sems):
     run_copies(sems, [(weight_ref.at[aligned(at_ref[0], out_ref.shape[0])], out_ref)])
+
+
+def state_sum(refs, head):
+    total = refs[0][head].astype(f32)
+    for ref in refs[1:]:
+        total = total + ref[head].astype(f32)
+    return total
 
 
 def state_kernel(with_state, parts_ref, vg_ref, qk_ref, *state_refs):
@@ -222,7 +224,7 @@
         if with_state:
             high, low = split(psi(feature_major(qk_ref, 1, head), False))
             v = rows_of(vg_ref, 0, head, 0, blocks * tok)
-            state_refs[0][head] = dot(high, v) + dot(low, v)
+            state_refs[0][head] = (dot(high, v) + dot(low, v)).astype(bf16)
 
 
 def numerator_kernel(qk_ref, vg_ref, num_ref):
@@ -246,7 +248,7 @@
 
 def normalize_kernel(with_state, qk_ref, vg_ref, num_ref, *rest):
     if with_state:
-        prefix_ref, attended_ref, grad_ref, carried_ref = rest
+        *prefix_refs, attended_ref, grad_ref, carried_ref = rest
     else:
         attended_ref, grad_ref = rest
     heads = qk_ref.shape[2]
@@ -257,7 +259,7 @@
         numerator = num_ref[:, cols]
         if with_state:
             feat = psi(feature_major(qk_ref, 0, head) * 0.25, True)
-            numerator = numerator + dot3(feat.T, prefix_ref[head])
+            numerator = numerator + dot3(feat.T, state_sum(prefix_refs, head))
         inv_rms = lax.rsqrt(jnp.mean(numerator * numerator, axis=-1, keepdims=True) + EPSILON)
         normed = numerator * inv_rms
         upstream = rows_of(vg_ref, 1, head, 0, length).astype(f32)
@@ -267,21 +269,11 @@
         attended_ref[:, cols] = normed.astype(bf16)
         grad_ref[:, cols] = grad
         if with_state:
-            carried_ref[head] = dot3(feat, grad)
-
-
-def leave_kernel(in_ref, out_ref, sems):
-    group, tok = out_ref.shape[:2]
-    run_copies(
-        sems, [(in_ref.at[i * tok : (i + 1) * tok], out_ref.at[i]) for i in range(group)]
-    )
+            carried_ref[head] = dot3(feat, grad).astype(bf16)
 
 
 def backward_kernel(with_state, qk_ref, vg_ref, grad_ref, *rest):
-    if with_state:
-        prefix_ref, grad_qk_ref, grad_v_ref = rest
-    else:
-        grad_qk_ref, grad_v_ref = rest
+    *prefix_refs, grad_qk_ref, grad_v_ref = rest
     length = qk_ref.shape[0] * qk_ref.shape[4]
     tile = min(TILE, length)
     for head in range(grad_v_ref.shape[0]):
@@ -294,7 +286,7 @@
         grad = grad_ref[:, cols]
         grad_t = grad.T
         if with_state:
-            grad_q = pull_psi(q, dot3(prefix_ref[head], grad_t), True)
+            grad_q = pull_psi(q, dot3(state_sum(prefix_refs, head), grad_t), True)
         for at in reversed(range(0, length, tile)):
             width = at + tile
             scores = dot(left[at:width], right[:, :width])
@@ -305,17 +297,18 @@
                 jnp.concatenate([high, low], axis=1), jnp.concatenate([v, v], axis=1), NT
             )
             more = 1.0 + scores
-            slope = jnp.where(causal, mixing * more, 0.0).astype(bf16)
-            kernel = jnp.where(causal, more + 0.5 * scores * scores, 0.0).astype(bf16)
-            both = dot(k_both[:, :width], slope, NT)
-            piece = both[:F] + both[F:]
+            slopes = split(jnp.where(causal, mixing * more, 0.0))
+            kernels = split(jnp.where(causal, more + 0.5 * scores * scores, 0.0))
+            both = dot(k_both[:, :width], slopes[0], NT)
+            piece = both[:F] + (both[F:] + dot(k_both[:F, :width], slopes[1], NT))
             if with_state:
                 piece = piece + grad_q[:, at:width]
             grad_qk_ref[0, head, :, at:width] = piece * 0.25
-            both = dot(q_both[:, at:width], slope)
-            piece_k = both[:F] + both[F:]
-            both = dot(jnp.concatenate(split(grad_t[:, at:width]), axis=0), kernel)
-            piece_v = both[:DH] + both[DH:]
+            both = dot(q_both[:, at:width], slopes[0])
+            piece_k = both[:F] + (both[F:] + dot(q_both[:F, at:width], slopes[1]))
+            high, low = split(grad_t[:, at:width])
+            both = dot(jnp.concatenate([high, low], axis=0), kernels[0])
+            piece_v = both[:DH] + (both[DH:] + dot(high, kernels[1]))
             if width == length:
                 grad_qk_ref[1, head] = piece_k
                 grad_v_ref[head] = piece_v
@@ -333,29 +326,35 @@
         if with_state:
             k = feature_major(qk_ref, 1, head)
             v = rows_of(vg_ref, 0, head, 0, length)
-            high, low = split(suffix_refs[0][head])
+            high, low = split(state_sum(suffix_refs, head))
             grad_k = grad_k + pull_psi(k, dot(high, v, NT) + dot(low, v, NT), False)
         held_ref[head * F : (head + 1) * F] = grad_qk_ref[0, head].astype(bf16)
         held_ref[(heads + head) * F : (heads + head + 1) * F] = grad_k.astype(bf16)
     run_copies(sems, [(held_ref, out_ref)])
 
 
-def grad_values_kernel(with_state, qk_ref, grad_v_ref, *rest):
-    *suffix_refs, out_ref, held_ref, sems = rest
-    heads = qk_ref.shape[2]
+def grad_values_kernel(with_state, group, at_ref, qk_ref, attended_ref, grad_v_ref, *rest):
+    suffix_refs, out_refs, held_ref = rest[: -group - 1], rest[-group - 1 : -1], rest[-1]
+    heads, tok = qk_ref.shape[2], qk_ref.shape[4]
     for head in range(heads):
         grad_v = grad_v_ref[head]
         if with_state:
             feat = psi(feature_major(qk_ref, 1, head), False)
-            grad_v = grad_v + dot3(suffix_refs[0][head].T, feat)
+            grad_v = grad_v + dot3(state_sum(suffix_refs, head).T, feat)
         held_ref[:, head * DH : (head + 1) * DH] = grad_v.T.astype(bf16)
-    leave_kernel(held_ref, out_ref, sems)
-
-
-def unpack_heads_kernel(in_ref, out_ref):
-    group, _, width = in_ref.shape
-    for member in range(group):
-        out_ref[0, :, member * width : (member + 1) * width] = in_ref[member]
+    for shift, out_ref in enumerate(out_refs):
+        rows = aligned(lax.rem(at_ref[0] + shift, group), tok)
+        out_ref[0] = attended_ref[rows, :]
+        out_ref[1] = held_ref[rows, :]
+
+
+def unpack_heads_kernel(at_ref, *rest):
+    *part_refs, attended_ref, values_ref = rest
+    group, width = len(part_refs), part_refs[0].shape[2]
+    for shift, part_ref in enumerate(part_refs):
+        cols = aligned(lax.rem(at_ref[0] + group - shift, group), width)
+        attended_ref[0, :, cols] = part_ref[0]
+        values_ref[0, :, cols] = part_ref[1]
 
 
 def place_rows(at, part_refs, cols, held_ref):
@@ -497,8 +496,8 @@
         return lax.ppermute(x, "ctx", pairs)
 
     qk_shape = ((group, 2, heads, F, tok), f32)
-    state_shape = ((heads, PSI, DH), f32)
-    blocks_shape = ((group, tok, heads * DH), bf16)
+    state_shape = ((heads, PSI, DH), bf16)
+    blocks_shape = ((2, tok, heads * DH), bf16)
     rows_shape = ((length, heads * DH), f32)
 
     parts, token = call(
@@ -508,7 +507,8 @@
         scalars=(dp_at,),
         far_in=(0,),
         far_out=True,
-        copies=(dp_size - 1,),
+        scratch=[pltpu.VMEM((dp_size - 1, tok, share), bf16)],
+        copies=(2 * dp_size - 2,),
         limit=VMEM_MOST,
     )
     arrived = [to_dp(part, shift) for shift, part in enumerate(parts, 1)]
@@ -521,7 +521,8 @@
         after=(token,),
         far_in=(0, 1),
         far_out=True,
-        copies=(2 * group,),
+        scratch=[pltpu.VMEM((2 * group, tok, heads * DH), bf16)],
+        copies=(4 * group,),
         limit=VMEM_MOST,
     )
     parts = to_members(parts)
@@ -531,9 +532,9 @@
         *parts,
         scalars=(member,),
     )
-    (projected,), token = call(
+    (projected, weight), token = call(
         project_kernel,
-        [qk_shape],
+        [qk_shape, (proj_weight.shape, bf16)],
         tokens,
         proj_weight,
         scalars=(dp_at,),
@@ -553,7 +554,6 @@
             far_in=(0,),
             far_out=True,
             copies=(group * dp_size * runs,),
-            limit=VMEM_MOST,
         )
     else:
         blocks = tokens[0].reshape(tok, dp_size * runs, group, depth).transpose(2, 0, 1, 3)
@@ -569,17 +569,10 @@
         project_rest_kernel,
         [((dp_size,) + qk_shape[0], f32)],
         projected,
-        proj_weight,
+        weight,
         *arrived,
         scalars=(dp_at,),
         after=(vg_token, token),
-        far_in=(1,),
-        far_out=True,
-        scratch=[
-            pltpu.VMEM((dp_size - 1,) + qk_shape[0], f32),
-            pltpu.VMEM((4, share // 4, cols), bf16),
-        ],
-        copies=(4, dp_size),
     )
     qk_parts = lax.all_to_all(
         projected.reshape((dp_size * group,) + qk_shape[0][1:]),
@@ -602,7 +595,6 @@
         far_in=(0,),
         far_out=True,
         copies=(1,),
-        limit=VMEM_MOST,
     )
     fetched = [to_dp(mine, shift) for shift in range(1, dp_size)]
     weights, firsts = [proj_weight], [dp_at * share]
@@ -622,7 +614,7 @@
     )
     prefix, suffix = (), ()
     if with_state:
-        prefix = (sum(to_run(state[0], shift, False) for shift in range(1, runs)),)
+        prefix = [to_run(state[0], shift, False) for shift in range(1, runs)]
     (numerator,), token = call(numerator_kernel, [rows_shape], qk, vg)
     (attended, grad_num, *carried), token = call(
         functools.partial(normalize_kernel, with_state),
@@ -631,10 +623,9 @@
         vg,
         numerator,
         *prefix,
-        after_far=token_parts[1:],
     )
     if with_state:
-        suffix = (sum(to_run(carried[0], -shift, False) for shift in range(1, runs)),)
+        suffix = [to_run(carried[0], -shift, False) for shift in range(1, runs)]
     (grad_qk, grad_v), token = call(
         functools.partial(backward_kernel, with_state),
         [((2, heads, F, length), f32), ((heads, DH, length), f32)],
@@ -642,17 +633,8 @@
         vg,
         grad_num,
         *prefix,
-        after_far=fetched,
-    )
-    (attended,), attended_token = call(
-        leave_kernel,
-        [blocks_shape],
-        attended,
-        after=(token,),
-        far_out=True,
-        copies=(group,),
-    )
-    attended = exchange(attended)
+        after_far=[*fetched, *token_parts[1:]],
+    )
     (rows,), token = call(
         functools.partial(rows_kernel, with_state),
         [((2 * heads * F, length), bf16)],
@@ -672,21 +654,18 @@
         scalars=(member,),
         after=(token,),
     )
-    (grad_values,), token = call(
-        functools.partial(grad_values_kernel, with_state),
-        [blocks_shape],
+    results, token = call(
+        functools.partial(grad_values_kernel, with_state, group),
+        [blocks_shape] * group,
         qk,
+        attended,
         grad_v,
         *suffix,
+        scalars=(member,),
         after=(token,),
-        far_out=True,
         scratch=[pltpu.VMEM((length, heads * DH), bf16)],
-        copies=(group,),
-    )
-    grad_values = exchange(grad_values)
-    (attended,), attended_token = call(
-        unpack_heads_kernel, [((1, tok, H * DH), bf16)], attended
-    )
+    )
+    results = to_members(results)
 
     held = pltpu.VMEM((cols, length), bf16)
     (own, *parts), token = call(
@@ -695,26 +674,20 @@
         *rows,
         token_cols,
         scalars=(dp_at, member),
-        after=(attended_token, token),
+        after=(token,),
         scratch=[pltpu.VMEM((dp_size * runs * depth, cols), f32), held],
     )
     parts = [to_dp(part, shift) for shift, part in enumerate(parts, 1)]
-    (grad_values,), values_token = call(
-        unpack_heads_kernel,
-        [((1, tok, H * DH), bf16)],
-        grad_values,
-        after=(token,),
-    )
     (grad_proj, *parts), token = call(
         functools.partial(run_sum_kernel, len(parts)),
         [((depth, cols), f32)] + [((depth, cols), bf16)] * (runs - 1),
         own,
         *parts,
         scalars=(run_at,),
-        after=(values_token,),
+        after_far=results[1 : 1 + group // 2],
         scratch=[pltpu.VMEM((runs * depth, cols), f32)],
     )
-    (grad_tokens,), token = call(
+    (grad_tokens,), tokens_token = call(
         functools.partial(grad_tokens_kernel, group),
         [((1, tok, width), bf16)],
         *rows,
@@ -723,12 +696,19 @@
         after=(token,),
         scratch=[pltpu.VMEM((cols, tok), bf16)],
     )
+    (attended, grad_values), token = call(
+        unpack_heads_kernel,
+        [((1, tok, H * DH), bf16)] * 2,
+        *results,
+        scalars=(member,),
+        after=(token,),
+    )
     (grad_proj,), _ = call(
         final_sum_kernel,
         [((depth, cols), f32)],
         grad_proj,
         *[to_run(part, shift, True) for shift, part in enumerate(parts, 1)],
-        after=(token,),
+        after=(tokens_token, token),
     )
     return (attended, grad_tokens, grad_values, grad_proj)
 

time: 256 us -> 151 us (0.59)
  Pallas kernels: 147 us -> 38.7 us
  starting transfers between devices: 57.1 us -> 49.1 us
  local copies, waits for them, and re-layouts: 18.5 us -> 25.6 us
  waiting for transfers between devices: 31.5 us -> 35.5 us
    pallas_call x21 -> x19, Pallas kernels: 147 us -> 38.7 us  [call(): pl.pallas_call(kernel, out_shape=[jax.ShapeDtypeStruct(shape, kind) for s...]
    ppermute x3, waiting for transfers between devices: 7.8 us -> 24.2 us  [to_dp(): lax.ppermute(x, 'dp', [(i, (i + shift) % dp_size) for i in range(dp_size)])]
    all_to_all x2 -> x0, starting transfers between devices: 12.2 us -> none  [exchange(): lax.all_to_all(x, 'ctx', split_axis=0, concat_axis=0, tiled=True, axis_in...]
    ppermute x3, waiting for transfers between devices: 12.4 us -> 1.06 us  [to_run(): return lax.ppermute(x, 'ctx', pairs)]
    unnamed x86, local copies, waits for them, and re-layouts: 18.5 us -> 25.6 us
    ppermute x21 -> x28, starting transfers between devices: 29.2 us -> 32.4 us  [to_member(): return lax.ppermute(x, 'ctx', pairs)]
    ppermute x21 -> x28, waiting for transfers between devices: 11.3 us -> 10.3 us  [to_member(): return lax.ppermute(x, 'ctx', pairs)]
  transfers between devices with their start and end apart: 31 -> 36, of which waited for: 10 -> 10; matrix products, arithmetic and copies ran while one was open for 0% -> 0% of each run, Pallas kernels for 47% -> 21%
where the time goes in v5:
time: 151 us; the launch traced here: 150 us
  starting transfers between devices  49.1 us (33%)
  Pallas kernels  38.7 us (26%)
  waiting for transfers between devices  35.5 us (24%)
  local copies, waits for them, and re-layouts  25.6 us (17%)
    pallas_call x19, Pallas kernels, call(): pl.pallas_call(kernel, out_shape=[jax.ShapeDtypeStruct(shape, kind) for s...  38.7 us
    ppermute x28, starting transfers between devices, to_member(): return lax.ppermute(x, 'ctx', pairs)  32.4 us
    unnamed x86, local copies, waits for them, and re-layouts  25.6 us
    ppermute x3, waiting for transfers between devices, to_dp(): lax.ppermute(x, 'dp', [(i, (i + shift) % dp_size) for i in range(dp_size)])  24.2 us
    ppermute x28, waiting for transfers between devices, to_member(): return lax.ppermute(x, 'ctx', pairs)  10.3 us
    ppermute x3, starting transfers between devices, to_run(): return lax.ppermute(x, 'ctx', pairs)  8.33 us
    all_to_all x1, starting transfers between devices, local(): lax.all_to_all(projected.reshape((dp_size * group,) + qk_shape[0][1:]), (...  4.26 us
    ppermute x3, starting transfers between devices, to_dp(): lax.ppermute(x, 'dp', [(i, (i + shift) % dp_size) for i in range(dp_size)])  4.14 us
  transfers between devices with their start and end apart: 36, of which 10 were waited for; matrix products, arithmetic and copies ran while one was open for 0% of the time, Pallas kernels for 21%

profile of v5, /device:TPU:0, one launch (start us, length us, event | category | flops | bytes accessed | tf_op | source)
XLA Modules:
  0.0 150.0 jit_solution(16228319565221461685)
XLA Ops:
  0.6 2.6 %shard_map.75 = (bf16[128,2048]{1,0:T(8,128)(2,1)}, f32[8,128]{1,0:T(8,128)}) custom-call(s32[1]{0:T(128)} %bitcast.1.refs_0_, bf16[1,128,4096]{2,1,0:T(8,128)(2,1)} %refs_1_.8), custom_call_target="tpu_custom_call" | custom-call | tf_op jit(solution)/shard_map/pallas_call | solution.py:443
  3.2 3.0 %collective-permute-start = (bf16[128,2048]{1,0:T(8,128)(2,1)}, bf16[128,2048]{1,0:T(8,128)(2,1)}, u32[]{:S(2)}, u32[]{:S(2)}) collective-permute-start(bf16[128,2048]{1,0:T(8,128)(2,1)} %get-tuple-element.67), channel_id=1, source_target_pairs={{0,16},{16,0},{1,17},{17,1},{2,18},{18,2},{3,19},{19,3},{4,20},{20... | collective-permute-start | bytes 1572872 | tf_op jit(solution)/shard_map/ppermute | solution.py:481
  6.3 2.7 %shard_map.76 = (bf16[2,128,256]{2,1,0:T(8,128)(2,1)}, bf16[2,128,256]{2,1,0:T(8,128)(2,1)}, bf16[2,128,256]{2,1,0:T(8,128)(2,1)}, bf16[2,128,256]{2,1,0:T(8,128...) custom-call(s32[1]{0:T(128)} %bitcast.refs_0_, ...), custom_call_target="tpu_custom_call" | custom-call | tf_op jit(solution)/shard_map/pallas_call | solution.py:443
  10.6 2.4 %collective-permute-start.3 = (bf16[2,128,256]{2,1,0:T(8,128)(2,1)}, bf16[2,128,256]{2,1,0:T(8,128)(2,1)S(1)}, u32[]{:S(2)}, u32[]{:S(2)}) collective-permute-start(bf16[2,128,256]{2,1,0:T(8,128)(2,1)} %get-tuple-element.71), channel_id=1, source_target_pairs={{0,3},{1,4},{2,5},{3,6},{4,7},{5,0},{6,1},{7,2},{8,11},{9,12},{10,... | collective-permute-start | bytes 393224 | tf_op jit(solution)/shard_map/ppermute | solution.py:485
  13.5 1.9 %collective-permute-done.1.refs_2_ = bf16[2,128,256]{2,1,0:T(8,128)(2,1)S(1)} collective-permute-done((bf16[2,128,256]{2,1,0:T(8,128)(2,1)}, bf16[2,128,256]{2,1,0:T(8,128)(2,1)S(1)}, u32[]{:S(2)}, u32[]{:S(2)}) %collective-permute-start.1) | collective-permute-done | bytes 131104 | tf_op jit(solution)/shard_map/ppermute | solution.py:485
  19.5 2.2 %collective-permute-start.7 = (bf16[2,128,256]{2,1,0:T(8,128)(2,1)}, bf16[2,128,256]{2,1,0:T(8,128)(2,1)S(1)}, u32[]{:S(2)}, u32[]{:S(2)}) collective-permute-start(bf16[2,128,256]{2,1,0:T(8,128)(2,1)} %get-tuple-element.75), channel_id=1, source_target_pairs={{0,7},{1,0},{2,1},{3,2},{4,3},{5,4},{6,5},{7,6},{8,15},{9,8},{10,9... | collective-permute-start | bytes 393224 | tf_op jit(solution)/shard_map/ppermute | solution.py:485
  45.2 4.3 %all-to-all-start = ((f32[16,2,2,16,128]{4,3,2,1,0:T(8,128)}), f32[16,2,2,16,128]{4,3,2,1,0:T(8,128)}, u32[]{:S(2)}, u32[]{:S(2)}) async-start(f32[16,2,2,16,128]{4,3,2,1,0:T(8,128)} %bitcast.9), calls=%async_computation | async-start | bytes 1048576 | tf_op jit(solution)/shard_map/all_to_all | solution.py:577
  49.4 24.2 %collective-permute-done.9.refs_4_.refs_10_ = bf16[1024,512]{1,0:T(8,128)(2,1)} collective-permute-done((bf16[1024,512]{1,0:T(8,128)(2,1)}, bf16[1024,512]{1,0:T(8,128)(2,1)}, u32[]{:S(2)}, u32[]{:S(2)}) %collective-permute-start.9) | collective-permute-done | bytes 1048608 | tf_op jit(solution)/shard_map/ppermute | solution.py:481
  78.4 4.5 %collective-permute-start.8 = (bf16[2,176,128]{2,1,0:T(8,128)(2,1)S(1)}, bf16[2,176,128]{2,1,0:T(8,128)(2,1)S(1)}, u32[]{:S(2)}, u32[]{:S(2)}) collective-permute-start(bf16[2,176,128]{2,1,0:T(8,128)(2,1)S(1)} %get-tuple-element.83), channel_id=1, source_target_pairs={{0,8},{1,9},{2,10},{3,11},{4,12},{5,13},{6,14},{7,15},{16,24},{17,... | collective-permute-start | bytes 270344 | tf_op jit(solution)/shard_map/ppermute | solution.py:496
  84.0 1.8 %collective-permute-start.15 = (bf16[128,512]{1,0:T(8,128)(2,1)}, bf16[128,512]{1,0:T(8,128)(2,1)S(1)}, u32[]{:S(2)}, u32[]{:S(2)}) collective-permute-start(bf16[128,512]{1,0:T(8,128)(2,1)} %copy-done.38), channel_id=1, source_target_pairs={{0,6},{1,7},{2,0},{3,1},{4,2},{5,3},{6,4},{7,5},{8,14},{9,15},{10,... | collective-permute-start | bytes 393224 | tf_op jit(solution)/shard_map/ppermute | solution.py:485
  87.0 3.6 %shard_map.82 = (f32[1024,256]{1,0:T(8,128)S(1)}, f32[8,128]{1,0:T(8,128)}) custom-call(f32[8,2,2,16,128]{4,3,2,1,0:T(8,128)S(1)} %get-tuple-element.81.refs_0_.refs_1_, bf16[8,2,128,256]{3,2,1,0:T(8,128)(2,1)S(1)} %get-tuple-element.80.refs_1_), custom_call_target="tpu_custom_call" | custom-call | tf_op jit(solution)/shard_map/pallas_call | solution.py:443
  90.7 2.6 %shard_map.83 = (bf16[1024,256]{1,0:T(8,128)(2,1)S(1)}, f32[1024,256]{1,0:T(8,128)S(1)}, bf16[2,176,128]{2,1,0:T(8,128)(2,1)S(1)}, f32[8,128]{1,0:T(8,128)}) custom-call(f32[8,2,2,16,128]{4,3,2,1,0:T(8,128)S(1)} %get-tuple-element.81.refs_0_.refs_1_, bf16[8,2,128,256]{3,2,1,0:T(8,128)(2,1)S(1)} %get-tuple-element.80.refs_1_, ...), custom_call_target="tpu_custom_call" | custom-call | tf_op jit(solution)/shard_map/pallas_call | solution.py:443
  94.8 6.3 %shard_map.85 = (f32[2,2,16,1024]{3,2,1,0:T(8,128)S(1)}, f32[2,128,1024]{2,1,0:T(8,128)S(1)}, f32[8,128]{1,0:T(8,128)}) custom-call(f32[8,2,2,16,128]{4,3,2,1,0:T(8,128)S(1)} %get-tuple-element.81.refs_0_.refs_1_, bf16[8,2,128,256]{3,2,1,0:T(8,128)(2,1)S(1)} %get-tuple-element.80.refs_1_, f32[1024,256]{1,0:T(8,128)S(1)} %get-tuple-element.85.refs_2_, ...), custom_call_target="tpu_custom_call" | custom-call | tf_op jit(solution)/shard_map/pallas_call | solution.py:443
  106.3 2.0 %collective-permute-done.31.refs_8_ = bf16[64,1024]{1,0:T(8,128)(2,1)S(1)} collective-permute-done((bf16[64,1024]{1,0:T(8,128)(2,1)S(1)}, bf16[64,1024]{1,0:T(8,128)(2,1)S(1)}, u32[]{:S(2)}, u32[]{:S(2)}) %collective-permute-start.31) | collective-permute-done | bytes 131104 | tf_op jit(solution)/shard_map/ppermute | solution.py:485
  111.1 2.2 %collective-permute-start.26 = (bf16[64,1024]{1,0:T(8,128)(2,1)S(1)}, bf16[64,1024]{1,0:T(8,128)(2,1)S(1)}, u32[]{:S(2)}, u32[]{:S(2)}) collective-permute-start(bf16[64,1024]{1,0:T(8,128)(2,1)S(1)} %get-tuple-element.107.refs_1_), channel_id=1, source_target_pairs={{0,2},{1,3},{2,4},{3,5},{4,6},{5,7},{6,0},{7,1},{8,10},{9,11},{10,... | collective-permute-start | bytes 393224 | tf_op jit(solution)/shard_map/ppermute | solution.py:485
  119.2 2.2 %shard_map.89 = (f32[256,512]{1,0:T(8,128)S(1)}, bf16[256,512]{1,0:T(8,128)(2,1)}, f32[8,128]{1,0:T(8,128)}) custom-call(s32[2]{0:T(128)S(1)} %pad_add_fusion.refs_0_, bf16[64,1024]{1,0:T(8,128)(2,1)S(1)} %get-tuple-element.107.refs_1_, bf16[64,1024]{1,0:T(8,128)(2,1)S(1)} %collective-permute-done.25.refs_2_, ...), custom_call_target="tpu_custom_call" | custom-call | tf_op jit(solution)/shard_map/pallas_call | solution.py:443
  124.3 1.7 %collective-permute-start.21 = (bf16[2,128,256]{2,1,0:T(8,128)(2,1)}, bf16[2,128,256]{2,1,0:T(8,128)(2,1)}, u32[]{:S(2)}, u32[]{:S(2)}) collective-permute-start(bf16[2,128,256]{2,1,0:T(8,128)(2,1)} %get-tuple-element.103), channel_id=1, source_target_pairs={{0,4},{1,5},{2,6},{3,7},{4,0},{5,1},{6,2},{7,3},{8,12},{9,13},{10,... | collective-permute-start | bytes 393224 | tf_op jit(solution)/shard_map/ppermute | solution.py:485
  125.9 2.6 %collective-permute-done.19.refs_4_.refs_3_ = bf16[2,128,256]{2,1,0:T(8,128)(2,1)} collective-permute-done((bf16[2,128,256]{2,1,0:T(8,128)(2,1)}, bf16[2,128,256]{2,1,0:T(8,128)(2,1)}, u32[]{:S(2)}, u32[]{:S(2)}) %collective-permute-start.19) | collective-permute-done | bytes 131104 | tf_op jit(solution)/shard_map/ppermute | solution.py:485
  128.6 2.3 %collective-permute-start.23 = (bf16[2,128,256]{2,1,0:T(8,128)(2,1)}, bf16[2,128,256]{2,1,0:T(8,128)(2,1)}, u32[]{:S(2)}, u32[]{:S(2)}) collective-permute-start(bf16[2,128,256]{2,1,0:T(8,128)(2,1)} %copy-done.37), channel_id=1, source_target_pairs={{0,6},{1,7},{2,0},{3,1},{4,2},{5,3},{6,4},{7,5},{8,14},{9,15},{10,... | collective-permute-start | bytes 393224 | tf_op jit(solution)/shard_map/ppermute | solution.py:485
  130.9 3.5 %collective-permute-start.24 = (bf16[2,128,256]{2,1,0:T(8,128)(2,1)}, bf16[2,128,256]{2,1,0:T(8,128)(2,1)}, u32[]{:S(2)}, u32[]{:S(2)}) collective-permute-start(bf16[2,128,256]{2,1,0:T(8,128)(2,1)} %copy-done.35), channel_id=1, source_target_pairs={{0,7},{1,0},{2,1},{3,2},{4,3},{5,4},{6,5},{7,6},{8,15},{9,8},{10,9... | collective-permute-start | bytes 393224 | tf_op jit(solution)/shard_map/ppermute | solution.py:485
  135.3 1.7 %shard_map.90 = (f32[128,512]{1,0:T(8,128)S(1)}, bf16[128,512]{1,0:T(8,128)(2,1)}, f32[8,128]{1,0:T(8,128)S(1)}) custom-call(s32[1]{0:T(128)} %bitcast.5.refs_0_, f32[256,512]{1,0:T(8,128)S(1)} %get-tuple-element.111.refs_1_, bf16[256,512]{1,0:T(8,128)(2,1)} %collective-permute-done.32.refs_2_, bf16[2,128,256]{2,1,0:T(8,128)(2,1)S(1)} %copy-done.9, ...), custom_call_target="tpu_custom_call" | custom-call | tf_op jit(solution)/shard_map/pallas_call | solution.py:443
  137.7 2.4 %collective-permute-start.34 = (bf16[128,512]{1,0:T(8,128)(2,1)}, bf16[128,512]{1,0:T(8,128)(2,1)S(1)}, u32[]{:S(2)}, u32[]{:S(2)}) collective-permute-start(bf16[128,512]{1,0:T(8,128)(2,1)} %get-tuple-element.118), channel_id=1, source_target_pairs={{0,8},{1,9},{2,10},{3,11},{4,12},{5,13},{6,14},{7,15},{8,0},{9,1},... | collective-permute-start | bytes 393224 | tf_op jit(solution)/shard_map/ppermute | solution.py:496
  142.0 2.3 %shard_map.91 = (bf16[1,128,2048]{2,1,0:T(8,128)(2,1)}, bf16[1,128,2048]{2,1,0:T(8,128)(2,1)}, f32[8,128]{1,0:T(8,128)S(1)}) custom-call(s32[1]{0:T(128)} %bitcast.refs_0_, bf16[2,128,256]{2,1,0:T(8,128)(2,1)S(1)} %copy-done.18, bf16[2,128,256]{2,1,0:T(8,128)(2,1)S(1)} %copy-done.10, bf16[2,128,256]{2,1,0:T(8,128)(2,1)} %collective-permute-done.19.refs_4_.refs_3_, ...), custom_call_target="tpu_custom_call" | custom-call | tf_op jit(solution)/shard_map/pallas_call | solution.py:443
  145.2 4.1 %shard_map.92 = (bf16[1,128,4096]{2,1,0:T(8,128)(2,1)}, f32[8,128]{1,0:T(8,128)S(1)}) custom-call(s32[4]{0:T(128)S(1)} %pad_add_fusion.1.refs_0_, bf16[64,1024]{1,0:T(8,128)(2,1)S(1)} %get-tuple-element.107.refs_1_, bf16[64,1024]{1,0:T(8,128)(2,1)S(1)} %copy-done.6, bf16[64,1024]{1,0:T(8,128)(2,1)S(1)} %collective-permute-done.26.refs_3_, ...), custom_call_target="tpu_custom_call" | custom-call | tf_op jit(solution)/shard_map/pallas_call | solution.py:443
  (155 shorter events, 60.1 us)
Async XLA Ops:
  3.2 36.5 %collective-permute-start = (bf16[128,2048]{1,0:T(8,128)(2,1)}, bf16[128,2048]{1,0:T(8,128)(2,1)}, u32[]{:S(2)}, u32[]{:S(2)}) collective-permute-start(bf16[128,2048]{1,0:T(8,128)(2,1)} %get-tuple-element.67), channel_id=1, source_target_pairs={{0,16},{16,0},{1,17},{17,1},{2,18},{18,2},{3,19},{19,3},{4,20},{20... | collective-permute-start | bytes 1572872 | tf_op jit(solution)/shard_map/ppermute | solution.py:481
  13.0 17.6 %collective-permute-start.4 = (bf16[2,128,256]{2,1,0:T(8,128)(2,1)}, bf16[2,128,256]{2,1,0:T(8,128)(2,1)S(1)}, u32[]{:S(2)}, u32[]{:S(2)}) collective-permute-start(bf16[2,128,256]{2,1,0:T(8,128)(2,1)} %get-tuple-element.72), channel_id=1, source_target_pairs={{0,4},{1,5},{2,6},{3,7},{4,0},{5,1},{6,2},{7,3},{8,12},{9,13},{10,... | collective-permute-start | bytes 393224 | tf_op jit(solution)/shard_map/ppermute | solution.py:485
  16.0 15.3 %collective-permute-start.5 = (bf16[2,128,256]{2,1,0:T(8,128)(2,1)}, bf16[2,128,256]{2,1,0:T(8,128)(2,1)S(1)}, u32[]{:S(2)}, u32[]{:S(2)}) collective-permute-start(bf16[2,128,256]{2,1,0:T(8,128)(2,1)} %get-tuple-element.73), channel_id=1, source_target_pairs={{0,5},{1,6},{2,7},{3,0},{4,1},{5,2},{6,3},{7,4},{8,13},{9,14},{10,... | collective-permute-start | bytes 393224 | tf_op jit(solution)/shard_map/ppermute | solution.py:485
  17.2 14.8 %collective-permute-start.6 = (bf16[2,128,256]{2,1,0:T(8,128)(2,1)}, bf16[2,128,256]{2,1,0:T(8,128)(2,1)S(1)}, u32[]{:S(2)}, u32[]{:S(2)}) collective-permute-start(bf16[2,128,256]{2,1,0:T(8,128)(2,1)} %get-tuple-element.74), channel_id=1, source_target_pairs={{0,6},{1,7},{2,0},{3,1},{4,2},{5,3},{6,4},{7,5},{8,14},{9,15},{10,... | collective-permute-start | bytes 393224 | tf_op jit(solution)/shard_map/ppermute | solution.py:485
  19.5 13.1 %collective-permute-start.7 = (bf16[2,128,256]{2,1,0:T(8,128)(2,1)}, bf16[2,128,256]{2,1,0:T(8,128)(2,1)S(1)}, u32[]{:S(2)}, u32[]{:S(2)}) collective-permute-start(bf16[2,128,256]{2,1,0:T(8,128)(2,1)} %get-tuple-element.75), channel_id=1, source_target_pairs={{0,7},{1,0},{2,1},{3,2},{4,3},{5,4},{6,5},{7,6},{8,15},{9,8},{10,9... | collective-permute-start | bytes 393224 | tf_op jit(solution)/shard_map/ppermute | solution.py:485
  44.6 29.1 %collective-permute-start.9 = (bf16[1024,512]{1,0:T(8,128)(2,1)}, bf16[1024,512]{1,0:T(8,128)(2,1)}, u32[]{:S(2)}, u32[]{:S(2)}) collective-permute-start(bf16[1024,512]{1,0:T(8,128)(2,1)} %get-tuple-element.87), channel_id=1, source_target_pairs={{0,16},{16,0},{1,17},{17,1},{2,18},{18,2},{3,19},{19,3},{4,20},{20... | collective-permute-start | bytes 3145736 | tf_op jit(solution)/shard_map/ppermute | solution.py:481
  45.2 31.6 %all-to-all-start = ((f32[16,2,2,16,128]{4,3,2,1,0:T(8,128)}), f32[16,2,2,16,128]{4,3,2,1,0:T(8,128)}, u32[]{:S(2)}, u32[]{:S(2)}) async-start(f32[16,2,2,16,128]{4,3,2,1,0:T(8,128)} %bitcast.9), calls=%async_computation | async-start | bytes 1048576 | tf_op jit(solution)/shard_map/all_to_all | solution.py:577
  73.6 70.7 %collective-permute-start.33 = (bf16[1024,512]{1,0:T(8,128)(2,1)}, bf16[1024,512]{1,0:T(8,128)(2,1)}, u32[]{:S(2)}, u32[]{:S(2)}) collective-permute-start(bf16[1024,512]{1,0:T(8,128)(2,1)} %collective-permute-done.9.refs_4_.refs_10_), channel_id=1, source_target_pairs={{0,1},{1,0},{2,3},{3,2},{4,5},{5,4},{6,7},{7,6},{8,9},{9,8},{10,11... | collective-permute-start | bytes 3145736 | tf_op jit(solution)/shard_map/ppermute | solution.py:606
  73.6 9.3 %collective-permute-start.10 = (bf16[128,512]{1,0:T(8,128)(2,1)}, bf16[128,512]{1,0:T(8,128)(2,1)S(1)}, u32[]{:S(2)}, u32[]{:S(2)}) collective-permute-start(bf16[128,512]{1,0:T(8,128)(2,1)} %get-tuple-element.88), channel_id=1, source_target_pairs={{0,1},{1,2},{2,3},{3,4},{4,5},{5,6},{6,7},{7,0},{8,9},{9,10},{10,1... | collective-permute-start | bytes 393224 | tf_op jit(solution)/shard_map/ppermute | solution.py:485
  74.1 9.8 %collective-permute-start.11 = (bf16[128,512]{1,0:T(8,128)(2,1)}, bf16[128,512]{1,0:T(8,128)(2,1)S(1)}, u32[]{:S(2)}, u32[]{:S(2)}) collective-permute-start(bf16[128,512]{1,0:T(8,128)(2,1)} %get-tuple-element.89), channel_id=1, source_target_pairs={{0,2},{1,3},{2,4},{3,5},{4,6},{5,7},{6,0},{7,1},{8,10},{9,11},{10,... | collective-permute-start | bytes 393224 | tf_op jit(solution)/shard_map/ppermute | solution.py:485
  75.3 8.7 %collective-permute-start.12 = (bf16[128,512]{1,0:T(8,128)(2,1)}, bf16[128,512]{1,0:T(8,128)(2,1)S(1)}, u32[]{:S(2)}, u32[]{:S(2)}) collective-permute-start(bf16[128,512]{1,0:T(8,128)(2,1)} %copy-done.42), channel_id=1, source_target_pairs={{0,3},{1,4},{2,5},{3,6},{4,7},{5,0},{6,1},{7,2},{8,11},{9,12},{10,... | collective-permute-start | bytes 393224 | tf_op jit(solution)/shard_map/ppermute | solution.py:485
  82.9 10.4 %collective-permute-start.13 = (bf16[128,512]{1,0:T(8,128)(2,1)}, bf16[128,512]{1,0:T(8,128)(2,1)S(1)}, u32[]{:S(2)}, u32[]{:S(2)}) collective-permute-start(bf16[128,512]{1,0:T(8,128)(2,1)} %copy-done.41), channel_id=1, source_target_pairs={{0,4},{1,5},{2,6},{3,7},{4,0},{5,1},{6,2},{7,3},{8,12},{9,13},{10,... | collective-permute-start | bytes 393224 | tf_op jit(solution)/shard_map/ppermute | solution.py:485
  84.0 10.8 %collective-permute-start.14 = (bf16[128,512]{1,0:T(8,128)(2,1)}, bf16[128,512]{1,0:T(8,128)(2,1)S(1)}, u32[]{:S(2)}, u32[]{:S(2)}) collective-permute-start(bf16[128,512]{1,0:T(8,128)(2,1)} %copy-done.40), channel_id=1, source_target_pairs={{0,5},{1,6},{2,7},{3,0},{4,1},{5,2},{6,3},{7,4},{8,13},{9,14},{10,... | collective-permute-start | bytes 393224 | tf_op jit(solution)/shard_map/ppermute | solution.py:485
  84.0 10.8 %collective-permute-start.15 = (bf16[128,512]{1,0:T(8,128)(2,1)}, bf16[128,512]{1,0:T(8,128)(2,1)S(1)}, u32[]{:S(2)}, u32[]{:S(2)}) collective-permute-start(bf16[128,512]{1,0:T(8,128)(2,1)} %copy-done.38), channel_id=1, source_target_pairs={{0,6},{1,7},{2,0},{3,1},{4,2},{5,3},{6,4},{7,5},{8,14},{9,15},{10,... | collective-permute-start | bytes 393224 | tf_op jit(solution)/shard_map/ppermute | solution.py:485
  85.8 8.9 %collective-permute-start.16 = (bf16[128,512]{1,0:T(8,128)(2,1)}, bf16[128,512]{1,0:T(8,128)(2,1)S(1)}, u32[]{:S(2)}, u32[]{:S(2)}) collective-permute-start(bf16[128,512]{1,0:T(8,128)(2,1)} %copy-done.36), channel_id=1, source_target_pairs={{0,7},{1,0},{2,1},{3,2},{4,3},{5,4},{6,5},{7,6},{8,15},{9,8},{10,9... | collective-permute-start | bytes 393224 | tf_op jit(solution)/shard_map/ppermute | solution.py:485
  93.3 8.8 %collective-permute-start.17 = (bf16[2,176,128]{2,1,0:T(8,128)(2,1)S(1)}, bf16[2,176,128]{2,1,0:T(8,128)(2,1)S(1)}, u32[]{:S(2)}, u32[]{:S(2)}) collective-permute-start(bf16[2,176,128]{2,1,0:T(8,128)(2,1)S(1)} %get-tuple-element.96), channel_id=1, source_target_pairs={{8,0},{9,1},{10,2},{11,3},{12,4},{13,5},{14,6},{15,7},{24,16},{25,... | collective-permute-start | bytes 270344 | tf_op jit(solution)/shard_map/ppermute | solution.py:496
  104.5 9.4 %collective-permute-start.29 = (bf16[64,1024]{1,0:T(8,128)(2,1)S(1)}, bf16[64,1024]{1,0:T(8,128)(2,1)S(1)}, u32[]{:S(2)}, u32[]{:S(2)}) collective-permute-start(bf16[64,1024]{1,0:T(8,128)(2,1)S(1)} %get-tuple-element.107.refs_1_), channel_id=1, source_target_pairs={{0,5},{1,6},{2,7},{3,0},{4,1},{5,2},{6,3},{7,4},{8,13},{9,14},{10,... | collective-permute-start | bytes 393224 | tf_op jit(solution)/shard_map/ppermute | solution.py:485
  105.4 12.4 %collective-permute-start.28 = (bf16[64,1024]{1,0:T(8,128)(2,1)S(1)}, bf16[64,1024]{1,0:T(8,128)(2,1)S(1)}, u32[]{:S(2)}, u32[]{:S(2)}) collective-permute-start(bf16[64,1024]{1,0:T(8,128)(2,1)S(1)} %get-tuple-element.107.refs_1_), channel_id=1, source_target_pairs={{0,4},{1,5},{2,6},{3,7},{4,0},{5,1},{6,2},{7,3},{8,12},{9,13},{10,... | collective-permute-start | bytes 393224 | tf_op jit(solution)/shard_map/ppermute | solution.py:485
  108.3 9.5 %collective-permute-start.27 = (bf16[64,1024]{1,0:T(8,128)(2,1)S(1)}, bf16[64,1024]{1,0:T(8,128)(2,1)S(1)}, u32[]{:S(2)}, u32[]{:S(2)}) collective-permute-start(bf16[64,1024]{1,0:T(8,128)(2,1)S(1)} %get-tuple-element.107.refs_1_), channel_id=1, source_target_pairs={{0,3},{1,4},{2,5},{3,6},{4,7},{5,0},{6,1},{7,2},{8,11},{9,12},{10,... | collective-permute-start | bytes 393224 | tf_op jit(solution)/shard_map/ppermute | solution.py:485
  121.4 13.0 %collective-permute-start.32 = (bf16[256,512]{1,0:T(8,128)(2,1)}, bf16[256,512]{1,0:T(8,128)(2,1)}, u32[]{:S(2)}, u32[]{:S(2)}) collective-permute-start(bf16[256,512]{1,0:T(8,128)(2,1)} %get-tuple-element.112), channel_id=1, source_target_pairs={{0,16},{16,0},{1,17},{17,1},{2,18},{18,2},{3,19},{19,3},{4,20},{20... | collective-permute-start | bytes 786440 | tf_op jit(solution)/shard_map/ppermute | solution.py:481
  128.6 11.6 %collective-permute-start.22 = (bf16[2,128,256]{2,1,0:T(8,128)(2,1)}, bf16[2,128,256]{2,1,0:T(8,128)(2,1)}, u32[]{:S(2)}, u32[]{:S(2)}) collective-permute-start(bf16[2,128,256]{2,1,0:T(8,128)(2,1)} %copy-done.39), channel_id=1, source_target_pairs={{0,5},{1,6},{2,7},{3,0},{4,1},{5,2},{6,3},{7,4},{8,13},{9,14},{10,... | collective-permute-start | bytes 393224 | tf_op jit(solution)/shard_map/ppermute | solution.py:485
  128.6 11.6 %collective-permute-start.23 = (bf16[2,128,256]{2,1,0:T(8,128)(2,1)}, bf16[2,128,256]{2,1,0:T(8,128)(2,1)}, u32[]{:S(2)}, u32[]{:S(2)}) collective-permute-start(bf16[2,128,256]{2,1,0:T(8,128)(2,1)} %copy-done.37), channel_id=1, source_target_pairs={{0,6},{1,7},{2,0},{3,1},{4,2},{5,3},{6,4},{7,5},{8,14},{9,15},{10,... | collective-permute-start | bytes 393224 | tf_op jit(solution)/shard_map/ppermute | solution.py:485
  130.9 9.3 %collective-permute-start.24 = (bf16[2,128,256]{2,1,0:T(8,128)(2,1)}, bf16[2,128,256]{2,1,0:T(8,128)(2,1)}, u32[]{:S(2)}, u32[]{:S(2)}) collective-permute-start(bf16[2,128,256]{2,1,0:T(8,128)(2,1)} %copy-done.35), channel_id=1, source_target_pairs={{0,7},{1,0},{2,1},{3,2},{4,3},{5,4},{6,5},{7,6},{8,15},{9,8},{10,9... | collective-permute-start | bytes 393224 | tf_op jit(solution)/shard_map/ppermute | solution.py:485
  137.7 11.6 %collective-permute-start.34 = (bf16[128,512]{1,0:T(8,128)(2,1)}, bf16[128,512]{1,0:T(8,128)(2,1)S(1)}, u32[]{:S(2)}, u32[]{:S(2)}) collective-permute-start(bf16[128,512]{1,0:T(8,128)(2,1)} %get-tuple-element.118), channel_id=1, source_target_pairs={{0,8},{1,9},{2,10},{3,11},{4,12},{5,13},{6,14},{7,15},{8,0},{9,1},... | collective-permute-start | bytes 393224 | tf_op jit(solution)/shard_map/ppermute | solution.py:496
  (55 other events, 207.6 us)

commit v6 on v5

--- a/solution.py
+++ b/solution.py
@@ -14,7 +14,6 @@
 GROUP = 8
 TILE = 256
 VMEM_LIMIT = 16 * 1024 * 1024
-VMEM_MOST = 60 * 1024 * 1024
 PSI = 9 * F + 2 * F
 PSI_SCALE = (0.5,) + (1.0,) * 7 + (0.5,)
 
@@ -102,29 +101,14 @@
         copy.wait()
 
 
-def relay(held_ref, sems, pairs):
-    loads, stores = [], []
-    for i, (source, target) in enumerate(pairs):
-        held = held_ref.at[i]
-        loads.append(pltpu.make_async_copy(source, held, sems.at[2 * i]))
-        stores.append(pltpu.make_async_copy(held, target, sems.at[2 * i + 1]))
-        loads[-1].start()
-    for load, store in zip(loads, stores):
-        load.wait()
-        store.start()
-    for store in stores:
-        store.wait()
-
-
 def aligned(at, size):
     return pl.ds(pl.multiple_of(at * size, size), size)
 
 
 def token_parts_kernel(at_ref, tokens_ref, *rest):
-    *out_refs, held_ref, sems = rest
+    *out_refs, sems = rest
     count, share = len(out_refs) + 1, out_refs[0].shape[1]
-    relay(
-        held_ref,
+    run_copies(
         sems,
         [
             (tokens_ref.at[0, :, aligned(lax.rem(at_ref[0] + shift, count), share)], out_ref)
@@ -133,15 +117,12 @@
     )
 
 
-def pack_heads_kernel(at_ref, values_ref, grad_ref, *rest):
-    *out_refs, held_ref, sems = rest
+def pack_heads_kernel(at_ref, values_ref, grad_ref, *out_refs):
     width = out_refs[0].shape[2]
-    pairs = []
     for shift, out_ref in enumerate(out_refs):
         cols = aligned(lax.rem(at_ref[0] + shift, len(out_refs)), width)
-        pairs.append((values_ref.at[0, :, cols], out_ref.at[0]))
-        pairs.append((grad_ref.at[0, :, cols], out_ref.at[1]))
-    relay(held_ref, sems, pairs)
+        out_ref[0] = values_ref[0, :, cols]
+        out_ref[1] = grad_ref[0, :, cols]
 
 
 def collect_heads_kernel(at_ref, *rest):
@@ -151,28 +132,10 @@
         out_ref[lax.rem(at_ref[0] + group - shift, group)] = part_ref[...]
 
 
-def pack_tokens_kernel(depth, at_ref, tokens_ref, *rest):
-    *out_refs, sems = rest
-    group = len(out_refs)
-    pairs = []
-    for shift, out_ref in enumerate(out_refs):
-        member = lax.rem(at_ref[0] + shift, group)
-        for part in range(out_ref.shape[1] // depth):
-            pairs.append(
-                (
-                    tokens_ref.at[0, :, aligned(part * group + member, depth)],
-                    out_ref.at[:, part * depth : (part + 1) * depth],
-                )
-            )
-    run_copies(sems, pairs)
-
-
-def collect_tokens_kernel(at_ref, *rest):
-    *part_refs, out_ref = rest
-    group, tok = len(part_refs), part_refs[0].shape[0]
-    for shift, part_ref in enumerate(part_refs):
-        src = lax.rem(at_ref[0] + group - shift, group)
-        out_ref[:, aligned(src, tok)] = part_ref[...].T
+def collect_tokens_kernel(in_ref, out_ref):
+    group, tok = in_ref.shape[:2]
+    for src in range(group):
+        out_ref[:, src * tok : (src + 1) * tok] = in_ref[src].T
 
 
 def write_blocks(projected, out_ref):
@@ -184,10 +147,9 @@
                 out_ref[member, which, head] = projected[first : first + feat]
 
 
-def project_kernel(at_ref, tokens_ref, weight_ref, out_ref, weight_out_ref, part_ref, sem):
+def project_kernel(at_ref, tokens_ref, weight_ref, out_ref, part_ref, sem):
     share = part_ref.shape[1]
     run_copies(sem, [(tokens_ref.at[0, :, aligned(at_ref[0], share)], part_ref)])
-    weight_out_ref[...] = weight_ref[...]
     write_blocks(dot(part_ref[...], weight_ref[...]).T, out_ref)
 
 
@@ -227,7 +189,23 @@
             state_refs[0][head] = (dot(high, v) + dot(low, v)).astype(bf16)
 
 
-def numerator_kernel(qk_ref, vg_ref, num_ref):
+def numerator_kernel(depth, qk_ref, vg_ref, *rest):
+    if depth:
+        tokens_ref, num_ref, out_ref, sems = rest
+        group = out_ref.shape[0]
+        copies = [
+            pltpu.make_async_copy(
+                tokens_ref.at[0, :, (part * group + i) * depth : (part * group + i + 1) * depth],
+                out_ref.at[i, :, part * depth : (part + 1) * depth],
+                sems.at[part * group + i],
+            )
+            for i in range(group)
+            for part in range(out_ref.shape[2] // depth)
+        ]
+    else:
+        (num_ref,), copies = rest, []
+    for copy in copies:
+        copy.start()
     heads = qk_ref.shape[2]
     length = qk_ref.shape[0] * qk_ref.shape[4]
     tile = min(TILE, length)
@@ -244,6 +222,8 @@
             high, low = split(kernel)
             v = rows_of(vg_ref, 0, head, 0, width)
             num_ref[at:width, head * DH : (head + 1) * DH] = dot(high, v) + dot(low, v)
+    for copy in copies:
+        copy.wait()
 
 
 def normalize_kernel(with_state, qk_ref, vg_ref, num_ref, *rest):
@@ -333,8 +313,8 @@
     run_copies(sems, [(held_ref, out_ref)])
 
 
-def grad_values_kernel(with_state, group, at_ref, qk_ref, attended_ref, grad_v_ref, *rest):
-    suffix_refs, out_refs, held_ref = rest[: -group - 1], rest[-group - 1 : -1], rest[-1]
+def grad_values_kernel(with_state, at_ref, qk_ref, attended_ref, grad_v_ref, *rest):
+    *suffix_refs, keep_ref, send_ref, held_ref = rest
     heads, tok = qk_ref.shape[2], qk_ref.shape[4]
     for head in range(heads):
         grad_v = grad_v_ref[head]
@@ -342,34 +322,47 @@
             feat = psi(feature_major(qk_ref, 1, head), False)
             grad_v = grad_v + dot3(state_sum(suffix_refs, head).T, feat)
         held_ref[:, head * DH : (head + 1) * DH] = grad_v.T.astype(bf16)
+    chips = keep_ref.shape[0]
+    for shift in range(chips):
+        chip = lax.rem(at_ref[0] + shift, chips)
+        for core, out_ref in ((at_ref[1], keep_ref), (1 - at_ref[1], send_ref)):
+            rows = aligned(2 * chip + core, tok)
+            out_ref[shift, 0] = attended_ref[rows, :]
+            out_ref[shift, 1] = held_ref[rows, :]
+
+
+def pair_kernel(at_ref, keep_ref, got_ref, *out_refs):
     for shift, out_ref in enumerate(out_refs):
-        rows = aligned(lax.rem(at_ref[0] + shift, group), tok)
-        out_ref[0] = attended_ref[rows, :]
-        out_ref[1] = held_ref[rows, :]
+        out_ref[at_ref[1]] = keep_ref[shift]
+        out_ref[1 - at_ref[1]] = got_ref[shift]
 
 
 def unpack_heads_kernel(at_ref, *rest):
     *part_refs, attended_ref, values_ref = rest
-    group, width = len(part_refs), part_refs[0].shape[2]
+    chips, width = len(part_refs), part_refs[0].shape[3]
     for shift, part_ref in enumerate(part_refs):
-        cols = aligned(lax.rem(at_ref[0] + group - shift, group), width)
-        attended_ref[0, :, cols] = part_ref[0]
-        values_ref[0, :, cols] = part_ref[1]
-
-
-def place_rows(at, part_refs, cols, held_ref):
-    group, half = len(part_refs), part_refs[0].shape[0] // 2
-    for shift, part_ref in enumerate(part_refs):
-        src = lax.rem(at + group - shift, group)
-        for which in range(2):
-            rows = aligned(which * group + src, half)
-            held_ref[rows, :] = part_ref[which * half : (which + 1) * half, cols]
+        chip = lax.rem(at_ref[0] + chips - shift, chips)
+        for core in range(2):
+            cols = aligned(2 * chip + core, width)
+            attended_ref[0, :, cols] = part_ref[core, 0]
+            values_ref[0, :, cols] = part_ref[core, 1]
+
+
+def place_rows(chip_at, core_at, part_refs, cols, held_ref):
+    chips, half = len(part_refs) // 2, part_refs[0].shape[0] // 2
+    for shift in range(chips):
+        chip = lax.rem(chip_at + chips - shift, chips)
+        for side, core in ((0, core_at), (1, 1 - core_at)):
+            part_ref = part_refs[2 * shift + side]
+            for which in range(2):
+                rows = aligned(which * 2 * chips + 2 * chip + core, half)
+                held_ref[rows, :] = part_ref[which * half : (which + 1) * half, cols]
 
 
 def product_kernel(group, at_ref, *rest):
     rows_refs, rest = rest[:group], rest[group:]
     tokens_ref, *part_refs, total_ref, held_ref = rest
-    place_rows(at_ref[1], rows_refs, slice(None), held_ref)
+    place_rows(at_ref[1], at_ref[2], rows_refs, slice(None), held_ref)
     total_ref[...] = dot(tokens_ref[...], held_ref[...], NT)
     count = len(part_refs)
     size = part_refs[0].shape[0]
@@ -397,11 +390,12 @@
 def grad_tokens_kernel(group, at_ref, *rest):
     rows_refs, rest = rest[:group], rest[group:]
     *weight_refs, out_ref, held_ref = rest
-    place_rows(at_ref[0], rows_refs, aligned(at_ref[0], out_ref.shape[1]), held_ref)
+    member = 2 * at_ref[0] + at_ref[1]
+    place_rows(at_ref[0], at_ref[1], rows_refs, aligned(member, out_ref.shape[1]), held_ref)
     rows = held_ref[...].T
     for i, weight_ref in enumerate(weight_refs):
         size = weight_ref.shape[0]
-        first = pl.multiple_of(at_ref[1 + i], size)
+        first = pl.multiple_of(at_ref[2 + i], size)
         out_ref[0, :, pl.ds(first, size)] = dot(rows, weight_ref[...], NT).astype(bf16)
 
 
@@ -430,7 +424,6 @@
     far_in=(),
     far_out=False,
     copies=(),
-    limit=VMEM_LIMIT,
 ):
     at = [jnp.stack([jnp.int32(s) for s in scalars])] if scalars else []
     count = len(at) + len(operands)
@@ -449,7 +442,7 @@
         + [FAR] * len(after_far),
         out_specs=[FAR if far_out else VMEM] * len(outs) + [VMEM],
         scratch_shapes=[*scratch] + [pltpu.SemaphoreType.DMA((n,)) for n in copies],
-        compiler_params=pltpu.CompilerParams(vmem_limit_bytes=limit),
+        compiler_params=pltpu.CompilerParams(vmem_limit_bytes=VMEM_LIMIT),
         cost_estimate=pl.CostEstimate(flops=0, bytes_accessed=0, transcendentals=0),
     )(*at, *operands, *after, *after_far)
     return results, token
@@ -507,9 +500,7 @@
         scalars=(dp_at,),
         far_in=(0,),
         far_out=True,
-        scratch=[pltpu.VMEM((dp_size - 1, tok, share), bf16)],
-        copies=(2 * dp_size - 2,),
-        limit=VMEM_MOST,
+        copies=(dp_size - 1,),
     )
     arrived = [to_dp(part, shift) for shift, part in enumerate(parts, 1)]
     parts, token = call(
@@ -519,11 +510,6 @@
         grad_out,
         scalars=(member,),
         after=(token,),
-        far_in=(0, 1),
-        far_out=True,
-        scratch=[pltpu.VMEM((2 * group, tok, heads * DH), bf16)],
-        copies=(4 * group,),
-        limit=VMEM_MOST,
     )
     parts = to_members(parts)
     (vg,), vg_token = call(
@@ -532,9 +518,9 @@
         *parts,
         scalars=(member,),
     )
-    (projected, weight), token = call(
+    (projected,), token = call(
         project_kernel,
-        [qk_shape, (proj_weight.shape, bf16)],
+        [qk_shape],
         tokens,
         proj_weight,
         scalars=(dp_at,),
@@ -543,33 +529,11 @@
         copies=(1,),
         scratch=[pltpu.VMEM((tok, share), bf16)],
     )
-    part_shape = (tok, dp_size * runs * depth)
-    if depth % 128 == 0:
-        parts, token = call(
-            functools.partial(pack_tokens_kernel, depth),
-            [(part_shape, bf16)] * group,
-            tokens,
-            scalars=(member,),
-            after=(token,),
-            far_in=(0,),
-            far_out=True,
-            copies=(group * dp_size * runs,),
-        )
-    else:
-        blocks = tokens[0].reshape(tok, dp_size * runs, group, depth).transpose(2, 0, 1, 3)
-        parts = [
-            lax.dynamic_index_in_dim(blocks, (member + shift) % group, 0, keepdims=False).reshape(
-                part_shape
-            )
-            for shift in range(group)
-        ]
-    token_parts = to_members(parts)
-
     (projected,), token = call(
         project_rest_kernel,
         [((dp_size,) + qk_shape[0], f32)],
         projected,
-        weight,
+        proj_weight,
         *arrived,
         scalars=(dp_at,),
         after=(vg_token, token),
@@ -615,7 +579,23 @@
     prefix, suffix = (), ()
     if with_state:
         prefix = [to_run(state[0], shift, False) for shift in range(1, runs)]
-    (numerator,), token = call(numerator_kernel, [rows_shape], qk, vg)
+    cols_shape = (group, tok, dp_size * runs * depth)
+    if depth % 128 == 0:
+        (numerator, token_cols), token = call(
+            functools.partial(numerator_kernel, depth),
+            [rows_shape, (cols_shape, bf16)],
+            qk,
+            vg,
+            tokens,
+            copies=(group * dp_size * runs,),
+        )
+    else:
+        (numerator,), token = call(
+            functools.partial(numerator_kernel, 0), [rows_shape], qk, vg
+        )
+        token_cols = tokens[0].reshape(tok, dp_size * runs, group, depth)
+        token_cols = token_cols.transpose(2, 0, 1, 3).reshape(cols_shape)
+    token_cols = exchange(token_cols)
     (attended, grad_num, *carried), token = call(
         functools.partial(normalize_kernel, with_state),
         [((length, heads * DH), bf16), rows_shape] + [state_shape] * with_state,
@@ -633,7 +613,7 @@
         vg,
         grad_num,
         *prefix,
-        after_far=[*fetched, *token_parts[1:]],
+        after_far=fetched,
     )
     (rows,), token = call(
         functools.partial(rows_kernel, with_state),
@@ -646,61 +626,77 @@
         scratch=[pltpu.VMEM((2 * heads * F, length), bf16)],
         copies=(1,),
     )
-    rows = [rows] + [to_member(rows, shift) for shift in range(1, group)]
+    chips = group // 2
+    chip_at = member // 2
+
+    def to_chip(x, shift):
+        return x if shift == 0 else to_member(x, 2 * shift)
+
+    def to_other_core(x):
+        return lax.ppermute(x, "ctx", [(i, i ^ 1) for i in range(ctx_size)])
+
+    rows = [to_chip(rows, shift) for shift in range(chips)]
+    rows = [side for part in rows for side in (part, to_other_core(part))]
     (token_cols,), tokens_token = call(
         collect_tokens_kernel,
-        [(part_shape[1:] + (length,), bf16)],
-        *token_parts,
-        scalars=(member,),
-        after=(token,),
-    )
-    results, token = call(
-        functools.partial(grad_values_kernel, with_state, group),
-        [blocks_shape] * group,
+        [((cols_shape[2], length), bf16)],
+        token_cols,
+        after=(token,),
+    )
+    (keep, send), token = call(
+        functools.partial(grad_values_kernel, with_state),
+        [((chips, 2, tok, heads * DH), bf16)] * 2,
         qk,
         attended,
         grad_v,
         *suffix,
-        scalars=(member,),
+        scalars=(chip_at, ctx_at % 2),
         after=(token,),
         scratch=[pltpu.VMEM((length, heads * DH), bf16)],
     )
-    results = to_members(results)
+    results, token = call(
+        pair_kernel,
+        [((2, 2, tok, heads * DH), bf16)] * chips,
+        keep,
+        to_other_core(send),
+        scalars=(chip_at, ctx_at % 2),
+    )
+    results = [to_chip(part, shift) for shift, part in enumerate(results)]
 
     held = pltpu.VMEM((cols, length), bf16)
     (own, *parts), token = call(
-        functools.partial(product_kernel, group),
+        functools.partial(product_kernel, 2 * chips),
         [((runs * depth, cols), f32)] + [((runs * depth, cols), bf16)] * (dp_size - 1),
         *rows,
         token_cols,
-        scalars=(dp_at, member),
+        scalars=(dp_at, chip_at, ctx_at % 2),
         after=(token,),
         scratch=[pltpu.VMEM((dp_size * runs * depth, cols), f32), held],
     )
     parts = [to_dp(part, shift) for shift, part in enumerate(parts, 1)]
+    (grad_tokens,), tokens_token = call(
+        functools.partial(grad_tokens_kernel, 2 * chips),
+        [((1, tok, width), bf16)],
+        *rows,
+        *weights,
+        scalars=(chip_at, ctx_at % 2, *firsts),
+        after=(token,),
+        scratch=[pltpu.VMEM((cols, tok), bf16)],
+    )
     (grad_proj, *parts), token = call(
         functools.partial(run_sum_kernel, len(parts)),
         [((depth, cols), f32)] + [((depth, cols), bf16)] * (runs - 1),
         own,
         *parts,
         scalars=(run_at,),
-        after_far=results[1 : 1 + group // 2],
+        after=(tokens_token,),
         scratch=[pltpu.VMEM((runs * depth, cols), f32)],
-    )
-    (grad_tokens,), tokens_token = call(
-        functools.partial(grad_tokens_kernel, group),
-        [((1, tok, width), bf16)],
-        *rows,
-        *weights,
-        scalars=(member, *firsts),
-        after=(token,),
-        scratch=[pltpu.VMEM((cols, tok), bf16)],
     )
     (attended, grad_values), token = call(
         unpack_heads_kernel,
         [((1, tok, H * DH), bf16)] * 2,
         *results,
-        scalars=(member,),
+        scalars=(chip_at,),
         after=(token,),
     )
     (grad_proj,), _ = call(
@@ -708,7 +704,7 @@
         [((depth, cols), f32)],
         grad_proj,
         *[to_run(part, shift, True) for shift, part in enumerate(parts, 1)],
-        after=(tokens_token, token),
+        after=(token,),
     )
     return (attended, grad_tokens, grad_values, grad_proj)
 

time: 151 us -> 134 us (0.89)
  the two profiles are of different devices: /device:TPU:0 before, /device:TPU:4 now
where the time goes in v6:
time: 134 us; the launch traced here: 133 us
  waiting for transfers between devices  53.4 us (40%)
  Pallas kernels  35.3 us (26%)
  starting transfers between devices  33.1 us (25%)
  local copies, waits for them, and re-layouts  10.1 us (8%)
    pallas_call x19, Pallas kernels, call(): pl.pallas_call(kernel, out_shape=[jax.ShapeDtypeStruct(shape, kind) for s...  35.3 us
    ppermute x13, waiting for transfers between devices, to_member(): return lax.ppermute(x, 'ctx', pairs)  21.8 us
    ppermute x3, waiting for transfers between devices, to_dp(): lax.ppermute(x, 'dp', [(i, (i + shift) % dp_size) for i in range(dp_size)])  21.7 us
    ppermute x13, starting transfers between devices, to_member(): return lax.ppermute(x, 'ctx', pairs)  10.4 us
    unnamed x26, local copies, waits for them, and re-layouts  10.1 us
    all_to_all x1, waiting for transfers between devices, local(): lax.all_to_all(projected.reshape((dp_size * group,) + qk_shape[0][1:]), (...  8.02 us
    ppermute x3, starting transfers between devices, to_run(): return lax.ppermute(x, 'ctx', pairs)  7.71 us
    all_to_all x1, starting transfers between devices, exchange(): lax.all_to_all(x, 'ctx', split_axis=0, concat_axis=0, tiled=True, axis_in...  6.87 us
  transfers between devices with their start and end apart: 27, of which 14 were waited for; matrix products, arithmetic and copies ran while one was open for 0% of the time, Pallas kernels for 20%

profile of v6, /device:TPU:4, one launch (start us, length us, event | category | flops | bytes accessed | tf_op | source)
XLA Modules:
  0.0 132.9 jit_solution(7447980090044360740)
XLA Ops:
  9.5 1.6 %collective-permute-start.4 = (bf16[2,128,256]{2,1,0:T(8,128)(2,1)S(1)}, bf16[2,128,256]{2,1,0:T(8,128)(2,1)S(1)}, u32[]{:S(2)}, u32[]{:S(2)}) collective-permute-start(bf16[2,128,256]{2,1,0:T(8,128)(2,1)S(1)} %get-tuple-element.61), channel_id=1, source_target_pairs={{0,4},{1,5},{2,6},{3,7},{4,0},{5,1},{6,2},{7,3},{8,12},{9,13},{10,... | collective-permute-start | bytes 393224 | tf_op jit(solution)/shard_map/ppermute | solution.py:478
  14.4 3.0 %collective-permute-done.3.refs_4_ = bf16[2,128,256]{2,1,0:T(8,128)(2,1)S(1)} collective-permute-done((bf16[2,128,256]{2,1,0:T(8,128)(2,1)S(1)}, bf16[2,128,256]{2,1,0:T(8,128)(2,1)S(1)}, u32[]{:S(2)}, u32[]{:S(2)}) %collective-permute-start.3) | collective-permute-done | bytes 131104 | tf_op jit(solution)/shard_map/ppermute | solution.py:478
  21.5 1.6 %shard_map.79 = (f32[2,8,2,2,16,128]{5,4,3,2,1,0:T(8,128)S(1)}, f32[8,128]{1,0:T(8,128)S(1)}) custom-call(s32[1]{0:T(128)} %bitcast.2.refs_0_, f32[8,2,2,16,128]{4,3,2,1,0:T(8,128)S(1)} %get-tuple-element.55.refs_1_, bf16[2048,512]{1,0:T(8,128)(2,1)S(1)} %copy-done, bf16[128,2048]{1,0:T(8,128)(2,1)} %collective-permute-done.refs_3_, ...), custom_call_target="tpu_custom_call" | custom-call | tf_op jit(solution)/shard_map/pallas_call | solution.py:436
  23.9 4.8 %all-to-all-start = ((f32[16,2,2,16,128]{4,3,2,1,0:T(8,128)}), f32[16,2,2,16,128]{4,3,2,1,0:T(8,128)}, u32[]{:S(2)}, u32[]{:S(2)}) async-start(f32[16,2,2,16,128]{4,3,2,1,0:T(8,128)} %bitcast.10), calls=%async_computation | async-start | bytes 1048576 | tf_op jit(solution)/shard_map/all_to_all | solution.py:541
  28.7 8.0 %all-to-all-done = f32[16,2,2,16,128]{4,3,2,1,0:T(8,128)} async-done(((f32[16,2,2,16,128]{4,3,2,1,0:T(8,128)}), f32[16,2,2,16,128]{4,3,2,1,0:T(8,128)}, u32[]{:S(2)}, u32[]{:S(2)}) %all-to-all-start) | async-done | bytes 524320 | tf_op jit(solution)/shard_map/all_to_all | solution.py:541
  36.7 1.7 %shard_map.80 = (f32[8,2,2,16,128]{4,3,2,1,0:T(8,128)S(1)}, bf16[2,176,128]{2,1,0:T(8,128)(2,1)S(1)}, f32[8,128]{1,0:T(8,128)}) custom-call(f32[2,8,2,2,16,128]{5,4,3,2,1,0:T(8,128)} %bitcast.5.refs_0_, bf16[8,2,128,256]{3,2,1,0:T(8,128)(2,1)S(1)} %get-tuple-element.68.refs_1_), custom_call_target="tpu_custom_call" | custom-call | tf_op jit(solution)/shard_map/pallas_call | solution.py:436
  39.1 4.3 %shard_map.81 = (f32[1024,256]{1,0:T(8,128)S(1)}, bf16[8,128,512]{2,1,0:T(8,128)(2,1)S(1)}, f32[8,128]{1,0:T(8,128)}) custom-call(f32[8,2,2,16,128]{4,3,2,1,0:T(8,128)S(1)} %get-tuple-element.69.refs_0_.refs_1_, bf16[8,2,128,256]{3,2,1,0:T(8,128)(2,1)S(1)} %get-tuple-element.68.refs_1_, bf16[1,128,4096]{2,1,0:T(8,128)(2,1)S(1)} %copy-done.3), custom_call_target="tpu_custom_call" | custom-call | tf_op jit(solution)/shard_map/pallas_call | solution.py:436
  45.3 6.9 %all-to-all-start.1 = ((bf16[8,128,512]{2,1,0:T(8,128)(2,1)}), bf16[8,128,512]{2,1,0:T(8,128)(2,1)}, u32[]{:S(2)}, u32[]{:S(2)}) async-start(bf16[8,128,512]{2,1,0:T(8,128)(2,1)} %copy-done.6), calls=%async_computation.1 | async-start | bytes 2097152 | tf_op jit(solution)/shard_map/all_to_all | solution.py:469
  53.5 4.5 %collective-permute-start.8 = (bf16[2,176,128]{2,1,0:T(8,128)(2,1)}, bf16[2,176,128]{2,1,0:T(8,128)(2,1)S(1)}, u32[]{:S(2)}, u32[]{:S(2)}) collective-permute-start(bf16[2,176,128]{2,1,0:T(8,128)(2,1)} %copy-done.12), channel_id=1, source_target_pairs={{0,8},{1,9},{2,10},{3,11},{4,12},{5,13},{6,14},{7,15},{16,24},{17,... | collective-permute-start | bytes 270344 | tf_op jit(solution)/shard_map/ppermute | solution.py:489
  58.0 20.2 %collective-permute-done.9.refs_4_.refs_10_ = bf16[1024,512]{1,0:T(8,128)(2,1)} collective-permute-done((bf16[1024,512]{1,0:T(8,128)(2,1)S(1)}, bf16[1024,512]{1,0:T(8,128)(2,1)}, u32[]{:S(2)}, u32[]{:S(2)}) %collective-permute-start.9) | collective-permute-done | bytes 1048608 | tf_op jit(solution)/shard_map/ppermute | solution.py:474
  79.5 2.6 %shard_map.82 = (bf16[1024,256]{1,0:T(8,128)(2,1)S(1)}, f32[1024,256]{1,0:T(8,128)S(1)}, bf16[2,176,128]{2,1,0:T(8,128)(2,1)S(1)}, f32[8,128]{1,0:T(8,128)}) custom-call(f32[8,2,2,16,128]{4,3,2,1,0:T(8,128)S(1)} %get-tuple-element.69.refs_0_.refs_1_, bf16[8,2,128,256]{3,2,1,0:T(8,128)(2,1)S(1)} %get-tuple-element.68.refs_1_, f32[1024,256]{1,0:T(8,128)S(1)} %copy-done.5, ...), custom_call_target="tpu_custom_call" | custom-call | tf_op jit(solution)/shard_map/pallas_call | solution.py:436
  83.7 6.3 %shard_map.84 = (f32[2,2,16,1024]{3,2,1,0:T(8,128)S(1)}, f32[2,128,1024]{2,1,0:T(8,128)S(1)}, f32[8,128]{1,0:T(8,128)}) custom-call(f32[8,2,2,16,128]{4,3,2,1,0:T(8,128)S(1)} %get-tuple-element.69.refs_0_.refs_1_, bf16[8,2,128,256]{3,2,1,0:T(8,128)(2,1)S(1)} %get-tuple-element.68.refs_1_, f32[1024,256]{1,0:T(8,128)S(1)} %get-tuple-element.73.refs_2_, ...), custom_call_target="tpu_custom_call" | custom-call | tf_op jit(solution)/shard_map/pallas_call | solution.py:436
  90.0 1.8 %collective-permute-done.10.refs_3_.refs_4_ = bf16[2,176,128]{2,1,0:T(8,128)(2,1)S(1)} collective-permute-done((bf16[2,176,128]{2,1,0:T(8,128)(2,1)S(1)}, bf16[2,176,128]{2,1,0:T(8,128)(2,1)S(1)}, u32[]{:S(2)}, u32[]{:S(2)}) %collective-permute-start.10) | collective-permute-done | bytes 90144 | tf_op jit(solution)/shard_map/ppermute | solution.py:489
  92.6 1.8 %shard_map.86 = (bf16[4,2,128,256]{3,2,1,0:T(8,128)(2,1)S(1)}, bf16[4,2,128,256]{3,2,1,0:T(8,128)(2,1)S(1)}, f32[8,128]{1,0:T(8,128)}) custom-call(s32[2]{0:T(128)S(1)} %pad_add_fusion.refs_0_, f32[8,2,2,16,128]{4,3,2,1,0:T(8,128)S(1)} %get-tuple-element.69.refs_0_.refs_1_, bf16[1024,256]{1,0:T(8,128)(2,1)S(1)} %get-tuple-element.72.refs_2_, ...), custom_call_target="tpu_custom_call" | custom-call | tf_op jit(solution)/shard_map/pallas_call | solution.py:436
  94.6 1.7 %collective-permute-start.18 = (bf16[64,1024]{1,0:T(8,128)(2,1)S(1)}, bf16[64,1024]{1,0:T(8,128)(2,1)S(1)}, u32[]{:S(2)}, u32[]{:S(2)}) collective-permute-start(bf16[64,1024]{1,0:T(8,128)(2,1)S(1)} %get-tuple-element.86.refs_1_), channel_id=1, source_target_pairs={{0,4},{1,5},{2,6},{3,7},{4,0},{5,1},{6,2},{7,3},{8,12},{9,13},{10,... | collective-permute-start | bytes 393224 | tf_op jit(solution)/shard_map/ppermute | solution.py:478
  96.6 3.7 %collective-permute-done.16.refs_3_ = bf16[64,1024]{1,0:T(8,128)(2,1)S(1)} collective-permute-done((bf16[64,1024]{1,0:T(8,128)(2,1)S(1)}, bf16[64,1024]{1,0:T(8,128)(2,1)S(1)}, u32[]{:S(2)}, u32[]{:S(2)}) %collective-permute-start.16) | collective-permute-done | bytes 131104 | tf_op jit(solution)/shard_map/ppermute | solution.py:478
  100.4 2.6 %collective-permute-done.18.refs_5_ = bf16[64,1024]{1,0:T(8,128)(2,1)S(1)} collective-permute-done((bf16[64,1024]{1,0:T(8,128)(2,1)S(1)}, bf16[64,1024]{1,0:T(8,128)(2,1)S(1)}, u32[]{:S(2)}, u32[]{:S(2)}) %collective-permute-start.18) | collective-permute-done | bytes 131104 | tf_op jit(solution)/shard_map/ppermute | solution.py:478
  106.4 2.1 %shard_map.88 = (bf16[512,1024]{1,0:T(8,128)(2,1)S(1)}, f32[8,128]{1,0:T(8,128)}) custom-call(bf16[8,128,512]{2,1,0:T(8,128)(2,1)} %all-to-all-done.1.refs_0_, f32[8,128]{1,0:T(8,128)S(1)} %get-tuple-element.79.refs_5_.refs_1_), custom_call_target="tpu_custom_call" | custom-call | tf_op jit(solution)/shard_map/pallas_call | solution.py:436
  108.5 2.2 %shard_map.89 = (f32[256,512]{1,0:T(8,128)S(1)}, bf16[256,512]{1,0:T(8,128)(2,1)}, f32[8,128]{1,0:T(8,128)S(1)}) custom-call(s32[3]{0:T(128)S(1)} %pad_add_fusion.1.refs_0_, bf16[64,1024]{1,0:T(8,128)(2,1)S(1)} %get-tuple-element.86.refs_1_, bf16[64,1024]{1,0:T(8,128)(2,1)S(1)} %collective-permute-done.15.refs_2_, ...), custom_call_target="tpu_custom_call" | custom-call | tf_op jit(solution)/shard_map/pallas_call | solution.py:436
  114.5 4.1 %shard_map.90 = (bf16[1,128,4096]{2,1,0:T(8,128)(2,1)}, f32[8,128]{1,0:T(8,128)S(1)}) custom-call(s32[5]{0:T(128)S(1)} %stack.56.refs_0_, bf16[64,1024]{1,0:T(8,128)(2,1)S(1)} %get-tuple-element.86.refs_1_, bf16[64,1024]{1,0:T(8,128)(2,1)S(1)} %collective-permute-done.15.refs_2_, bf16[64,1024]{1,0:T(8,128)(2,1)S(1)} %collective-permute-done.16.refs_3_, ...), custom_call_target="tpu_custom_call" | custom-call | tf_op jit(solution)/shard_map/pallas_call | solution.py:436
  121.1 1.8 %collective-permute-start.24 = (bf16[128,512]{1,0:T(8,128)(2,1)S(1)}, bf16[128,512]{1,0:T(8,128)(2,1)S(1)}, u32[]{:S(2)}, u32[]{:S(2)}) collective-permute-start(bf16[128,512]{1,0:T(8,128)(2,1)S(1)} %get-tuple-element.99), channel_id=1, source_target_pairs={{0,8},{1,9},{2,10},{3,11},{4,12},{5,13},{6,14},{7,15},{8,0},{9,1},... | collective-permute-start | bytes 393224 | tf_op jit(solution)/shard_map/ppermute | solution.py:489
  122.9 5.3 %collective-permute-done.13.refs_3_ = bf16[2,2,128,256]{3,2,1,0:T(8,128)(2,1)} collective-permute-done((bf16[2,2,128,256]{3,2,1,0:T(8,128)(2,1)}, bf16[2,2,128,256]{3,2,1,0:T(8,128)(2,1)}, u32[]{:S(2)}, u32[]{:S(2)}) %collective-permute-start.13) | collective-permute-done | bytes 262176 | tf_op jit(solution)/shard_map/ppermute | solution.py:478
  128.2 1.8 %collective-permute-done.14.refs_4_ = bf16[2,2,128,256]{3,2,1,0:T(8,128)(2,1)} collective-permute-done((bf16[2,2,128,256]{3,2,1,0:T(8,128)(2,1)}, bf16[2,2,128,256]{3,2,1,0:T(8,128)(2,1)}, u32[]{:S(2)}, u32[]{:S(2)}) %collective-permute-start.14) | collective-permute-done | bytes 262176 | tf_op jit(solution)/shard_map/ppermute | solution.py:478
  130.0 2.1 %shard_map.92 = (bf16[1,128,2048]{2,1,0:T(8,128)(2,1)}, bf16[1,128,2048]{2,1,0:T(8,128)(2,1)}, f32[8,128]{1,0:T(8,128)S(1)}) custom-call(s32[1]{0:T(128)} %bitcast.refs_0_, bf16[2,2,128,256]{3,2,1,0:T(8,128)(2,1)S(1)} %get-tuple-element.82.refs_1_, bf16[2,2,128,256]{3,2,1,0:T(8,128)(2,1)} %collective-permute-done.12.refs_2_, ...), custom_call_target="tpu_custom_call" | custom-call | tf_op jit(solution)/shard_map/pallas_call | solution.py:436
  (78 shorter events, 35.3 us)
Async XLA Ops:
  2.8 18.6 %collective-permute-start = (bf16[128,2048]{1,0:T(8,128)(2,1)}, bf16[128,2048]{1,0:T(8,128)(2,1)}, u32[]{:S(2)}, u32[]{:S(2)}) collective-permute-start(bf16[128,2048]{1,0:T(8,128)(2,1)} %get-tuple-element.56), channel_id=1, source_target_pairs={{0,16},{16,0},{1,17},{17,1},{2,18},{18,2},{3,19},{19,3},{4,20},{20... | collective-permute-start | bytes 1572872 | tf_op jit(solution)/shard_map/ppermute | solution.py:474
  6.6 5.3 %collective-permute-start.1 = (bf16[2,128,256]{2,1,0:T(8,128)(2,1)S(1)}, bf16[2,128,256]{2,1,0:T(8,128)(2,1)S(1)}, u32[]{:S(2)}, u32[]{:S(2)}) collective-permute-start(bf16[2,128,256]{2,1,0:T(8,128)(2,1)S(1)} %get-tuple-element.58), channel_id=1, source_target_pairs={{0,1},{1,2},{2,3},{3,4},{4,5},{5,6},{6,7},{7,0},{8,9},{9,10},{10,1... | collective-permute-start | bytes 393224 | tf_op jit(solution)/shard_map/ppermute | solution.py:478
  6.7 6.4 %collective-permute-start.2 = (bf16[2,128,256]{2,1,0:T(8,128)(2,1)S(1)}, bf16[2,128,256]{2,1,0:T(8,128)(2,1)S(1)}, u32[]{:S(2)}, u32[]{:S(2)}) collective-permute-start(bf16[2,128,256]{2,1,0:T(8,128)(2,1)S(1)} %get-tuple-element.59), channel_id=1, source_target_pairs={{0,2},{1,3},{2,4},{3,5},{4,6},{5,7},{6,0},{7,1},{8,10},{9,11},{10,... | collective-permute-start | bytes 393224 | tf_op jit(solution)/shard_map/ppermute | solution.py:478
  8.2 9.2 %collective-permute-start.3 = (bf16[2,128,256]{2,1,0:T(8,128)(2,1)S(1)}, bf16[2,128,256]{2,1,0:T(8,128)(2,1)S(1)}, u32[]{:S(2)}, u32[]{:S(2)}) collective-permute-start(bf16[2,128,256]{2,1,0:T(8,128)(2,1)S(1)} %get-tuple-element.60), channel_id=1, source_target_pairs={{0,3},{1,4},{2,5},{3,6},{4,7},{5,0},{6,1},{7,2},{8,11},{9,12},{10,... | collective-permute-start | bytes 393224 | tf_op jit(solution)/shard_map/ppermute | solution.py:478
  9.5 9.7 %collective-permute-start.4 = (bf16[2,128,256]{2,1,0:T(8,128)(2,1)S(1)}, bf16[2,128,256]{2,1,0:T(8,128)(2,1)S(1)}, u32[]{:S(2)}, u32[]{:S(2)}) collective-permute-start(bf16[2,128,256]{2,1,0:T(8,128)(2,1)S(1)} %get-tuple-element.61), channel_id=1, source_target_pairs={{0,4},{1,5},{2,6},{3,7},{4,0},{5,1},{6,2},{7,3},{8,12},{9,13},{10,... | collective-permute-start | bytes 393224 | tf_op jit(solution)/shard_map/ppermute | solution.py:478
  11.9 8.1 %collective-permute-start.5 = (bf16[2,128,256]{2,1,0:T(8,128)(2,1)S(1)}, bf16[2,128,256]{2,1,0:T(8,128)(2,1)S(1)}, u32[]{:S(2)}, u32[]{:S(2)}) collective-permute-start(bf16[2,128,256]{2,1,0:T(8,128)(2,1)S(1)} %get-tuple-element.62), channel_id=1, source_target_pairs={{0,5},{1,6},{2,7},{3,0},{4,1},{5,2},{6,3},{7,4},{8,13},{9,14},{10,... | collective-permute-start | bytes 393224 | tf_op jit(solution)/shard_map/ppermute | solution.py:478
  13.0 8.3 %collective-permute-start.6 = (bf16[2,128,256]{2,1,0:T(8,128)(2,1)S(1)}, bf16[2,128,256]{2,1,0:T(8,128)(2,1)S(1)}, u32[]{:S(2)}, u32[]{:S(2)}) collective-permute-start(bf16[2,128,256]{2,1,0:T(8,128)(2,1)S(1)} %get-tuple-element.63), channel_id=1, source_target_pairs={{0,6},{1,7},{2,0},{3,1},{4,2},{5,3},{6,4},{7,5},{8,14},{9,15},{10,... | collective-permute-start | bytes 393224 | tf_op jit(solution)/shard_map/ppermute | solution.py:478
  23.9 12.8 %all-to-all-start = ((f32[16,2,2,16,128]{4,3,2,1,0:T(8,128)}), f32[16,2,2,16,128]{4,3,2,1,0:T(8,128)}, u32[]{:S(2)}, u32[]{:S(2)}) async-start(f32[16,2,2,16,128]{4,3,2,1,0:T(8,128)} %bitcast.10), calls=%async_computation | async-start | bytes 1048576 | tf_op jit(solution)/shard_map/all_to_all | solution.py:541
  45.3 61.1 %all-to-all-start.1 = ((bf16[8,128,512]{2,1,0:T(8,128)(2,1)}), bf16[8,128,512]{2,1,0:T(8,128)(2,1)}, u32[]{:S(2)}, u32[]{:S(2)}) async-start(bf16[8,128,512]{2,1,0:T(8,128)(2,1)} %copy-done.6), calls=%async_computation.1 | async-start | bytes 2097152 | tf_op jit(solution)/shard_map/all_to_all | solution.py:469
  52.9 25.4 %collective-permute-start.9 = (bf16[1024,512]{1,0:T(8,128)(2,1)S(1)}, bf16[1024,512]{1,0:T(8,128)(2,1)}, u32[]{:S(2)}, u32[]{:S(2)}) collective-permute-start(bf16[1024,512]{1,0:T(8,128)(2,1)S(1)} %get-tuple-element.75), channel_id=1, source_target_pairs={{0,16},{16,0},{1,17},{17,1},{2,18},{18,2},{3,19},{19,3},{4,20},{20... | collective-permute-start | bytes 3145736 | tf_op jit(solution)/shard_map/ppermute | solution.py:474
  53.5 24.7 %collective-permute-start.8 = (bf16[2,176,128]{2,1,0:T(8,128)(2,1)}, bf16[2,176,128]{2,1,0:T(8,128)(2,1)S(1)}, u32[]{:S(2)}, u32[]{:S(2)}) collective-permute-start(bf16[2,176,128]{2,1,0:T(8,128)(2,1)} %copy-done.12), channel_id=1, source_target_pairs={{0,8},{1,9},{2,10},{3,11},{4,12},{5,13},{6,14},{7,15},{16,24},{17,... | collective-permute-start | bytes 270344 | tf_op jit(solution)/shard_map/ppermute | solution.py:489
  78.3 36.2 %collective-permute-start.23 = (bf16[1024,512]{1,0:T(8,128)(2,1)}, bf16[1024,512]{1,0:T(8,128)(2,1)}, u32[]{:S(2)}, u32[]{:S(2)}) collective-permute-start(bf16[1024,512]{1,0:T(8,128)(2,1)} %collective-permute-done.9.refs_4_.refs_10_), channel_id=1, source_target_pairs={{0,1},{1,0},{2,3},{3,2},{4,5},{5,4},{6,7},{7,6},{8,9},{9,8},{10,11... | collective-permute-start | bytes 3145736 | tf_op jit(solution)/shard_map/ppermute | solution.py:570
  82.1 9.7 %collective-permute-start.10 = (bf16[2,176,128]{2,1,0:T(8,128)(2,1)S(1)}, bf16[2,176,128]{2,1,0:T(8,128)(2,1)S(1)}, u32[]{:S(2)}, u32[]{:S(2)}) collective-permute-start(bf16[2,176,128]{2,1,0:T(8,128)(2,1)S(1)} %get-tuple-element.77), channel_id=1, source_target_pairs={{8,0},{9,1},{10,2},{11,3},{12,4},{13,5},{14,6},{15,7},{24,16},{25,... | collective-permute-start | bytes 270344 | tf_op jit(solution)/shard_map/ppermute | solution.py:489
  94.4 9.9 %collective-permute-start.11 = (bf16[4,2,128,256]{3,2,1,0:T(8,128)(2,1)S(1)}, bf16[4,2,128,256]{3,2,1,0:T(8,128)(2,1)S(1)}, u32[]{:S(2)}, u32[]{:S(2)}) collective-permute-start(bf16[4,2,128,256]{3,2,1,0:T(8,128)(2,1)S(1)} %get-tuple-element.81), channel_id=1, source_target_pairs={{0,1},{1,0},{2,3},{3,2},{4,5},{5,4},{6,7},{7,6},{8,9},{9,8},{10,11... | collective-permute-start | bytes 1572872 | tf_op jit(solution)/shard_map/ppermute | solution.py:636
  94.4 5.9 %collective-permute-start.16 = (bf16[64,1024]{1,0:T(8,128)(2,1)S(1)}, bf16[64,1024]{1,0:T(8,128)(2,1)S(1)}, u32[]{:S(2)}, u32[]{:S(2)}) collective-permute-start(bf16[64,1024]{1,0:T(8,128)(2,1)S(1)} %get-tuple-element.86.refs_1_), channel_id=1, source_target_pairs={{0,2},{1,3},{2,4},{3,5},{4,6},{5,7},{6,0},{7,1},{8,10},{9,11},{10,... | collective-permute-start | bytes 393224 | tf_op jit(solution)/shard_map/ppermute | solution.py:478
  94.6 8.4 %collective-permute-start.18 = (bf16[64,1024]{1,0:T(8,128)(2,1)S(1)}, bf16[64,1024]{1,0:T(8,128)(2,1)S(1)}, u32[]{:S(2)}, u32[]{:S(2)}) collective-permute-start(bf16[64,1024]{1,0:T(8,128)(2,1)S(1)} %get-tuple-element.86.refs_1_), channel_id=1, source_target_pairs={{0,4},{1,5},{2,6},{3,7},{4,0},{5,1},{6,2},{7,3},{8,12},{9,13},{10,... | collective-permute-start | bytes 393224 | tf_op jit(solution)/shard_map/ppermute | solution.py:478
  96.3 8.1 %collective-permute-start.20 = (bf16[64,1024]{1,0:T(8,128)(2,1)S(1)}, bf16[64,1024]{1,0:T(8,128)(2,1)S(1)}, u32[]{:S(2)}, u32[]{:S(2)}) collective-permute-start(bf16[64,1024]{1,0:T(8,128)(2,1)S(1)} %get-tuple-element.86.refs_1_), channel_id=1, source_target_pairs={{0,6},{1,7},{2,0},{3,1},{4,2},{5,3},{6,4},{7,5},{8,14},{9,15},{10,... | collective-permute-start | bytes 393224 | tf_op jit(solution)/shard_map/ppermute | solution.py:478
  100.4 8.2 %collective-permute-start.15 = (bf16[64,1024]{1,0:T(8,128)(2,1)S(1)}, bf16[64,1024]{1,0:T(8,128)(2,1)S(1)}, u32[]{:S(2)}, u32[]{:S(2)}) collective-permute-start(bf16[64,1024]{1,0:T(8,128)(2,1)S(1)} %get-tuple-element.86.refs_1_), channel_id=1, source_target_pairs={{0,1},{1,0},{2,3},{3,2},{4,5},{5,4},{6,7},{7,6},{8,9},{9,8},{10,11... | collective-permute-start | bytes 393224 | tf_op jit(solution)/shard_map/ppermute | solution.py:636
  103.0 5.5 %collective-permute-start.17 = (bf16[64,1024]{1,0:T(8,128)(2,1)S(1)}, bf16[64,1024]{1,0:T(8,128)(2,1)S(1)}, u32[]{:S(2)}, u32[]{:S(2)}) collective-permute-start(bf16[64,1024]{1,0:T(8,128)(2,1)S(1)} %collective-permute-done.16.refs_3_), channel_id=1, source_target_pairs={{0,1},{1,0},{2,3},{3,2},{4,5},{5,4},{6,7},{7,6},{8,9},{9,8},{10,11... | collective-permute-start | bytes 393224 | tf_op jit(solution)/shard_map/ppermute | solution.py:636
  111.5 8.5 %collective-permute-start.22 = (bf16[256,512]{1,0:T(8,128)(2,1)}, bf16[256,512]{1,0:T(8,128)(2,1)}, u32[]{:S(2)}, u32[]{:S(2)}) collective-permute-start(bf16[256,512]{1,0:T(8,128)(2,1)} %get-tuple-element.91), channel_id=1, source_target_pairs={{0,16},{16,0},{1,17},{17,1},{2,18},{18,2},{3,19},{19,3},{4,20},{20... | collective-permute-start | bytes 786440 | tf_op jit(solution)/shard_map/ppermute | solution.py:474
  112.1 10.8 %collective-permute-start.12 = (bf16[2,2,128,256]{3,2,1,0:T(8,128)(2,1)}, bf16[2,2,128,256]{3,2,1,0:T(8,128)(2,1)}, u32[]{:S(2)}, u32[]{:S(2)}) collective-permute-start(bf16[2,2,128,256]{3,2,1,0:T(8,128)(2,1)} %get-tuple-element.83), channel_id=1, source_target_pairs={{0,2},{1,3},{2,4},{3,5},{4,6},{5,7},{6,0},{7,1},{8,10},{9,11},{10,... | collective-permute-start | bytes 786440 | tf_op jit(solution)/shard_map/ppermute | solution.py:478
  112.1 16.1 %collective-permute-start.13 = (bf16[2,2,128,256]{3,2,1,0:T(8,128)(2,1)}, bf16[2,2,128,256]{3,2,1,0:T(8,128)(2,1)}, u32[]{:S(2)}, u32[]{:S(2)}) collective-permute-start(bf16[2,2,128,256]{3,2,1,0:T(8,128)(2,1)} %get-tuple-element.84), channel_id=1, source_target_pairs={{0,4},{1,5},{2,6},{3,7},{4,0},{5,1},{6,2},{7,3},{8,12},{9,13},{10,... | collective-permute-start | bytes 786440 | tf_op jit(solution)/shard_map/ppermute | solution.py:478
  113.7 16.3 %collective-permute-start.14 = (bf16[2,2,128,256]{3,2,1,0:T(8,128)(2,1)}, bf16[2,2,128,256]{3,2,1,0:T(8,128)(2,1)}, u32[]{:S(2)}, u32[]{:S(2)}) collective-permute-start(bf16[2,2,128,256]{3,2,1,0:T(8,128)(2,1)} %get-tuple-element.85), channel_id=1, source_target_pairs={{0,6},{1,7},{2,0},{3,1},{4,2},{5,3},{6,4},{7,5},{8,14},{9,15},{10,... | collective-permute-start | bytes 786440 | tf_op jit(solution)/shard_map/ppermute | solution.py:478
  121.1 11.0 %collective-permute-start.24 = (bf16[128,512]{1,0:T(8,128)(2,1)S(1)}, bf16[128,512]{1,0:T(8,128)(2,1)S(1)}, u32[]{:S(2)}, u32[]{:S(2)}) collective-permute-start(bf16[128,512]{1,0:T(8,128)(2,1)S(1)} %get-tuple-element.99), channel_id=1, source_target_pairs={{0,8},{1,9},{2,10},{3,11},{4,12},{5,13},{6,14},{7,15},{8,0},{9,1},... | collective-permute-start | bytes 393224 | tf_op jit(solution)/shard_map/ppermute | solution.py:489
  (16 other events, 47.1 us)

commit v7 on v6

--- a/solution.py
+++ b/solution.py
@@ -132,10 +132,23 @@
         out_ref[lax.rem(at_ref[0] + group - shift, group)] = part_ref[...]
 
 
-def collect_tokens_kernel(in_ref, out_ref):
-    group, tok = in_ref.shape[:2]
-    for src in range(group):
-        out_ref[:, src * tok : (src + 1) * tok] = in_ref[src].T
+def pack_tokens_kernel(depth, at_ref, tokens_ref, keep_ref, send_ref):
+    chips, _, rows = keep_ref.shape
+    for shift in range(chips):
+        chip = lax.rem(at_ref[0] + shift, chips)
+        for core, out_ref in ((at_ref[1], keep_ref), (1 - at_ref[1], send_ref)):
+            for part in range(rows // depth):
+                cols = aligned(2 * (part * chips + chip) + core, depth)
+                out_ref[shift, :, part * depth : (part + 1) * depth] = tokens_ref[0, :, cols]
+
+
+def collect_tokens_kernel(at_ref, *rest):
+    *part_refs, out_ref = rest
+    chips, tok = len(part_refs), part_refs[0].shape[1]
+    for shift, part_ref in enumerate(part_refs):
+        chip = lax.rem(at_ref[0] + chips - shift, chips)
+        for core in range(2):
+            out_ref[:, aligned(2 * chip + core, tok)] = part_ref[core].T
 
 
 def write_blocks(projected, out_ref):
@@ -189,23 +202,7 @@
             state_refs[0][head] = (dot(high, v) + dot(low, v)).astype(bf16)
 
 
-def numerator_kernel(depth, qk_ref, vg_ref, *rest):
-    if depth:
-        tokens_ref, num_ref, out_ref, sems = rest
-        group = out_ref.shape[0]
-        copies = [
-            pltpu.make_async_copy(
-                tokens_ref.at[0, :, (part * group + i) * depth : (part * group + i + 1) * depth],
-                out_ref.at[i, :, part * depth : (part + 1) * depth],
-                sems.at[part * group + i],
-            )
-            for i in range(group)
-            for part in range(out_ref.shape[2] // depth)
-        ]
-    else:
-        (num_ref,), copies = rest, []
-    for copy in copies:
-        copy.start()
+def numerator_kernel(qk_ref, vg_ref, num_ref):
     heads = qk_ref.shape[2]
     length = qk_ref.shape[0] * qk_ref.shape[4]
     tile = min(TILE, length)
@@ -222,8 +219,6 @@
             high, low = split(kernel)
             v = rows_of(vg_ref, 0, head, 0, width)
             num_ref[at:width, head * DH : (head + 1) * DH] = dot(high, v) + dot(low, v)
-    for copy in copies:
-        copy.wait()
 
 
 def normalize_kernel(with_state, qk_ref, vg_ref, num_ref, *rest):
@@ -480,6 +475,15 @@
     def to_members(parts):
         return [part if not shift else to_member(part, shift) for shift, part in enumerate(parts)]
 
+    chips = group // 2
+    chip_at = member // 2
+
+    def to_chip(x, shift):
+        return x if shift == 0 else to_member(x, 2 * shift)
+
+    def to_other_core(x):
+        return lax.ppermute(x, "ctx", [(i, i ^ 1) for i in range(ctx_size)])
+
     def to_run(x, shift, wrap):
         pairs = [
             (i, (i + shift * group) % ctx_size)
@@ -512,7 +516,7 @@
         after=(token,),
     )
     parts = to_members(parts)
-    (vg,), vg_token = call(
+    (vg,), _ = call(
         collect_heads_kernel,
         [((group, 2, tok, heads * DH), bf16)],
         *parts,
@@ -536,8 +540,31 @@
         proj_weight,
         *arrived,
         scalars=(dp_at,),
-        after=(vg_token, token),
-    )
+        after=(token,),
+        after_far=parts[1 : 1 + group // 2],
+    )
+    part_shape = (tok, dp_size * runs * depth)
+    if depth % 128 == 0:
+        (keep, send), _ = call(
+            functools.partial(pack_tokens_kernel, depth),
+            [((chips,) + part_shape, bf16)] * 2,
+            tokens,
+            scalars=(chip_at, ctx_at % 2),
+        )
+    else:
+        blocks = tokens[0].reshape(tok, dp_size * runs, chips, 2, depth).transpose(2, 3, 0, 1, 4)
+        blocks = blocks.reshape(chips, 2, *part_shape)
+        blocks = jnp.stack([blocks[(chip_at + shift) % chips] for shift in range(chips)])
+        keep, send = blocks[:, ctx_at % 2], blocks[:, 1 - ctx_at % 2]
+    token_parts, _ = call(
+        pair_kernel,
+        [((2,) + part_shape, bf16)] * chips,
+        keep,
+        to_other_core(send),
+        scalars=(chip_at, ctx_at % 2),
+        after=(token,),
+    )
+    token_parts = [to_chip(part, shift) for shift, part in enumerate(token_parts)]
     qk_parts = lax.all_to_all(
         projected.reshape((dp_size * group,) + qk_shape[0][1:]),
         ("dp", "ctx"),
@@ -579,23 +606,9 @@
     prefix, suffix = (), ()
     if with_state:
         prefix = [to_run(state[0], shift, False) for shift in range(1, runs)]
-    cols_shape = (group, tok, dp_size * runs * depth)
-    if depth % 128 == 0:
-        (numerator, token_cols), token = call(
-            functools.partial(numerator_kernel, depth),
-            [rows_shape, (cols_shape, bf16)],
-            qk,
-            vg,
-            tokens,
-            copies=(group * dp_size * runs,),
-        )
-    else:
-        (numerator,), token = call(
-            functools.partial(numerator_kernel, 0), [rows_shape], qk, vg
-        )
-        token_cols = tokens[0].reshape(tok, dp_size * runs, group, depth)
-        token_cols = token_cols.transpose(2, 0, 1, 3).reshape(cols_shape)
-    token_cols = exchange(token_cols)
+    (numerator,), token = call(
+        numerator_kernel, [rows_shape], qk, vg, after_far=token_parts[1:]
+    )
     (attended, grad_num, *carried), token = call(
         functools.partial(normalize_kernel, with_state),
         [((length, heads * DH), bf16), rows_shape] + [state_shape] * with_state,
@@ -615,6 +628,13 @@
         *prefix,
         after_far=fetched,
     )
+    (token_cols,), token = call(
+        collect_tokens_kernel,
+        [(part_shape[1:] + (length,), bf16)],
+        *token_parts,
+        scalars=(chip_at,),
+        after=(token,),
+    )
     (rows,), token = call(
         functools.partial(rows_kernel, with_state),
         [((2 * heads * F, length), bf16)],
@@ -622,27 +642,13 @@
         vg,
         grad_qk,
         *suffix,
+        after=(token,),
         far_out=True,
         scratch=[pltpu.VMEM((2 * heads * F, length), bf16)],
         copies=(1,),
     )
-    chips = group // 2
-    chip_at = member // 2
-
-    def to_chip(x, shift):
-        return x if shift == 0 else to_member(x, 2 * shift)
-
-    def to_other_core(x):
-        return lax.ppermute(x, "ctx", [(i, i ^ 1) for i in range(ctx_size)])
-
     rows = [to_chip(rows, shift) for shift in range(chips)]
     rows = [side for part in rows for side in (part, to_other_core(part))]
-    (token_cols,), tokens_token = call(
-        collect_tokens_kernel,
-        [((cols_shape[2], length), bf16)],
-        token_cols,
-        after=(token,),
-    )
     (keep, send), token = call(
         functools.partial(grad_values_kernel, with_state),
         [((chips, 2, tok, heads * DH), bf16)] * 2,
@@ -651,7 +657,7 @@
         grad_v,
         *suffix,
         scalars=(chip_at, ctx_at % 2),
-        after=(token,),
+        after_far=rows[1:2],
         scratch=[pltpu.VMEM((length, heads * DH), bf16)],
     )
     results, token = call(

time: 134 us -> 127 us (0.948)
  the two profiles are of different devices: /device:TPU:4 before, /device:TPU:0 now
where the time goes in v7:
time: 127 us; the launch traced here: 125 us
  starting transfers between devices  44.3 us (35%)
  Pallas kernels  37.9 us (30%)
  waiting for transfers between devices  27.9 us (22%)
  local copies, waits for them, and re-layouts  13.9 us (11%)
    pallas_call x21, Pallas kernels, call(): pl.pallas_call(kernel, out_shape=[jax.ShapeDtypeStruct(shape, kind) for s...  37.9 us
    ppermute x16, waiting for transfers between devices, to_member(): return lax.ppermute(x, 'ctx', pairs)  25.6 us
    ppermute x16, starting transfers between devices, to_member(): return lax.ppermute(x, 'ctx', pairs)  20.2 us
    unnamed x42, local copies, waits for them, and re-layouts  13.8 us
    ppermute x3, starting transfers between devices, to_run(): return lax.ppermute(x, 'ctx', pairs)  9.72 us
    all_to_all x1, starting transfers between devices, local(): lax.all_to_all(projected.reshape((dp_size * group,) + qk_shape[0][1:]), (...  7.99 us
    ppermute x3, starting transfers between devices, to_dp(): lax.ppermute(x, 'dp', [(i, (i + shift) % dp_size) for i in range(dp_size)])  5.2 us
  transfers between devices with their start and end apart: 30, of which 10 were waited for; matrix products, arithmetic and copies ran while one was open for 0% of the time, Pallas kernels for 27%

profile of v7, /device:TPU:0, one launch (start us, length us, event | category | flops | bytes accessed | tf_op | source)
XLA Modules:
  0.0 125.0 jit_solution(67044920558537917)
XLA Ops:
  2.8 3.0 %collective-permute-start = (bf16[128,2048]{1,0:T(8,128)(2,1)}, bf16[128,2048]{1,0:T(8,128)(2,1)S(1)}, u32[]{:S(2)}, u32[]{:S(2)}) collective-permute-start(bf16[128,2048]{1,0:T(8,128)(2,1)} %get-tuple-element.61), channel_id=1, source_target_pairs={{0,16},{16,0},{1,17},{17,1},{2,18},{18,2},{3,19},{19,3},{4,20},{20... | collective-permute-start | bytes 1572872 | tf_op jit(solution)/shard_map/ppermute | solution.py:469
  11.6 1.8 %collective-permute-start.3 = (bf16[2,128,256]{2,1,0:T(8,128)(2,1)}, bf16[2,128,256]{2,1,0:T(8,128)(2,1)S(1)}, u32[]{:S(2)}, u32[]{:S(2)}) collective-permute-start(bf16[2,128,256]{2,1,0:T(8,128)(2,1)} %get-tuple-element.65), channel_id=1, source_target_pairs={{0,3},{1,4},{2,5},{3,6},{4,7},{5,0},{6,1},{7,2},{8,11},{9,12},{10,... | collective-permute-start | bytes 393224 | tf_op jit(solution)/shard_map/ppermute | solution.py:473
  15.7 1.9 %collective-permute-done.2.refs_6_.refs_3_ = bf16[2,128,256]{2,1,0:T(8,128)(2,1)S(1)} collective-permute-done((bf16[2,128,256]{2,1,0:T(8,128)(2,1)}, bf16[2,128,256]{2,1,0:T(8,128)(2,1)S(1)}, u32[]{:S(2)}, u32[]{:S(2)}) %collective-permute-start.2) | collective-permute-done | bytes 131104 | tf_op jit(solution)/shard_map/ppermute | solution.py:473
  24.7 8.0 %all-to-all-start = ((f32[16,2,2,16,128]{4,3,2,1,0:T(8,128)}), f32[16,2,2,16,128]{4,3,2,1,0:T(8,128)}, u32[]{:S(2)}, u32[]{:S(2)}) async-start(f32[16,2,2,16,128]{4,3,2,1,0:T(8,128)} %bitcast.10), calls=%async_computation | async-start | bytes 1048576 | tf_op jit(solution)/shard_map/all_to_all | solution.py:568
  34.4 1.6 %collective-permute-start.5 = (bf16[2,128,256]{2,1,0:T(8,128)(2,1)}, bf16[2,128,256]{2,1,0:T(8,128)(2,1)S(1)}, u32[]{:S(2)}, u32[]{:S(2)}) collective-permute-start(bf16[2,128,256]{2,1,0:T(8,128)(2,1)} %copy-done.20), channel_id=1, source_target_pairs={{0,5},{1,6},{2,7},{3,0},{4,1},{5,2},{6,3},{7,4},{8,13},{9,14},{10,... | collective-permute-start | bytes 393224 | tf_op jit(solution)/shard_map/ppermute | solution.py:473
  42.4 2.9 %collective-permute-start.11 = (bf16[2,128,512]{2,1,0:T(8,128)(2,1)}, bf16[2,128,512]{2,1,0:T(8,128)(2,1)}, u32[]{:S(2)}, u32[]{:S(2)}) collective-permute-start(bf16[2,128,512]{2,1,0:T(8,128)(2,1)} %get-tuple-element.79), channel_id=1, source_target_pairs={{0,6},{1,7},{2,0},{3,1},{4,2},{5,3},{6,4},{7,5},{8,14},{9,15},{10,... | collective-permute-start | bytes 786440 | tf_op jit(solution)/shard_map/ppermute | solution.py:473
  45.3 4.5 %collective-permute-done.6.refs_7_ = bf16[2,128,256]{2,1,0:T(8,128)(2,1)S(1)} collective-permute-done((bf16[2,128,256]{2,1,0:T(8,128)(2,1)}, bf16[2,128,256]{2,1,0:T(8,128)(2,1)S(1)}, u32[]{:S(2)}, u32[]{:S(2)}) %collective-permute-start.6) | collective-permute-done | bytes 131104 | tf_op jit(solution)/shard_map/ppermute | solution.py:473
  51.4 7.5 %collective-permute-done.7.refs_8_ = bf16[2,128,256]{2,1,0:T(8,128)(2,1)S(1)} collective-permute-done((bf16[2,128,256]{2,1,0:T(8,128)(2,1)S(1)}, bf16[2,128,256]{2,1,0:T(8,128)(2,1)S(1)}, u32[]{:S(2)}, u32[]{:S(2)}) %collective-permute-start.7) | collective-permute-done | bytes 131104 | tf_op jit(solution)/shard_map/ppermute | solution.py:473
  63.2 1.6 %shard_map.80 = (f32[8,2,2,16,128]{4,3,2,1,0:T(8,128)S(1)}, bf16[2,176,128]{2,1,0:T(8,128)(2,1)S(1)}, f32[8,128]{1,0:T(8,128)}) custom-call(f32[2,8,2,2,16,128]{5,4,3,2,1,0:T(8,128)} %bitcast.5.refs_0_, bf16[8,2,128,256]{3,2,1,0:T(8,128)(2,1)S(1)} %get-tuple-element.72.refs_1_), custom_call_target="tpu_custom_call" | custom-call | tf_op jit(solution)/shard_map/pallas_call | solution.py:431
  64.9 4.5 %collective-permute-start.12 = (bf16[2,176,128]{2,1,0:T(8,128)(2,1)S(1)}, bf16[2,176,128]{2,1,0:T(8,128)(2,1)S(1)}, u32[]{:S(2)}, u32[]{:S(2)}) collective-permute-start(bf16[2,176,128]{2,1,0:T(8,128)(2,1)S(1)} %get-tuple-element.81), channel_id=1, source_target_pairs={{0,8},{1,9},{2,10},{3,11},{4,12},{5,13},{6,14},{7,15},{16,24},{17,... | collective-permute-start | bytes 270344 | tf_op jit(solution)/shard_map/ppermute | solution.py:493
  69.5 3.6 %shard_map.83 = (f32[1024,256]{1,0:T(8,128)S(1)}, f32[8,128]{1,0:T(8,128)}) custom-call(f32[8,2,2,16,128]{4,3,2,1,0:T(8,128)S(1)} %get-tuple-element.73.refs_0_.refs_1_, bf16[8,2,128,256]{3,2,1,0:T(8,128)(2,1)S(1)} %get-tuple-element.72.refs_1_, bf16[2,128,512]{2,1,0:T(8,128)(2,1)S(1)} %collective-permute-done.9.refs_2_, ...), custom_call_target="tpu_custom_call" | custom-call | tf_op jit(solution)/shard_map/pallas_call | solution.py:431
  73.1 2.6 %shard_map.84 = (bf16[1024,256]{1,0:T(8,128)(2,1)S(1)}, f32[1024,256]{1,0:T(8,128)S(1)}, bf16[2,176,128]{2,1,0:T(8,128)(2,1)S(1)}, f32[8,128]{1,0:T(8,128)}) custom-call(f32[8,2,2,16,128]{4,3,2,1,0:T(8,128)S(1)} %get-tuple-element.73.refs_0_.refs_1_, bf16[8,2,128,256]{3,2,1,0:T(8,128)(2,1)S(1)} %get-tuple-element.72.refs_1_, ...), custom_call_target="tpu_custom_call" | custom-call | tf_op jit(solution)/shard_map/pallas_call | solution.py:431
  77.3 5.9 %shard_map.86 = (f32[2,2,16,1024]{3,2,1,0:T(8,128)S(1)}, f32[2,128,1024]{2,1,0:T(8,128)S(1)}, f32[8,128]{1,0:T(8,128)S(1)}) custom-call(f32[8,2,2,16,128]{4,3,2,1,0:T(8,128)S(1)} %get-tuple-element.73.refs_0_.refs_1_, bf16[8,2,128,256]{3,2,1,0:T(8,128)(2,1)S(1)} %get-tuple-element.72.refs_1_, f32[1024,256]{1,0:T(8,128)S(1)} %get-tuple-element.83.refs_2_, ...), custom_call_target="tpu_custom_call" | custom-call | tf_op jit(solution)/shard_map/pallas_call | solution.py:431
  88.3 1.8 %shard_map.89 = (bf16[4,2,128,256]{3,2,1,0:T(8,128)(2,1)S(1)}, bf16[4,2,128,256]{3,2,1,0:T(8,128)(2,1)S(1)}, f32[8,128]{1,0:T(8,128)}) custom-call(s32[2]{0:T(128)S(1)} %pad_add_fusion.refs_0_, f32[8,2,2,16,128]{4,3,2,1,0:T(8,128)S(1)} %get-tuple-element.73.refs_0_.refs_1_, bf16[1024,256]{1,0:T(8,128)(2,1)S(1)} %get-tuple-element.82.refs_2_, ...), custom_call_target="tpu_custom_call" | custom-call | tf_op jit(solution)/shard_map/pallas_call | solution.py:431
  90.3 2.1 %collective-permute-start.24 = (bf16[64,1024]{1,0:T(8,128)(2,1)S(1)}, bf16[64,1024]{1,0:T(8,128)(2,1)S(1)}, u32[]{:S(2)}, u32[]{:S(2)}) collective-permute-start(bf16[64,1024]{1,0:T(8,128)(2,1)S(1)} %get-tuple-element.91.refs_1_), channel_id=1, source_target_pairs={{0,6},{1,7},{2,0},{3,1},{4,2},{5,3},{6,4},{7,5},{8,14},{9,15},{10,... | collective-permute-start | bytes 393224 | tf_op jit(solution)/shard_map/ppermute | solution.py:473
  92.3 1.9 %collective-permute-start.22 = (bf16[64,1024]{1,0:T(8,128)(2,1)S(1)}, bf16[64,1024]{1,0:T(8,128)(2,1)S(1)}, u32[]{:S(2)}, u32[]{:S(2)}) collective-permute-start(bf16[64,1024]{1,0:T(8,128)(2,1)S(1)} %get-tuple-element.91.refs_1_), channel_id=1, source_target_pairs={{0,4},{1,5},{2,6},{3,7},{4,0},{5,1},{6,2},{7,3},{8,12},{9,13},{10,... | collective-permute-start | bytes 393224 | tf_op jit(solution)/shard_map/ppermute | solution.py:473
  94.3 2.5 %collective-permute-done.24.refs_7_ = bf16[64,1024]{1,0:T(8,128)(2,1)S(1)} collective-permute-done((bf16[64,1024]{1,0:T(8,128)(2,1)S(1)}, bf16[64,1024]{1,0:T(8,128)(2,1)S(1)}, u32[]{:S(2)}, u32[]{:S(2)}) %collective-permute-start.24) | collective-permute-done | bytes 131104 | tf_op jit(solution)/shard_map/ppermute | solution.py:473
  96.8 4.0 %collective-permute-done.22.refs_5_ = bf16[64,1024]{1,0:T(8,128)(2,1)S(1)} collective-permute-done((bf16[64,1024]{1,0:T(8,128)(2,1)S(1)}, bf16[64,1024]{1,0:T(8,128)(2,1)S(1)}, u32[]{:S(2)}, u32[]{:S(2)}) %collective-permute-start.22) | collective-permute-done | bytes 131104 | tf_op jit(solution)/shard_map/ppermute | solution.py:473
  102.9 2.2 %shard_map.91 = (f32[256,512]{1,0:T(8,128)S(1)}, bf16[256,512]{1,0:T(8,128)(2,1)}, f32[8,128]{1,0:T(8,128)S(1)}) custom-call(s32[3]{0:T(128)S(1)} %pad_add_fusion.1.refs_0_, bf16[64,1024]{1,0:T(8,128)(2,1)S(1)} %get-tuple-element.91.refs_1_, bf16[64,1024]{1,0:T(8,128)(2,1)S(1)} %collective-permute-done.15.refs_5_.refs_2_, ...), custom_call_target="tpu_custom_call" | custom-call | tf_op jit(solution)/shard_map/pallas_call | solution.py:431
  108.5 2.0 %collective-permute-start.19 = (bf16[2,2,128,256]{3,2,1,0:T(8,128)(2,1)}, bf16[2,2,128,256]{3,2,1,0:T(8,128)(2,1)}, u32[]{:S(2)}, u32[]{:S(2)}) collective-permute-start(bf16[2,2,128,256]{3,2,1,0:T(8,128)(2,1)} %get-tuple-element.97), channel_id=1, source_target_pairs={{0,6},{1,7},{2,0},{3,1},{4,2},{5,3},{6,4},{7,5},{8,14},{9,15},{10,... | collective-permute-start | bytes 786440 | tf_op jit(solution)/shard_map/ppermute | solution.py:473
  110.6 4.1 %shard_map.92 = (bf16[1,128,4096]{2,1,0:T(8,128)(2,1)}, f32[8,128]{1,0:T(8,128)S(1)}) custom-call(s32[5]{0:T(128)S(1)} %stack.63.refs_0_, bf16[64,1024]{1,0:T(8,128)(2,1)S(1)} %get-tuple-element.91.refs_1_, bf16[64,1024]{1,0:T(8,128)(2,1)S(1)} %collective-permute-done.15.refs_5_.refs_2_, bf16[64,1024]{1,0:T(8,128)(2,1)S(1)} %collective-permute-done.20.refs_3_, ...), custom_call_target="tpu_custom_call" | custom-call | tf_op jit(solution)/shard_map/pallas_call | solution.py:431
  115.8 3.6 %collective-permute-start.28 = (bf16[128,512]{1,0:T(8,128)(2,1)S(1)}, bf16[128,512]{1,0:T(8,128)(2,1)S(1)}, u32[]{:S(2)}, u32[]{:S(2)}) collective-permute-start(bf16[128,512]{1,0:T(8,128)(2,1)S(1)} %get-tuple-element.109), channel_id=1, source_target_pairs={{0,8},{1,9},{2,10},{3,11},{4,12},{5,13},{6,14},{7,15},{8,0},{9,1},... | collective-permute-start | bytes 393224 | tf_op jit(solution)/shard_map/ppermute | solution.py:493
  119.4 2.7 %collective-permute-done.19.refs_4_ = bf16[2,2,128,256]{3,2,1,0:T(8,128)(2,1)} collective-permute-done((bf16[2,2,128,256]{3,2,1,0:T(8,128)(2,1)}, bf16[2,2,128,256]{3,2,1,0:T(8,128)(2,1)}, u32[]{:S(2)}, u32[]{:S(2)}) %collective-permute-start.19) | collective-permute-done | bytes 262176 | tf_op jit(solution)/shard_map/ppermute | solution.py:473
  122.1 2.1 %shard_map.94 = (bf16[1,128,2048]{2,1,0:T(8,128)(2,1)}, bf16[1,128,2048]{2,1,0:T(8,128)(2,1)}, f32[8,128]{1,0:T(8,128)S(1)}) custom-call(s32[1]{0:T(128)} %bitcast.refs_0_, bf16[2,2,128,256]{3,2,1,0:T(8,128)(2,1)S(1)} %get-tuple-element.94.refs_1_, bf16[2,2,128,256]{3,2,1,0:T(8,128)(2,1)} %collective-permute-done.17.refs_2_, ...), custom_call_target="tpu_custom_call" | custom-call | tf_op jit(solution)/shard_map/pallas_call | solution.py:431
  (102 shorter events, 45.4 us)
Async XLA Ops:
  2.8 16.2 %collective-permute-start = (bf16[128,2048]{1,0:T(8,128)(2,1)}, bf16[128,2048]{1,0:T(8,128)(2,1)S(1)}, u32[]{:S(2)}, u32[]{:S(2)}) collective-permute-start(bf16[128,2048]{1,0:T(8,128)(2,1)} %get-tuple-element.61), channel_id=1, source_target_pairs={{0,16},{16,0},{1,17},{17,1},{2,18},{18,2},{3,19},{19,3},{4,20},{20... | collective-permute-start | bytes 1572872 | tf_op jit(solution)/shard_map/ppermute | solution.py:469
  9.5 6.3 %collective-permute-start.1 = (bf16[2,128,256]{2,1,0:T(8,128)(2,1)}, bf16[2,128,256]{2,1,0:T(8,128)(2,1)S(1)}, u32[]{:S(2)}, u32[]{:S(2)}) collective-permute-start(bf16[2,128,256]{2,1,0:T(8,128)(2,1)} %get-tuple-element.63), channel_id=1, source_target_pairs={{0,1},{1,2},{2,3},{3,4},{4,5},{5,6},{6,7},{7,0},{8,9},{9,10},{10,1... | collective-permute-start | bytes 393224 | tf_op jit(solution)/shard_map/ppermute | solution.py:473
  10.1 7.5 %collective-permute-start.2 = (bf16[2,128,256]{2,1,0:T(8,128)(2,1)}, bf16[2,128,256]{2,1,0:T(8,128)(2,1)S(1)}, u32[]{:S(2)}, u32[]{:S(2)}) collective-permute-start(bf16[2,128,256]{2,1,0:T(8,128)(2,1)} %get-tuple-element.64), channel_id=1, source_target_pairs={{0,2},{1,3},{2,4},{3,5},{4,6},{5,7},{6,0},{7,1},{8,10},{9,11},{10,... | collective-permute-start | bytes 393224 | tf_op jit(solution)/shard_map/ppermute | solution.py:473
  23.9 45.4 %collective-permute-start.13 = (bf16[1024,512]{1,0:T(8,128)(2,1)}, bf16[1024,512]{1,0:T(8,128)(2,1)}, u32[]{:S(2)}, u32[]{:S(2)}) collective-permute-start(bf16[1024,512]{1,0:T(8,128)(2,1)} %get-tuple-element.84), channel_id=1, source_target_pairs={{0,16},{16,0},{1,17},{17,1},{2,18},{18,2},{3,19},{19,3},{4,20},{20... | collective-permute-start | bytes 3145736 | tf_op jit(solution)/shard_map/ppermute | solution.py:469
  24.7 38.5 %all-to-all-start = ((f32[16,2,2,16,128]{4,3,2,1,0:T(8,128)}), f32[16,2,2,16,128]{4,3,2,1,0:T(8,128)}, u32[]{:S(2)}, u32[]{:S(2)}) async-start(f32[16,2,2,16,128]{4,3,2,1,0:T(8,128)} %bitcast.10), calls=%async_computation | async-start | bytes 1048576 | tf_op jit(solution)/shard_map/all_to_all | solution.py:568
  34.4 8.0 %collective-permute-start.5 = (bf16[2,128,256]{2,1,0:T(8,128)(2,1)}, bf16[2,128,256]{2,1,0:T(8,128)(2,1)S(1)}, u32[]{:S(2)}, u32[]{:S(2)}) collective-permute-start(bf16[2,128,256]{2,1,0:T(8,128)(2,1)} %copy-done.20), channel_id=1, source_target_pairs={{0,5},{1,6},{2,7},{3,0},{4,1},{5,2},{6,3},{7,4},{8,13},{9,14},{10,... | collective-permute-start | bytes 393224 | tf_op jit(solution)/shard_map/ppermute | solution.py:473
  36.1 13.8 %collective-permute-start.6 = (bf16[2,128,256]{2,1,0:T(8,128)(2,1)}, bf16[2,128,256]{2,1,0:T(8,128)(2,1)S(1)}, u32[]{:S(2)}, u32[]{:S(2)}) collective-permute-start(bf16[2,128,256]{2,1,0:T(8,128)(2,1)} %copy-done.19), channel_id=1, source_target_pairs={{0,6},{1,7},{2,0},{3,1},{4,2},{5,3},{6,4},{7,5},{8,14},{9,15},{10,... | collective-permute-start | bytes 393224 | tf_op jit(solution)/shard_map/ppermute | solution.py:473
  39.7 29.8 %collective-permute-start.9 = (bf16[2,128,512]{2,1,0:T(8,128)(2,1)}, bf16[2,128,512]{2,1,0:T(8,128)(2,1)S(1)}, u32[]{:S(2)}, u32[]{:S(2)}) collective-permute-start(bf16[2,128,512]{2,1,0:T(8,128)(2,1)} %get-tuple-element.77), channel_id=1, source_target_pairs={{0,2},{1,3},{2,4},{3,5},{4,6},{5,7},{6,0},{7,1},{8,10},{9,11},{10,... | collective-permute-start | bytes 786440 | tf_op jit(solution)/shard_map/ppermute | solution.py:473
  40.3 29.2 %collective-permute-start.10 = (bf16[2,128,512]{2,1,0:T(8,128)(2,1)}, bf16[2,128,512]{2,1,0:T(8,128)(2,1)}, u32[]{:S(2)}, u32[]{:S(2)}) collective-permute-start(bf16[2,128,512]{2,1,0:T(8,128)(2,1)} %get-tuple-element.78), channel_id=1, source_target_pairs={{0,4},{1,5},{2,6},{3,7},{4,0},{5,1},{6,2},{7,3},{8,12},{9,13},{10,... | collective-permute-start | bytes 786440 | tf_op jit(solution)/shard_map/ppermute | solution.py:473
  42.4 27.1 %collective-permute-start.11 = (bf16[2,128,512]{2,1,0:T(8,128)(2,1)}, bf16[2,128,512]{2,1,0:T(8,128)(2,1)}, u32[]{:S(2)}, u32[]{:S(2)}) collective-permute-start(bf16[2,128,512]{2,1,0:T(8,128)(2,1)} %get-tuple-element.79), channel_id=1, source_target_pairs={{0,6},{1,7},{2,0},{3,1},{4,2},{5,3},{6,4},{7,5},{8,14},{9,15},{10,... | collective-permute-start | bytes 786440 | tf_op jit(solution)/shard_map/ppermute | solution.py:473
  49.9 9.1 %collective-permute-start.7 = (bf16[2,128,256]{2,1,0:T(8,128)(2,1)S(1)}, bf16[2,128,256]{2,1,0:T(8,128)(2,1)S(1)}, u32[]{:S(2)}, u32[]{:S(2)}) collective-permute-start(bf16[2,128,256]{2,1,0:T(8,128)(2,1)S(1)} %get-tuple-element.71), channel_id=1, source_target_pairs={{0,7},{1,0},{2,1},{3,2},{4,3},{5,4},{6,5},{7,6},{8,15},{9,8},{10,9... | collective-permute-start | bytes 393224 | tf_op jit(solution)/shard_map/ppermute | solution.py:473
  64.9 8.2 %collective-permute-start.12 = (bf16[2,176,128]{2,1,0:T(8,128)(2,1)S(1)}, bf16[2,176,128]{2,1,0:T(8,128)(2,1)S(1)}, u32[]{:S(2)}, u32[]{:S(2)}) collective-permute-start(bf16[2,176,128]{2,1,0:T(8,128)(2,1)S(1)} %get-tuple-element.81), channel_id=1, source_target_pairs={{0,8},{1,9},{2,10},{3,11},{4,12},{5,13},{6,14},{7,15},{16,24},{17,... | collective-permute-start | bytes 270344 | tf_op jit(solution)/shard_map/ppermute | solution.py:493
  69.4 41.2 %collective-permute-start.27 = (bf16[1024,512]{1,0:T(8,128)(2,1)}, bf16[1024,512]{1,0:T(8,128)(2,1)}, u32[]{:S(2)}, u32[]{:S(2)}) collective-permute-start(bf16[1024,512]{1,0:T(8,128)(2,1)} %collective-permute-done.13.refs_4_.refs_10_), channel_id=1, source_target_pairs={{0,1},{1,0},{2,3},{3,2},{4,5},{5,4},{6,7},{7,6},{8,9},{9,8},{10,11... | collective-permute-start | bytes 3145736 | tf_op jit(solution)/shard_map/ppermute | solution.py:597
  75.7 9.8 %collective-permute-start.14 = (bf16[2,176,128]{2,1,0:T(8,128)(2,1)S(1)}, bf16[2,176,128]{2,1,0:T(8,128)(2,1)S(1)}, u32[]{:S(2)}, u32[]{:S(2)}) collective-permute-start(bf16[2,176,128]{2,1,0:T(8,128)(2,1)S(1)} %get-tuple-element.86), channel_id=1, source_target_pairs={{8,0},{9,1},{10,2},{11,3},{12,4},{13,5},{14,6},{15,7},{24,16},{25,... | collective-permute-start | bytes 270344 | tf_op jit(solution)/shard_map/ppermute | solution.py:493
  90.1 11.3 %collective-permute-start.16 = (bf16[4,2,128,256]{3,2,1,0:T(8,128)(2,1)S(1)}, bf16[4,2,128,256]{3,2,1,0:T(8,128)(2,1)S(1)}, u32[]{:S(2)}, u32[]{:S(2)}) collective-permute-start(bf16[4,2,128,256]{3,2,1,0:T(8,128)(2,1)S(1)} %get-tuple-element.93), channel_id=1, source_target_pairs={{0,1},{1,0},{2,3},{3,2},{4,5},{5,4},{6,7},{7,6},{8,9},{9,8},{10,11... | collective-permute-start | bytes 1572872 | tf_op jit(solution)/shard_map/ppermute | solution.py:485
  90.3 6.5 %collective-permute-start.24 = (bf16[64,1024]{1,0:T(8,128)(2,1)S(1)}, bf16[64,1024]{1,0:T(8,128)(2,1)S(1)}, u32[]{:S(2)}, u32[]{:S(2)}) collective-permute-start(bf16[64,1024]{1,0:T(8,128)(2,1)S(1)} %get-tuple-element.91.refs_1_), channel_id=1, source_target_pairs={{0,6},{1,7},{2,0},{3,1},{4,2},{5,3},{6,4},{7,5},{8,14},{9,15},{10,... | collective-permute-start | bytes 393224 | tf_op jit(solution)/shard_map/ppermute | solution.py:473
  92.3 8.5 %collective-permute-start.22 = (bf16[64,1024]{1,0:T(8,128)(2,1)S(1)}, bf16[64,1024]{1,0:T(8,128)(2,1)S(1)}, u32[]{:S(2)}, u32[]{:S(2)}) collective-permute-start(bf16[64,1024]{1,0:T(8,128)(2,1)S(1)} %get-tuple-element.91.refs_1_), channel_id=1, source_target_pairs={{0,4},{1,5},{2,6},{3,7},{4,0},{5,1},{6,2},{7,3},{8,12},{9,13},{10,... | collective-permute-start | bytes 393224 | tf_op jit(solution)/shard_map/ppermute | solution.py:473
  94.3 6.6 %collective-permute-start.20 = (bf16[64,1024]{1,0:T(8,128)(2,1)S(1)}, bf16[64,1024]{1,0:T(8,128)(2,1)S(1)}, u32[]{:S(2)}, u32[]{:S(2)}) collective-permute-start(bf16[64,1024]{1,0:T(8,128)(2,1)S(1)} %get-tuple-element.91.refs_1_), channel_id=1, source_target_pairs={{0,2},{1,3},{2,4},{3,5},{4,6},{5,7},{6,0},{7,1},{8,10},{9,11},{10,... | collective-permute-start | bytes 393224 | tf_op jit(solution)/shard_map/ppermute | solution.py:473
  96.8 6.1 %collective-permute-start.25 = (bf16[64,1024]{1,0:T(8,128)(2,1)S(1)}, bf16[64,1024]{1,0:T(8,128)(2,1)S(1)}, u32[]{:S(2)}, u32[]{:S(2)}) collective-permute-start(bf16[64,1024]{1,0:T(8,128)(2,1)S(1)} %collective-permute-done.24.refs_7_), channel_id=1, source_target_pairs={{0,1},{1,0},{2,3},{3,2},{4,5},{5,4},{6,7},{7,6},{8,9},{9,8},{10,11... | collective-permute-start | bytes 393224 | tf_op jit(solution)/shard_map/ppermute | solution.py:485
  105.9 8.8 %collective-permute-start.26 = (bf16[256,512]{1,0:T(8,128)(2,1)}, bf16[256,512]{1,0:T(8,128)(2,1)}, u32[]{:S(2)}, u32[]{:S(2)}) collective-permute-start(bf16[256,512]{1,0:T(8,128)(2,1)} %get-tuple-element.101), channel_id=1, source_target_pairs={{0,16},{16,0},{1,17},{17,1},{2,18},{18,2},{3,19},{19,3},{4,20},{20... | collective-permute-start | bytes 786440 | tf_op jit(solution)/shard_map/ppermute | solution.py:469
  107.4 12.0 %collective-permute-start.17 = (bf16[2,2,128,256]{3,2,1,0:T(8,128)(2,1)}, bf16[2,2,128,256]{3,2,1,0:T(8,128)(2,1)}, u32[]{:S(2)}, u32[]{:S(2)}) collective-permute-start(bf16[2,2,128,256]{3,2,1,0:T(8,128)(2,1)} %get-tuple-element.95), channel_id=1, source_target_pairs={{0,2},{1,3},{2,4},{3,5},{4,6},{5,7},{6,0},{7,1},{8,10},{9,11},{10,... | collective-permute-start | bytes 786440 | tf_op jit(solution)/shard_map/ppermute | solution.py:473
  108.3 11.1 %collective-permute-start.18 = (bf16[2,2,128,256]{3,2,1,0:T(8,128)(2,1)}, bf16[2,2,128,256]{3,2,1,0:T(8,128)(2,1)}, u32[]{:S(2)}, u32[]{:S(2)}) collective-permute-start(bf16[2,2,128,256]{3,2,1,0:T(8,128)(2,1)} %get-tuple-element.96), channel_id=1, source_target_pairs={{0,4},{1,5},{2,6},{3,7},{4,0},{5,1},{6,2},{7,3},{8,12},{9,13},{10,... | collective-permute-start | bytes 786440 | tf_op jit(solution)/shard_map/ppermute | solution.py:473
  108.5 13.6 %collective-permute-start.19 = (bf16[2,2,128,256]{3,2,1,0:T(8,128)(2,1)}, bf16[2,2,128,256]{3,2,1,0:T(8,128)(2,1)}, u32[]{:S(2)}, u32[]{:S(2)}) collective-permute-start(bf16[2,2,128,256]{3,2,1,0:T(8,128)(2,1)} %get-tuple-element.97), channel_id=1, source_target_pairs={{0,6},{1,7},{2,0},{3,1},{4,2},{5,3},{6,4},{7,5},{8,14},{9,15},{10,... | collective-permute-start | bytes 786440 | tf_op jit(solution)/shard_map/ppermute | solution.py:473
  115.8 8.5 %collective-permute-start.28 = (bf16[128,512]{1,0:T(8,128)(2,1)S(1)}, bf16[128,512]{1,0:T(8,128)(2,1)S(1)}, u32[]{:S(2)}, u32[]{:S(2)}) collective-permute-start(bf16[128,512]{1,0:T(8,128)(2,1)S(1)} %get-tuple-element.109), channel_id=1, source_target_pairs={{0,8},{1,9},{2,10},{3,11},{4,12},{5,13},{6,14},{7,15},{8,0},{9,1},... | collective-permute-start | bytes 393224 | tf_op jit(solution)/shard_map/ppermute | solution.py:493
  (27 other events, 79.4 us)

commit v8 on v7

--- a/solution.py
+++ b/solution.py
@@ -516,7 +516,7 @@
         after=(token,),
     )
     parts = to_members(parts)
-    (vg,), _ = call(
+    (vg,), vg_token = call(
         collect_heads_kernel,
         [((group, 2, tok, heads * DH), bf16)],
         *parts,
@@ -540,8 +540,7 @@
         proj_weight,
         *arrived,
         scalars=(dp_at,),
-        after=(token,),
-        after_far=parts[1 : 1 + group // 2],
+        after=(vg_token, token),
     )
     part_shape = (tok, dp_size * runs * depth)
     if depth % 128 == 0:
@@ -606,9 +605,7 @@
     prefix, suffix = (), ()
     if with_state:
         prefix = [to_run(state[0], shift, False) for shift in range(1, runs)]
-    (numerator,), token = call(
-        numerator_kernel, [rows_shape], qk, vg, after_far=token_parts[1:]
-    )
+    (numerator,), token = call(numerator_kernel, [rows_shape], qk, vg)
     (attended, grad_num, *carried), token = call(
         functools.partial(normalize_kernel, with_state),
         [((length, heads * DH), bf16), rows_shape] + [state_shape] * with_state,
@@ -616,6 +613,7 @@
         vg,
         numerator,
         *prefix,
+        after_far=token_parts[1:],
     )
     if with_state:
         suffix = [to_run(carried[0], -shift, False) for shift in range(1, runs)]
@@ -657,14 +655,15 @@
         grad_v,
         *suffix,
         scalars=(chip_at, ctx_at % 2),
-        after_far=rows[1:2],
+        after_far=rows[2::2],
         scratch=[pltpu.VMEM((length, heads * DH), bf16)],
     )
-    results, token = call(
+    got = to_other_core(send)
+    results, _ = call(
         pair_kernel,
         [((2, 2, tok, heads * DH), bf16)] * chips,
         keep,
-        to_other_core(send),
+        got,
         scalars=(chip_at, ctx_at % 2),
     )
     results = [to_chip(part, shift) for shift, part in enumerate(results)]
@@ -677,9 +676,18 @@
         token_cols,
         scalars=(dp_at, chip_at, ctx_at % 2),
         after=(token,),
+        after_far=(got,),
         scratch=[pltpu.VMEM((dp_size * runs * depth, cols), f32), held],
     )
     parts = [to_dp(part, shift) for shift, part in enumerate(parts, 1)]
+    (grad_proj, *parts), token = call(
+        functools.partial(run_sum_kernel, len(parts)),
+        [((depth, cols), f32)] + [((depth, cols), bf16)] * (runs - 1),
+        own,
+        *parts,
+        scalars=(run_at,),
+        scratch=[pltpu.VMEM((runs * depth, cols), f32)],
+    )
     (grad_tokens,), tokens_token = call(
         functools.partial(grad_tokens_kernel, 2 * chips),
         [((1, tok, width), bf16)],
@@ -689,15 +697,6 @@
         after=(token,),
         scratch=[pltpu.VMEM((cols, tok), bf16)],
     )
-    (grad_proj, *parts), token = call(
-        functools.partial(run_sum_kernel, len(parts)),
-        [((depth, cols), f32)] + [((depth, cols), bf16)] * (runs - 1),
-        own,
-        *parts,
-        scalars=(run_at,),
-        after=(tokens_token,),
-        scratch=[pltpu.VMEM((runs * depth, cols), f32)],
-    )
     (attended, grad_values), token = call(
         unpack_heads_kernel,
         [((1, tok, H * DH), bf16)] * 2,
@@ -710,7 +709,7 @@
         [((depth, cols), f32)],
         grad_proj,
         *[to_run(part, shift, True) for shift, part in enumerate(parts, 1)],
-        after=(token,),
+        after=(token, tokens_token),
     )
     return (attended, grad_tokens, grad_values, grad_proj)
 

time: 127 us -> 120 us (0.945)
  waiting for transfers between devices: 27.9 us -> 21.6 us
  starting transfers between devices: 44.3 us -> 40.7 us
  local copies, waits for them, and re-layouts: 13.9 us -> 16.2 us
    ppermute x16, waiting for transfers between devices: 25.6 us -> 14.5 us  [to_member(): return lax.ppermute(x, 'ctx', pairs)]
    all_to_all x1, starting transfers between devices: 7.99 us -> 4.25 us  [local(): lax.all_to_all(projected.reshape((dp_size * group,) + qk_shape[0][1:]), (...]
    ppermute x6, waiting for transfers between devices: 1.35 us -> 4.12 us  [to_other_core(): return lax.ppermute(x, 'ctx', [(i, i ^ 1) for i in range(ctx_size)])]
    unnamed x42 -> x50, local copies, waits for them, and re-layouts: 13.8 us -> 16.1 us
    ppermute x3, waiting for transfers between devices: 0.01 us -> 2.08 us  [to_dp(): lax.ppermute(x, 'dp', [(i, (i + shift) % dp_size) for i in range(dp_size)])]
  transfers between devices with their start and end apart: 30 -> 30, of which waited for: 10 -> 16; matrix products, arithmetic and copies ran while one was open for 0% -> 0% of each run, Pallas kernels for 27% -> 28%
where the time goes in v8:
time: 120 us; the launch traced here: 118 us
  starting transfers between devices  40.7 us (34%)
  Pallas kernels  38.3 us (32%)
  waiting for transfers between devices  21.6 us (18%)
  local copies, waits for them, and re-layouts  16.2 us (14%)
    pallas_call x21, Pallas kernels, call(): pl.pallas_call(kernel, out_shape=[jax.ShapeDtypeStruct(shape, kind) for s...  38.3 us
    ppermute x16, starting transfers between devices, to_member(): return lax.ppermute(x, 'ctx', pairs)  20.6 us
    unnamed x50, local copies, waits for them, and re-layouts  16.1 us
    ppermute x16, waiting for transfers between devices, to_member(): return lax.ppermute(x, 'ctx', pairs)  14.5 us
    ppermute x3, starting transfers between devices, to_run(): return lax.ppermute(x, 'ctx', pairs)  9.07 us
    ppermute x3, starting transfers between devices, to_dp(): lax.ppermute(x, 'dp', [(i, (i + shift) % dp_size) for i in range(dp_size)])  5.56 us
    all_to_all x1, starting transfers between devices, local(): lax.all_to_all(projected.reshape((dp_size * group,) + qk_shape[0][1:]), (...  4.25 us
    ppermute x6, waiting for transfers between devices, to_other_core(): return lax.ppermute(x, 'ctx', [(i, i ^ 1) for i in range(ctx_size)])  4.12 us
  transfers between devices with their start and end apart: 30, of which 16 were waited for; matrix products, arithmetic and copies ran while one was open for 0% of the time, Pallas kernels for 28%

profile of v8, /device:TPU:0, one launch (start us, length us, event | category | flops | bytes accessed | tf_op | source)
XLA Modules:
  0.0 117.8 jit_solution(1610636562374451911)
XLA Ops:
  2.8 3.0 %collective-permute-start = (bf16[128,2048]{1,0:T(8,128)(2,1)}, bf16[128,2048]{1,0:T(8,128)(2,1)}, u32[]{:S(2)}, u32[]{:S(2)}) collective-permute-start(bf16[128,2048]{1,0:T(8,128)(2,1)} %get-tuple-element.61), channel_id=1, source_target_pairs={{0,16},{16,0},{1,17},{17,1},{2,18},{18,2},{3,19},{19,3},{4,20},{20... | collective-permute-start | bytes 1572872 | tf_op jit(solution)/shard_map/ppermute | solution.py:469
  9.7 2.4 %collective-permute-start.3 = (bf16[2,128,256]{2,1,0:T(8,128)(2,1)S(1)}, bf16[2,128,256]{2,1,0:T(8,128)(2,1)S(1)}, u32[]{:S(2)}, u32[]{:S(2)}) collective-permute-start(bf16[2,128,256]{2,1,0:T(8,128)(2,1)S(1)} %get-tuple-element.65), channel_id=1, source_target_pairs={{0,3},{1,4},{2,5},{3,6},{4,7},{5,0},{6,1},{7,2},{8,11},{9,12},{10,... | collective-permute-start | bytes 393224 | tf_op jit(solution)/shard_map/ppermute | solution.py:473
  12.6 1.7 %collective-permute-done.1.refs_2_ = bf16[2,128,256]{2,1,0:T(8,128)(2,1)S(1)} collective-permute-done((bf16[2,128,256]{2,1,0:T(8,128)(2,1)S(1)}, bf16[2,128,256]{2,1,0:T(8,128)(2,1)S(1)}, u32[]{:S(2)}, u32[]{:S(2)}) %collective-permute-start.1) | collective-permute-done | bytes 131104 | tf_op jit(solution)/shard_map/ppermute | solution.py:473
  15.4 1.6 %collective-permute-start.6 = (bf16[2,128,256]{2,1,0:T(8,128)(2,1)S(1)}, bf16[2,128,256]{2,1,0:T(8,128)(2,1)S(1)}, u32[]{:S(2)}, u32[]{:S(2)}) collective-permute-start(bf16[2,128,256]{2,1,0:T(8,128)(2,1)S(1)} %get-tuple-element.68), channel_id=1, source_target_pairs={{0,6},{1,7},{2,0},{3,1},{4,2},{5,3},{6,4},{7,5},{8,14},{9,15},{10,... | collective-permute-start | bytes 393224 | tf_op jit(solution)/shard_map/ppermute | solution.py:473
  17.0 2.2 %collective-permute-start.7 = (bf16[2,128,256]{2,1,0:T(8,128)(2,1)S(1)}, bf16[2,128,256]{2,1,0:T(8,128)(2,1)S(1)}, u32[]{:S(2)}, u32[]{:S(2)}) collective-permute-start(bf16[2,128,256]{2,1,0:T(8,128)(2,1)S(1)} %get-tuple-element.69), channel_id=1, source_target_pairs={{0,7},{1,0},{2,1},{3,2},{4,3},{5,4},{6,5},{7,6},{8,15},{9,8},{10,9... | collective-permute-start | bytes 393224 | tf_op jit(solution)/shard_map/ppermute | solution.py:473
  25.5 4.3 %all-to-all-start = ((f32[16,2,2,16,128]{4,3,2,1,0:T(8,128)}), f32[16,2,2,16,128]{4,3,2,1,0:T(8,128)}, u32[]{:S(2)}, u32[]{:S(2)}) async-start(f32[16,2,2,16,128]{4,3,2,1,0:T(8,128)} %bitcast.10), calls=%async_computation | async-start | bytes 1048576 | tf_op jit(solution)/shard_map/all_to_all | solution.py:567
  31.4 1.9 %collective-permute-start.13 = (bf16[1024,512]{1,0:T(8,128)(2,1)}, bf16[1024,512]{1,0:T(8,128)(2,1)}, u32[]{:S(2)}, u32[]{:S(2)}) collective-permute-start(bf16[1024,512]{1,0:T(8,128)(2,1)} %get-tuple-element.85), channel_id=1, source_target_pairs={{0,16},{16,0},{1,17},{17,1},{2,18},{18,2},{3,19},{19,3},{4,20},{20... | collective-permute-start | bytes 3145736 | tf_op jit(solution)/shard_map/ppermute | solution.py:469
  35.9 1.9 %collective-permute-done.9.refs_2_ = bf16[4,128,512]{2,1,0:T(8,128)(2,1)S(1)} collective-permute-done((bf16[4,128,512]{2,1,0:T(8,128)(2,1)S(1)}, bf16[4,128,512]{2,1,0:T(8,128)(2,1)S(1)}, u32[]{:S(2)}, u32[]{:S(2)}) %collective-permute-start.9) | collective-permute-done | bytes 524320 | tf_op jit(solution)/shard_map/ppermute | solution.py:485
  44.4 1.6 %shard_map.80 = (f32[8,2,2,16,128]{4,3,2,1,0:T(8,128)S(1)}, bf16[2,176,128]{2,1,0:T(8,128)(2,1)S(1)}, f32[8,128]{1,0:T(8,128)}) custom-call(f32[2,8,2,2,16,128]{5,4,3,2,1,0:T(8,128)} %bitcast.5.refs_0_, bf16[8,2,128,256]{3,2,1,0:T(8,128)(2,1)S(1)} %get-tuple-element.73.refs_1_), custom_call_target="tpu_custom_call" | custom-call | tf_op jit(solution)/shard_map/pallas_call | solution.py:431
  46.1 4.5 %collective-permute-start.8 = (bf16[2,176,128]{2,1,0:T(8,128)(2,1)S(1)}, bf16[2,176,128]{2,1,0:T(8,128)(2,1)S(1)}, u32[]{:S(2)}, u32[]{:S(2)}) collective-permute-start(bf16[2,176,128]{2,1,0:T(8,128)(2,1)S(1)} %get-tuple-element.76), channel_id=1, source_target_pairs={{0,8},{1,9},{2,10},{3,11},{4,12},{5,13},{6,14},{7,15},{16,24},{17,... | collective-permute-start | bytes 270344 | tf_op jit(solution)/shard_map/ppermute | solution.py:493
  50.5 3.6 %shard_map.81 = (f32[1024,256]{1,0:T(8,128)S(1)}, f32[8,128]{1,0:T(8,128)}) custom-call(f32[8,2,2,16,128]{4,3,2,1,0:T(8,128)S(1)} %get-tuple-element.74.refs_0_.refs_1_, bf16[8,2,128,256]{3,2,1,0:T(8,128)(2,1)S(1)} %get-tuple-element.73.refs_1_), custom_call_target="tpu_custom_call" | custom-call | tf_op jit(solution)/shard_map/pallas_call | solution.py:431
  56.3 2.6 %shard_map.84 = (bf16[1024,256]{1,0:T(8,128)(2,1)S(1)}, f32[1024,256]{1,0:T(8,128)S(1)}, bf16[2,176,128]{2,1,0:T(8,128)(2,1)S(1)}, f32[8,128]{1,0:T(8,128)}) custom-call(f32[8,2,2,16,128]{4,3,2,1,0:T(8,128)S(1)} %get-tuple-element.74.refs_0_.refs_1_, bf16[8,2,128,256]{3,2,1,0:T(8,128)(2,1)S(1)} %get-tuple-element.73.refs_1_, ...), custom_call_target="tpu_custom_call" | custom-call | tf_op jit(solution)/shard_map/pallas_call | solution.py:431
  61.0 5.9 %shard_map.86 = (f32[2,2,16,1024]{3,2,1,0:T(8,128)S(1)}, f32[2,128,1024]{2,1,0:T(8,128)S(1)}, f32[8,128]{1,0:T(8,128)S(1)}) custom-call(f32[8,2,2,16,128]{4,3,2,1,0:T(8,128)S(1)} %get-tuple-element.74.refs_0_.refs_1_, bf16[8,2,128,256]{3,2,1,0:T(8,128)(2,1)S(1)} %get-tuple-element.73.refs_1_, f32[1024,256]{1,0:T(8,128)S(1)} %get-tuple-element.84.refs_2_, ...), custom_call_target="tpu_custom_call" | custom-call | tf_op jit(solution)/shard_map/pallas_call | solution.py:431
  69.8 2.4 %collective-permute-start.17 = (bf16[64,1024]{1,0:T(8,128)(2,1)S(1)}, bf16[64,1024]{1,0:T(8,128)(2,1)S(1)}, u32[]{:S(2)}, u32[]{:S(2)}) collective-permute-start(bf16[64,1024]{1,0:T(8,128)(2,1)S(1)} %get-tuple-element.92.refs_1_), channel_id=1, source_target_pairs={{0,6},{1,7},{2,0},{3,1},{4,2},{5,3},{6,4},{7,5},{8,14},{9,15},{10,... | collective-permute-start | bytes 393224 | tf_op jit(solution)/shard_map/ppermute | solution.py:473
  73.3 2.8 %collective-permute-done.17.refs_7_ = bf16[64,1024]{1,0:T(8,128)(2,1)S(1)} collective-permute-done((bf16[64,1024]{1,0:T(8,128)(2,1)S(1)}, bf16[64,1024]{1,0:T(8,128)(2,1)S(1)}, u32[]{:S(2)}, u32[]{:S(2)}) %collective-permute-start.17) | collective-permute-done | bytes 131104 | tf_op jit(solution)/shard_map/ppermute | solution.py:473
  76.1 2.5 %collective-permute-done.16.refs_6_.refs_5_ = bf16[64,1024]{1,0:T(8,128)(2,1)S(1)} collective-permute-done((bf16[64,1024]{1,0:T(8,128)(2,1)S(1)}, bf16[64,1024]{1,0:T(8,128)(2,1)S(1)}, u32[]{:S(2)}, u32[]{:S(2)}) %collective-permute-start.16) | collective-permute-done | bytes 131104 | tf_op jit(solution)/shard_map/ppermute | solution.py:473
  83.9 2.2 %shard_map.91 = (f32[256,512]{1,0:T(8,128)S(1)}, bf16[256,512]{1,0:T(8,128)(2,1)}, f32[8,128]{1,0:T(8,128)}) custom-call(s32[3]{0:T(128)S(1)} %pad_add_fusion.1.refs_0_, bf16[64,1024]{1,0:T(8,128)(2,1)S(1)} %get-tuple-element.92.refs_1_, bf16[64,1024]{1,0:T(8,128)(2,1)S(1)} %collective-permute-done.22.refs_2_, ...), custom_call_target="tpu_custom_call" | custom-call | tf_op jit(solution)/shard_map/pallas_call | solution.py:431
  92.1 1.9 %collective-permute-start.21 = (bf16[2,2,128,256]{3,2,1,0:T(8,128)(2,1)}, bf16[2,2,128,256]{3,2,1,0:T(8,128)(2,1)}, u32[]{:S(2)}, u32[]{:S(2)}) collective-permute-start(bf16[2,2,128,256]{3,2,1,0:T(8,128)(2,1)} %get-tuple-element.98), channel_id=1, source_target_pairs={{0,6},{1,7},{2,0},{3,1},{4,2},{5,3},{6,4},{7,5},{8,14},{9,15},{10,... | collective-permute-start | bytes 786440 | tf_op jit(solution)/shard_map/ppermute | solution.py:473
  96.6 1.7 %shard_map.92 = (f32[128,512]{1,0:T(8,128)S(1)}, bf16[128,512]{1,0:T(8,128)(2,1)}, f32[8,128]{1,0:T(8,128)S(1)}) custom-call(s32[1]{0:T(128)} %bitcast.6.refs_0_, f32[256,512]{1,0:T(8,128)S(1)} %copy-done.16, bf16[256,512]{1,0:T(8,128)(2,1)} %collective-permute-done.26.refs_2_), custom_call_target="tpu_custom_call" | custom-call | tf_op jit(solution)/shard_map/pallas_call | solution.py:431
  99.0 3.0 %collective-permute-start.28 = (bf16[128,512]{1,0:T(8,128)(2,1)}, bf16[128,512]{1,0:T(8,128)(2,1)}, u32[]{:S(2)}, u32[]{:S(2)}) collective-permute-start(bf16[128,512]{1,0:T(8,128)(2,1)} %get-tuple-element.108), channel_id=1, source_target_pairs={{0,8},{1,9},{2,10},{3,11},{4,12},{5,13},{6,14},{7,15},{8,0},{9,1},... | collective-permute-start | bytes 393224 | tf_op jit(solution)/shard_map/ppermute | solution.py:493
  102.1 2.7 %collective-permute-done.21.refs_4_ = bf16[2,2,128,256]{3,2,1,0:T(8,128)(2,1)} collective-permute-done((bf16[2,2,128,256]{3,2,1,0:T(8,128)(2,1)}, bf16[2,2,128,256]{3,2,1,0:T(8,128)(2,1)}, u32[]{:S(2)}, u32[]{:S(2)}) %collective-permute-start.21) | collective-permute-done | bytes 262176 | tf_op jit(solution)/shard_map/ppermute | solution.py:473
  105.7 2.1 %shard_map.93 = (bf16[1,128,2048]{2,1,0:T(8,128)(2,1)}, bf16[1,128,2048]{2,1,0:T(8,128)(2,1)}, f32[8,128]{1,0:T(8,128)S(1)}) custom-call(s32[1]{0:T(128)} %bitcast.refs_0_, bf16[2,2,128,256]{3,2,1,0:T(8,128)(2,1)S(1)} %copy-done.22, bf16[2,2,128,256]{3,2,1,0:T(8,128)(2,1)} %collective-permute-done.19.refs_2_, ...), custom_call_target="tpu_custom_call" | custom-call | tf_op jit(solution)/shard_map/pallas_call | solution.py:431
  112.4 3.8 %shard_map.94 = (bf16[1,128,4096]{2,1,0:T(8,128)(2,1)}, f32[8,128]{1,0:T(8,128)S(1)}) custom-call(s32[5]{0:T(128)S(1)} %stack.63.refs_0_, bf16[64,1024]{1,0:T(8,128)(2,1)S(1)} %copy-done.5, bf16[64,1024]{1,0:T(8,128)(2,1)S(1)} %copy-done.7, bf16[64,1024]{1,0:T(8,128)(2,1)S(1)} %collective-permute-done.15.refs_5_.refs_3_, bf16[64,1024]{1,0:T(8,128)(2,1)S(1)} %copy-done.13, ...), custom_call_target="tpu_custom_call" | custom-call | tf_op jit(solution)/shard_map/pallas_call | solution.py:431
  116.2 1.6 %shard_map.95 = (f32[128,512]{1,0:T(8,128)}, f32[8,128]{1,0:T(8,128)}) custom-call(f32[128,512]{1,0:T(8,128)S(1)} %copy-done.20, bf16[128,512]{1,0:T(8,128)(2,1)} %collective-permute-done.28.refs_1_, f32[8,128]{1,0:T(8,128)S(1)} %get-tuple-element.109.refs_2_, f32[8,128]{1,0:T(8,128)S(1)} %get-tuple-element.110.refs_3_), custom_call_target="tpu_custom_call" | custom-call | tf_op jit(solution)/shard_map/pallas_call | solution.py:431
  (110 shorter events, 53.0 us)
Async XLA Ops:
  2.8 20.3 %collective-permute-start = (bf16[128,2048]{1,0:T(8,128)(2,1)}, bf16[128,2048]{1,0:T(8,128)(2,1)}, u32[]{:S(2)}, u32[]{:S(2)}) collective-permute-start(bf16[128,2048]{1,0:T(8,128)(2,1)} %get-tuple-element.61), channel_id=1, source_target_pairs={{0,16},{16,0},{1,17},{17,1},{2,18},{18,2},{3,19},{19,3},{4,20},{20... | collective-permute-start | bytes 1572872 | tf_op jit(solution)/shard_map/ppermute | solution.py:469
  8.1 6.2 %collective-permute-start.1 = (bf16[2,128,256]{2,1,0:T(8,128)(2,1)S(1)}, bf16[2,128,256]{2,1,0:T(8,128)(2,1)S(1)}, u32[]{:S(2)}, u32[]{:S(2)}) collective-permute-start(bf16[2,128,256]{2,1,0:T(8,128)(2,1)S(1)} %get-tuple-element.63), channel_id=1, source_target_pairs={{0,1},{1,2},{2,3},{3,4},{4,5},{5,6},{6,7},{7,0},{8,9},{9,10},{10,1... | collective-permute-start | bytes 393224 | tf_op jit(solution)/shard_map/ppermute | solution.py:473
  8.1 7.3 %collective-permute-start.2 = (bf16[2,128,256]{2,1,0:T(8,128)(2,1)S(1)}, bf16[2,128,256]{2,1,0:T(8,128)(2,1)S(1)}, u32[]{:S(2)}, u32[]{:S(2)}) collective-permute-start(bf16[2,128,256]{2,1,0:T(8,128)(2,1)S(1)} %get-tuple-element.64), channel_id=1, source_target_pairs={{0,2},{1,3},{2,4},{3,5},{4,6},{5,7},{6,0},{7,1},{8,10},{9,11},{10,... | collective-permute-start | bytes 393224 | tf_op jit(solution)/shard_map/ppermute | solution.py:473
  9.7 7.3 %collective-permute-start.3 = (bf16[2,128,256]{2,1,0:T(8,128)(2,1)S(1)}, bf16[2,128,256]{2,1,0:T(8,128)(2,1)S(1)}, u32[]{:S(2)}, u32[]{:S(2)}) collective-permute-start(bf16[2,128,256]{2,1,0:T(8,128)(2,1)S(1)} %get-tuple-element.65), channel_id=1, source_target_pairs={{0,3},{1,4},{2,5},{3,6},{4,7},{5,0},{6,1},{7,2},{8,11},{9,12},{10,... | collective-permute-start | bytes 393224 | tf_op jit(solution)/shard_map/ppermute | solution.py:473
  12.1 8.9 %collective-permute-start.4 = (bf16[2,128,256]{2,1,0:T(8,128)(2,1)S(1)}, bf16[2,128,256]{2,1,0:T(8,128)(2,1)S(1)}, u32[]{:S(2)}, u32[]{:S(2)}) collective-permute-start(bf16[2,128,256]{2,1,0:T(8,128)(2,1)S(1)} %get-tuple-element.66), channel_id=1, source_target_pairs={{0,4},{1,5},{2,6},{3,7},{4,0},{5,1},{6,2},{7,3},{8,12},{9,13},{10,... | collective-permute-start | bytes 393224 | tf_op jit(solution)/shard_map/ppermute | solution.py:473
  14.2 6.8 %collective-permute-start.5 = (bf16[2,128,256]{2,1,0:T(8,128)(2,1)S(1)}, bf16[2,128,256]{2,1,0:T(8,128)(2,1)S(1)}, u32[]{:S(2)}, u32[]{:S(2)}) collective-permute-start(bf16[2,128,256]{2,1,0:T(8,128)(2,1)S(1)} %get-tuple-element.67), channel_id=1, source_target_pairs={{0,5},{1,6},{2,7},{3,0},{4,1},{5,2},{6,3},{7,4},{8,13},{9,14},{10,... | collective-permute-start | bytes 393224 | tf_op jit(solution)/shard_map/ppermute | solution.py:473
  15.4 6.2 %collective-permute-start.6 = (bf16[2,128,256]{2,1,0:T(8,128)(2,1)S(1)}, bf16[2,128,256]{2,1,0:T(8,128)(2,1)S(1)}, u32[]{:S(2)}, u32[]{:S(2)}) collective-permute-start(bf16[2,128,256]{2,1,0:T(8,128)(2,1)S(1)} %get-tuple-element.68), channel_id=1, source_target_pairs={{0,6},{1,7},{2,0},{3,1},{4,2},{5,3},{6,4},{7,5},{8,14},{9,15},{10,... | collective-permute-start | bytes 393224 | tf_op jit(solution)/shard_map/ppermute | solution.py:473
  17.0 6.0 %collective-permute-start.7 = (bf16[2,128,256]{2,1,0:T(8,128)(2,1)S(1)}, bf16[2,128,256]{2,1,0:T(8,128)(2,1)S(1)}, u32[]{:S(2)}, u32[]{:S(2)}) collective-permute-start(bf16[2,128,256]{2,1,0:T(8,128)(2,1)S(1)} %get-tuple-element.69), channel_id=1, source_target_pairs={{0,7},{1,0},{2,1},{3,2},{4,3},{5,4},{6,5},{7,6},{8,15},{9,8},{10,9... | collective-permute-start | bytes 393224 | tf_op jit(solution)/shard_map/ppermute | solution.py:473
  25.5 18.9 %all-to-all-start = ((f32[16,2,2,16,128]{4,3,2,1,0:T(8,128)}), f32[16,2,2,16,128]{4,3,2,1,0:T(8,128)}, u32[]{:S(2)}, u32[]{:S(2)}) async-start(f32[16,2,2,16,128]{4,3,2,1,0:T(8,128)} %bitcast.10), calls=%async_computation | async-start | bytes 1048576 | tf_op jit(solution)/shard_map/all_to_all | solution.py:567
  31.4 29.7 %collective-permute-start.13 = (bf16[1024,512]{1,0:T(8,128)(2,1)}, bf16[1024,512]{1,0:T(8,128)(2,1)}, u32[]{:S(2)}, u32[]{:S(2)}) collective-permute-start(bf16[1024,512]{1,0:T(8,128)(2,1)} %get-tuple-element.85), channel_id=1, source_target_pairs={{0,16},{16,0},{1,17},{17,1},{2,18},{18,2},{3,19},{19,3},{4,20},{20... | collective-permute-start | bytes 3145736 | tf_op jit(solution)/shard_map/ppermute | solution.py:469
  40.0 14.2 %collective-permute-start.10 = (bf16[2,128,512]{2,1,0:T(8,128)(2,1)}, bf16[2,128,512]{2,1,0:T(8,128)(2,1)S(1)}, u32[]{:S(2)}, u32[]{:S(2)}) collective-permute-start(bf16[2,128,512]{2,1,0:T(8,128)(2,1)} %get-tuple-element.80), channel_id=1, source_target_pairs={{0,2},{1,3},{2,4},{3,5},{4,6},{5,7},{6,0},{7,1},{8,10},{9,11},{10,... | collective-permute-start | bytes 786440 | tf_op jit(solution)/shard_map/ppermute | solution.py:473
  41.5 12.7 %collective-permute-start.11 = (bf16[2,128,512]{2,1,0:T(8,128)(2,1)}, bf16[2,128,512]{2,1,0:T(8,128)(2,1)}, u32[]{:S(2)}, u32[]{:S(2)}) collective-permute-start(bf16[2,128,512]{2,1,0:T(8,128)(2,1)} %get-tuple-element.81), channel_id=1, source_target_pairs={{0,4},{1,5},{2,6},{3,7},{4,0},{5,1},{6,2},{7,3},{8,12},{9,13},{10,... | collective-permute-start | bytes 786440 | tf_op jit(solution)/shard_map/ppermute | solution.py:473
  42.9 12.5 %collective-permute-start.12 = (bf16[2,128,512]{2,1,0:T(8,128)(2,1)}, bf16[2,128,512]{2,1,0:T(8,128)(2,1)}, u32[]{:S(2)}, u32[]{:S(2)}) collective-permute-start(bf16[2,128,512]{2,1,0:T(8,128)(2,1)} %get-tuple-element.82), channel_id=1, source_target_pairs={{0,6},{1,7},{2,0},{3,1},{4,2},{5,3},{6,4},{7,5},{8,14},{9,15},{10,... | collective-permute-start | bytes 786440 | tf_op jit(solution)/shard_map/ppermute | solution.py:473
  46.1 10.2 %collective-permute-start.8 = (bf16[2,176,128]{2,1,0:T(8,128)(2,1)S(1)}, bf16[2,176,128]{2,1,0:T(8,128)(2,1)S(1)}, u32[]{:S(2)}, u32[]{:S(2)}) collective-permute-start(bf16[2,176,128]{2,1,0:T(8,128)(2,1)S(1)} %get-tuple-element.76), channel_id=1, source_target_pairs={{0,8},{1,9},{2,10},{3,11},{4,12},{5,13},{6,14},{7,15},{16,24},{17,... | collective-permute-start | bytes 270344 | tf_op jit(solution)/shard_map/ppermute | solution.py:493
  58.9 9.5 %collective-permute-start.14 = (bf16[2,176,128]{2,1,0:T(8,128)(2,1)S(1)}, bf16[2,176,128]{2,1,0:T(8,128)(2,1)S(1)}, u32[]{:S(2)}, u32[]{:S(2)}) collective-permute-start(bf16[2,176,128]{2,1,0:T(8,128)(2,1)S(1)} %get-tuple-element.87), channel_id=1, source_target_pairs={{8,0},{9,1},{10,2},{11,3},{12,4},{13,5},{14,6},{15,7},{24,16},{25,... | collective-permute-start | bytes 270344 | tf_op jit(solution)/shard_map/ppermute | solution.py:493
  69.8 6.3 %collective-permute-start.17 = (bf16[64,1024]{1,0:T(8,128)(2,1)S(1)}, bf16[64,1024]{1,0:T(8,128)(2,1)S(1)}, u32[]{:S(2)}, u32[]{:S(2)}) collective-permute-start(bf16[64,1024]{1,0:T(8,128)(2,1)S(1)} %get-tuple-element.92.refs_1_), channel_id=1, source_target_pairs={{0,6},{1,7},{2,0},{3,1},{4,2},{5,3},{6,4},{7,5},{8,14},{9,15},{10,... | collective-permute-start | bytes 393224 | tf_op jit(solution)/shard_map/ppermute | solution.py:473
  72.2 6.4 %collective-permute-start.16 = (bf16[64,1024]{1,0:T(8,128)(2,1)S(1)}, bf16[64,1024]{1,0:T(8,128)(2,1)S(1)}, u32[]{:S(2)}, u32[]{:S(2)}) collective-permute-start(bf16[64,1024]{1,0:T(8,128)(2,1)S(1)} %get-tuple-element.92.refs_1_), channel_id=1, source_target_pairs={{0,4},{1,5},{2,6},{3,7},{4,0},{5,1},{6,2},{7,3},{8,12},{9,13},{10,... | collective-permute-start | bytes 393224 | tf_op jit(solution)/shard_map/ppermute | solution.py:473
  72.7 6.3 %collective-permute-start.15 = (bf16[64,1024]{1,0:T(8,128)(2,1)S(1)}, bf16[64,1024]{1,0:T(8,128)(2,1)S(1)}, u32[]{:S(2)}, u32[]{:S(2)}) collective-permute-start(bf16[64,1024]{1,0:T(8,128)(2,1)S(1)} %get-tuple-element.92.refs_1_), channel_id=1, source_target_pairs={{0,2},{1,3},{2,4},{3,5},{4,6},{5,7},{6,0},{7,1},{8,10},{9,11},{10,... | collective-permute-start | bytes 393224 | tf_op jit(solution)/shard_map/ppermute | solution.py:473
  73.3 34.6 %collective-permute-start.27 = (bf16[1024,512]{1,0:T(8,128)(2,1)}, bf16[1024,512]{1,0:T(8,128)(2,1)S(1)}, u32[]{:S(2)}, u32[]{:S(2)}) collective-permute-start(bf16[1024,512]{1,0:T(8,128)(2,1)} %collective-permute-done.13.refs_4_.refs_10_), channel_id=1, source_target_pairs={{0,1},{1,0},{2,3},{3,2},{4,5},{5,4},{6,7},{7,6},{8,9},{9,8},{10,11... | collective-permute-start | bytes 3145736 | tf_op jit(solution)/shard_map/ppermute | solution.py:596
  86.9 8.7 %collective-permute-start.26 = (bf16[256,512]{1,0:T(8,128)(2,1)}, bf16[256,512]{1,0:T(8,128)(2,1)}, u32[]{:S(2)}, u32[]{:S(2)}) collective-permute-start(bf16[256,512]{1,0:T(8,128)(2,1)} %get-tuple-element.102), channel_id=1, source_target_pairs={{0,16},{16,0},{1,17},{17,1},{2,18},{18,2},{3,19},{19,3},{4,20},{20... | collective-permute-start | bytes 786440 | tf_op jit(solution)/shard_map/ppermute | solution.py:469
  89.7 12.3 %collective-permute-start.19 = (bf16[2,2,128,256]{3,2,1,0:T(8,128)(2,1)}, bf16[2,2,128,256]{3,2,1,0:T(8,128)(2,1)}, u32[]{:S(2)}, u32[]{:S(2)}) collective-permute-start(bf16[2,2,128,256]{3,2,1,0:T(8,128)(2,1)} %get-tuple-element.96), channel_id=1, source_target_pairs={{0,2},{1,3},{2,4},{3,5},{4,6},{5,7},{6,0},{7,1},{8,10},{9,11},{10,... | collective-permute-start | bytes 786440 | tf_op jit(solution)/shard_map/ppermute | solution.py:473
  91.1 11.0 %collective-permute-start.20 = (bf16[2,2,128,256]{3,2,1,0:T(8,128)(2,1)}, bf16[2,2,128,256]{3,2,1,0:T(8,128)(2,1)}, u32[]{:S(2)}, u32[]{:S(2)}) collective-permute-start(bf16[2,2,128,256]{3,2,1,0:T(8,128)(2,1)} %get-tuple-element.97), channel_id=1, source_target_pairs={{0,4},{1,5},{2,6},{3,7},{4,0},{5,1},{6,2},{7,3},{8,12},{9,13},{10,... | collective-permute-start | bytes 786440 | tf_op jit(solution)/shard_map/ppermute | solution.py:473
  92.1 12.7 %collective-permute-start.21 = (bf16[2,2,128,256]{3,2,1,0:T(8,128)(2,1)}, bf16[2,2,128,256]{3,2,1,0:T(8,128)(2,1)}, u32[]{:S(2)}, u32[]{:S(2)}) collective-permute-start(bf16[2,2,128,256]{3,2,1,0:T(8,128)(2,1)} %get-tuple-element.98), channel_id=1, source_target_pairs={{0,6},{1,7},{2,0},{3,1},{4,2},{5,3},{6,4},{7,5},{8,14},{9,15},{10,... | collective-permute-start | bytes 786440 | tf_op jit(solution)/shard_map/ppermute | solution.py:473
  99.0 17.2 %collective-permute-start.28 = (bf16[128,512]{1,0:T(8,128)(2,1)}, bf16[128,512]{1,0:T(8,128)(2,1)}, u32[]{:S(2)}, u32[]{:S(2)}) collective-permute-start(bf16[128,512]{1,0:T(8,128)(2,1)} %get-tuple-element.108), channel_id=1, source_target_pairs={{0,8},{1,9},{2,10},{3,11},{4,12},{5,13},{6,14},{7,15},{8,0},{9,1},... | collective-permute-start | bytes 393224 | tf_op jit(solution)/shard_map/ppermute | solution.py:493
  (31 other events, 96.5 us)

commit v9 on v7

--- a/solution.py
+++ b/solution.py
@@ -117,19 +117,23 @@
     )
 
 
-def pack_heads_kernel(at_ref, values_ref, grad_ref, *out_refs):
-    width = out_refs[0].shape[2]
-    for shift, out_ref in enumerate(out_refs):
-        cols = aligned(lax.rem(at_ref[0] + shift, len(out_refs)), width)
-        out_ref[0] = values_ref[0, :, cols]
-        out_ref[1] = grad_ref[0, :, cols]
+def pack_heads_kernel(at_ref, values_ref, grad_ref, keep_ref, send_ref):
+    chips, width = keep_ref.shape[0], keep_ref.shape[3]
+    for shift in range(chips):
+        chip = lax.rem(at_ref[0] + shift, chips)
+        for core, out_ref in ((at_ref[1], keep_ref), (1 - at_ref[1], send_ref)):
+            cols = aligned(2 * chip + core, width)
+            out_ref[shift, 0] = values_ref[0, :, cols]
+            out_ref[shift, 1] = grad_ref[0, :, cols]
 
 
 def collect_heads_kernel(at_ref, *rest):
     *part_refs, out_ref = rest
-    group = len(part_refs)
+    chips = len(part_refs)
     for shift, part_ref in enumerate(part_refs):
-        out_ref[lax.rem(at_ref[0] + group - shift, group)] = part_ref[...]
+        chip = lax.rem(at_ref[0] + chips - shift, chips)
+        for core in range(2):
+            out_ref[2 * chip + core] = part_ref[core]
 
 
 def pack_tokens_kernel(depth, at_ref, tokens_ref, keep_ref, send_ref):
@@ -472,9 +476,6 @@
         pairs = [(i, i - i % group + (i + shift) % group) for i in range(ctx_size)]
         return lax.ppermute(x, "ctx", pairs)
 
-    def to_members(parts):
-        return [part if not shift else to_member(part, shift) for shift, part in enumerate(parts)]
-
     chips = group // 2
     chip_at = member // 2
 
@@ -507,20 +508,26 @@
         copies=(dp_size - 1,),
     )
     arrived = [to_dp(part, shift) for shift, part in enumerate(parts, 1)]
-    parts, token = call(
+    (keep, send), token = call(
         pack_heads_kernel,
-        [((2, tok, heads * DH), bf16)] * group,
+        [((chips, 2, tok, heads * DH), bf16)] * 2,
         values,
         grad_out,
-        scalars=(member,),
-        after=(token,),
-    )
-    parts = to_members(parts)
+        scalars=(chip_at, ctx_at % 2),
+        after=(token,),
+    )
+    parts, heads_token = call(
+        pair_kernel,
+        [((2, 2, tok, heads * DH), bf16)] * chips,
+        keep,
+        to_other_core(send),
+        scalars=(chip_at, ctx_at % 2),
+    )
     (vg,), _ = call(
         collect_heads_kernel,
         [((group, 2, tok, heads * DH), bf16)],
-        *parts,
-        scalars=(member,),
+        *[to_chip(part, shift) for shift, part in enumerate(parts)],
+        scalars=(chip_at,),
     )
     (projected,), token = call(
         project_kernel,
@@ -540,8 +547,7 @@
         proj_weight,
         *arrived,
         scalars=(dp_at,),
-        after=(token,),
-        after_far=parts[1 : 1 + group // 2],
+        after=(heads_token, token),
     )
     part_shape = (tok, dp_size * runs * depth)
     if depth % 128 == 0:
@@ -606,9 +612,7 @@
     prefix, suffix = (), ()
     if with_state:
         prefix = [to_run(state[0], shift, False) for shift in range(1, runs)]
-    (numerator,), token = call(
-        numerator_kernel, [rows_shape], qk, vg, after_far=token_parts[1:]
-    )
+    (numerator,), token = call(numerator_kernel, [rows_shape], qk, vg)
     (attended, grad_num, *carried), token = call(
         functools.partial(normalize_kernel, with_state),
         [((length, heads * DH), bf16), rows_shape] + [state_shape] * with_state,
@@ -616,6 +620,7 @@
         vg,
         numerator,
         *prefix,
+        after_far=token_parts[1:],
     )
     if with_state:
         suffix = [to_run(carried[0], -shift, False) for shift in range(1, runs)]
@@ -657,14 +662,15 @@
         grad_v,
         *suffix,
         scalars=(chip_at, ctx_at % 2),
-        after_far=rows[1:2],
+        after_far=rows[4::2],
         scratch=[pltpu.VMEM((length, heads * DH), bf16)],
     )
+    got = to_other_core(send)
     results, token = call(
         pair_kernel,
         [((2, 2, tok, heads * DH), bf16)] * chips,
         keep,
-        to_other_core(send),
+        got,
         scalars=(chip_at, ctx_at % 2),
     )
     results = [to_chip(part, shift) for shift, part in enumerate(results)]

time: 127 us -> 120 us (0.945); the launches traced: 125 us -> 120 us
  starting transfers between devices: 44.3 us -> 39.8 us
  local copies, waits for them, and re-layouts: 13.9 us -> 12.3 us
    ppermute x3, waiting for transfers between devices: 0.01 us -> 10 us  [to_dp(): lax.ppermute(x, 'dp', [(i, (i + shift) % dp_size) for i in range(dp_size)])]
    ppermute x16 -> x12, waiting for transfers between devices: 25.6 us -> 15.6 us  [to_member(): return lax.ppermute(x, 'ctx', pairs)]
    ppermute x16 -> x12, starting transfers between devices: 20.2 us -> 16.9 us  [to_member(): return lax.ppermute(x, 'ctx', pairs)]
    all_to_all x1, starting transfers between devices: 7.99 us -> 5.3 us  [local(): lax.all_to_all(projected.reshape((dp_size * group,) + qk_shape[0][1:]), (...]
    ppermute x3, waiting for transfers between devices: 0.89 us -> 3.46 us  [to_run(): return lax.ppermute(x, 'ctx', pairs)]
    unnamed x42 -> x62, local copies, waits for them, and re-layouts: 13.8 us -> 12.3 us
    ppermute x6 -> x7, waiting for transfers between devices: 1.35 us -> 0.02 us  [to_other_core(): return lax.ppermute(x, 'ctx', [(i, i ^ 1) for i in range(ctx_size)])]
    pallas_call x21 -> x22, Pallas kernels: 37.9 us -> 37.3 us  [call(): pl.pallas_call(kernel, out_shape=[jax.ShapeDtypeStruct(shape, kind) for s...]
  transfers between devices with their start and end apart: 30 -> 27, of which waited for: 10 -> 8; matrix products, arithmetic and copies ran while one was open for 0% -> 0% of each run, Pallas kernels for 27% -> 28%
where the time goes in v9:
time: 120 us
  starting transfers between devices  39.8 us (33%)
  Pallas kernels  37.3 us (31%)
  waiting for transfers between devices  29.1 us (24%)
  local copies, waits for them, and re-layouts  12.3 us (10%)
    pallas_call x22, Pallas kernels, call(): pl.pallas_call(kernel, out_shape=[jax.ShapeDtypeStruct(shape, kind) for s...  37.3 us
    ppermute x12, starting transfers between devices, to_member(): return lax.ppermute(x, 'ctx', pairs)  16.9 us
    ppermute x12, waiting for transfers between devices, to_member(): return lax.ppermute(x, 'ctx', pairs)  15.6 us
    unnamed x62, local copies, waits for them, and re-layouts  12.3 us
    ppermute x3, starting transfers between devices, to_run(): return lax.ppermute(x, 'ctx', pairs)  10.3 us
    ppermute x3, waiting for transfers between devices, to_dp(): lax.ppermute(x, 'dp', [(i, (i + shift) % dp_size) for i in range(dp_size)])  10 us
    ppermute x3, starting transfers between devices, to_dp(): lax.ppermute(x, 'dp', [(i, (i + shift) % dp_size) for i in range(dp_size)])  5.71 us
    all_to_all x1, starting transfers between devices, local(): lax.all_to_all(projected.reshape((dp_size * group,) + qk_shape[0][1:]), (...  5.3 us
  transfers between devices with their start and end apart: 27, of which 8 were waited for; matrix products, arithmetic and copies ran while one was open for 0% of the time, Pallas kernels for 28%

profile of v9, /device:TPU:0, one launch (start us, length us, event | category | flops | bytes accessed | tf_op | source)
XLA Modules:
  0.0 119.7 jit_solution(15178234119096505257)
XLA Ops:
  5.5 2.6 %collective-permute-start = (bf16[128,2048]{1,0:T(8,128)(2,1)S(1)}, bf16[128,2048]{1,0:T(8,128)(2,1)S(1)}, u32[]{:S(2)}, u32[]{:S(2)}) collective-permute-start(bf16[128,2048]{1,0:T(8,128)(2,1)S(1)} %get-tuple-element.60), channel_id=1, source_target_pairs={{0,16},{16,0},{1,17},{17,1},{2,18},{18,2},{3,19},{19,3},{4,20},{20... | collective-permute-start | bytes 1572872 | tf_op jit(solution)/shard_map/ppermute | solution.py:473
  10.5 10.0 %collective-permute-done.refs_3_ = bf16[128,2048]{1,0:T(8,128)(2,1)S(1)} collective-permute-done((bf16[128,2048]{1,0:T(8,128)(2,1)S(1)}, bf16[128,2048]{1,0:T(8,128)(2,1)S(1)}, u32[]{:S(2)}, u32[]{:S(2)}) %collective-permute-start) | collective-permute-done | bytes 524320 | tf_op jit(solution)/shard_map/ppermute | solution.py:473
  21.9 5.3 %all-to-all-start = ((f32[16,2,2,16,128]{4,3,2,1,0:T(8,128)}), f32[16,2,2,16,128]{4,3,2,1,0:T(8,128)}, u32[]{:S(2)}, u32[]{:S(2)}) async-start(f32[16,2,2,16,128]{4,3,2,1,0:T(8,128)} %bitcast.9), calls=%async_computation | async-start | bytes 1048576 | tf_op jit(solution)/shard_map/all_to_all | solution.py:574
  27.3 1.6 %shard_map.86 = (bf16[1024,512]{1,0:T(8,128)(2,1)}, f32[8,128]{1,0:T(8,128)}) custom-call(s32[1]{0:T(128)} %bitcast.1.refs_0_, bf16[2048,512]{1,0:T(8,128)(2,1)S(1)} %copy-done, f32[8,128]{1,0:T(8,128)S(1)} %get-tuple-element.76.refs_3_.refs_2_), custom_call_target="tpu_custom_call" | custom-call | tf_op jit(solution)/shard_map/pallas_call | solution.py:435
  28.8 1.9 %collective-permute-start.10 = (bf16[1024,512]{1,0:T(8,128)(2,1)}, bf16[1024,512]{1,0:T(8,128)(2,1)}, u32[]{:S(2)}, u32[]{:S(2)}) collective-permute-start(bf16[1024,512]{1,0:T(8,128)(2,1)} %get-tuple-element.82), channel_id=1, source_target_pairs={{0,16},{16,0},{1,17},{17,1},{2,18},{18,2},{3,19},{19,3},{4,20},{20... | collective-permute-start | bytes 3145736 | tf_op jit(solution)/shard_map/ppermute | solution.py:473
  39.3 4.0 %collective-permute-done.2.refs_2_ = bf16[2,2,128,256]{3,2,1,0:T(8,128)(2,1)S(1)} collective-permute-done((bf16[2,2,128,256]{3,2,1,0:T(8,128)(2,1)S(1)}, bf16[2,2,128,256]{3,2,1,0:T(8,128)(2,1)S(1)}, u32[]{:S(2)}, u32[]{:S(2)}) %collective-permute-start.2) | collective-permute-done | bytes 262176 | tf_op jit(solution)/shard_map/ppermute | solution.py:477
  43.7 5.6 %collective-permute-start.9 = (bf16[2,128,512]{2,1,0:T(8,128)(2,1)}, bf16[2,128,512]{2,1,0:T(8,128)(2,1)}, u32[]{:S(2)}, u32[]{:S(2)}) collective-permute-start(bf16[2,128,512]{2,1,0:T(8,128)(2,1)} %get-tuple-element.79), channel_id=1, source_target_pairs={{0,6},{1,7},{2,0},{3,1},{4,2},{5,3},{6,4},{7,5},{8,14},{9,15},{10,... | collective-permute-start | bytes 786440 | tf_op jit(solution)/shard_map/ppermute | solution.py:477
  50.0 1.6 %shard_map.81 = (f32[8,2,2,16,128]{4,3,2,1,0:T(8,128)S(1)}, bf16[2,176,128]{2,1,0:T(8,128)(2,1)S(1)}, f32[8,128]{1,0:T(8,128)}) custom-call(f32[2,8,2,2,16,128]{5,4,3,2,1,0:T(8,128)} %bitcast.4.refs_0_, bf16[8,2,128,256]{3,2,1,0:T(8,128)(2,1)S(1)} %get-tuple-element.70.refs_1_), custom_call_target="tpu_custom_call" | custom-call | tf_op jit(solution)/shard_map/pallas_call | solution.py:435
  51.6 4.5 %collective-permute-start.5 = (bf16[2,176,128]{2,1,0:T(8,128)(2,1)S(1)}, bf16[2,176,128]{2,1,0:T(8,128)(2,1)S(1)}, u32[]{:S(2)}, u32[]{:S(2)}) collective-permute-start(bf16[2,176,128]{2,1,0:T(8,128)(2,1)S(1)} %get-tuple-element.73), channel_id=1, source_target_pairs={{0,8},{1,9},{2,10},{3,11},{4,12},{5,13},{6,14},{7,15},{16,24},{17,... | collective-permute-start | bytes 270344 | tf_op jit(solution)/shard_map/ppermute | solution.py:494
  56.1 3.6 %shard_map.82 = (f32[1024,256]{1,0:T(8,128)S(1)}, f32[8,128]{1,0:T(8,128)}) custom-call(f32[8,2,2,16,128]{4,3,2,1,0:T(8,128)S(1)} %get-tuple-element.71.refs_0_.refs_1_, bf16[8,2,128,256]{3,2,1,0:T(8,128)(2,1)S(1)} %get-tuple-element.70.refs_1_), custom_call_target="tpu_custom_call" | custom-call | tf_op jit(solution)/shard_map/pallas_call | solution.py:435
  59.9 2.6 %shard_map.85 = (bf16[1024,256]{1,0:T(8,128)(2,1)S(1)}, f32[1024,256]{1,0:T(8,128)S(1)}, bf16[2,176,128]{2,1,0:T(8,128)(2,1)S(1)}, f32[8,128]{1,0:T(8,128)}) custom-call(f32[8,2,2,16,128]{4,3,2,1,0:T(8,128)S(1)} %get-tuple-element.71.refs_0_.refs_1_, bf16[8,2,128,256]{3,2,1,0:T(8,128)(2,1)S(1)} %get-tuple-element.70.refs_1_, ...), custom_call_target="tpu_custom_call" | custom-call | tf_op jit(solution)/shard_map/pallas_call | solution.py:435
  62.5 1.6 %collective-permute-start.11 = (bf16[2,176,128]{2,1,0:T(8,128)(2,1)S(1)}, bf16[2,176,128]{2,1,0:T(8,128)(2,1)S(1)}, u32[]{:S(2)}, u32[]{:S(2)}) collective-permute-start(bf16[2,176,128]{2,1,0:T(8,128)(2,1)S(1)} %get-tuple-element.84), channel_id=1, source_target_pairs={{8,0},{9,1},{10,2},{11,3},{12,4},{13,5},{14,6},{15,7},{24,16},{25,... | collective-permute-start | bytes 270344 | tf_op jit(solution)/shard_map/ppermute | solution.py:494
  64.1 5.9 %shard_map.87 = (f32[2,2,16,1024]{3,2,1,0:T(8,128)S(1)}, f32[2,128,1024]{2,1,0:T(8,128)S(1)}, f32[8,128]{1,0:T(8,128)S(1)}) custom-call(f32[8,2,2,16,128]{4,3,2,1,0:T(8,128)S(1)} %get-tuple-element.71.refs_0_.refs_1_, bf16[8,2,128,256]{3,2,1,0:T(8,128)(2,1)S(1)} %get-tuple-element.70.refs_1_, f32[1024,256]{1,0:T(8,128)S(1)} %get-tuple-element.81.refs_2_, ...), custom_call_target="tpu_custom_call" | custom-call | tf_op jit(solution)/shard_map/pallas_call | solution.py:435
  73.1 2.0 %collective-permute-start.13 = (bf16[64,1024]{1,0:T(8,128)(2,1)S(1)}, bf16[64,1024]{1,0:T(8,128)(2,1)S(1)}, u32[]{:S(2)}, u32[]{:S(2)}) collective-permute-start(bf16[64,1024]{1,0:T(8,128)(2,1)S(1)} %get-tuple-element.89.refs_1_), channel_id=1, source_target_pairs={{0,6},{1,7},{2,0},{3,1},{4,2},{5,3},{6,4},{7,5},{8,14},{9,15},{10,... | collective-permute-start | bytes 393224 | tf_op jit(solution)/shard_map/ppermute | solution.py:477
  75.3 3.2 %collective-permute-done.13.refs_6_.refs_7_ = bf16[64,1024]{1,0:T(8,128)(2,1)S(1)} collective-permute-done((bf16[64,1024]{1,0:T(8,128)(2,1)S(1)}, bf16[64,1024]{1,0:T(8,128)(2,1)S(1)}, u32[]{:S(2)}, u32[]{:S(2)}) %collective-permute-start.13) | collective-permute-done | bytes 131104 | tf_op jit(solution)/shard_map/ppermute | solution.py:477
  78.6 2.1 %collective-permute-done.12.refs_5_ = bf16[64,1024]{1,0:T(8,128)(2,1)S(1)} collective-permute-done((bf16[64,1024]{1,0:T(8,128)(2,1)S(1)}, bf16[64,1024]{1,0:T(8,128)(2,1)S(1)}, u32[]{:S(2)}, u32[]{:S(2)}) %collective-permute-start.12) | collective-permute-done | bytes 131104 | tf_op jit(solution)/shard_map/ppermute | solution.py:477
  80.7 1.8 %shard_map.90 = (bf16[4,2,128,256]{3,2,1,0:T(8,128)(2,1)S(1)}, bf16[4,2,128,256]{3,2,1,0:T(8,128)(2,1)S(1)}, f32[8,128]{1,0:T(8,128)}) custom-call(s32[2]{0:T(128)S(1)} %pad_add_fusion.refs_0_, f32[8,2,2,16,128]{4,3,2,1,0:T(8,128)S(1)} %get-tuple-element.71.refs_0_.refs_1_, bf16[1024,256]{1,0:T(8,128)(2,1)S(1)} %get-tuple-element.80.refs_2_, ...), custom_call_target="tpu_custom_call" | custom-call | tf_op jit(solution)/shard_map/pallas_call | solution.py:435
  83.0 6.2 %collective-permute-done.19.refs_3_ = bf16[64,1024]{1,0:T(8,128)(2,1)S(1)} collective-permute-done((bf16[64,1024]{1,0:T(8,128)(2,1)S(1)}, bf16[64,1024]{1,0:T(8,128)(2,1)S(1)}, u32[]{:S(2)}, u32[]{:S(2)}) %collective-permute-start.19) | collective-permute-done | bytes 131104 | tf_op jit(solution)/shard_map/ppermute | solution.py:477
  92.1 2.2 %shard_map.92 = (f32[256,512]{1,0:T(8,128)S(1)}, bf16[256,512]{1,0:T(8,128)(2,1)}, f32[8,128]{1,0:T(8,128)S(1)}) custom-call(s32[3]{0:T(128)S(1)} %pad_add_fusion.1.refs_0_, bf16[64,1024]{1,0:T(8,128)(2,1)S(1)} %get-tuple-element.89.refs_1_, bf16[64,1024]{1,0:T(8,128)(2,1)S(1)} %collective-permute-done.18.refs_2_, ...), custom_call_target="tpu_custom_call" | custom-call | tf_op jit(solution)/shard_map/pallas_call | solution.py:435
  97.2 2.8 %collective-permute-start.17 = (bf16[2,2,128,256]{3,2,1,0:T(8,128)(2,1)}, bf16[2,2,128,256]{3,2,1,0:T(8,128)(2,1)}, u32[]{:S(2)}, u32[]{:S(2)}) collective-permute-start(bf16[2,2,128,256]{3,2,1,0:T(8,128)(2,1)} %get-tuple-element.95), channel_id=1, source_target_pairs={{0,6},{1,7},{2,0},{3,1},{4,2},{5,3},{6,4},{7,5},{8,14},{9,15},{10,... | collective-permute-start | bytes 786440 | tf_op jit(solution)/shard_map/ppermute | solution.py:477
  104.7 3.8 %shard_map.93 = (bf16[1,128,4096]{2,1,0:T(8,128)(2,1)}, f32[8,128]{1,0:T(8,128)S(1)}) custom-call(s32[5]{0:T(128)S(1)} %stack.29.refs_0_, bf16[64,1024]{1,0:T(8,128)(2,1)S(1)} %get-tuple-element.89.refs_1_, bf16[64,1024]{1,0:T(8,128)(2,1)S(1)} %copy-done.7, bf16[64,1024]{1,0:T(8,128)(2,1)S(1)} %copy-done.5, bf16[64,1024]{1,0:T(8,128)(2,1)S(1)} %copy-done.11, ...), custom_call_target="tpu_custom_call" | custom-call | tf_op jit(solution)/shard_map/pallas_call | solution.py:435
  109.5 4.2 %collective-permute-start.25 = (bf16[128,512]{1,0:T(8,128)(2,1)S(1)}, bf16[128,512]{1,0:T(8,128)(2,1)S(1)}, u32[]{:S(2)}, u32[]{:S(2)}) collective-permute-start(bf16[128,512]{1,0:T(8,128)(2,1)S(1)} %get-tuple-element.107), channel_id=1, source_target_pairs={{0,8},{1,9},{2,10},{3,11},{4,12},{5,13},{6,14},{7,15},{8,0},{9,1},... | collective-permute-start | bytes 393224 | tf_op jit(solution)/shard_map/ppermute | solution.py:494
  113.8 2.2 %shard_map.95 = (bf16[1,128,2048]{2,1,0:T(8,128)(2,1)}, bf16[1,128,2048]{2,1,0:T(8,128)(2,1)}, f32[8,128]{1,0:T(8,128)S(1)}) custom-call(s32[1]{0:T(128)} %bitcast.refs_0_, bf16[2,2,128,256]{3,2,1,0:T(8,128)(2,1)S(1)} %copy-done.20, bf16[2,2,128,256]{3,2,1,0:T(8,128)(2,1)} %collective-permute-done.15.refs_2_, ...), custom_call_target="tpu_custom_call" | custom-call | tf_op jit(solution)/shard_map/pallas_call | solution.py:435
  115.9 3.0 %collective-permute-done.25.refs_1_ = bf16[128,512]{1,0:T(8,128)(2,1)S(1)} collective-permute-done((bf16[128,512]{1,0:T(8,128)(2,1)S(1)}, bf16[128,512]{1,0:T(8,128)(2,1)S(1)}, u32[]{:S(2)}, u32[]{:S(2)}) %collective-permute-start.25) | collective-permute-done | bytes 131104 | tf_op jit(solution)/shard_map/ppermute | solution.py:494
  (117 shorter events, 34.3 us)
Async XLA Ops:
  4.9 4.9 %collective-permute-start.1 = (bf16[4,2,128,256]{3,2,1,0:T(8,128)(2,1)S(1)}, bf16[4,2,128,256]{3,2,1,0:T(8,128)(2,1)S(1)}, u32[]{:S(2)}, u32[]{:S(2)}) collective-permute-start(bf16[4,2,128,256]{3,2,1,0:T(8,128)(2,1)S(1)} %get-tuple-element.62), channel_id=1, source_target_pairs={{0,1},{1,0},{2,3},{3,2},{4,5},{5,4},{6,7},{7,6},{8,9},{9,8},{10,11... | collective-permute-start | bytes 1572872 | tf_op jit(solution)/shard_map/ppermute | solution.py:486
  5.5 15.1 %collective-permute-start = (bf16[128,2048]{1,0:T(8,128)(2,1)S(1)}, bf16[128,2048]{1,0:T(8,128)(2,1)S(1)}, u32[]{:S(2)}, u32[]{:S(2)}) collective-permute-start(bf16[128,2048]{1,0:T(8,128)(2,1)S(1)} %get-tuple-element.60), channel_id=1, source_target_pairs={{0,16},{16,0},{1,17},{17,1},{2,18},{18,2},{3,19},{19,3},{4,20},{20... | collective-permute-start | bytes 1572872 | tf_op jit(solution)/shard_map/ppermute | solution.py:473
  21.9 28.1 %all-to-all-start = ((f32[16,2,2,16,128]{4,3,2,1,0:T(8,128)}), f32[16,2,2,16,128]{4,3,2,1,0:T(8,128)}, u32[]{:S(2)}, u32[]{:S(2)}) async-start(f32[16,2,2,16,128]{4,3,2,1,0:T(8,128)} %bitcast.9), calls=%async_computation | async-start | bytes 1048576 | tf_op jit(solution)/shard_map/all_to_all | solution.py:574
  28.8 35.2 %collective-permute-start.10 = (bf16[1024,512]{1,0:T(8,128)(2,1)}, bf16[1024,512]{1,0:T(8,128)(2,1)}, u32[]{:S(2)}, u32[]{:S(2)}) collective-permute-start(bf16[1024,512]{1,0:T(8,128)(2,1)} %get-tuple-element.82), channel_id=1, source_target_pairs={{0,16},{16,0},{1,17},{17,1},{2,18},{18,2},{3,19},{19,3},{4,20},{20... | collective-permute-start | bytes 3145736 | tf_op jit(solution)/shard_map/ppermute | solution.py:473
  32.1 11.2 %collective-permute-start.2 = (bf16[2,2,128,256]{3,2,1,0:T(8,128)(2,1)S(1)}, bf16[2,2,128,256]{3,2,1,0:T(8,128)(2,1)S(1)}, u32[]{:S(2)}, u32[]{:S(2)}) collective-permute-start(bf16[2,2,128,256]{3,2,1,0:T(8,128)(2,1)S(1)} %copy-done.30), channel_id=1, source_target_pairs={{0,2},{1,3},{2,4},{3,5},{4,6},{5,7},{6,0},{7,1},{8,10},{9,11},{10,... | collective-permute-start | bytes 786440 | tf_op jit(solution)/shard_map/ppermute | solution.py:477
  33.6 10.1 %collective-permute-start.3 = (bf16[2,2,128,256]{3,2,1,0:T(8,128)(2,1)S(1)}, bf16[2,2,128,256]{3,2,1,0:T(8,128)(2,1)S(1)}, u32[]{:S(2)}, u32[]{:S(2)}) collective-permute-start(bf16[2,2,128,256]{3,2,1,0:T(8,128)(2,1)S(1)} %copy-done.28), channel_id=1, source_target_pairs={{0,4},{1,5},{2,6},{3,7},{4,0},{5,1},{6,2},{7,3},{8,12},{9,13},{10,... | collective-permute-start | bytes 786440 | tf_op jit(solution)/shard_map/ppermute | solution.py:477
  35.1 14.2 %collective-permute-start.4 = (bf16[2,2,128,256]{3,2,1,0:T(8,128)(2,1)S(1)}, bf16[2,2,128,256]{3,2,1,0:T(8,128)(2,1)S(1)}, u32[]{:S(2)}, u32[]{:S(2)}) collective-permute-start(bf16[2,2,128,256]{3,2,1,0:T(8,128)(2,1)S(1)} %copy-done.26), channel_id=1, source_target_pairs={{0,6},{1,7},{2,0},{3,1},{4,2},{5,3},{6,4},{7,5},{8,14},{9,15},{10,... | collective-permute-start | bytes 786440 | tf_op jit(solution)/shard_map/ppermute | solution.py:477
  38.7 21.0 %collective-permute-start.7 = (bf16[2,128,512]{2,1,0:T(8,128)(2,1)}, bf16[2,128,512]{2,1,0:T(8,128)(2,1)S(1)}, u32[]{:S(2)}, u32[]{:S(2)}) collective-permute-start(bf16[2,128,512]{2,1,0:T(8,128)(2,1)} %get-tuple-element.77), channel_id=1, source_target_pairs={{0,2},{1,3},{2,4},{3,5},{4,6},{5,7},{6,0},{7,1},{8,10},{9,11},{10,... | collective-permute-start | bytes 786440 | tf_op jit(solution)/shard_map/ppermute | solution.py:477
  43.3 16.5 %collective-permute-start.8 = (bf16[2,128,512]{2,1,0:T(8,128)(2,1)}, bf16[2,128,512]{2,1,0:T(8,128)(2,1)}, u32[]{:S(2)}, u32[]{:S(2)}) collective-permute-start(bf16[2,128,512]{2,1,0:T(8,128)(2,1)} %get-tuple-element.78), channel_id=1, source_target_pairs={{0,4},{1,5},{2,6},{3,7},{4,0},{5,1},{6,2},{7,3},{8,12},{9,13},{10,... | collective-permute-start | bytes 786440 | tf_op jit(solution)/shard_map/ppermute | solution.py:477
  43.7 16.1 %collective-permute-start.9 = (bf16[2,128,512]{2,1,0:T(8,128)(2,1)}, bf16[2,128,512]{2,1,0:T(8,128)(2,1)}, u32[]{:S(2)}, u32[]{:S(2)}) collective-permute-start(bf16[2,128,512]{2,1,0:T(8,128)(2,1)} %get-tuple-element.79), channel_id=1, source_target_pairs={{0,6},{1,7},{2,0},{3,1},{4,2},{5,3},{6,4},{7,5},{8,14},{9,15},{10,... | collective-permute-start | bytes 786440 | tf_op jit(solution)/shard_map/ppermute | solution.py:477
  51.6 8.3 %collective-permute-start.5 = (bf16[2,176,128]{2,1,0:T(8,128)(2,1)S(1)}, bf16[2,176,128]{2,1,0:T(8,128)(2,1)S(1)}, u32[]{:S(2)}, u32[]{:S(2)}) collective-permute-start(bf16[2,176,128]{2,1,0:T(8,128)(2,1)S(1)} %get-tuple-element.73), channel_id=1, source_target_pairs={{0,8},{1,9},{2,10},{3,11},{4,12},{5,13},{6,14},{7,15},{16,24},{17,... | collective-permute-start | bytes 270344 | tf_op jit(solution)/shard_map/ppermute | solution.py:494
  62.5 9.3 %collective-permute-start.11 = (bf16[2,176,128]{2,1,0:T(8,128)(2,1)S(1)}, bf16[2,176,128]{2,1,0:T(8,128)(2,1)S(1)}, u32[]{:S(2)}, u32[]{:S(2)}) collective-permute-start(bf16[2,176,128]{2,1,0:T(8,128)(2,1)S(1)} %get-tuple-element.84), channel_id=1, source_target_pairs={{8,0},{9,1},{10,2},{11,3},{12,4},{13,5},{14,6},{15,7},{24,16},{25,... | collective-permute-start | bytes 270344 | tf_op jit(solution)/shard_map/ppermute | solution.py:494
  73.1 5.4 %collective-permute-start.13 = (bf16[64,1024]{1,0:T(8,128)(2,1)S(1)}, bf16[64,1024]{1,0:T(8,128)(2,1)S(1)}, u32[]{:S(2)}, u32[]{:S(2)}) collective-permute-start(bf16[64,1024]{1,0:T(8,128)(2,1)S(1)} %get-tuple-element.89.refs_1_), channel_id=1, source_target_pairs={{0,6},{1,7},{2,0},{3,1},{4,2},{5,3},{6,4},{7,5},{8,14},{9,15},{10,... | collective-permute-start | bytes 393224 | tf_op jit(solution)/shard_map/ppermute | solution.py:477
  75.1 5.6 %collective-permute-start.12 = (bf16[64,1024]{1,0:T(8,128)(2,1)S(1)}, bf16[64,1024]{1,0:T(8,128)(2,1)S(1)}, u32[]{:S(2)}, u32[]{:S(2)}) collective-permute-start(bf16[64,1024]{1,0:T(8,128)(2,1)S(1)} %get-tuple-element.89.refs_1_), channel_id=1, source_target_pairs={{0,4},{1,5},{2,6},{3,7},{4,0},{5,1},{6,2},{7,3},{8,12},{9,13},{10,... | collective-permute-start | bytes 393224 | tf_op jit(solution)/shard_map/ppermute | solution.py:477
  75.3 24.8 %collective-permute-start.24 = (bf16[1024,512]{1,0:T(8,128)(2,1)}, bf16[1024,512]{1,0:T(8,128)(2,1)S(1)}, u32[]{:S(2)}, u32[]{:S(2)}) collective-permute-start(bf16[1024,512]{1,0:T(8,128)(2,1)} %collective-permute-done.10.refs_4_.refs_10_), channel_id=1, source_target_pairs={{0,1},{1,0},{2,3},{3,2},{4,5},{5,4},{6,7},{7,6},{8,9},{9,8},{10,11... | collective-permute-start | bytes 3145736 | tf_op jit(solution)/shard_map/ppermute | solution.py:603
  82.5 6.8 %collective-permute-start.14 = (bf16[4,2,128,256]{3,2,1,0:T(8,128)(2,1)S(1)}, bf16[4,2,128,256]{3,2,1,0:T(8,128)(2,1)S(1)}, u32[]{:S(2)}, u32[]{:S(2)}) collective-permute-start(bf16[4,2,128,256]{3,2,1,0:T(8,128)(2,1)S(1)} %get-tuple-element.91), channel_id=1, source_target_pairs={{0,1},{1,0},{2,3},{3,2},{4,5},{5,4},{6,7},{7,6},{8,9},{9,8},{10,11... | collective-permute-start | bytes 1572872 | tf_op jit(solution)/shard_map/ppermute | solution.py:486
  82.5 6.8 %collective-permute-start.19 = (bf16[64,1024]{1,0:T(8,128)(2,1)S(1)}, bf16[64,1024]{1,0:T(8,128)(2,1)S(1)}, u32[]{:S(2)}, u32[]{:S(2)}) collective-permute-start(bf16[64,1024]{1,0:T(8,128)(2,1)S(1)} %get-tuple-element.89.refs_1_), channel_id=1, source_target_pairs={{0,2},{1,3},{2,4},{3,5},{4,6},{5,7},{6,0},{7,1},{8,10},{9,11},{10,... | collective-permute-start | bytes 393224 | tf_op jit(solution)/shard_map/ppermute | solution.py:477
  82.5 9.5 %collective-permute-start.18 = (bf16[64,1024]{1,0:T(8,128)(2,1)S(1)}, bf16[64,1024]{1,0:T(8,128)(2,1)S(1)}, u32[]{:S(2)}, u32[]{:S(2)}) collective-permute-start(bf16[64,1024]{1,0:T(8,128)(2,1)S(1)} %get-tuple-element.89.refs_1_), channel_id=1, source_target_pairs={{0,1},{1,0},{2,3},{3,2},{4,5},{5,4},{6,7},{7,6},{8,9},{9,8},{10,11... | collective-permute-start | bytes 393224 | tf_op jit(solution)/shard_map/ppermute | solution.py:486
  83.0 9.1 %collective-permute-start.22 = (bf16[64,1024]{1,0:T(8,128)(2,1)S(1)}, bf16[64,1024]{1,0:T(8,128)(2,1)S(1)}, u32[]{:S(2)}, u32[]{:S(2)}) collective-permute-start(bf16[64,1024]{1,0:T(8,128)(2,1)S(1)} %collective-permute-done.13.refs_6_.refs_7_), channel_id=1, source_target_pairs={{0,1},{1,0},{2,3},{3,2},{4,5},{5,4},{6,7},{7,6},{8,9},{9,8},{10,11... | collective-permute-start | bytes 393224 | tf_op jit(solution)/shard_map/ppermute | solution.py:486
  95.1 13.4 %collective-permute-start.23 = (bf16[256,512]{1,0:T(8,128)(2,1)}, bf16[256,512]{1,0:T(8,128)(2,1)}, u32[]{:S(2)}, u32[]{:S(2)}) collective-permute-start(bf16[256,512]{1,0:T(8,128)(2,1)} %get-tuple-element.99), channel_id=1, source_target_pairs={{0,16},{16,0},{1,17},{17,1},{2,18},{18,2},{3,19},{19,3},{4,20},{20... | collective-permute-start | bytes 786440 | tf_op jit(solution)/shard_map/ppermute | solution.py:473
  96.3 17.4 %collective-permute-start.15 = (bf16[2,2,128,256]{3,2,1,0:T(8,128)(2,1)}, bf16[2,2,128,256]{3,2,1,0:T(8,128)(2,1)}, u32[]{:S(2)}, u32[]{:S(2)}) collective-permute-start(bf16[2,2,128,256]{3,2,1,0:T(8,128)(2,1)} %get-tuple-element.93), channel_id=1, source_target_pairs={{0,2},{1,3},{2,4},{3,5},{4,6},{5,7},{6,0},{7,1},{8,10},{9,11},{10,... | collective-permute-start | bytes 786440 | tf_op jit(solution)/shard_map/ppermute | solution.py:477
  96.3 17.4 %collective-permute-start.16 = (bf16[2,2,128,256]{3,2,1,0:T(8,128)(2,1)}, bf16[2,2,128,256]{3,2,1,0:T(8,128)(2,1)}, u32[]{:S(2)}, u32[]{:S(2)}) collective-permute-start(bf16[2,2,128,256]{3,2,1,0:T(8,128)(2,1)} %get-tuple-element.94), channel_id=1, source_target_pairs={{0,4},{1,5},{2,6},{3,7},{4,0},{5,1},{6,2},{7,3},{8,12},{9,13},{10,... | collective-permute-start | bytes 786440 | tf_op jit(solution)/shard_map/ppermute | solution.py:477
  97.2 16.5 %collective-permute-start.17 = (bf16[2,2,128,256]{3,2,1,0:T(8,128)(2,1)}, bf16[2,2,128,256]{3,2,1,0:T(8,128)(2,1)}, u32[]{:S(2)}, u32[]{:S(2)}) collective-permute-start(bf16[2,2,128,256]{3,2,1,0:T(8,128)(2,1)} %get-tuple-element.95), channel_id=1, source_target_pairs={{0,6},{1,7},{2,0},{3,1},{4,2},{5,3},{6,4},{7,5},{8,14},{9,15},{10,... | collective-permute-start | bytes 786440 | tf_op jit(solution)/shard_map/ppermute | solution.py:477
  109.5 9.4 %collective-permute-start.25 = (bf16[128,512]{1,0:T(8,128)(2,1)S(1)}, bf16[128,512]{1,0:T(8,128)(2,1)S(1)}, u32[]{:S(2)}, u32[]{:S(2)}) collective-permute-start(bf16[128,512]{1,0:T(8,128)(2,1)S(1)} %get-tuple-element.107), channel_id=1, source_target_pairs={{0,8},{1,9},{2,10},{3,11},{4,12},{5,13},{6,14},{7,15},{8,0},{9,1},... | collective-permute-start | bytes 393224 | tf_op jit(solution)/shard_map/ppermute | solution.py:494
  (34 other events, 165.6 us)

commit v10 on v9

--- a/solution.py
+++ b/solution.py
@@ -117,23 +117,29 @@
     )
 
 
-def pack_heads_kernel(at_ref, values_ref, grad_ref, keep_ref, send_ref):
-    chips, width = keep_ref.shape[0], keep_ref.shape[3]
+def pack_heads_kernel(at_ref, values_ref, grad_ref, *out_refs):
+    chips, width = len(out_refs), out_refs[0].shape[3]
+    for shift, out_ref in enumerate(out_refs):
+        chip = lax.rem(at_ref[0] + shift, chips)
+        for core in range(2):
+            cols = aligned(2 * chip + core, width)
+            out_ref[core, 0] = values_ref[0, :, cols]
+            out_ref[core, 1] = grad_ref[0, :, cols]
+
+
+def split_cores_kernel(at_ref, *rest):
+    *part_refs, keep_ref, send_ref = rest
+    for shift, part_ref in enumerate(part_refs):
+        keep_ref[shift] = part_ref[at_ref[1]]
+        send_ref[shift] = part_ref[1 - at_ref[1]]
+
+
+def collect_heads_kernel(at_ref, keep_ref, got_ref, out_ref):
+    chips = keep_ref.shape[0]
     for shift in range(chips):
-        chip = lax.rem(at_ref[0] + shift, chips)
-        for core, out_ref in ((at_ref[1], keep_ref), (1 - at_ref[1], send_ref)):
-            cols = aligned(2 * chip + core, width)
-            out_ref[shift, 0] = values_ref[0, :, cols]
-            out_ref[shift, 1] = grad_ref[0, :, cols]
-
-
-def collect_heads_kernel(at_ref, *rest):
-    *part_refs, out_ref = rest
-    chips = len(part_refs)
-    for shift, part_ref in enumerate(part_refs):
         chip = lax.rem(at_ref[0] + chips - shift, chips)
-        for core in range(2):
-            out_ref[2 * chip + core] = part_ref[core]
+        out_ref[2 * chip + at_ref[1]] = keep_ref[shift]
+        out_ref[2 * chip + 1 - at_ref[1]] = got_ref[shift]
 
 
 def pack_tokens_kernel(depth, at_ref, tokens_ref, keep_ref, send_ref):
@@ -296,38 +302,29 @@
                 grad_v_ref[head, :, :width] += piece_v
 
 
-def rows_kernel(with_state, qk_ref, vg_ref, grad_qk_ref, *rest):
-    *suffix_refs, out_ref, held_ref, sems = rest
-    heads = qk_ref.shape[2]
-    length = qk_ref.shape[0] * qk_ref.shape[4]
+def rows_kernel(with_state, at_ref, qk_ref, vg_ref, attended_ref, grad_qk_ref, grad_v_ref, *rest):
+    *suffix_refs, rows_ref, keep_ref, send_ref, held_ref = rest
+    heads, tok = qk_ref.shape[2], qk_ref.shape[4]
+    length = qk_ref.shape[0] * tok
     for head in range(heads):
-        grad_k = grad_qk_ref[1, head]
+        grad_k, grad_v = grad_qk_ref[1, head], grad_v_ref[head]
         if with_state:
             k = feature_major(qk_ref, 1, head)
             v = rows_of(vg_ref, 0, head, 0, length)
-            high, low = split(state_sum(suffix_refs, head))
+            suffix = state_sum(suffix_refs, head)
+            high, low = split(suffix)
             grad_k = grad_k + pull_psi(k, dot(high, v, NT) + dot(low, v, NT), False)
-        held_ref[head * F : (head + 1) * F] = grad_qk_ref[0, head].astype(bf16)
-        held_ref[(heads + head) * F : (heads + head + 1) * F] = grad_k.astype(bf16)
-    run_copies(sems, [(held_ref, out_ref)])
-
-
-def grad_values_kernel(with_state, at_ref, qk_ref, attended_ref, grad_v_ref, *rest):
-    *suffix_refs, keep_ref, send_ref, held_ref = rest
-    heads, tok = qk_ref.shape[2], qk_ref.shape[4]
-    for head in range(heads):
-        grad_v = grad_v_ref[head]
-        if with_state:
-            feat = psi(feature_major(qk_ref, 1, head), False)
-            grad_v = grad_v + dot3(state_sum(suffix_refs, head).T, feat)
+            grad_v = grad_v + dot3(suffix.T, psi(k, False))
+        rows_ref[head * F : (head + 1) * F] = grad_qk_ref[0, head].astype(bf16)
+        rows_ref[(heads + head) * F : (heads + head + 1) * F] = grad_k.astype(bf16)
         held_ref[:, head * DH : (head + 1) * DH] = grad_v.T.astype(bf16)
     chips = keep_ref.shape[0]
     for shift in range(chips):
         chip = lax.rem(at_ref[0] + shift, chips)
         for core, out_ref in ((at_ref[1], keep_ref), (1 - at_ref[1], send_ref)):
-            rows = aligned(2 * chip + core, tok)
-            out_ref[shift, 0] = attended_ref[rows, :]
-            out_ref[shift, 1] = held_ref[rows, :]
+            block = aligned(2 * chip + core, tok)
+            out_ref[shift, 0] = attended_ref[block, :]
+            out_ref[shift, 1] = held_ref[block, :]
 
 
 def pair_kernel(at_ref, keep_ref, got_ref, *out_refs):
@@ -347,7 +344,7 @@
             values_ref[0, :, cols] = part_ref[core, 1]
 
 
-def place_rows(chip_at, core_at, part_refs, cols, held_ref):
+def place_rows(chip_at, core_at, part_refs, held_ref):
     chips, half = len(part_refs) // 2, part_refs[0].shape[0] // 2
     for shift in range(chips):
         chip = lax.rem(chip_at + chips - shift, chips)
@@ -355,14 +352,16 @@
             part_ref = part_refs[2 * shift + side]
             for which in range(2):
                 rows = aligned(which * 2 * chips + 2 * chip + core, half)
-                held_ref[rows, :] = part_ref[which * half : (which + 1) * half, cols]
+                held_ref[rows, :] = part_ref[which * half : (which + 1) * half, :]
 
 
 def product_kernel(group, at_ref, *rest):
     rows_refs, rest = rest[:group], rest[group:]
-    tokens_ref, *part_refs, total_ref, held_ref = rest
-    place_rows(at_ref[1], at_ref[2], rows_refs, slice(None), held_ref)
+    tokens_ref, own_rows_ref, *part_refs, total_ref, held_ref = rest
+    place_rows(at_ref[1], at_ref[2], rows_refs, held_ref)
     total_ref[...] = dot(tokens_ref[...], held_ref[...], NT)
+    tok = own_rows_ref.shape[0]
+    own_rows_ref[...] = held_ref[:, aligned(2 * at_ref[1] + at_ref[2], tok)].T
     count = len(part_refs)
     size = part_refs[0].shape[0]
     for shift, part_ref in enumerate(part_refs):
@@ -386,16 +385,12 @@
         part_ref[...] = part.astype(part_ref.dtype)
 
 
-def grad_tokens_kernel(group, at_ref, *rest):
-    rows_refs, rest = rest[:group], rest[group:]
-    *weight_refs, out_ref, held_ref = rest
-    member = 2 * at_ref[0] + at_ref[1]
-    place_rows(at_ref[0], at_ref[1], rows_refs, aligned(member, out_ref.shape[1]), held_ref)
-    rows = held_ref[...].T
+def grad_tokens_kernel(at_ref, rows_ref, *rest):
+    *weight_refs, out_ref = rest
     for i, weight_ref in enumerate(weight_refs):
         size = weight_ref.shape[0]
-        first = pl.multiple_of(at_ref[2 + i], size)
-        out_ref[0, :, pl.ds(first, size)] = dot(rows, weight_ref[...], NT).astype(bf16)
+        first = pl.multiple_of(at_ref[i], size)
+        out_ref[0, :, pl.ds(first, size)] = dot(rows_ref[...], weight_ref[...], NT).astype(bf16)
 
 
 def final_sum_kernel(own_ref, *rest):
@@ -477,7 +472,7 @@
         return lax.ppermute(x, "ctx", pairs)
 
     chips = group // 2
-    chip_at = member // 2
+    chip_at, core_at = member // 2, member % 2
 
     def to_chip(x, shift):
         return x if shift == 0 else to_member(x, 2 * shift)
@@ -508,26 +503,26 @@
         copies=(dp_size - 1,),
     )
     arrived = [to_dp(part, shift) for shift, part in enumerate(parts, 1)]
-    (keep, send), token = call(
+    parts, token = call(
         pack_heads_kernel,
-        [((chips, 2, tok, heads * DH), bf16)] * 2,
+        [((2, 2, tok, heads * DH), bf16)] * chips,
         values,
         grad_out,
-        scalars=(chip_at, ctx_at % 2),
-        after=(token,),
-    )
-    parts, heads_token = call(
-        pair_kernel,
-        [((2, 2, tok, heads * DH), bf16)] * chips,
-        keep,
-        to_other_core(send),
-        scalars=(chip_at, ctx_at % 2),
+        scalars=(chip_at, core_at),
+        after=(token,),
+    )
+    (keep, send), heads_token = call(
+        split_cores_kernel,
+        [((chips, 2, tok, heads * DH), bf16)] * 2,
+        *[to_chip(part, shift) for shift, part in enumerate(parts)],
+        scalars=(chip_at, core_at),
     )
     (vg,), _ = call(
         collect_heads_kernel,
         [((group, 2, tok, heads * DH), bf16)],
-        *[to_chip(part, shift) for shift, part in enumerate(parts)],
-        scalars=(chip_at,),
+        keep,
+        to_other_core(send),
+        scalars=(chip_at, core_at),
     )
     (projected,), token = call(
         project_kernel,
@@ -555,19 +550,19 @@
             functools.partial(pack_tokens_kernel, depth),
             [((chips,) + part_shape, bf16)] * 2,
             tokens,
-            scalars=(chip_at, ctx_at % 2),
+            scalars=(chip_at, core_at),
         )
     else:
         blocks = tokens[0].reshape(tok, dp_size * runs, chips, 2, depth).transpose(2, 3, 0, 1, 4)
         blocks = blocks.reshape(chips, 2, *part_shape)
         blocks = jnp.stack([blocks[(chip_at + shift) % chips] for shift in range(chips)])
-        keep, send = blocks[:, ctx_at % 2], blocks[:, 1 - ctx_at % 2]
+        keep, send = blocks[:, core_at], blocks[:, 1 - core_at]
     token_parts, _ = call(
         pair_kernel,
         [((2,) + part_shape, bf16)] * chips,
         keep,
         to_other_core(send),
-        scalars=(chip_at, ctx_at % 2),
+        scalars=(chip_at, core_at),
         after=(token,),
     )
     token_parts = [to_chip(part, shift) for shift, part in enumerate(token_parts)]
@@ -640,60 +635,49 @@
         scalars=(chip_at,),
         after=(token,),
     )
-    (rows,), token = call(
+    (rows, keep, send), token = call(
         functools.partial(rows_kernel, with_state),
-        [((2 * heads * F, length), bf16)],
+        [((2 * heads * F, length), bf16)] + [((chips, 2, tok, heads * DH), bf16)] * 2,
         qk,
         vg,
+        attended,
         grad_qk,
+        grad_v,
         *suffix,
-        after=(token,),
-        far_out=True,
-        scratch=[pltpu.VMEM((2 * heads * F, length), bf16)],
-        copies=(1,),
+        scalars=(chip_at, core_at),
+        after=(token,),
+        scratch=[pltpu.VMEM((length, heads * DH), bf16)],
     )
     rows = [to_chip(rows, shift) for shift in range(chips)]
     rows = [side for part in rows for side in (part, to_other_core(part))]
-    (keep, send), token = call(
-        functools.partial(grad_values_kernel, with_state),
-        [((chips, 2, tok, heads * DH), bf16)] * 2,
-        qk,
-        attended,
-        grad_v,
-        *suffix,
-        scalars=(chip_at, ctx_at % 2),
-        after_far=rows[4::2],
-        scratch=[pltpu.VMEM((length, heads * DH), bf16)],
-    )
     got = to_other_core(send)
     results, token = call(
         pair_kernel,
         [((2, 2, tok, heads * DH), bf16)] * chips,
         keep,
         got,
-        scalars=(chip_at, ctx_at % 2),
+        scalars=(chip_at, core_at),
     )
     results = [to_chip(part, shift) for shift, part in enumerate(results)]
 
     held = pltpu.VMEM((cols, length), bf16)
-    (own, *parts), token = call(
+    (own_rows, own, *parts), token = call(
         functools.partial(product_kernel, 2 * chips),
-        [((runs * depth, cols), f32)] + [((runs * depth, cols), bf16)] * (dp_size - 1),
+        [((tok, cols), bf16), ((runs * depth, cols), f32)] + [((runs * depth, cols), bf16)] * (dp_size - 1),
         *rows,
         token_cols,
-        scalars=(dp_at, chip_at, ctx_at % 2),
+        scalars=(dp_at, chip_at, core_at),
         after=(token,),
         scratch=[pltpu.VMEM((dp_size * runs * depth, cols), f32), held],
     )
     parts = [to_dp(part, shift) for shift, part in enumerate(parts, 1)]
     (grad_tokens,), tokens_token = call(
-        functools.partial(grad_tokens_kernel, 2 * chips),
+        grad_tokens_kernel,
         [((1, tok, width), bf16)],
-        *rows,
+        own_rows,
         *weights,
-        scalars=(chip_at, ctx_at % 2, *firsts),
-        after=(token,),
-        scratch=[pltpu.VMEM((cols, tok), bf16)],
+        scalars=firsts,
+        after=(token,),
     )
     (grad_proj, *parts), token = call(
         functools.partial(run_sum_kernel, len(parts)),

time: 120 us -> 120 us (level); the launches traced: 120 us -> 117 us
  local copies, waits for them, and re-layouts: 12.3 us -> 7.74 us
  waiting for transfers between devices: 29.1 us -> 31.9 us
  starting transfers between devices: 39.8 us -> 37.5 us
  Pallas kernels: 37.3 us -> 38.9 us
    all_to_all x1, waiting for transfers between devices: 0.01 us -> 12.8 us  [local(): lax.all_to_all(projected.reshape((dp_size * group,) + qk_shape[0][1:]), (...]
    ppermute x3, waiting for transfers between devices: 10 us -> 0.09 us  [to_dp(): lax.ppermute(x, 'dp', [(i, (i + shift) % dp_size) for i in range(dp_size)])]
    unnamed x62 -> x24, local copies, waits for them, and re-layouts: 12.3 us -> 7.74 us
    ppermute x3, waiting for transfers between devices: 3.46 us -> 0.59 us  [to_run(): return lax.ppermute(x, 'ctx', pairs)]
    pallas_call x22 -> x21, Pallas kernels: 37.3 us -> 38.9 us  [call(): pl.pallas_call(kernel, out_shape=[jax.ShapeDtypeStruct(shape, kind) for s...]
    ppermute x3, starting transfers between devices: 5.71 us -> 4.04 us  [to_dp(): lax.ppermute(x, 'dp', [(i, (i + shift) % dp_size) for i in range(dp_size)])]
    ppermute x12, waiting for transfers between devices: 15.6 us -> 17.1 us  [to_member(): return lax.ppermute(x, 'ctx', pairs)]
    ppermute x7, waiting for transfers between devices: 0.02 us -> 1.42 us  [to_other_core(): return lax.ppermute(x, 'ctx', [(i, i ^ 1) for i in range(ctx_size)])]
  transfers between devices with their start and end apart: 27 -> 27, of which waited for: 8 -> 10; matrix products, arithmetic and copies ran while one was open for 0% -> 0% of each run, Pallas kernels for 28% -> 30%
where the time goes in v10:
time: 120 us; the launch traced here: 117 us
  Pallas kernels  38.9 us (32%)
  starting transfers between devices  37.5 us (31%)
  waiting for transfers between devices  31.9 us (27%)
  local copies, waits for them, and re-layouts  7.74 us (6%)
    pallas_call x21, Pallas kernels, call(): pl.pallas_call(kernel, out_shape=[jax.ShapeDtypeStruct(shape, kind) for s...  38.9 us
    ppermute x12, waiting for transfers between devices, to_member(): return lax.ppermute(x, 'ctx', pairs)  17.1 us
    ppermute x12, starting transfers between devices, to_member(): return lax.ppermute(x, 'ctx', pairs)  17.1 us
    all_to_all x1, waiting for transfers between devices, local(): lax.all_to_all(projected.reshape((dp_size * group,) + qk_shape[0][1:]), (...  12.8 us
    ppermute x3, starting transfers between devices, to_run(): return lax.ppermute(x, 'ctx', pairs)  9.6 us
    unnamed x24, local copies, waits for them, and re-layouts  7.74 us
    all_to_all x1, starting transfers between devices, local(): lax.all_to_all(projected.reshape((dp_size * group,) + qk_shape[0][1:]), (...  5.28 us
    ppermute x3, starting transfers between devices, to_dp(): lax.ppermute(x, 'dp', [(i, (i + shift) % dp_size) for i in range(dp_size)])  4.04 us
  transfers between devices with their start and end apart: 27, of which 10 were waited for; matrix products, arithmetic and copies ran while one was open for 0% of the time, Pallas kernels for 30%

profile of v10, /device:TPU:0, one launch (start us, length us, event | category | flops | bytes accessed | tf_op | source)
XLA Modules:
  0.0 117.2 jit_solution(17592931130659774324)
XLA Ops:
  2.8 3.0 %collective-permute-start = (bf16[128,2048]{1,0:T(8,128)(2,1)}, bf16[128,2048]{1,0:T(8,128)(2,1)S(1)}, u32[]{:S(2)}, u32[]{:S(2)}) collective-permute-start(bf16[128,2048]{1,0:T(8,128)(2,1)} %get-tuple-element.61), channel_id=1, source_target_pairs={{0,16},{16,0},{1,17},{17,1},{2,18},{18,2},{3,19},{19,3},{4,20},{20... | collective-permute-start | bytes 1572872 | tf_op jit(solution)/shard_map/ppermute | solution.py:468
  11.0 1.6 %collective-permute-start.2 = (bf16[2,2,128,256]{3,2,1,0:T(8,128)(2,1)}, bf16[2,2,128,256]{3,2,1,0:T(8,128)(2,1)S(1)}, u32[]{:S(2)}, u32[]{:S(2)}) collective-permute-start(bf16[2,2,128,256]{3,2,1,0:T(8,128)(2,1)} %get-tuple-element.64), channel_id=1, source_target_pairs={{0,4},{1,5},{2,6},{3,7},{4,0},{5,1},{6,2},{7,3},{8,12},{9,13},{10,... | collective-permute-start | bytes 786440 | tf_op jit(solution)/shard_map/ppermute | solution.py:472
  15.8 4.1 %collective-permute-done.1.refs_2_ = bf16[2,2,128,256]{3,2,1,0:T(8,128)(2,1)S(1)} collective-permute-done((bf16[2,2,128,256]{3,2,1,0:T(8,128)(2,1)}, bf16[2,2,128,256]{3,2,1,0:T(8,128)(2,1)S(1)}, u32[]{:S(2)}, u32[]{:S(2)}) %collective-permute-start.1) | collective-permute-done | bytes 262176 | tf_op jit(solution)/shard_map/ppermute | solution.py:472
  20.5 3.6 %collective-permute-done.3.refs_4_ = bf16[2,2,128,256]{3,2,1,0:T(8,128)(2,1)} collective-permute-done((bf16[2,2,128,256]{3,2,1,0:T(8,128)(2,1)}, bf16[2,2,128,256]{3,2,1,0:T(8,128)(2,1)}, u32[]{:S(2)}, u32[]{:S(2)}) %collective-permute-start.3) | collective-permute-done | bytes 262176 | tf_op jit(solution)/shard_map/ppermute | solution.py:472
  28.1 1.6 %shard_map.86 = (bf16[1024,512]{1,0:T(8,128)(2,1)}, f32[8,128]{1,0:T(8,128)}) custom-call(s32[1]{0:T(128)} %bitcast.5.refs_0_, bf16[2048,512]{1,0:T(8,128)(2,1)S(1)} %copy-done, f32[8,128]{1,0:T(8,128)S(1)} %get-tuple-element.77.refs_3_.refs_2_), custom_call_target="tpu_custom_call" | custom-call | tf_op jit(solution)/shard_map/pallas_call | solution.py:430
  30.2 5.3 %all-to-all-start = ((f32[16,2,2,16,128]{4,3,2,1,0:T(8,128)}), f32[16,2,2,16,128]{4,3,2,1,0:T(8,128)}, u32[]{:S(2)}, u32[]{:S(2)}) async-start(f32[16,2,2,16,128]{4,3,2,1,0:T(8,128)} %bitcast.10), calls=%async_computation | async-start | bytes 1048576 | tf_op jit(solution)/shard_map/all_to_all | solution.py:569
  40.9 1.9 %collective-permute-start.7 = (bf16[2,128,512]{2,1,0:T(8,128)(2,1)}, bf16[2,128,512]{2,1,0:T(8,128)(2,1)S(1)}, u32[]{:S(2)}, u32[]{:S(2)}) collective-permute-start(bf16[2,128,512]{2,1,0:T(8,128)(2,1)} %get-tuple-element.78), channel_id=1, source_target_pairs={{0,2},{1,3},{2,4},{3,5},{4,6},{5,7},{6,0},{7,1},{8,10},{9,11},{10,... | collective-permute-start | bytes 786440 | tf_op jit(solution)/shard_map/ppermute | solution.py:472
  46.8 12.8 %all-to-all-done = f32[16,2,2,16,128]{4,3,2,1,0:T(8,128)} async-done(((f32[16,2,2,16,128]{4,3,2,1,0:T(8,128)}), f32[16,2,2,16,128]{4,3,2,1,0:T(8,128)}, u32[]{:S(2)}, u32[]{:S(2)}) %all-to-all-start) | async-done | bytes 524320 | tf_op jit(solution)/shard_map/all_to_all | solution.py:569
  59.6 1.6 %shard_map.81 = (f32[8,2,2,16,128]{4,3,2,1,0:T(8,128)S(1)}, bf16[2,176,128]{2,1,0:T(8,128)(2,1)S(1)}, f32[8,128]{1,0:T(8,128)}) custom-call(f32[2,8,2,2,16,128]{5,4,3,2,1,0:T(8,128)} %bitcast.4.refs_0_, bf16[8,2,128,256]{3,2,1,0:T(8,128)(2,1)S(1)} %get-tuple-element.71.refs_1_.refs_2_), custom_call_target="tpu_custom_call" | custom-call | tf_op jit(solution)/shard_map/pallas_call | solution.py:430
  61.2 4.5 %collective-permute-start.5 = (bf16[2,176,128]{2,1,0:T(8,128)(2,1)S(1)}, bf16[2,176,128]{2,1,0:T(8,128)(2,1)S(1)}, u32[]{:S(2)}, u32[]{:S(2)}) collective-permute-start(bf16[2,176,128]{2,1,0:T(8,128)(2,1)S(1)} %get-tuple-element.74), channel_id=1, source_target_pairs={{0,8},{1,9},{2,10},{3,11},{4,12},{5,13},{6,14},{7,15},{16,24},{17,... | collective-permute-start | bytes 270344 | tf_op jit(solution)/shard_map/ppermute | solution.py:489
  66.2 3.6 %shard_map.82 = (f32[1024,256]{1,0:T(8,128)S(1)}, f32[8,128]{1,0:T(8,128)}) custom-call(f32[8,2,2,16,128]{4,3,2,1,0:T(8,128)S(1)} %get-tuple-element.72.refs_0_.refs_1_, bf16[8,2,128,256]{3,2,1,0:T(8,128)(2,1)S(1)} %get-tuple-element.71.refs_1_.refs_2_), custom_call_target="tpu_custom_call" | custom-call | tf_op jit(solution)/shard_map/pallas_call | solution.py:430
  69.8 2.6 %shard_map.85 = (bf16[1024,256]{1,0:T(8,128)(2,1)S(1)}, f32[1024,256]{1,0:T(8,128)S(1)}, bf16[2,176,128]{2,1,0:T(8,128)(2,1)S(1)}, f32[8,128]{1,0:T(8,128)}) custom-call(f32[8,2,2,16,128]{4,3,2,1,0:T(8,128)S(1)} %get-tuple-element.72.refs_0_.refs_1_, bf16[8,2,128,256]{3,2,1,0:T(8,128)(2,1)S(1)} %get-tuple-element.71.refs_1_.refs_2_, ...), custom_call_target="tpu_custom_call" | custom-call | tf_op jit(solution)/shard_map/pallas_call | solution.py:430
  72.4 1.6 %collective-permute-start.11 = (bf16[2,176,128]{2,1,0:T(8,128)(2,1)S(1)}, bf16[2,176,128]{2,1,0:T(8,128)(2,1)S(1)}, u32[]{:S(2)}, u32[]{:S(2)}) collective-permute-start(bf16[2,176,128]{2,1,0:T(8,128)(2,1)S(1)} %get-tuple-element.86), channel_id=1, source_target_pairs={{8,0},{9,1},{10,2},{11,3},{12,4},{13,5},{14,6},{15,7},{24,16},{25,... | collective-permute-start | bytes 270344 | tf_op jit(solution)/shard_map/ppermute | solution.py:489
  74.0 5.9 %shard_map.87 = (f32[2,2,16,1024]{3,2,1,0:T(8,128)S(1)}, f32[2,128,1024]{2,1,0:T(8,128)S(1)}, f32[8,128]{1,0:T(8,128)S(1)}) custom-call(f32[8,2,2,16,128]{4,3,2,1,0:T(8,128)S(1)} %get-tuple-element.72.refs_0_.refs_1_, bf16[8,2,128,256]{3,2,1,0:T(8,128)(2,1)S(1)} %get-tuple-element.71.refs_1_.refs_2_, f32[1024,256]{1,0:T(8,128)S(1)} %get-tuple-element.82.refs_2_, ...), custom_call_target="tpu_custom_call" | custom-call | tf_op jit(solution)/shard_map/pallas_call | solution.py:430
  81.9 2.3 %shard_map.89 = (bf16[64,1024]{1,0:T(8,128)(2,1)S(1)}, bf16[4,2,128,256]{3,2,1,0:T(8,128)(2,1)S(1)}, bf16[4,2,128,256]{3,2,1,0:T(8,128)(2,1)S(1)}, f32[8,128]{1,0:T(8,128)}) custom-call(s32[2]{0:T(128)S(1)} %pad_add_fusion.refs_0_, f32[8,2,2,16,128]{4,3,2,1,0:T(8,128)S(1)} %get-tuple-element.72.refs_0_.refs_1_, ...), custom_call_target="tpu_custom_call" | custom-call | tf_op jit(solution)/shard_map/pallas_call | solution.py:430
  84.2 2.7 %collective-permute-start.21 = (bf16[64,1024]{1,0:T(8,128)(2,1)S(1)}, bf16[64,1024]{1,0:T(8,128)(2,1)S(1)}, u32[]{:S(2)}, u32[]{:S(2)}) collective-permute-start(bf16[64,1024]{1,0:T(8,128)(2,1)S(1)} %get-tuple-element.96.refs_1_), channel_id=1, source_target_pairs={{0,6},{1,7},{2,0},{3,1},{4,2},{5,3},{6,4},{7,5},{8,14},{9,15},{10,... | collective-permute-start | bytes 393224 | tf_op jit(solution)/shard_map/ppermute | solution.py:472
  87.7 3.1 %collective-permute-done.21.refs_7_ = bf16[64,1024]{1,0:T(8,128)(2,1)S(1)} collective-permute-done((bf16[64,1024]{1,0:T(8,128)(2,1)S(1)}, bf16[64,1024]{1,0:T(8,128)(2,1)S(1)}, u32[]{:S(2)}, u32[]{:S(2)}) %collective-permute-start.21) | collective-permute-done | bytes 131104 | tf_op jit(solution)/shard_map/ppermute | solution.py:472
  90.8 3.5 %collective-permute-done.19.refs_5_ = bf16[64,1024]{1,0:T(8,128)(2,1)S(1)} collective-permute-done((bf16[64,1024]{1,0:T(8,128)(2,1)S(1)}, bf16[64,1024]{1,0:T(8,128)(2,1)S(1)}, u32[]{:S(2)}, u32[]{:S(2)}) %collective-permute-start.19) | collective-permute-done | bytes 131104 | tf_op jit(solution)/shard_map/ppermute | solution.py:472
  96.5 2.2 %shard_map.91 = (bf16[128,512]{1,0:T(8,128)(2,1)S(1)}, f32[256,512]{1,0:T(8,128)S(1)}, bf16[256,512]{1,0:T(8,128)(2,1)}, f32[8,128]{1,0:T(8,128)S(1)}) custom-call(s32[3]{0:T(128)S(1)} %pad_add_fusion.1.refs_0_, bf16[64,1024]{1,0:T(8,128)(2,1)S(1)} %get-tuple-element.96.refs_1_, bf16[64,1024]{1,0:T(8,128)(2,1)S(1)} %collective-permute-done.16.refs_2_, ...), custom_call_target="tpu_custom_call" | custom-call | tf_op jit(solution)/shard_map/pallas_call | solution.py:430
  101.9 1.6 %collective-permute-start.15 = (bf16[2,2,128,256]{3,2,1,0:T(8,128)(2,1)}, bf16[2,2,128,256]{3,2,1,0:T(8,128)(2,1)}, u32[]{:S(2)}, u32[]{:S(2)}) collective-permute-start(bf16[2,2,128,256]{3,2,1,0:T(8,128)(2,1)} %get-tuple-element.95), channel_id=1, source_target_pairs={{0,6},{1,7},{2,0},{3,1},{4,2},{5,3},{6,4},{7,5},{8,14},{9,15},{10,... | collective-permute-start | bytes 786440 | tf_op jit(solution)/shard_map/ppermute | solution.py:472
  103.5 4.0 %shard_map.92 = (bf16[1,128,4096]{2,1,0:T(8,128)(2,1)}, f32[8,128]{1,0:T(8,128)S(1)}) custom-call(s32[3]{0:T(128)S(1)} %pad_add_fusion.2.refs_0_, bf16[128,512]{1,0:T(8,128)(2,1)S(1)} %get-tuple-element.101.refs_1_, bf16[2048,512]{1,0:T(8,128)(2,1)S(1)} %copy-done, bf16[1024,512]{1,0:T(8,128)(2,1)} %collective-permute-done.10.refs_4_.refs_3_, ...), custom_call_target="tpu_custom_call" | custom-call | tf_op jit(solution)/shard_map/pallas_call | solution.py:430
  108.7 3.5 %collective-permute-start.25 = (bf16[128,512]{1,0:T(8,128)(2,1)S(1)}, bf16[128,512]{1,0:T(8,128)(2,1)S(1)}, u32[]{:S(2)}, u32[]{:S(2)}) collective-permute-start(bf16[128,512]{1,0:T(8,128)(2,1)S(1)} %get-tuple-element.109), channel_id=1, source_target_pairs={{0,8},{1,9},{2,10},{3,11},{4,12},{5,13},{6,14},{7,15},{8,0},{9,1},... | collective-permute-start | bytes 393224 | tf_op jit(solution)/shard_map/ppermute | solution.py:489
  112.2 2.2 %collective-permute-done.15.refs_4_ = bf16[2,2,128,256]{3,2,1,0:T(8,128)(2,1)} collective-permute-done((bf16[2,2,128,256]{3,2,1,0:T(8,128)(2,1)}, bf16[2,2,128,256]{3,2,1,0:T(8,128)(2,1)}, u32[]{:S(2)}, u32[]{:S(2)}) %collective-permute-start.15) | collective-permute-done | bytes 262176 | tf_op jit(solution)/shard_map/ppermute | solution.py:472
  114.4 2.0 %shard_map.94 = (bf16[1,128,2048]{2,1,0:T(8,128)(2,1)}, bf16[1,128,2048]{2,1,0:T(8,128)(2,1)}, f32[8,128]{1,0:T(8,128)S(1)}) custom-call(s32[1]{0:T(128)} %bitcast.refs_0_, bf16[2,2,128,256]{3,2,1,0:T(8,128)(2,1)S(1)} %get-tuple-element.92.refs_1_, bf16[2,2,128,256]{3,2,1,0:T(8,128)(2,1)S(1)} %collective-permute-done.13.refs_2_, ...), custom_call_target="tpu_custom_call" | custom-call | tf_op jit(solution)/shard_map/pallas_call | solution.py:430
  (78 shorter events, 35.6 us)
Async XLA Ops:
  2.8 23.1 %collective-permute-start = (bf16[128,2048]{1,0:T(8,128)(2,1)}, bf16[128,2048]{1,0:T(8,128)(2,1)S(1)}, u32[]{:S(2)}, u32[]{:S(2)}) collective-permute-start(bf16[128,2048]{1,0:T(8,128)(2,1)} %get-tuple-element.61), channel_id=1, source_target_pairs={{0,16},{16,0},{1,17},{17,1},{2,18},{18,2},{3,19},{19,3},{4,20},{20... | collective-permute-start | bytes 1572872 | tf_op jit(solution)/shard_map/ppermute | solution.py:468
  9.5 10.4 %collective-permute-start.1 = (bf16[2,2,128,256]{3,2,1,0:T(8,128)(2,1)}, bf16[2,2,128,256]{3,2,1,0:T(8,128)(2,1)S(1)}, u32[]{:S(2)}, u32[]{:S(2)}) collective-permute-start(bf16[2,2,128,256]{3,2,1,0:T(8,128)(2,1)} %get-tuple-element.63), channel_id=1, source_target_pairs={{0,2},{1,3},{2,4},{3,5},{4,6},{5,7},{6,0},{7,1},{8,10},{9,11},{10,... | collective-permute-start | bytes 786440 | tf_op jit(solution)/shard_map/ppermute | solution.py:472
  11.0 9.5 %collective-permute-start.2 = (bf16[2,2,128,256]{3,2,1,0:T(8,128)(2,1)}, bf16[2,2,128,256]{3,2,1,0:T(8,128)(2,1)S(1)}, u32[]{:S(2)}, u32[]{:S(2)}) collective-permute-start(bf16[2,2,128,256]{3,2,1,0:T(8,128)(2,1)} %get-tuple-element.64), channel_id=1, source_target_pairs={{0,4},{1,5},{2,6},{3,7},{4,0},{5,1},{6,2},{7,3},{8,12},{9,13},{10,... | collective-permute-start | bytes 786440 | tf_op jit(solution)/shard_map/ppermute | solution.py:472
  12.6 11.5 %collective-permute-start.3 = (bf16[2,2,128,256]{3,2,1,0:T(8,128)(2,1)}, bf16[2,2,128,256]{3,2,1,0:T(8,128)(2,1)}, u32[]{:S(2)}, u32[]{:S(2)}) collective-permute-start(bf16[2,2,128,256]{3,2,1,0:T(8,128)(2,1)} %get-tuple-element.65), channel_id=1, source_target_pairs={{0,6},{1,7},{2,0},{3,1},{4,2},{5,3},{6,4},{7,5},{8,14},{9,15},{10,... | collective-permute-start | bytes 786440 | tf_op jit(solution)/shard_map/ppermute | solution.py:472
  29.7 36.1 %collective-permute-start.10 = (bf16[1024,512]{1,0:T(8,128)(2,1)}, bf16[1024,512]{1,0:T(8,128)(2,1)}, u32[]{:S(2)}, u32[]{:S(2)}) collective-permute-start(bf16[1024,512]{1,0:T(8,128)(2,1)} %get-tuple-element.83), channel_id=1, source_target_pairs={{0,16},{16,0},{1,17},{17,1},{2,18},{18,2},{3,19},{19,3},{4,20},{20... | collective-permute-start | bytes 3145736 | tf_op jit(solution)/shard_map/ppermute | solution.py:468
  30.2 29.4 %all-to-all-start = ((f32[16,2,2,16,128]{4,3,2,1,0:T(8,128)}), f32[16,2,2,16,128]{4,3,2,1,0:T(8,128)}, u32[]{:S(2)}, u32[]{:S(2)}) async-start(f32[16,2,2,16,128]{4,3,2,1,0:T(8,128)} %bitcast.10), calls=%async_computation | async-start | bytes 1048576 | tf_op jit(solution)/shard_map/all_to_all | solution.py:569
  37.2 8.5 %collective-permute-start.4 = (bf16[4,2,128,256]{3,2,1,0:T(8,128)(2,1)}, bf16[4,2,128,256]{3,2,1,0:T(8,128)(2,1)S(1)}, u32[]{:S(2)}, u32[]{:S(2)}) collective-permute-start(bf16[4,2,128,256]{3,2,1,0:T(8,128)(2,1)} %copy-done.11), channel_id=1, source_target_pairs={{0,1},{1,0},{2,3},{3,2},{4,5},{5,4},{6,7},{7,6},{8,9},{9,8},{10,11... | collective-permute-start | bytes 1572872 | tf_op jit(solution)/shard_map/ppermute | solution.py:481
  40.9 28.9 %collective-permute-start.7 = (bf16[2,128,512]{2,1,0:T(8,128)(2,1)}, bf16[2,128,512]{2,1,0:T(8,128)(2,1)S(1)}, u32[]{:S(2)}, u32[]{:S(2)}) collective-permute-start(bf16[2,128,512]{2,1,0:T(8,128)(2,1)} %get-tuple-element.78), channel_id=1, source_target_pairs={{0,2},{1,3},{2,4},{3,5},{4,6},{5,7},{6,0},{7,1},{8,10},{9,11},{10,... | collective-permute-start | bytes 786440 | tf_op jit(solution)/shard_map/ppermute | solution.py:472
  42.8 27.0 %collective-permute-start.8 = (bf16[2,128,512]{2,1,0:T(8,128)(2,1)}, bf16[2,128,512]{2,1,0:T(8,128)(2,1)}, u32[]{:S(2)}, u32[]{:S(2)}) collective-permute-start(bf16[2,128,512]{2,1,0:T(8,128)(2,1)} %get-tuple-element.79), channel_id=1, source_target_pairs={{0,4},{1,5},{2,6},{3,7},{4,0},{5,1},{6,2},{7,3},{8,12},{9,13},{10,... | collective-permute-start | bytes 786440 | tf_op jit(solution)/shard_map/ppermute | solution.py:472
  44.2 25.6 %collective-permute-start.9 = (bf16[2,128,512]{2,1,0:T(8,128)(2,1)}, bf16[2,128,512]{2,1,0:T(8,128)(2,1)}, u32[]{:S(2)}, u32[]{:S(2)}) collective-permute-start(bf16[2,128,512]{2,1,0:T(8,128)(2,1)} %get-tuple-element.80), channel_id=1, source_target_pairs={{0,6},{1,7},{2,0},{3,1},{4,2},{5,3},{6,4},{7,5},{8,14},{9,15},{10,... | collective-permute-start | bytes 786440 | tf_op jit(solution)/shard_map/ppermute | solution.py:472
  61.2 8.6 %collective-permute-start.5 = (bf16[2,176,128]{2,1,0:T(8,128)(2,1)S(1)}, bf16[2,176,128]{2,1,0:T(8,128)(2,1)S(1)}, u32[]{:S(2)}, u32[]{:S(2)}) collective-permute-start(bf16[2,176,128]{2,1,0:T(8,128)(2,1)S(1)} %get-tuple-element.74), channel_id=1, source_target_pairs={{0,8},{1,9},{2,10},{3,11},{4,12},{5,13},{6,14},{7,15},{16,24},{17,... | collective-permute-start | bytes 270344 | tf_op jit(solution)/shard_map/ppermute | solution.py:489
  65.7 37.8 %collective-permute-start.24 = (bf16[1024,512]{1,0:T(8,128)(2,1)}, bf16[1024,512]{1,0:T(8,128)(2,1)}, u32[]{:S(2)}, u32[]{:S(2)}) collective-permute-start(bf16[1024,512]{1,0:T(8,128)(2,1)} %collective-permute-done.10.refs_4_.refs_3_), channel_id=1, source_target_pairs={{0,1},{1,0},{2,3},{3,2},{4,5},{5,4},{6,7},{7,6},{8,9},{9,8},{10,11... | collective-permute-start | bytes 3145736 | tf_op jit(solution)/shard_map/ppermute | solution.py:598
  72.4 9.5 %collective-permute-start.11 = (bf16[2,176,128]{2,1,0:T(8,128)(2,1)S(1)}, bf16[2,176,128]{2,1,0:T(8,128)(2,1)S(1)}, u32[]{:S(2)}, u32[]{:S(2)}) collective-permute-start(bf16[2,176,128]{2,1,0:T(8,128)(2,1)S(1)} %get-tuple-element.86), channel_id=1, source_target_pairs={{8,0},{9,1},{10,2},{11,3},{12,4},{13,5},{14,6},{15,7},{24,16},{25,... | collective-permute-start | bytes 270344 | tf_op jit(solution)/shard_map/ppermute | solution.py:489
  84.2 10.6 %collective-permute-start.12 = (bf16[4,2,128,256]{3,2,1,0:T(8,128)(2,1)S(1)}, bf16[4,2,128,256]{3,2,1,0:T(8,128)(2,1)S(1)}, u32[]{:S(2)}, u32[]{:S(2)}) collective-permute-start(bf16[4,2,128,256]{3,2,1,0:T(8,128)(2,1)S(1)} %get-tuple-element.91), channel_id=1, source_target_pairs={{0,1},{1,0},{2,3},{3,2},{4,5},{5,4},{6,7},{7,6},{8,9},{9,8},{10,11... | collective-permute-start | bytes 1572872 | tf_op jit(solution)/shard_map/ppermute | solution.py:481
  84.2 6.6 %collective-permute-start.21 = (bf16[64,1024]{1,0:T(8,128)(2,1)S(1)}, bf16[64,1024]{1,0:T(8,128)(2,1)S(1)}, u32[]{:S(2)}, u32[]{:S(2)}) collective-permute-start(bf16[64,1024]{1,0:T(8,128)(2,1)S(1)} %get-tuple-element.96.refs_1_), channel_id=1, source_target_pairs={{0,6},{1,7},{2,0},{3,1},{4,2},{5,3},{6,4},{7,5},{8,14},{9,15},{10,... | collective-permute-start | bytes 393224 | tf_op jit(solution)/shard_map/ppermute | solution.py:472
  86.9 7.4 %collective-permute-start.19 = (bf16[64,1024]{1,0:T(8,128)(2,1)S(1)}, bf16[64,1024]{1,0:T(8,128)(2,1)S(1)}, u32[]{:S(2)}, u32[]{:S(2)}) collective-permute-start(bf16[64,1024]{1,0:T(8,128)(2,1)S(1)} %get-tuple-element.96.refs_1_), channel_id=1, source_target_pairs={{0,4},{1,5},{2,6},{3,7},{4,0},{5,1},{6,2},{7,3},{8,12},{9,13},{10,... | collective-permute-start | bytes 393224 | tf_op jit(solution)/shard_map/ppermute | solution.py:472
  87.6 6.7 %collective-permute-start.17 = (bf16[64,1024]{1,0:T(8,128)(2,1)S(1)}, bf16[64,1024]{1,0:T(8,128)(2,1)S(1)}, u32[]{:S(2)}, u32[]{:S(2)}) collective-permute-start(bf16[64,1024]{1,0:T(8,128)(2,1)S(1)} %get-tuple-element.96.refs_1_), channel_id=1, source_target_pairs={{0,2},{1,3},{2,4},{3,5},{4,6},{5,7},{6,0},{7,1},{8,10},{9,11},{10,... | collective-permute-start | bytes 393224 | tf_op jit(solution)/shard_map/ppermute | solution.py:472
  90.8 5.7 %collective-permute-start.16 = (bf16[64,1024]{1,0:T(8,128)(2,1)S(1)}, bf16[64,1024]{1,0:T(8,128)(2,1)S(1)}, u32[]{:S(2)}, u32[]{:S(2)}) collective-permute-start(bf16[64,1024]{1,0:T(8,128)(2,1)S(1)} %get-tuple-element.96.refs_1_), channel_id=1, source_target_pairs={{0,1},{1,0},{2,3},{3,2},{4,5},{5,4},{6,7},{7,6},{8,9},{9,8},{10,11... | collective-permute-start | bytes 393224 | tf_op jit(solution)/shard_map/ppermute | solution.py:481
  94.3 2.1 %collective-permute-start.22 = (bf16[64,1024]{1,0:T(8,128)(2,1)S(1)}, bf16[64,1024]{1,0:T(8,128)(2,1)S(1)}, u32[]{:S(2)}, u32[]{:S(2)}) collective-permute-start(bf16[64,1024]{1,0:T(8,128)(2,1)S(1)} %collective-permute-done.21.refs_7_), channel_id=1, source_target_pairs={{0,1},{1,0},{2,3},{3,2},{4,5},{5,4},{6,7},{7,6},{8,9},{9,8},{10,11... | collective-permute-start | bytes 393224 | tf_op jit(solution)/shard_map/ppermute | solution.py:481
  98.7 9.0 %collective-permute-start.23 = (bf16[256,512]{1,0:T(8,128)(2,1)}, bf16[256,512]{1,0:T(8,128)(2,1)}, u32[]{:S(2)}, u32[]{:S(2)}) collective-permute-start(bf16[256,512]{1,0:T(8,128)(2,1)} %get-tuple-element.100), channel_id=1, source_target_pairs={{0,16},{16,0},{1,17},{17,1},{2,18},{18,2},{3,19},{19,3},{4,20},{20... | collective-permute-start | bytes 786440 | tf_op jit(solution)/shard_map/ppermute | solution.py:468
  99.2 13.0 %collective-permute-start.13 = (bf16[2,2,128,256]{3,2,1,0:T(8,128)(2,1)}, bf16[2,2,128,256]{3,2,1,0:T(8,128)(2,1)S(1)}, u32[]{:S(2)}, u32[]{:S(2)}) collective-permute-start(bf16[2,2,128,256]{3,2,1,0:T(8,128)(2,1)} %get-tuple-element.93), channel_id=1, source_target_pairs={{0,2},{1,3},{2,4},{3,5},{4,6},{5,7},{6,0},{7,1},{8,10},{9,11},{10,... | collective-permute-start | bytes 786440 | tf_op jit(solution)/shard_map/ppermute | solution.py:472
  100.6 11.7 %collective-permute-start.14 = (bf16[2,2,128,256]{3,2,1,0:T(8,128)(2,1)}, bf16[2,2,128,256]{3,2,1,0:T(8,128)(2,1)S(1)}, u32[]{:S(2)}, u32[]{:S(2)}) collective-permute-start(bf16[2,2,128,256]{3,2,1,0:T(8,128)(2,1)} %get-tuple-element.94), channel_id=1, source_target_pairs={{0,4},{1,5},{2,6},{3,7},{4,0},{5,1},{6,2},{7,3},{8,12},{9,13},{10,... | collective-permute-start | bytes 786440 | tf_op jit(solution)/shard_map/ppermute | solution.py:472
  101.9 12.5 %collective-permute-start.15 = (bf16[2,2,128,256]{3,2,1,0:T(8,128)(2,1)}, bf16[2,2,128,256]{3,2,1,0:T(8,128)(2,1)}, u32[]{:S(2)}, u32[]{:S(2)}) collective-permute-start(bf16[2,2,128,256]{3,2,1,0:T(8,128)(2,1)} %get-tuple-element.95), channel_id=1, source_target_pairs={{0,6},{1,7},{2,0},{3,1},{4,2},{5,3},{6,4},{7,5},{8,14},{9,15},{10,... | collective-permute-start | bytes 786440 | tf_op jit(solution)/shard_map/ppermute | solution.py:472
  108.7 7.7 %collective-permute-start.25 = (bf16[128,512]{1,0:T(8,128)(2,1)S(1)}, bf16[128,512]{1,0:T(8,128)(2,1)S(1)}, u32[]{:S(2)}, u32[]{:S(2)}) collective-permute-start(bf16[128,512]{1,0:T(8,128)(2,1)S(1)} %get-tuple-element.109), channel_id=1, source_target_pairs={{0,8},{1,9},{2,10},{3,11},{4,12},{5,13},{6,14},{7,15},{8,0},{9,1},... | collective-permute-start | bytes 393224 | tf_op jit(solution)/shard_map/ppermute | solution.py:489
  (15 other events, 52.0 us)

commit v11 on v10

--- a/solution.py
+++ b/solution.py
@@ -511,10 +511,11 @@
         scalars=(chip_at, core_at),
         after=(token,),
     )
-    (keep, send), heads_token = call(
+    heads_parts = [to_chip(part, shift) for shift, part in enumerate(parts)]
+    (keep, send), _ = call(
         split_cores_kernel,
         [((chips, 2, tok, heads * DH), bf16)] * 2,
-        *[to_chip(part, shift) for shift, part in enumerate(parts)],
+        *heads_parts,
         scalars=(chip_at, core_at),
     )
     (vg,), _ = call(
@@ -542,7 +543,8 @@
         proj_weight,
         *arrived,
         scalars=(dp_at,),
-        after=(heads_token, token),
+        after=(token,),
+        after_far=heads_parts[1:],
     )
     part_shape = (tok, dp_size * runs * depth)
     if depth % 128 == 0:
@@ -575,6 +577,12 @@
         axis_index_groups=wide_groups,
     ).reshape(projected.shape)
 
+    (qk, *state), token = call(
+        functools.partial(state_kernel, with_state),
+        [qk_shape] + [state_shape] * with_state,
+        qk_parts,
+        vg,
+    )
     pair = 2 if ctx_size % 2 == 0 else 1
     parity = ctx_at % pair
     piece = share // pair
@@ -598,12 +606,6 @@
             weights.append(lax.ppermute(half, "ctx", [(i, i ^ 1) for i in range(ctx_size)]))
             firsts.append(base + (1 - parity) * piece)
 
-    (qk, *state), token = call(
-        functools.partial(state_kernel, with_state),
-        [qk_shape] + [state_shape] * with_state,
-        qk_parts,
-        vg,
-    )
     prefix, suffix = (), ()
     if with_state:
         prefix = [to_run(state[0], shift, False) for shift in range(1, runs)]
@@ -626,7 +628,6 @@
         vg,
         grad_num,
         *prefix,
-        after_far=fetched,
     )
     (token_cols,), token = call(
         collect_tokens_kernel,
@@ -634,6 +635,7 @@
         *token_parts,
         scalars=(chip_at,),
         after=(token,),
+        after_far=fetched,
     )
     (rows, keep, send), token = call(
         functools.partial(rows_kernel, with_state),

time: 120 us -> 120 us (level)
  the two profiles are of different devices: /device:TPU:0 before, /device:TPU:4 now
where the time goes in v11:
time: 120 us
  waiting for transfers between devices  42.5 us (35%)
  Pallas kernels  36.2 us (30%)
  starting transfers between devices  29.2 us (24%)
  local copies, waits for them, and re-layouts  10.8 us (9%)
    pallas_call x21, Pallas kernels, call(): pl.pallas_call(kernel, out_shape=[jax.ShapeDtypeStruct(shape, kind) for s...  36.2 us
    ppermute x12, waiting for transfers between devices, to_member(): return lax.ppermute(x, 'ctx', pairs)  24.5 us
    ppermute x3, waiting for transfers between devices, to_dp(): lax.ppermute(x, 'dp', [(i, (i + shift) % dp_size) for i in range(dp_size)])  12.2 us
    ppermute x12, starting transfers between devices, to_member(): return lax.ppermute(x, 'ctx', pairs)  11.5 us
    unnamed x26, local copies, waits for them, and re-layouts  10.8 us
    ppermute x3, starting transfers between devices, to_run(): return lax.ppermute(x, 'ctx', pairs)  8.1 us
    ppermute x3, starting transfers between devices, to_dp(): lax.ppermute(x, 'dp', [(i, (i + shift) % dp_size) for i in range(dp_size)])  4.55 us
    all_to_all x1, starting transfers between devices, local(): lax.all_to_all(projected.reshape((dp_size * group,) + qk_shape[0][1:]), (...  4.33 us
  transfers between devices with their start and end apart: 27, of which 13 were waited for; matrix products, arithmetic and copies ran while one was open for 0% of the time, Pallas kernels for 27%

profile of v11, /device:TPU:4, one launch (start us, length us, event | category | flops | bytes accessed | tf_op | source)
XLA Modules:
  0.0 119.8 jit_solution(919576428842979253)
XLA Ops:
  2.8 1.6 %collective-permute-start = (bf16[128,2048]{1,0:T(8,128)(2,1)}, bf16[128,2048]{1,0:T(8,128)(2,1)S(1)}, u32[]{:S(2)}, u32[]{:S(2)}) collective-permute-start(bf16[128,2048]{1,0:T(8,128)(2,1)} %get-tuple-element.61), channel_id=1, source_target_pairs={{0,16},{16,0},{1,17},{17,1},{2,18},{18,2},{3,19},{19,3},{4,20},{20... | collective-permute-start | bytes 1572872 | tf_op jit(solution)/shard_map/ppermute | solution.py:468
  9.9 1.6 %collective-permute-start.3 = (bf16[2,2,128,256]{3,2,1,0:T(8,128)(2,1)S(1)}, bf16[2,2,128,256]{3,2,1,0:T(8,128)(2,1)S(1)}, u32[]{:S(2)}, u32[]{:S(2)}) collective-permute-start(bf16[2,2,128,256]{3,2,1,0:T(8,128)(2,1)S(1)} %get-tuple-element.65), channel_id=1, source_target_pairs={{0,6},{1,7},{2,0},{3,1},{4,2},{5,3},{6,4},{7,5},{8,14},{9,15},{10,... | collective-permute-start | bytes 786440 | tf_op jit(solution)/shard_map/ppermute | solution.py:472
  13.4 2.9 %collective-permute-done.1.refs_5_.refs_2_ = bf16[2,2,128,256]{3,2,1,0:T(8,128)(2,1)S(1)} collective-permute-done((bf16[2,2,128,256]{3,2,1,0:T(8,128)(2,1)S(1)}, bf16[2,2,128,256]{3,2,1,0:T(8,128)(2,1)S(1)}, u32[]{:S(2)}, u32[]{:S(2)}) %collective-permute-start.1) | collective-permute-done | bytes 262176 | tf_op jit(solution)/shard_map/ppermute | solution.py:472
  16.3 5.0 %collective-permute-done.2.refs_6_.refs_3_ = bf16[2,2,128,256]{3,2,1,0:T(8,128)(2,1)S(1)} collective-permute-done((bf16[2,2,128,256]{3,2,1,0:T(8,128)(2,1)S(1)}, bf16[2,2,128,256]{3,2,1,0:T(8,128)(2,1)S(1)}, u32[]{:S(2)}, u32[]{:S(2)}) %collective-permute-start.2) | collective-permute-done | bytes 262176 | tf_op jit(solution)/shard_map/ppermute | solution.py:472
  23.9 4.3 %all-to-all-start = ((f32[16,2,2,16,128]{4,3,2,1,0:T(8,128)}), f32[16,2,2,16,128]{4,3,2,1,0:T(8,128)}, u32[]{:S(2)}, u32[]{:S(2)}) async-start(f32[16,2,2,16,128]{4,3,2,1,0:T(8,128)} %bitcast.10), calls=%async_computation | async-start | bytes 1048576 | tf_op jit(solution)/shard_map/all_to_all | solution.py:571
  31.5 2.0 %collective-permute-done.4.refs_2_ = bf16[4,2,128,256]{3,2,1,0:T(8,128)(2,1)S(1)} collective-permute-done((bf16[4,2,128,256]{3,2,1,0:T(8,128)(2,1)}, bf16[4,2,128,256]{3,2,1,0:T(8,128)(2,1)S(1)}, u32[]{:S(2)}, u32[]{:S(2)}) %collective-permute-start.4) | collective-permute-done | bytes 524320 | tf_op jit(solution)/shard_map/ppermute | solution.py:481
  37.5 1.7 %shard_map.81 = (f32[8,2,2,16,128]{4,3,2,1,0:T(8,128)S(1)}, bf16[2,176,128]{2,1,0:T(8,128)(2,1)S(1)}, f32[8,128]{1,0:T(8,128)S(1)}) custom-call(f32[2,8,2,2,16,128]{5,4,3,2,1,0:T(8,128)} %bitcast.4.refs_0_, bf16[8,2,128,256]{3,2,1,0:T(8,128)(2,1)S(1)} %get-tuple-element.70.refs_1_.refs_2_), custom_call_target="tpu_custom_call" | custom-call | tf_op jit(solution)/shard_map/pallas_call | solution.py:430
  42.7 1.9 %collective-permute-done.6.refs_2_ = bf16[4,128,512]{2,1,0:T(8,128)(2,1)S(1)} collective-permute-done((bf16[4,128,512]{2,1,0:T(8,128)(2,1)S(1)}, bf16[4,128,512]{2,1,0:T(8,128)(2,1)S(1)}, u32[]{:S(2)}, u32[]{:S(2)}) %collective-permute-start.6) | collective-permute-done | bytes 524320 | tf_op jit(solution)/shard_map/ppermute | solution.py:481
  49.3 4.5 %collective-permute-start.5 = (bf16[2,176,128]{2,1,0:T(8,128)(2,1)S(1)}, bf16[2,176,128]{2,1,0:T(8,128)(2,1)S(1)}, u32[]{:S(2)}, u32[]{:S(2)}) collective-permute-start(bf16[2,176,128]{2,1,0:T(8,128)(2,1)S(1)} %get-tuple-element.73), channel_id=1, source_target_pairs={{0,8},{1,9},{2,10},{3,11},{4,12},{5,13},{6,14},{7,15},{16,24},{17,... | collective-permute-start | bytes 270344 | tf_op jit(solution)/shard_map/ppermute | solution.py:489
  53.8 11.5 %collective-permute-done.11.refs_6_.refs_3_ = bf16[1024,512]{1,0:T(8,128)(2,1)} collective-permute-done((bf16[1024,512]{1,0:T(8,128)(2,1)S(1)}, bf16[1024,512]{1,0:T(8,128)(2,1)}, u32[]{:S(2)}, u32[]{:S(2)}) %collective-permute-start.11) | collective-permute-done | bytes 1048608 | tf_op jit(solution)/shard_map/ppermute | solution.py:468
  65.3 3.6 %shard_map.82 = (f32[1024,256]{1,0:T(8,128)S(1)}, f32[8,128]{1,0:T(8,128)}) custom-call(f32[8,2,2,16,128]{4,3,2,1,0:T(8,128)S(1)} %get-tuple-element.71.refs_0_.refs_1_, bf16[8,2,128,256]{3,2,1,0:T(8,128)(2,1)S(1)} %get-tuple-element.70.refs_1_.refs_2_), custom_call_target="tpu_custom_call" | custom-call | tf_op jit(solution)/shard_map/pallas_call | solution.py:430
  68.9 2.6 %shard_map.85 = (bf16[1024,256]{1,0:T(8,128)(2,1)S(1)}, f32[1024,256]{1,0:T(8,128)S(1)}, bf16[2,176,128]{2,1,0:T(8,128)(2,1)S(1)}, f32[8,128]{1,0:T(8,128)}) custom-call(f32[8,2,2,16,128]{4,3,2,1,0:T(8,128)S(1)} %get-tuple-element.71.refs_0_.refs_1_, bf16[8,2,128,256]{3,2,1,0:T(8,128)(2,1)S(1)} %get-tuple-element.70.refs_1_.refs_2_, ...), custom_call_target="tpu_custom_call" | custom-call | tf_op jit(solution)/shard_map/pallas_call | solution.py:430
  73.0 5.9 %shard_map.86 = (f32[2,2,16,1024]{3,2,1,0:T(8,128)S(1)}, f32[2,128,1024]{2,1,0:T(8,128)S(1)}, f32[8,128]{1,0:T(8,128)S(1)}) custom-call(f32[8,2,2,16,128]{4,3,2,1,0:T(8,128)S(1)} %get-tuple-element.71.refs_0_.refs_1_, bf16[8,2,128,256]{3,2,1,0:T(8,128)(2,1)S(1)} %get-tuple-element.70.refs_1_.refs_2_, f32[1024,256]{1,0:T(8,128)S(1)} %get-tuple-element.81.refs_2_, ...), custom_call_target="tpu_custom_call" | custom-call | tf_op jit(solution)/shard_map/pallas_call | solution.py:430
  79.3 2.0 %collective-permute-done.10.refs_6_ = bf16[2,176,128]{2,1,0:T(8,128)(2,1)S(1)} collective-permute-done((bf16[2,176,128]{2,1,0:T(8,128)(2,1)S(1)}, bf16[2,176,128]{2,1,0:T(8,128)(2,1)S(1)}, u32[]{:S(2)}, u32[]{:S(2)}) %collective-permute-start.10) | collective-permute-done | bytes 90144 | tf_op jit(solution)/shard_map/ppermute | solution.py:489
  81.2 2.3 %shard_map.89 = (bf16[64,1024]{1,0:T(8,128)(2,1)S(1)}, bf16[4,2,128,256]{3,2,1,0:T(8,128)(2,1)S(1)}, bf16[4,2,128,256]{3,2,1,0:T(8,128)(2,1)S(1)}, f32[8,128]{1,0:T(8,128)}) custom-call(s32[2]{0:T(128)S(1)} %pad_add_fusion.refs_0_, f32[8,2,2,16,128]{4,3,2,1,0:T(8,128)S(1)} %get-tuple-element.71.refs_0_.refs_1_, ...), custom_call_target="tpu_custom_call" | custom-call | tf_op jit(solution)/shard_map/pallas_call | solution.py:430
  83.5 2.1 %collective-permute-start.19 = (bf16[64,1024]{1,0:T(8,128)(2,1)S(1)}, bf16[64,1024]{1,0:T(8,128)(2,1)S(1)}, u32[]{:S(2)}, u32[]{:S(2)}) collective-permute-start(bf16[64,1024]{1,0:T(8,128)(2,1)S(1)} %get-tuple-element.96.refs_1_), channel_id=1, source_target_pairs={{0,4},{1,5},{2,6},{3,7},{4,0},{5,1},{6,2},{7,3},{8,12},{9,13},{10,... | collective-permute-start | bytes 393224 | tf_op jit(solution)/shard_map/ppermute | solution.py:472
  85.6 3.8 %collective-permute-done.17.refs_3_ = bf16[64,1024]{1,0:T(8,128)(2,1)S(1)} collective-permute-done((bf16[64,1024]{1,0:T(8,128)(2,1)S(1)}, bf16[64,1024]{1,0:T(8,128)(2,1)S(1)}, u32[]{:S(2)}, u32[]{:S(2)}) %collective-permute-start.17) | collective-permute-done | bytes 131104 | tf_op jit(solution)/shard_map/ppermute | solution.py:472
  89.4 2.9 %collective-permute-done.19.refs_5_ = bf16[64,1024]{1,0:T(8,128)(2,1)S(1)} collective-permute-done((bf16[64,1024]{1,0:T(8,128)(2,1)S(1)}, bf16[64,1024]{1,0:T(8,128)(2,1)S(1)}, u32[]{:S(2)}, u32[]{:S(2)}) %collective-permute-start.19) | collective-permute-done | bytes 131104 | tf_op jit(solution)/shard_map/ppermute | solution.py:472
  95.5 2.2 %shard_map.91 = (bf16[128,512]{1,0:T(8,128)(2,1)S(1)}, f32[256,512]{1,0:T(8,128)S(1)}, bf16[256,512]{1,0:T(8,128)(2,1)}, f32[8,128]{1,0:T(8,128)S(1)}) custom-call(s32[3]{0:T(128)S(1)} %pad_add_fusion.1.refs_0_, bf16[64,1024]{1,0:T(8,128)(2,1)S(1)} %get-tuple-element.96.refs_1_, bf16[64,1024]{1,0:T(8,128)(2,1)S(1)} %collective-permute-done.16.refs_2_, ...), custom_call_target="tpu_custom_call" | custom-call | tf_op jit(solution)/shard_map/pallas_call | solution.py:430
  99.2 1.7 %collective-permute-start.14 = (bf16[2,2,128,256]{3,2,1,0:T(8,128)(2,1)}, bf16[2,2,128,256]{3,2,1,0:T(8,128)(2,1)S(1)}, u32[]{:S(2)}, u32[]{:S(2)}) collective-permute-start(bf16[2,2,128,256]{3,2,1,0:T(8,128)(2,1)} %get-tuple-element.94), channel_id=1, source_target_pairs={{0,4},{1,5},{2,6},{3,7},{4,0},{5,1},{6,2},{7,3},{8,12},{9,13},{10,... | collective-permute-start | bytes 786440 | tf_op jit(solution)/shard_map/ppermute | solution.py:472
  101.6 4.0 %shard_map.92 = (bf16[1,128,4096]{2,1,0:T(8,128)(2,1)}, f32[8,128]{1,0:T(8,128)S(1)}) custom-call(s32[3]{0:T(128)S(1)} %pad_add_fusion.2.refs_0_, bf16[128,512]{1,0:T(8,128)(2,1)S(1)} %get-tuple-element.101.refs_1_, bf16[2048,512]{1,0:T(8,128)(2,1)S(1)} %copy-done, bf16[1024,512]{1,0:T(8,128)(2,1)} %collective-permute-done.11.refs_6_.refs_3_, ...), custom_call_target="tpu_custom_call" | custom-call | tf_op jit(solution)/shard_map/pallas_call | solution.py:430
  107.3 2.2 %collective-permute-start.25 = (bf16[128,512]{1,0:T(8,128)(2,1)S(1)}, bf16[128,512]{1,0:T(8,128)(2,1)S(1)}, u32[]{:S(2)}, u32[]{:S(2)}) collective-permute-start(bf16[128,512]{1,0:T(8,128)(2,1)S(1)} %get-tuple-element.109), channel_id=1, source_target_pairs={{0,8},{1,9},{2,10},{3,11},{4,12},{5,13},{6,14},{7,15},{8,0},{9,1},... | collective-permute-start | bytes 393224 | tf_op jit(solution)/shard_map/ppermute | solution.py:489
  109.5 6.1 %collective-permute-done.14.refs_3_ = bf16[2,2,128,256]{3,2,1,0:T(8,128)(2,1)S(1)} collective-permute-done((bf16[2,2,128,256]{3,2,1,0:T(8,128)(2,1)}, bf16[2,2,128,256]{3,2,1,0:T(8,128)(2,1)S(1)}, u32[]{:S(2)}, u32[]{:S(2)}) %collective-permute-start.14) | collective-permute-done | bytes 262176 | tf_op jit(solution)/shard_map/ppermute | solution.py:472
  117.0 2.0 %shard_map.94 = (bf16[1,128,2048]{2,1,0:T(8,128)(2,1)}, bf16[1,128,2048]{2,1,0:T(8,128)(2,1)}, f32[8,128]{1,0:T(8,128)S(1)}) custom-call(s32[1]{0:T(128)} %bitcast.refs_0_, bf16[2,2,128,256]{3,2,1,0:T(8,128)(2,1)S(1)} %get-tuple-element.92.refs_1_, bf16[2,2,128,256]{3,2,1,0:T(8,128)(2,1)S(1)} %collective-permute-done.13.refs_2_, ...), custom_call_target="tpu_custom_call" | custom-call | tf_op jit(solution)/shard_map/pallas_call | solution.py:430
  (80 shorter events, 38.6 us)
Async XLA Ops:
  2.8 19.7 %collective-permute-start = (bf16[128,2048]{1,0:T(8,128)(2,1)}, bf16[128,2048]{1,0:T(8,128)(2,1)S(1)}, u32[]{:S(2)}, u32[]{:S(2)}) collective-permute-start(bf16[128,2048]{1,0:T(8,128)(2,1)} %get-tuple-element.61), channel_id=1, source_target_pairs={{0,16},{16,0},{1,17},{17,1},{2,18},{18,2},{3,19},{19,3},{4,20},{20... | collective-permute-start | bytes 1572872 | tf_op jit(solution)/shard_map/ppermute | solution.py:468
  7.9 8.3 %collective-permute-start.1 = (bf16[2,2,128,256]{3,2,1,0:T(8,128)(2,1)S(1)}, bf16[2,2,128,256]{3,2,1,0:T(8,128)(2,1)S(1)}, u32[]{:S(2)}, u32[]{:S(2)}) collective-permute-start(bf16[2,2,128,256]{3,2,1,0:T(8,128)(2,1)S(1)} %get-tuple-element.63), channel_id=1, source_target_pairs={{0,2},{1,3},{2,4},{3,5},{4,6},{5,7},{6,0},{7,1},{8,10},{9,11},{10,... | collective-permute-start | bytes 786440 | tf_op jit(solution)/shard_map/ppermute | solution.py:472
  9.5 11.8 %collective-permute-start.2 = (bf16[2,2,128,256]{3,2,1,0:T(8,128)(2,1)S(1)}, bf16[2,2,128,256]{3,2,1,0:T(8,128)(2,1)S(1)}, u32[]{:S(2)}, u32[]{:S(2)}) collective-permute-start(bf16[2,2,128,256]{3,2,1,0:T(8,128)(2,1)S(1)} %get-tuple-element.64), channel_id=1, source_target_pairs={{0,4},{1,5},{2,6},{3,7},{4,0},{5,1},{6,2},{7,3},{8,12},{9,13},{10,... | collective-permute-start | bytes 786440 | tf_op jit(solution)/shard_map/ppermute | solution.py:472
  9.9 12.6 %collective-permute-start.3 = (bf16[2,2,128,256]{3,2,1,0:T(8,128)(2,1)S(1)}, bf16[2,2,128,256]{3,2,1,0:T(8,128)(2,1)S(1)}, u32[]{:S(2)}, u32[]{:S(2)}) collective-permute-start(bf16[2,2,128,256]{3,2,1,0:T(8,128)(2,1)S(1)} %get-tuple-element.65), channel_id=1, source_target_pairs={{0,6},{1,7},{2,0},{3,1},{4,2},{5,3},{6,4},{7,5},{8,14},{9,15},{10,... | collective-permute-start | bytes 786440 | tf_op jit(solution)/shard_map/ppermute | solution.py:472
  23.9 13.6 %all-to-all-start = ((f32[16,2,2,16,128]{4,3,2,1,0:T(8,128)}), f32[16,2,2,16,128]{4,3,2,1,0:T(8,128)}, u32[]{:S(2)}, u32[]{:S(2)}) async-start(f32[16,2,2,16,128]{4,3,2,1,0:T(8,128)} %bitcast.10), calls=%async_computation | async-start | bytes 1048576 | tf_op jit(solution)/shard_map/all_to_all | solution.py:571
  31.3 2.1 %collective-permute-start.4 = (bf16[4,2,128,256]{3,2,1,0:T(8,128)(2,1)}, bf16[4,2,128,256]{3,2,1,0:T(8,128)(2,1)S(1)}, u32[]{:S(2)}, u32[]{:S(2)}) collective-permute-start(bf16[4,2,128,256]{3,2,1,0:T(8,128)(2,1)} %get-tuple-element.69), channel_id=1, source_target_pairs={{0,1},{1,0},{2,3},{3,2},{4,5},{5,4},{6,7},{7,6},{8,9},{9,8},{10,11... | collective-permute-start | bytes 1572872 | tf_op jit(solution)/shard_map/ppermute | solution.py:481
  39.9 25.4 %collective-permute-start.11 = (bf16[1024,512]{1,0:T(8,128)(2,1)S(1)}, bf16[1024,512]{1,0:T(8,128)(2,1)}, u32[]{:S(2)}, u32[]{:S(2)}) collective-permute-start(bf16[1024,512]{1,0:T(8,128)(2,1)S(1)} %get-tuple-element.88), channel_id=1, source_target_pairs={{0,16},{16,0},{1,17},{17,1},{2,18},{18,2},{3,19},{19,3},{4,20},{20... | collective-permute-start | bytes 3145736 | tf_op jit(solution)/shard_map/ppermute | solution.py:468
  45.8 23.1 %collective-permute-start.7 = (bf16[2,128,512]{2,1,0:T(8,128)(2,1)S(1)}, bf16[2,128,512]{2,1,0:T(8,128)(2,1)S(1)}, u32[]{:S(2)}, u32[]{:S(2)}) collective-permute-start(bf16[2,128,512]{2,1,0:T(8,128)(2,1)S(1)} %get-tuple-element.77), channel_id=1, source_target_pairs={{0,2},{1,3},{2,4},{3,5},{4,6},{5,7},{6,0},{7,1},{8,10},{9,11},{10,... | collective-permute-start | bytes 786440 | tf_op jit(solution)/shard_map/ppermute | solution.py:472
  47.2 21.6 %collective-permute-start.8 = (bf16[2,128,512]{2,1,0:T(8,128)(2,1)S(1)}, bf16[2,128,512]{2,1,0:T(8,128)(2,1)S(1)}, u32[]{:S(2)}, u32[]{:S(2)}) collective-permute-start(bf16[2,128,512]{2,1,0:T(8,128)(2,1)S(1)} %get-tuple-element.78), channel_id=1, source_target_pairs={{0,4},{1,5},{2,6},{3,7},{4,0},{5,1},{6,2},{7,3},{8,12},{9,13},{10,... | collective-permute-start | bytes 786440 | tf_op jit(solution)/shard_map/ppermute | solution.py:472
  47.8 21.1 %collective-permute-start.9 = (bf16[2,128,512]{2,1,0:T(8,128)(2,1)S(1)}, bf16[2,128,512]{2,1,0:T(8,128)(2,1)S(1)}, u32[]{:S(2)}, u32[]{:S(2)}) collective-permute-start(bf16[2,128,512]{2,1,0:T(8,128)(2,1)S(1)} %get-tuple-element.79), channel_id=1, source_target_pairs={{0,6},{1,7},{2,0},{3,1},{4,2},{5,3},{6,4},{7,5},{8,14},{9,15},{10,... | collective-permute-start | bytes 786440 | tf_op jit(solution)/shard_map/ppermute | solution.py:472
  49.3 19.6 %collective-permute-start.5 = (bf16[2,176,128]{2,1,0:T(8,128)(2,1)S(1)}, bf16[2,176,128]{2,1,0:T(8,128)(2,1)S(1)}, u32[]{:S(2)}, u32[]{:S(2)}) collective-permute-start(bf16[2,176,128]{2,1,0:T(8,128)(2,1)S(1)} %get-tuple-element.73), channel_id=1, source_target_pairs={{0,8},{1,9},{2,10},{3,11},{4,12},{5,13},{6,14},{7,15},{16,24},{17,... | collective-permute-start | bytes 270344 | tf_op jit(solution)/shard_map/ppermute | solution.py:489
  65.2 36.3 %collective-permute-start.24 = (bf16[1024,512]{1,0:T(8,128)(2,1)}, bf16[1024,512]{1,0:T(8,128)(2,1)}, u32[]{:S(2)}, u32[]{:S(2)}) collective-permute-start(bf16[1024,512]{1,0:T(8,128)(2,1)} %collective-permute-done.11.refs_6_.refs_3_), channel_id=1, source_target_pairs={{0,1},{1,0},{2,3},{3,2},{4,5},{5,4},{6,7},{7,6},{8,9},{9,8},{10,11... | collective-permute-start | bytes 3145736 | tf_op jit(solution)/shard_map/ppermute | solution.py:606
  71.5 9.8 %collective-permute-start.10 = (bf16[2,176,128]{2,1,0:T(8,128)(2,1)S(1)}, bf16[2,176,128]{2,1,0:T(8,128)(2,1)S(1)}, u32[]{:S(2)}, u32[]{:S(2)}) collective-permute-start(bf16[2,176,128]{2,1,0:T(8,128)(2,1)S(1)} %get-tuple-element.84), channel_id=1, source_target_pairs={{8,0},{9,1},{10,2},{11,3},{12,4},{13,5},{14,6},{15,7},{24,16},{25,... | collective-permute-start | bytes 270344 | tf_op jit(solution)/shard_map/ppermute | solution.py:489
  83.5 9.9 %collective-permute-start.12 = (bf16[4,2,128,256]{3,2,1,0:T(8,128)(2,1)S(1)}, bf16[4,2,128,256]{3,2,1,0:T(8,128)(2,1)S(1)}, u32[]{:S(2)}, u32[]{:S(2)}) collective-permute-start(bf16[4,2,128,256]{3,2,1,0:T(8,128)(2,1)S(1)} %get-tuple-element.91), channel_id=1, source_target_pairs={{0,1},{1,0},{2,3},{3,2},{4,5},{5,4},{6,7},{7,6},{8,9},{9,8},{10,11... | collective-permute-start | bytes 1572872 | tf_op jit(solution)/shard_map/ppermute | solution.py:481
  83.5 5.9 %collective-permute-start.17 = (bf16[64,1024]{1,0:T(8,128)(2,1)S(1)}, bf16[64,1024]{1,0:T(8,128)(2,1)S(1)}, u32[]{:S(2)}, u32[]{:S(2)}) collective-permute-start(bf16[64,1024]{1,0:T(8,128)(2,1)S(1)} %get-tuple-element.96.refs_1_), channel_id=1, source_target_pairs={{0,2},{1,3},{2,4},{3,5},{4,6},{5,7},{6,0},{7,1},{8,10},{9,11},{10,... | collective-permute-start | bytes 393224 | tf_op jit(solution)/shard_map/ppermute | solution.py:472
  83.5 8.8 %collective-permute-start.19 = (bf16[64,1024]{1,0:T(8,128)(2,1)S(1)}, bf16[64,1024]{1,0:T(8,128)(2,1)S(1)}, u32[]{:S(2)}, u32[]{:S(2)}) collective-permute-start(bf16[64,1024]{1,0:T(8,128)(2,1)S(1)} %get-tuple-element.96.refs_1_), channel_id=1, source_target_pairs={{0,4},{1,5},{2,6},{3,7},{4,0},{5,1},{6,2},{7,3},{8,12},{9,13},{10,... | collective-permute-start | bytes 393224 | tf_op jit(solution)/shard_map/ppermute | solution.py:472
  85.6 7.8 %collective-permute-start.21 = (bf16[64,1024]{1,0:T(8,128)(2,1)S(1)}, bf16[64,1024]{1,0:T(8,128)(2,1)S(1)}, u32[]{:S(2)}, u32[]{:S(2)}) collective-permute-start(bf16[64,1024]{1,0:T(8,128)(2,1)S(1)} %get-tuple-element.96.refs_1_), channel_id=1, source_target_pairs={{0,6},{1,7},{2,0},{3,1},{4,2},{5,3},{6,4},{7,5},{8,14},{9,15},{10,... | collective-permute-start | bytes 393224 | tf_op jit(solution)/shard_map/ppermute | solution.py:472
  89.4 6.1 %collective-permute-start.16 = (bf16[64,1024]{1,0:T(8,128)(2,1)S(1)}, bf16[64,1024]{1,0:T(8,128)(2,1)S(1)}, u32[]{:S(2)}, u32[]{:S(2)}) collective-permute-start(bf16[64,1024]{1,0:T(8,128)(2,1)S(1)} %get-tuple-element.96.refs_1_), channel_id=1, source_target_pairs={{0,1},{1,0},{2,3},{3,2},{4,5},{5,4},{6,7},{7,6},{8,9},{9,8},{10,11... | collective-permute-start | bytes 393224 | tf_op jit(solution)/shard_map/ppermute | solution.py:481
  92.4 3.1 %collective-permute-start.18 = (bf16[64,1024]{1,0:T(8,128)(2,1)S(1)}, bf16[64,1024]{1,0:T(8,128)(2,1)S(1)}, u32[]{:S(2)}, u32[]{:S(2)}) collective-permute-start(bf16[64,1024]{1,0:T(8,128)(2,1)S(1)} %collective-permute-done.17.refs_3_), channel_id=1, source_target_pairs={{0,1},{1,0},{2,3},{3,2},{4,5},{5,4},{6,7},{7,6},{8,9},{9,8},{10,11... | collective-permute-start | bytes 393224 | tf_op jit(solution)/shard_map/ppermute | solution.py:481
  97.7 8.5 %collective-permute-start.23 = (bf16[256,512]{1,0:T(8,128)(2,1)}, bf16[256,512]{1,0:T(8,128)(2,1)}, u32[]{:S(2)}, u32[]{:S(2)}) collective-permute-start(bf16[256,512]{1,0:T(8,128)(2,1)} %get-tuple-element.100), channel_id=1, source_target_pairs={{0,16},{16,0},{1,17},{17,1},{2,18},{18,2},{3,19},{19,3},{4,20},{20... | collective-permute-start | bytes 786440 | tf_op jit(solution)/shard_map/ppermute | solution.py:468
  99.2 10.3 %collective-permute-start.13 = (bf16[2,2,128,256]{3,2,1,0:T(8,128)(2,1)}, bf16[2,2,128,256]{3,2,1,0:T(8,128)(2,1)S(1)}, u32[]{:S(2)}, u32[]{:S(2)}) collective-permute-start(bf16[2,2,128,256]{3,2,1,0:T(8,128)(2,1)} %get-tuple-element.93), channel_id=1, source_target_pairs={{0,2},{1,3},{2,4},{3,5},{4,6},{5,7},{6,0},{7,1},{8,10},{9,11},{10,... | collective-permute-start | bytes 786440 | tf_op jit(solution)/shard_map/ppermute | solution.py:472
  99.2 16.4 %collective-permute-start.14 = (bf16[2,2,128,256]{3,2,1,0:T(8,128)(2,1)}, bf16[2,2,128,256]{3,2,1,0:T(8,128)(2,1)S(1)}, u32[]{:S(2)}, u32[]{:S(2)}) collective-permute-start(bf16[2,2,128,256]{3,2,1,0:T(8,128)(2,1)} %get-tuple-element.94), channel_id=1, source_target_pairs={{0,4},{1,5},{2,6},{3,7},{4,0},{5,1},{6,2},{7,3},{8,12},{9,13},{10,... | collective-permute-start | bytes 786440 | tf_op jit(solution)/shard_map/ppermute | solution.py:472
  100.9 16.1 %collective-permute-start.15 = (bf16[2,2,128,256]{3,2,1,0:T(8,128)(2,1)}, bf16[2,2,128,256]{3,2,1,0:T(8,128)(2,1)}, u32[]{:S(2)}, u32[]{:S(2)}) collective-permute-start(bf16[2,2,128,256]{3,2,1,0:T(8,128)(2,1)} %get-tuple-element.95), channel_id=1, source_target_pairs={{0,6},{1,7},{2,0},{3,1},{4,2},{5,3},{6,4},{7,5},{8,14},{9,15},{10,... | collective-permute-start | bytes 786440 | tf_op jit(solution)/shard_map/ppermute | solution.py:472
  107.3 11.7 %collective-permute-start.25 = (bf16[128,512]{1,0:T(8,128)(2,1)S(1)}, bf16[128,512]{1,0:T(8,128)(2,1)S(1)}, u32[]{:S(2)}, u32[]{:S(2)}) collective-permute-start(bf16[128,512]{1,0:T(8,128)(2,1)S(1)} %get-tuple-element.109), channel_id=1, source_target_pairs={{0,8},{1,9},{2,10},{3,11},{4,12},{5,13},{6,14},{7,15},{8,0},{9,1},... | collective-permute-start | bytes 393224 | tf_op jit(solution)/shard_map/ppermute | solution.py:489
  (16 other events, 31.7 us)

commit v12 on v10

--- a/solution.py
+++ b/solution.py
@@ -357,11 +357,12 @@
 
 def product_kernel(group, at_ref, *rest):
     rows_refs, rest = rest[:group], rest[group:]
-    tokens_ref, own_rows_ref, *part_refs, total_ref, held_ref = rest
+    tokens_ref, own_rows_ref, other_rows_ref, *part_refs, total_ref, held_ref = rest
     place_rows(at_ref[1], at_ref[2], rows_refs, held_ref)
     total_ref[...] = dot(tokens_ref[...], held_ref[...], NT)
     tok = own_rows_ref.shape[0]
     own_rows_ref[...] = held_ref[:, aligned(2 * at_ref[1] + at_ref[2], tok)].T
+    other_rows_ref[...] = held_ref[:, aligned(2 * at_ref[1] + 1 - at_ref[2], tok)].T
     count = len(part_refs)
     size = part_refs[0].shape[0]
     for shift, part_ref in enumerate(part_refs):
@@ -385,12 +386,27 @@
         part_ref[...] = part.astype(part_ref.dtype)
 
 
-def grad_tokens_kernel(at_ref, rows_ref, *rest):
-    *weight_refs, out_ref = rest
-    for i, weight_ref in enumerate(weight_refs):
-        size = weight_ref.shape[0]
+def grad_tokens_kernel(at_ref, rows_ref, other_rows_ref, weight_ref, *rest):
+    count = len(rest) // 2
+    fetched_refs, out_ref, other_refs = rest[:count], rest[count], rest[count + 1 :]
+    for i, ref in enumerate((weight_ref, *fetched_refs)):
+        size = ref.shape[0]
         first = pl.multiple_of(at_ref[i], size)
-        out_ref[0, :, pl.ds(first, size)] = dot(rows_ref[...], weight_ref[...], NT).astype(bf16)
+        out_ref[0, :, pl.ds(first, size)] = dot(rows_ref[...], ref[...], NT).astype(bf16)
+    for ref, other_ref in zip(fetched_refs, other_refs):
+        other_ref[...] = dot(other_rows_ref[...], ref[...], NT).astype(bf16)
+
+
+def merge_kernel(at_ref, main_ref, *rest):
+    *part_refs, out_ref, sems = rest
+    run_copies(
+        sems,
+        [
+            (part_ref, out_ref.at[0, :, pl.ds(pl.multiple_of(at_ref[i], size), size)])
+            for i, part_ref in enumerate(part_refs)
+            for size in part_ref.shape[1:]
+        ],
+    )
 
 
 def final_sum_kernel(own_ref, *rest):
@@ -418,6 +434,7 @@
     far_in=(),
     far_out=False,
     copies=(),
+    alias=False,
 ):
     at = [jnp.stack([jnp.int32(s) for s in scalars])] if scalars else []
     count = len(at) + len(operands)
@@ -436,6 +453,7 @@
         + [FAR] * len(after_far),
         out_specs=[FAR if far_out else VMEM] * len(outs) + [VMEM],
         scratch_shapes=[*scratch] + [pltpu.SemaphoreType.DMA((n,)) for n in copies],
+        input_output_aliases={len(at): 0} if alias else {},
         compiler_params=pltpu.CompilerParams(vmem_limit_bytes=VMEM_LIMIT),
         cost_estimate=pl.CostEstimate(flops=0, bytes_accessed=0, transcendentals=0),
     )(*at, *operands, *after, *after_far)
@@ -511,10 +529,11 @@
         scalars=(chip_at, core_at),
         after=(token,),
     )
-    (keep, send), heads_token = call(
+    heads_parts = [to_chip(part, shift) for shift, part in enumerate(parts)]
+    (keep, send), _ = call(
         split_cores_kernel,
         [((chips, 2, tok, heads * DH), bf16)] * 2,
-        *[to_chip(part, shift) for shift, part in enumerate(parts)],
+        *heads_parts,
         scalars=(chip_at, core_at),
     )
     (vg,), _ = call(
@@ -534,15 +553,6 @@
         far_in=(0,),
         copies=(1,),
         scratch=[pltpu.VMEM((tok, share), bf16)],
-    )
-    (projected,), token = call(
-        project_rest_kernel,
-        [((dp_size,) + qk_shape[0], f32)],
-        projected,
-        proj_weight,
-        *arrived,
-        scalars=(dp_at,),
-        after=(heads_token, token),
     )
     part_shape = (tok, dp_size * runs * depth)
     if depth % 128 == 0:
@@ -557,15 +567,24 @@
         blocks = blocks.reshape(chips, 2, *part_shape)
         blocks = jnp.stack([blocks[(chip_at + shift) % chips] for shift in range(chips)])
         keep, send = blocks[:, core_at], blocks[:, 1 - core_at]
-    token_parts, _ = call(
+    token_parts, pair_token = call(
         pair_kernel,
         [((2,) + part_shape, bf16)] * chips,
         keep,
         to_other_core(send),
         scalars=(chip_at, core_at),
-        after=(token,),
     )
     token_parts = [to_chip(part, shift) for shift, part in enumerate(token_parts)]
+    (projected,), rest_token = call(
+        project_rest_kernel,
+        [((dp_size,) + qk_shape[0], f32)],
+        projected,
+        proj_weight,
+        *arrived,
+        scalars=(dp_at,),
+        after=(token, pair_token),
+        after_far=heads_parts[1:],
+    )
     qk_parts = lax.all_to_all(
         projected.reshape((dp_size * group,) + qk_shape[0][1:]),
         ("dp", "ctx"),
@@ -575,28 +594,20 @@
         axis_index_groups=wide_groups,
     ).reshape(projected.shape)
 
-    pair = 2 if ctx_size % 2 == 0 else 1
-    parity = ctx_at % pair
-    piece = share // pair
-    (mine,), token = call(
+    parity = ctx_at % 2
+    piece = share // 2
+    (mine,), _ = call(
         weight_piece_kernel,
         [((piece, cols), bf16)],
         proj_weight,
         scalars=(parity,),
-        after=(token,),
+        after=(rest_token,),
         far_in=(0,),
         far_out=True,
         copies=(1,),
     )
     fetched = [to_dp(mine, shift) for shift in range(1, dp_size)]
-    weights, firsts = [proj_weight], [dp_at * share]
-    for shift, half in enumerate(fetched, 1):
-        base = (dp_at + dp_size - shift) % dp_size * share
-        weights.append(half)
-        firsts.append(base + parity * piece)
-        if pair == 2:
-            weights.append(lax.ppermute(half, "ctx", [(i, i ^ 1) for i in range(ctx_size)]))
-            firsts.append(base + (1 - parity) * piece)
+    bases = [(dp_at + dp_size - shift) % dp_size * share for shift in range(1, dp_size)]
 
     (qk, *state), token = call(
         functools.partial(state_kernel, with_state),
@@ -626,7 +637,6 @@
         vg,
         grad_num,
         *prefix,
-        after_far=fetched,
     )
     (token_cols,), token = call(
         collect_tokens_kernel,
@@ -661,9 +671,10 @@
     results = [to_chip(part, shift) for shift, part in enumerate(results)]
 
     held = pltpu.VMEM((cols, length), bf16)
-    (own_rows, own, *parts), token = call(
+    (own_rows, other_rows, own, *parts), token = call(
         functools.partial(product_kernel, 2 * chips),
-        [((tok, cols), bf16), ((runs * depth, cols), f32)] + [((runs * depth, cols), bf16)] * (dp_size - 1),
+        [((tok, cols), bf16)] * 2
+        + [((runs * depth, cols), f32)] + [((runs * depth, cols), bf16)] * (dp_size - 1),
         *rows,
         token_cols,
         scalars=(dp_at, chip_at, core_at),
@@ -671,12 +682,14 @@
         scratch=[pltpu.VMEM((dp_size * runs * depth, cols), f32), held],
     )
     parts = [to_dp(part, shift) for shift, part in enumerate(parts, 1)]
-    (grad_tokens,), tokens_token = call(
+    (grad_tokens, *others), tokens_token = call(
         grad_tokens_kernel,
-        [((1, tok, width), bf16)],
+        [((1, tok, width), bf16)] + [((tok, piece), bf16)] * (dp_size - 1),
         own_rows,
-        *weights,
-        scalars=firsts,
+        other_rows,
+        proj_weight,
+        *fetched,
+        scalars=[dp_at * share] + [base + parity * piece for base in bases],
         after=(token,),
     )
     (grad_proj, *parts), token = call(
@@ -695,12 +708,23 @@
         scalars=(chip_at,),
         after=(token,),
     )
+    (grad_tokens,), tokens_token = call(
+        merge_kernel,
+        [((1, tok, width), bf16)],
+        grad_tokens,
+        *[to_other_core(other) for other in others],
+        scalars=[base + (1 - parity) * piece for base in bases],
+        far_in=(0,),
+        far_out=True,
+        copies=(dp_size - 1,),
+        alias=True,
+    )
     (grad_proj,), _ = call(
         final_sum_kernel,
         [((depth, cols), f32)],
         grad_proj,
         *[to_run(part, shift, True) for shift, part in enumerate(parts, 1)],
-        after=(token,),
+        after=(token, tokens_token),
     )
     return (attended, grad_tokens, grad_values, grad_proj)
 

time: 120 us -> 107 us (0.89)
  waiting for transfers between devices: 31.9 us -> 21.4 us
  Pallas kernels: 38.9 us -> 36.8 us
    all_to_all x1, waiting for transfers between devices: 12.8 us -> 0.01 us  [local(): lax.all_to_all(projected.reshape((dp_size * group,) + qk_shape[0][1:]), (...]
    ppermute x12, waiting for transfers between devices: 17.1 us -> 20.6 us  [to_member(): return lax.ppermute(x, 'ctx', pairs)]
    pallas_call x21 -> x22, Pallas kernels: 38.9 us -> 36.8 us  [call(): pl.pallas_call(kernel, out_shape=[jax.ShapeDtypeStruct(shape, kind) for s...]
    ppermute x7 -> x8, waiting for transfers between devices: 1.42 us -> 0.02 us  [to_other_core(): return lax.ppermute(x, 'ctx', [(i, i ^ 1) for i in range(ctx_size)])]
    unnamed x24 -> x34, local copies, waits for them, and re-layouts: 7.74 us -> 7.33 us
  transfers between devices with their start and end apart: 27 -> 27, of which waited for: 10 -> 9; matrix products, arithmetic and copies ran while one was open for 0% -> 0% of each run, Pallas kernels for 30% -> 32%
where the time goes in v12:
time: 107 us; the launch traced here: 105 us
  starting transfers between devices  38.1 us (36%)
  Pallas kernels  36.8 us (34%)
  waiting for transfers between devices  21.4 us (20%)
  local copies, waits for them, and re-layouts  7.33 us (7%)
    pallas_call x22, Pallas kernels, call(): pl.pallas_call(kernel, out_shape=[jax.ShapeDtypeStruct(shape, kind) for s...  36.8 us
    ppermute x12, waiting for transfers between devices, to_member(): return lax.ppermute(x, 'ctx', pairs)  20.6 us
    ppermute x12, starting transfers between devices, to_member(): return lax.ppermute(x, 'ctx', pairs)  17.9 us
    ppermute x3, starting transfers between devices, to_run(): return lax.ppermute(x, 'ctx', pairs)  9.29 us
    unnamed x34, local copies, waits for them, and re-layouts  7.33 us
    ppermute x3, starting transfers between devices, to_dp(): lax.ppermute(x, 'dp', [(i, (i + shift) % dp_size) for i in range(dp_size)])  4.83 us
    all_to_all x1, starting transfers between devices, local(): lax.all_to_all(projected.reshape((dp_size * group,) + qk_shape[0][1:]), (...  4.27 us
  transfers between devices with their start and end apart: 27, of which 9 were waited for; matrix products, arithmetic and copies ran while one was open for 0% of the time, Pallas kernels for 32%

profile of v12, /device:TPU:0, one launch (start us, length us, event | category | flops | bytes accessed | tf_op | source)
XLA Modules:
  0.0 104.8 jit_solution(13272693366937147755)
XLA Ops:
  2.1 1.6 %shard_map.78 = (bf16[4,128,512]{2,1,0:T(8,128)(2,1)S(1)}, bf16[4,128,512]{2,1,0:T(8,128)(2,1)}, f32[8,128]{1,0:T(8,128)}) custom-call(s32[2]{0:T(128)S(1)} %pad_add_fusion.refs_0_, bf16[1,128,4096]{2,1,0:T(8,128)(2,1)S(1)} %copy-done.1), custom_call_target="tpu_custom_call" | custom-call | tf_op jit(solution)/shard_map/pallas_call | solution.py:447
  5.5 2.6 %collective-permute-start = (bf16[128,2048]{1,0:T(8,128)(2,1)S(1)}, bf16[128,2048]{1,0:T(8,128)(2,1)S(1)}, u32[]{:S(2)}, u32[]{:S(2)}) collective-permute-start(bf16[128,2048]{1,0:T(8,128)(2,1)S(1)} %get-tuple-element.65), channel_id=1, source_target_pairs={{0,16},{16,0},{1,17},{17,1},{2,18},{18,2},{3,19},{19,3},{4,20},{20... | collective-permute-start | bytes 1572872 | tf_op jit(solution)/shard_map/ppermute | solution.py:486
  10.8 1.6 %collective-permute-start.2 = (bf16[2,2,128,256]{3,2,1,0:T(8,128)(2,1)S(1)}, bf16[2,2,128,256]{3,2,1,0:T(8,128)(2,1)S(1)}, u32[]{:S(2)}, u32[]{:S(2)}) collective-permute-start(bf16[2,2,128,256]{3,2,1,0:T(8,128)(2,1)S(1)} %get-tuple-element.70), channel_id=1, source_target_pairs={{0,2},{1,3},{2,4},{3,5},{4,6},{5,7},{6,0},{7,1},{8,10},{9,11},{10,... | collective-permute-start | bytes 786440 | tf_op jit(solution)/shard_map/ppermute | solution.py:490
  12.4 1.6 %collective-permute-start.3 = (bf16[2,2,128,256]{3,2,1,0:T(8,128)(2,1)S(1)}, bf16[2,2,128,256]{3,2,1,0:T(8,128)(2,1)S(1)}, u32[]{:S(2)}, u32[]{:S(2)}) collective-permute-start(bf16[2,2,128,256]{3,2,1,0:T(8,128)(2,1)S(1)} %get-tuple-element.71), channel_id=1, source_target_pairs={{0,4},{1,5},{2,6},{3,7},{4,0},{5,1},{6,2},{7,3},{8,12},{9,13},{10,... | collective-permute-start | bytes 786440 | tf_op jit(solution)/shard_map/ppermute | solution.py:490
  17.2 3.8 %collective-permute-done.2.refs_6_.refs_2_ = bf16[2,2,128,256]{3,2,1,0:T(8,128)(2,1)S(1)} collective-permute-done((bf16[2,2,128,256]{3,2,1,0:T(8,128)(2,1)S(1)}, bf16[2,2,128,256]{3,2,1,0:T(8,128)(2,1)S(1)}, u32[]{:S(2)}, u32[]{:S(2)}) %collective-permute-start.2) | collective-permute-done | bytes 262176 | tf_op jit(solution)/shard_map/ppermute | solution.py:490
  21.6 4.3 %collective-permute-done.4.refs_8_.refs_4_ = bf16[2,2,128,256]{3,2,1,0:T(8,128)(2,1)S(1)} collective-permute-done((bf16[2,2,128,256]{3,2,1,0:T(8,128)(2,1)S(1)}, bf16[2,2,128,256]{3,2,1,0:T(8,128)(2,1)S(1)}, u32[]{:S(2)}, u32[]{:S(2)}) %collective-permute-start.4) | collective-permute-done | bytes 262176 | tf_op jit(solution)/shard_map/ppermute | solution.py:490
  27.2 4.3 %all-to-all-start = ((f32[16,2,2,16,128]{4,3,2,1,0:T(8,128)}), f32[16,2,2,16,128]{4,3,2,1,0:T(8,128)}, u32[]{:S(2)}, u32[]{:S(2)}) async-start(f32[16,2,2,16,128]{4,3,2,1,0:T(8,128)} %bitcast.3), calls=%async_computation | async-start | bytes 1048576 | tf_op jit(solution)/shard_map/all_to_all | solution.py:588
  34.0 1.7 %collective-permute-start.7 = (bf16[2,128,512]{2,1,0:T(8,128)(2,1)}, bf16[2,128,512]{2,1,0:T(8,128)(2,1)S(1)}, u32[]{:S(2)}, u32[]{:S(2)}) collective-permute-start(bf16[2,128,512]{2,1,0:T(8,128)(2,1)} %copy-done.16), channel_id=1, source_target_pairs={{0,2},{1,3},{2,4},{3,5},{4,6},{5,7},{6,0},{7,1},{8,10},{9,11},{10,... | collective-permute-start | bytes 786440 | tf_op jit(solution)/shard_map/ppermute | solution.py:490
  44.7 1.7 %shard_map.83 = (f32[8,2,2,16,128]{4,3,2,1,0:T(8,128)S(1)}, bf16[2,176,128]{2,1,0:T(8,128)(2,1)S(1)}, f32[8,128]{1,0:T(8,128)}) custom-call(f32[2,8,2,2,16,128]{5,4,3,2,1,0:T(8,128)} %bitcast.4.refs_0_, bf16[8,2,128,256]{3,2,1,0:T(8,128)(2,1)S(1)} %get-tuple-element.77.refs_1_.refs_2_), custom_call_target="tpu_custom_call" | custom-call | tf_op jit(solution)/shard_map/pallas_call | solution.py:447
  46.4 4.5 %collective-permute-start.6 = (bf16[2,176,128]{2,1,0:T(8,128)(2,1)S(1)}, bf16[2,176,128]{2,1,0:T(8,128)(2,1)S(1)}, u32[]{:S(2)}, u32[]{:S(2)}) collective-permute-start(bf16[2,176,128]{2,1,0:T(8,128)(2,1)S(1)} %get-tuple-element.80), channel_id=1, source_target_pairs={{0,8},{1,9},{2,10},{3,11},{4,12},{5,13},{6,14},{7,15},{16,24},{17,... | collective-permute-start | bytes 270344 | tf_op jit(solution)/shard_map/ppermute | solution.py:507
  50.9 3.6 %shard_map.84 = (f32[1024,256]{1,0:T(8,128)S(1)}, f32[8,128]{1,0:T(8,128)}) custom-call(f32[8,2,2,16,128]{4,3,2,1,0:T(8,128)S(1)} %get-tuple-element.78.refs_0_.refs_1_, bf16[8,2,128,256]{3,2,1,0:T(8,128)(2,1)S(1)} %get-tuple-element.77.refs_1_.refs_2_), custom_call_target="tpu_custom_call" | custom-call | tf_op jit(solution)/shard_map/pallas_call | solution.py:447
  54.5 2.6 %shard_map.85 = (bf16[1024,256]{1,0:T(8,128)(2,1)S(1)}, f32[1024,256]{1,0:T(8,128)S(1)}, bf16[2,176,128]{2,1,0:T(8,128)(2,1)S(1)}, f32[8,128]{1,0:T(8,128)}) custom-call(f32[8,2,2,16,128]{4,3,2,1,0:T(8,128)S(1)} %get-tuple-element.78.refs_0_.refs_1_, bf16[8,2,128,256]{3,2,1,0:T(8,128)(2,1)S(1)} %get-tuple-element.77.refs_1_.refs_2_, ...), custom_call_target="tpu_custom_call" | custom-call | tf_op jit(solution)/shard_map/pallas_call | solution.py:447
  58.6 5.9 %shard_map.86 = (f32[2,2,16,1024]{3,2,1,0:T(8,128)S(1)}, f32[2,128,1024]{2,1,0:T(8,128)S(1)}, f32[8,128]{1,0:T(8,128)S(1)}) custom-call(f32[8,2,2,16,128]{4,3,2,1,0:T(8,128)S(1)} %get-tuple-element.78.refs_0_.refs_1_, bf16[8,2,128,256]{3,2,1,0:T(8,128)(2,1)S(1)} %get-tuple-element.77.refs_1_.refs_2_, f32[1024,256]{1,0:T(8,128)S(1)} %get-tuple-element.85.refs_2_, ...), custom_call_target="tpu_custom_call" | custom-call | tf_op jit(solution)/shard_map/pallas_call | solution.py:447
  66.0 2.3 %shard_map.88 = (bf16[64,1024]{1,0:T(8,128)(2,1)S(1)}, bf16[4,2,128,256]{3,2,1,0:T(8,128)(2,1)S(1)}, bf16[4,2,128,256]{3,2,1,0:T(8,128)(2,1)S(1)}, f32[8,128]{1,0:T(8,128)}) custom-call(s32[2]{0:T(128)S(1)} %pad_add_fusion.refs_0_, f32[8,2,2,16,128]{4,3,2,1,0:T(8,128)S(1)} %get-tuple-element.78.refs_0_.refs_1_, ...), custom_call_target="tpu_custom_call" | custom-call | tf_op jit(solution)/shard_map/pallas_call | solution.py:447
  69.4 2.4 %collective-permute-start.20 = (bf16[64,1024]{1,0:T(8,128)(2,1)S(1)}, bf16[64,1024]{1,0:T(8,128)(2,1)S(1)}, u32[]{:S(2)}, u32[]{:S(2)}) collective-permute-start(bf16[64,1024]{1,0:T(8,128)(2,1)S(1)} %get-tuple-element.98.refs_1_), channel_id=1, source_target_pairs={{0,6},{1,7},{2,0},{3,1},{4,2},{5,3},{6,4},{7,5},{8,14},{9,15},{10,... | collective-permute-start | bytes 393224 | tf_op jit(solution)/shard_map/ppermute | solution.py:490
  71.7 3.8 %collective-permute-done.16.refs_3_ = bf16[64,1024]{1,0:T(8,128)(2,1)S(1)} collective-permute-done((bf16[64,1024]{1,0:T(8,128)(2,1)S(1)}, bf16[64,1024]{1,0:T(8,128)(2,1)S(1)}, u32[]{:S(2)}, u32[]{:S(2)}) %collective-permute-start.16) | collective-permute-done | bytes 131104 | tf_op jit(solution)/shard_map/ppermute | solution.py:490
  76.0 1.9 %collective-permute-done.20.refs_7_ = bf16[64,1024]{1,0:T(8,128)(2,1)S(1)} collective-permute-done((bf16[64,1024]{1,0:T(8,128)(2,1)S(1)}, bf16[64,1024]{1,0:T(8,128)(2,1)S(1)}, u32[]{:S(2)}, u32[]{:S(2)}) %collective-permute-start.20) | collective-permute-done | bytes 131104 | tf_op jit(solution)/shard_map/ppermute | solution.py:490
  80.0 2.2 %shard_map.90 = (bf16[128,512]{1,0:T(8,128)(2,1)S(1)}, bf16[128,512]{1,0:T(8,128)(2,1)S(1)}, f32[256,512]{1,0:T(8,128)S(1)}, bf16[256,512]{1,0:T(8,128)(2,1)}, f32[8,128]{1,0:T(8,128)S(1)}) custom-call(s32[3]{0:T(128)S(1)} %pad_add_fusion.1.refs_0_, bf16[64,1024]{1,0:T(8,128)(2,1)S(1)} %get-tuple-element.98.refs_1_, ...), custom_call_target="tpu_custom_call" | custom-call | tf_op jit(solution)/shard_map/pallas_call | solution.py:447
  83.0 3.5 %shard_map.92 = (bf16[1,128,4096]{2,1,0:T(8,128)(2,1)}, bf16[128,1024]{1,0:T(8,128)(2,1)}, f32[8,128]{1,0:T(8,128)S(1)}) custom-call(s32[2]{0:T(128)S(1)} %pad_add_fusion.2.refs_0_, bf16[128,512]{1,0:T(8,128)(2,1)S(1)} %get-tuple-element.103.refs_1_, bf16[128,512]{1,0:T(8,128)(2,1)S(1)} %get-tuple-element.104.refs_2_, bf16[2048,512]{1,0:T(8,128)(2,1)S(1)} %copy-done, ...), custom_call_target="tpu_custom_call" | custom-call | tf_op jit(solution)/shard_map/pallas_call | solution.py:447
  87.7 2.0 %collective-permute-start.13 = (bf16[2,2,128,256]{3,2,1,0:T(8,128)(2,1)}, bf16[2,2,128,256]{3,2,1,0:T(8,128)(2,1)S(1)}, u32[]{:S(2)}, u32[]{:S(2)}) collective-permute-start(bf16[2,2,128,256]{3,2,1,0:T(8,128)(2,1)} %get-tuple-element.96), channel_id=1, source_target_pairs={{0,4},{1,5},{2,6},{3,7},{4,0},{5,1},{6,2},{7,3},{8,12},{9,13},{10,... | collective-permute-start | bytes 786440 | tf_op jit(solution)/shard_map/ppermute | solution.py:490
  89.6 2.1 %collective-permute-start.14 = (bf16[2,2,128,256]{3,2,1,0:T(8,128)(2,1)}, bf16[2,2,128,256]{3,2,1,0:T(8,128)(2,1)S(1)}, u32[]{:S(2)}, u32[]{:S(2)}) collective-permute-start(bf16[2,2,128,256]{3,2,1,0:T(8,128)(2,1)} %get-tuple-element.97), channel_id=1, source_target_pairs={{0,6},{1,7},{2,0},{3,1},{4,2},{5,3},{6,4},{7,5},{8,14},{9,15},{10,... | collective-permute-start | bytes 786440 | tf_op jit(solution)/shard_map/ppermute | solution.py:490
  91.9 3.3 %collective-permute-start.25 = (bf16[128,512]{1,0:T(8,128)(2,1)S(1)}, bf16[128,512]{1,0:T(8,128)(2,1)S(1)}, u32[]{:S(2)}, u32[]{:S(2)}) collective-permute-start(bf16[128,512]{1,0:T(8,128)(2,1)S(1)} %get-tuple-element.116), channel_id=1, source_target_pairs={{0,8},{1,9},{2,10},{3,11},{4,12},{5,13},{6,14},{7,15},{8,0},{9,1},... | collective-permute-start | bytes 393224 | tf_op jit(solution)/shard_map/ppermute | solution.py:507
  95.9 3.6 %collective-permute-done.12.refs_2_ = bf16[2,2,128,256]{3,2,1,0:T(8,128)(2,1)S(1)} collective-permute-done((bf16[2,2,128,256]{3,2,1,0:T(8,128)(2,1)}, bf16[2,2,128,256]{3,2,1,0:T(8,128)(2,1)S(1)}, u32[]{:S(2)}, u32[]{:S(2)}) %collective-permute-start.12) | collective-permute-done | bytes 262176 | tf_op jit(solution)/shard_map/ppermute | solution.py:490
  99.8 2.4 %collective-permute-done.14.refs_4_ = bf16[2,2,128,256]{3,2,1,0:T(8,128)(2,1)S(1)} collective-permute-done((bf16[2,2,128,256]{3,2,1,0:T(8,128)(2,1)}, bf16[2,2,128,256]{3,2,1,0:T(8,128)(2,1)S(1)}, u32[]{:S(2)}, u32[]{:S(2)}) %collective-permute-start.14) | collective-permute-done | bytes 262176 | tf_op jit(solution)/shard_map/ppermute | solution.py:490
  (89 shorter events, 34.8 us)
Async XLA Ops:
  3.7 12.2 %collective-permute-start.1 = (bf16[4,128,512]{2,1,0:T(8,128)(2,1)}, bf16[4,128,512]{2,1,0:T(8,128)(2,1)}, u32[]{:S(2)}, u32[]{:S(2)}) collective-permute-start(bf16[4,128,512]{2,1,0:T(8,128)(2,1)} %get-tuple-element.68), channel_id=1, source_target_pairs={{0,1},{1,0},{2,3},{3,2},{4,5},{5,4},{6,7},{7,6},{8,9},{9,8},{10,11... | collective-permute-start | bytes 1572872 | tf_op jit(solution)/shard_map/ppermute | solution.py:499
  5.5 20.4 %collective-permute-start = (bf16[128,2048]{1,0:T(8,128)(2,1)S(1)}, bf16[128,2048]{1,0:T(8,128)(2,1)S(1)}, u32[]{:S(2)}, u32[]{:S(2)}) collective-permute-start(bf16[128,2048]{1,0:T(8,128)(2,1)S(1)} %get-tuple-element.65), channel_id=1, source_target_pairs={{0,16},{16,0},{1,17},{17,1},{2,18},{18,2},{3,19},{19,3},{4,20},{20... | collective-permute-start | bytes 1572872 | tf_op jit(solution)/shard_map/ppermute | solution.py:486
  10.8 10.1 %collective-permute-start.2 = (bf16[2,2,128,256]{3,2,1,0:T(8,128)(2,1)S(1)}, bf16[2,2,128,256]{3,2,1,0:T(8,128)(2,1)S(1)}, u32[]{:S(2)}, u32[]{:S(2)}) collective-permute-start(bf16[2,2,128,256]{3,2,1,0:T(8,128)(2,1)S(1)} %get-tuple-element.70), channel_id=1, source_target_pairs={{0,2},{1,3},{2,4},{3,5},{4,6},{5,7},{6,0},{7,1},{8,10},{9,11},{10,... | collective-permute-start | bytes 786440 | tf_op jit(solution)/shard_map/ppermute | solution.py:490
  12.4 9.2 %collective-permute-start.3 = (bf16[2,2,128,256]{3,2,1,0:T(8,128)(2,1)S(1)}, bf16[2,2,128,256]{3,2,1,0:T(8,128)(2,1)S(1)}, u32[]{:S(2)}, u32[]{:S(2)}) collective-permute-start(bf16[2,2,128,256]{3,2,1,0:T(8,128)(2,1)S(1)} %get-tuple-element.71), channel_id=1, source_target_pairs={{0,4},{1,5},{2,6},{3,7},{4,0},{5,1},{6,2},{7,3},{8,12},{9,13},{10,... | collective-permute-start | bytes 786440 | tf_op jit(solution)/shard_map/ppermute | solution.py:490
  13.9 11.9 %collective-permute-start.4 = (bf16[2,2,128,256]{3,2,1,0:T(8,128)(2,1)S(1)}, bf16[2,2,128,256]{3,2,1,0:T(8,128)(2,1)S(1)}, u32[]{:S(2)}, u32[]{:S(2)}) collective-permute-start(bf16[2,2,128,256]{3,2,1,0:T(8,128)(2,1)S(1)} %get-tuple-element.72), channel_id=1, source_target_pairs={{0,6},{1,7},{2,0},{3,1},{4,2},{5,3},{6,4},{7,5},{8,14},{9,15},{10,... | collective-permute-start | bytes 786440 | tf_op jit(solution)/shard_map/ppermute | solution.py:490
  27.2 17.5 %all-to-all-start = ((f32[16,2,2,16,128]{4,3,2,1,0:T(8,128)}), f32[16,2,2,16,128]{4,3,2,1,0:T(8,128)}, u32[]{:S(2)}, u32[]{:S(2)}) async-start(f32[16,2,2,16,128]{4,3,2,1,0:T(8,128)} %bitcast.3), calls=%async_computation | async-start | bytes 1048576 | tf_op jit(solution)/shard_map/all_to_all | solution.py:588
  33.7 8.1 %collective-permute-start.5 = (bf16[4,2,128,256]{3,2,1,0:T(8,128)(2,1)}, bf16[4,2,128,256]{3,2,1,0:T(8,128)(2,1)S(1)}, u32[]{:S(2)}, u32[]{:S(2)}) collective-permute-start(bf16[4,2,128,256]{3,2,1,0:T(8,128)(2,1)} %get-tuple-element.76), channel_id=1, source_target_pairs={{0,1},{1,0},{2,3},{3,2},{4,5},{5,4},{6,7},{7,6},{8,9},{9,8},{10,11... | collective-permute-start | bytes 1572872 | tf_op jit(solution)/shard_map/ppermute | solution.py:499
  34.0 20.5 %collective-permute-start.7 = (bf16[2,128,512]{2,1,0:T(8,128)(2,1)}, bf16[2,128,512]{2,1,0:T(8,128)(2,1)S(1)}, u32[]{:S(2)}, u32[]{:S(2)}) collective-permute-start(bf16[2,128,512]{2,1,0:T(8,128)(2,1)} %copy-done.16), channel_id=1, source_target_pairs={{0,2},{1,3},{2,4},{3,5},{4,6},{5,7},{6,0},{7,1},{8,10},{9,11},{10,... | collective-permute-start | bytes 786440 | tf_op jit(solution)/shard_map/ppermute | solution.py:490
  35.7 18.8 %collective-permute-start.8 = (bf16[2,128,512]{2,1,0:T(8,128)(2,1)}, bf16[2,128,512]{2,1,0:T(8,128)(2,1)}, u32[]{:S(2)}, u32[]{:S(2)}) collective-permute-start(bf16[2,128,512]{2,1,0:T(8,128)(2,1)} %copy-done.15), channel_id=1, source_target_pairs={{0,4},{1,5},{2,6},{3,7},{4,0},{5,1},{6,2},{7,3},{8,12},{9,13},{10,... | collective-permute-start | bytes 786440 | tf_op jit(solution)/shard_map/ppermute | solution.py:490
  37.2 17.4 %collective-permute-start.9 = (bf16[2,128,512]{2,1,0:T(8,128)(2,1)}, bf16[2,128,512]{2,1,0:T(8,128)(2,1)}, u32[]{:S(2)}, u32[]{:S(2)}) collective-permute-start(bf16[2,128,512]{2,1,0:T(8,128)(2,1)} %copy-done.14), channel_id=1, source_target_pairs={{0,6},{1,7},{2,0},{3,1},{4,2},{5,3},{6,4},{7,5},{8,14},{9,15},{10,... | collective-permute-start | bytes 786440 | tf_op jit(solution)/shard_map/ppermute | solution.py:490
  40.2 42.8 %collective-permute-start.23 = (bf16[1024,512]{1,0:T(8,128)(2,1)}, bf16[1024,512]{1,0:T(8,128)(2,1)}, u32[]{:S(2)}, u32[]{:S(2)}) collective-permute-start(bf16[1024,512]{1,0:T(8,128)(2,1)} %get-tuple-element.106), channel_id=1, source_target_pairs={{0,16},{16,0},{1,17},{17,1},{2,18},{18,2},{3,19},{19,3},{4,20},{20... | collective-permute-start | bytes 3145736 | tf_op jit(solution)/shard_map/ppermute | solution.py:486
  46.4 8.2 %collective-permute-start.6 = (bf16[2,176,128]{2,1,0:T(8,128)(2,1)S(1)}, bf16[2,176,128]{2,1,0:T(8,128)(2,1)S(1)}, u32[]{:S(2)}, u32[]{:S(2)}) collective-permute-start(bf16[2,176,128]{2,1,0:T(8,128)(2,1)S(1)} %get-tuple-element.80), channel_id=1, source_target_pairs={{0,8},{1,9},{2,10},{3,11},{4,12},{5,13},{6,14},{7,15},{16,24},{17,... | collective-permute-start | bytes 270344 | tf_op jit(solution)/shard_map/ppermute | solution.py:507
  57.1 8.8 %collective-permute-start.10 = (bf16[2,176,128]{2,1,0:T(8,128)(2,1)S(1)}, bf16[2,176,128]{2,1,0:T(8,128)(2,1)S(1)}, u32[]{:S(2)}, u32[]{:S(2)}) collective-permute-start(bf16[2,176,128]{2,1,0:T(8,128)(2,1)S(1)} %get-tuple-element.88), channel_id=1, source_target_pairs={{8,0},{9,1},{10,2},{11,3},{12,4},{13,5},{14,6},{15,7},{24,16},{25,... | collective-permute-start | bytes 270344 | tf_op jit(solution)/shard_map/ppermute | solution.py:507
  68.3 9.7 %collective-permute-start.11 = (bf16[4,2,128,256]{3,2,1,0:T(8,128)(2,1)S(1)}, bf16[4,2,128,256]{3,2,1,0:T(8,128)(2,1)S(1)}, u32[]{:S(2)}, u32[]{:S(2)}) collective-permute-start(bf16[4,2,128,256]{3,2,1,0:T(8,128)(2,1)S(1)} %get-tuple-element.93), channel_id=1, source_target_pairs={{0,1},{1,0},{2,3},{3,2},{4,5},{5,4},{6,7},{7,6},{8,9},{9,8},{10,11... | collective-permute-start | bytes 1572872 | tf_op jit(solution)/shard_map/ppermute | solution.py:499
  68.3 7.2 %collective-permute-start.16 = (bf16[64,1024]{1,0:T(8,128)(2,1)S(1)}, bf16[64,1024]{1,0:T(8,128)(2,1)S(1)}, u32[]{:S(2)}, u32[]{:S(2)}) collective-permute-start(bf16[64,1024]{1,0:T(8,128)(2,1)S(1)} %get-tuple-element.98.refs_1_), channel_id=1, source_target_pairs={{0,2},{1,3},{2,4},{3,5},{4,6},{5,7},{6,0},{7,1},{8,10},{9,11},{10,... | collective-permute-start | bytes 393224 | tf_op jit(solution)/shard_map/ppermute | solution.py:490
  68.8 6.7 %collective-permute-start.18 = (bf16[64,1024]{1,0:T(8,128)(2,1)S(1)}, bf16[64,1024]{1,0:T(8,128)(2,1)S(1)}, u32[]{:S(2)}, u32[]{:S(2)}) collective-permute-start(bf16[64,1024]{1,0:T(8,128)(2,1)S(1)} %get-tuple-element.98.refs_1_), channel_id=1, source_target_pairs={{0,4},{1,5},{2,6},{3,7},{4,0},{5,1},{6,2},{7,3},{8,12},{9,13},{10,... | collective-permute-start | bytes 393224 | tf_op jit(solution)/shard_map/ppermute | solution.py:490
  69.4 8.5 %collective-permute-start.20 = (bf16[64,1024]{1,0:T(8,128)(2,1)S(1)}, bf16[64,1024]{1,0:T(8,128)(2,1)S(1)}, u32[]{:S(2)}, u32[]{:S(2)}) collective-permute-start(bf16[64,1024]{1,0:T(8,128)(2,1)S(1)} %get-tuple-element.98.refs_1_), channel_id=1, source_target_pairs={{0,6},{1,7},{2,0},{3,1},{4,2},{5,3},{6,4},{7,5},{8,14},{9,15},{10,... | collective-permute-start | bytes 393224 | tf_op jit(solution)/shard_map/ppermute | solution.py:490
  75.5 4.5 %collective-permute-start.15 = (bf16[64,1024]{1,0:T(8,128)(2,1)S(1)}, bf16[64,1024]{1,0:T(8,128)(2,1)S(1)}, u32[]{:S(2)}, u32[]{:S(2)}) collective-permute-start(bf16[64,1024]{1,0:T(8,128)(2,1)S(1)} %get-tuple-element.98.refs_1_), channel_id=1, source_target_pairs={{0,1},{1,0},{2,3},{3,2},{4,5},{5,4},{6,7},{7,6},{8,9},{9,8},{10,11... | collective-permute-start | bytes 393224 | tf_op jit(solution)/shard_map/ppermute | solution.py:499
  82.2 9.6 %collective-permute-start.22 = (bf16[256,512]{1,0:T(8,128)(2,1)}, bf16[256,512]{1,0:T(8,128)(2,1)S(1)}, u32[]{:S(2)}, u32[]{:S(2)}) collective-permute-start(bf16[256,512]{1,0:T(8,128)(2,1)} %get-tuple-element.102), channel_id=1, source_target_pairs={{0,16},{16,0},{1,17},{17,1},{2,18},{18,2},{3,19},{19,3},{4,20},{20... | collective-permute-start | bytes 786440 | tf_op jit(solution)/shard_map/ppermute | solution.py:486
  86.5 8.7 %collective-permute-start.24 = (bf16[128,1024]{1,0:T(8,128)(2,1)}, bf16[128,1024]{1,0:T(8,128)(2,1)S(1)}, u32[]{:S(2)}, u32[]{:S(2)}) collective-permute-start(bf16[128,1024]{1,0:T(8,128)(2,1)} %get-tuple-element.112), channel_id=1, source_target_pairs={{0,1},{1,0},{2,3},{3,2},{4,5},{5,4},{6,7},{7,6},{8,9},{9,8},{10,11... | collective-permute-start | bytes 786440 | tf_op jit(solution)/shard_map/ppermute | solution.py:499
  86.5 13.1 %collective-permute-start.12 = (bf16[2,2,128,256]{3,2,1,0:T(8,128)(2,1)}, bf16[2,2,128,256]{3,2,1,0:T(8,128)(2,1)S(1)}, u32[]{:S(2)}, u32[]{:S(2)}) collective-permute-start(bf16[2,2,128,256]{3,2,1,0:T(8,128)(2,1)} %get-tuple-element.95), channel_id=1, source_target_pairs={{0,2},{1,3},{2,4},{3,5},{4,6},{5,7},{6,0},{7,1},{8,10},{9,11},{10,... | collective-permute-start | bytes 786440 | tf_op jit(solution)/shard_map/ppermute | solution.py:490
  87.7 12.2 %collective-permute-start.13 = (bf16[2,2,128,256]{3,2,1,0:T(8,128)(2,1)}, bf16[2,2,128,256]{3,2,1,0:T(8,128)(2,1)S(1)}, u32[]{:S(2)}, u32[]{:S(2)}) collective-permute-start(bf16[2,2,128,256]{3,2,1,0:T(8,128)(2,1)} %get-tuple-element.96), channel_id=1, source_target_pairs={{0,4},{1,5},{2,6},{3,7},{4,0},{5,1},{6,2},{7,3},{8,12},{9,13},{10,... | collective-permute-start | bytes 786440 | tf_op jit(solution)/shard_map/ppermute | solution.py:490
  89.6 12.6 %collective-permute-start.14 = (bf16[2,2,128,256]{3,2,1,0:T(8,128)(2,1)}, bf16[2,2,128,256]{3,2,1,0:T(8,128)(2,1)S(1)}, u32[]{:S(2)}, u32[]{:S(2)}) collective-permute-start(bf16[2,2,128,256]{3,2,1,0:T(8,128)(2,1)} %get-tuple-element.97), channel_id=1, source_target_pairs={{0,6},{1,7},{2,0},{3,1},{4,2},{5,3},{6,4},{7,5},{8,14},{9,15},{10,... | collective-permute-start | bytes 786440 | tf_op jit(solution)/shard_map/ppermute | solution.py:490
  91.9 12.2 %collective-permute-start.25 = (bf16[128,512]{1,0:T(8,128)(2,1)S(1)}, bf16[128,512]{1,0:T(8,128)(2,1)S(1)}, u32[]{:S(2)}, u32[]{:S(2)}) collective-permute-start(bf16[128,512]{1,0:T(8,128)(2,1)S(1)} %get-tuple-element.116), channel_id=1, source_target_pairs={{0,8},{1,9},{2,10},{3,11},{4,12},{5,13},{6,14},{7,15},{8,0},{9,1},... | collective-permute-start | bytes 393224 | tf_op jit(solution)/shard_map/ppermute | solution.py:507
  (20 other events, 105.5 us)

commit v13 on v12

--- a/solution.py
+++ b/solution.py
@@ -521,7 +521,7 @@
         copies=(dp_size - 1,),
     )
     arrived = [to_dp(part, shift) for shift, part in enumerate(parts, 1)]
-    parts, token = call(
+    parts, heads_token = call(
         pack_heads_kernel,
         [((2, 2, tok, heads * DH), bf16)] * chips,
         values,
@@ -561,6 +561,7 @@
             [((chips,) + part_shape, bf16)] * 2,
             tokens,
             scalars=(chip_at, core_at),
+            after=(heads_token,),
         )
     else:
         blocks = tokens[0].reshape(tok, dp_size * runs, chips, 2, depth).transpose(2, 3, 0, 1, 4)
@@ -575,14 +576,26 @@
         scalars=(chip_at, core_at),
     )
     token_parts = [to_chip(part, shift) for shift, part in enumerate(token_parts)]
-    (projected,), rest_token = call(
+    parity = ctx_at % 2
+    piece = share // 2
+    (mine,), mine_token = call(
+        weight_piece_kernel,
+        [((piece, cols), bf16)],
+        proj_weight,
+        scalars=(parity,),
+        after=(heads_token,),
+        far_in=(0,),
+        far_out=True,
+        copies=(1,),
+    )
+    (projected,), _ = call(
         project_rest_kernel,
         [((dp_size,) + qk_shape[0], f32)],
         projected,
         proj_weight,
         *arrived,
         scalars=(dp_at,),
-        after=(token, pair_token),
+        after=(token, pair_token, mine_token),
         after_far=heads_parts[1:],
     )
     qk_parts = lax.all_to_all(
@@ -594,18 +607,6 @@
         axis_index_groups=wide_groups,
     ).reshape(projected.shape)
 
-    parity = ctx_at % 2
-    piece = share // 2
-    (mine,), _ = call(
-        weight_piece_kernel,
-        [((piece, cols), bf16)],
-        proj_weight,
-        scalars=(parity,),
-        after=(rest_token,),
-        far_in=(0,),
-        far_out=True,
-        copies=(1,),
-    )
     fetched = [to_dp(mine, shift) for shift in range(1, dp_size)]
     bases = [(dp_at + dp_size - shift) % dp_size * share for shift in range(1, dp_size)]
 
@@ -690,7 +691,7 @@
         proj_weight,
         *fetched,
         scalars=[dp_at * share] + [base + parity * piece for base in bases],
-        after=(token,),
+        after_far=parts,
     )
     (grad_proj, *parts), token = call(
         functools.partial(run_sum_kernel, len(parts)),
@@ -698,7 +699,6 @@
         own,
         *parts,
         scalars=(run_at,),
-        after=(tokens_token,),
         scratch=[pltpu.VMEM((runs * depth, cols), f32)],
     )
     (attended, grad_values), token = call(

time: 107 us -> 112 us (1.047); the launches traced: 105 us -> 112 us
  local copies, waits for them, and re-layouts: 7.33 us -> 12.5 us
    ppermute x12, waiting for transfers between devices: 20.6 us -> 10.6 us  [to_member(): return lax.ppermute(x, 'ctx', pairs)]
    unnamed x34 -> x42, local copies, waits for them, and re-layouts: 7.33 us -> 12.5 us
    ppermute x3, waiting for transfers between devices: 0.01 us -> 3.71 us  [to_dp(): lax.ppermute(x, 'dp', [(i, (i + shift) % dp_size) for i in range(dp_size)])]
    ppermute x3, waiting for transfers between devices: 0.78 us -> 4.17 us  [to_run(): return lax.ppermute(x, 'ctx', pairs)]
    all_to_all x1, waiting for transfers between devices: 0.01 us -> 3.31 us  [local(): lax.all_to_all(projected.reshape((dp_size * group,) + qk_shape[0][1:]), (...]
    ppermute x12, starting transfers between devices: 17.9 us -> 20.6 us  [to_member(): return lax.ppermute(x, 'ctx', pairs)]
    ppermute x3, starting transfers between devices: 4.83 us -> 3.04 us  [to_dp(): lax.ppermute(x, 'dp', [(i, (i + shift) % dp_size) for i in range(dp_size)])]
  transfers between devices with their start and end apart: 27 -> 27, of which waited for: 9 -> 10; matrix products, arithmetic and copies ran while one was open for 0% -> 0% of each run, Pallas kernels for 32% -> 28%
where the time goes in v13:
time: 112 us
  starting transfers between devices  38.5 us (34%)
  Pallas kernels  37.3 us (33%)
  waiting for transfers between devices  22.1 us (20%)
  local copies, waits for them, and re-layouts  12.5 us (11%)
    pallas_call x22, Pallas kernels, call(): pl.pallas_call(kernel, out_shape=[jax.ShapeDtypeStruct(shape, kind) for s...  37.3 us
    ppermute x12, starting transfers between devices, to_member(): return lax.ppermute(x, 'ctx', pairs)  20.6 us
    unnamed x42, local copies, waits for them, and re-layouts  12.5 us
    ppermute x12, waiting for transfers between devices, to_member(): return lax.ppermute(x, 'ctx', pairs)  10.6 us
    ppermute x3, starting transfers between devices, to_run(): return lax.ppermute(x, 'ctx', pairs)  9.27 us
    all_to_all x1, starting transfers between devices, local(): lax.all_to_all(projected.reshape((dp_size * group,) + qk_shape[0][1:]), (...  4.27 us
    ppermute x3, waiting for transfers between devices, to_run(): return lax.ppermute(x, 'ctx', pairs)  4.17 us
    ppermute x3, waiting for transfers between devices, to_dp(): lax.ppermute(x, 'dp', [(i, (i + shift) % dp_size) for i in range(dp_size)])  3.71 us
  transfers between devices with their start and end apart: 27, of which 10 were waited for; matrix products, arithmetic and copies ran while one was open for 0% of the time, Pallas kernels for 28%

profile of v13, /device:TPU:0, one launch (start us, length us, event | category | flops | bytes accessed | tf_op | source)
XLA Modules:
  0.0 111.6 jit_solution(8450482178640203954)
XLA Ops:
  8.5 1.6 %shard_map.78 = (bf16[4,128,512]{2,1,0:T(8,128)(2,1)S(1)}, bf16[4,128,512]{2,1,0:T(8,128)(2,1)}, f32[8,128]{1,0:T(8,128)}) custom-call(s32[2]{0:T(128)S(1)} %pad_add_fusion.refs_0_, bf16[1,128,4096]{2,1,0:T(8,128)(2,1)S(1)} %copy-done.2, f32[8,128]{1,0:T(8,128)S(1)} %get-tuple-element.64.refs_2_), custom_call_target="tpu_custom_call" | custom-call | tf_op jit(solution)/shard_map/pallas_call | solution.py:447
  11.4 2.5 %collective-permute-start = (bf16[128,2048]{1,0:T(8,128)(2,1)}, bf16[128,2048]{1,0:T(8,128)(2,1)S(1)}, u32[]{:S(2)}, u32[]{:S(2)}) collective-permute-start(bf16[128,2048]{1,0:T(8,128)(2,1)} %get-tuple-element.62), channel_id=1, source_target_pairs={{0,16},{16,0},{1,17},{17,1},{2,18},{18,2},{3,19},{19,3},{4,20},{20... | collective-permute-start | bytes 1572872 | tf_op jit(solution)/shard_map/ppermute | solution.py:486
  15.4 1.6 %collective-permute-start.3 = (bf16[2,2,128,256]{3,2,1,0:T(8,128)(2,1)}, bf16[2,2,128,256]{3,2,1,0:T(8,128)(2,1)S(1)}, u32[]{:S(2)}, u32[]{:S(2)}) collective-permute-start(bf16[2,2,128,256]{3,2,1,0:T(8,128)(2,1)} %get-tuple-element.70), channel_id=1, source_target_pairs={{0,4},{1,5},{2,6},{3,7},{4,0},{5,1},{6,2},{7,3},{8,12},{9,13},{10,... | collective-permute-start | bytes 786440 | tf_op jit(solution)/shard_map/ppermute | solution.py:490
  22.1 2.0 %shard_map.79 = (bf16[2,128,512]{2,1,0:T(8,128)(2,1)S(1)}, bf16[2,128,512]{2,1,0:T(8,128)(2,1)}, bf16[2,128,512]{2,1,0:T(8,128)(2,1)}, bf16[2,128,512]{2,1,0:T(8,128)(2,1)}, f32[8,128]{1,0:T(8,128)S(1)}) custom-call(s32[2]{0:T(128)S(1)} %pad_add_fusion.refs_0_, bf16[4,128,512]{2,1,0:T(8,128)(2,1)S(1)} %copy-done.8, ...), custom_call_target="tpu_custom_call" | custom-call | tf_op jit(solution)/shard_map/pallas_call | solution.py:447
  24.8 4.3 %collective-permute-done.4.refs_9_.refs_4_ = bf16[2,2,128,256]{3,2,1,0:T(8,128)(2,1)S(1)} collective-permute-done((bf16[2,2,128,256]{3,2,1,0:T(8,128)(2,1)}, bf16[2,2,128,256]{3,2,1,0:T(8,128)(2,1)S(1)}, u32[]{:S(2)}, u32[]{:S(2)}) %collective-permute-start.4) | collective-permute-done | bytes 262176 | tf_op jit(solution)/shard_map/ppermute | solution.py:490
  30.9 4.3 %all-to-all-start = ((f32[16,2,2,16,128]{4,3,2,1,0:T(8,128)}), f32[16,2,2,16,128]{4,3,2,1,0:T(8,128)}, u32[]{:S(2)}, u32[]{:S(2)}) async-start(f32[16,2,2,16,128]{4,3,2,1,0:T(8,128)} %bitcast.10), calls=%async_computation | async-start | bytes 1048576 | tf_op jit(solution)/shard_map/all_to_all | solution.py:601
  37.6 1.7 %collective-permute-start.7 = (bf16[2,128,512]{2,1,0:T(8,128)(2,1)}, bf16[2,128,512]{2,1,0:T(8,128)(2,1)S(1)}, u32[]{:S(2)}, u32[]{:S(2)}) collective-permute-start(bf16[2,128,512]{2,1,0:T(8,128)(2,1)} %get-tuple-element.80), channel_id=1, source_target_pairs={{0,2},{1,3},{2,4},{3,5},{4,6},{5,7},{6,0},{7,1},{8,10},{9,11},{10,... | collective-permute-start | bytes 786440 | tf_op jit(solution)/shard_map/ppermute | solution.py:490
  43.4 3.3 %all-to-all-done = f32[16,2,2,16,128]{4,3,2,1,0:T(8,128)} async-done(((f32[16,2,2,16,128]{4,3,2,1,0:T(8,128)}), f32[16,2,2,16,128]{4,3,2,1,0:T(8,128)}, u32[]{:S(2)}, u32[]{:S(2)}) %all-to-all-start) | async-done | bytes 524320 | tf_op jit(solution)/shard_map/all_to_all | solution.py:601
  46.7 1.7 %shard_map.84 = (f32[8,2,2,16,128]{4,3,2,1,0:T(8,128)S(1)}, bf16[2,176,128]{2,1,0:T(8,128)(2,1)S(1)}, f32[8,128]{1,0:T(8,128)}) custom-call(f32[2,8,2,2,16,128]{5,4,3,2,1,0:T(8,128)} %bitcast.5.refs_0_, bf16[8,2,128,256]{3,2,1,0:T(8,128)(2,1)S(1)} %get-tuple-element.76.refs_1_.refs_2_), custom_call_target="tpu_custom_call" | custom-call | tf_op jit(solution)/shard_map/pallas_call | solution.py:447
  48.3 4.5 %collective-permute-start.6 = (bf16[2,176,128]{2,1,0:T(8,128)(2,1)S(1)}, bf16[2,176,128]{2,1,0:T(8,128)(2,1)S(1)}, u32[]{:S(2)}, u32[]{:S(2)}) collective-permute-start(bf16[2,176,128]{2,1,0:T(8,128)(2,1)S(1)} %get-tuple-element.79), channel_id=1, source_target_pairs={{0,8},{1,9},{2,10},{3,11},{4,12},{5,13},{6,14},{7,15},{16,24},{17,... | collective-permute-start | bytes 270344 | tf_op jit(solution)/shard_map/ppermute | solution.py:507
  53.1 3.6 %shard_map.85 = (f32[1024,256]{1,0:T(8,128)S(1)}, f32[8,128]{1,0:T(8,128)}) custom-call(f32[8,2,2,16,128]{4,3,2,1,0:T(8,128)S(1)} %get-tuple-element.77.refs_0_.refs_1_, bf16[8,2,128,256]{3,2,1,0:T(8,128)(2,1)S(1)} %get-tuple-element.76.refs_1_.refs_2_), custom_call_target="tpu_custom_call" | custom-call | tf_op jit(solution)/shard_map/pallas_call | solution.py:447
  56.7 2.6 %shard_map.86 = (bf16[1024,256]{1,0:T(8,128)(2,1)S(1)}, f32[1024,256]{1,0:T(8,128)S(1)}, bf16[2,176,128]{2,1,0:T(8,128)(2,1)S(1)}, f32[8,128]{1,0:T(8,128)}) custom-call(f32[8,2,2,16,128]{4,3,2,1,0:T(8,128)S(1)} %get-tuple-element.77.refs_0_.refs_1_, bf16[8,2,128,256]{3,2,1,0:T(8,128)(2,1)S(1)} %get-tuple-element.76.refs_1_.refs_2_, ...), custom_call_target="tpu_custom_call" | custom-call | tf_op jit(solution)/shard_map/pallas_call | solution.py:447
  60.8 5.9 %shard_map.87 = (f32[2,2,16,1024]{3,2,1,0:T(8,128)S(1)}, f32[2,128,1024]{2,1,0:T(8,128)S(1)}, f32[8,128]{1,0:T(8,128)S(1)}) custom-call(f32[8,2,2,16,128]{4,3,2,1,0:T(8,128)S(1)} %get-tuple-element.77.refs_0_.refs_1_, bf16[8,2,128,256]{3,2,1,0:T(8,128)(2,1)S(1)} %get-tuple-element.76.refs_1_.refs_2_, f32[1024,256]{1,0:T(8,128)S(1)} %get-tuple-element.84.refs_2_, ...), custom_call_target="tpu_custom_call" | custom-call | tf_op jit(solution)/shard_map/pallas_call | solution.py:447
  68.2 2.3 %shard_map.89 = (bf16[64,1024]{1,0:T(8,128)(2,1)S(1)}, bf16[4,2,128,256]{3,2,1,0:T(8,128)(2,1)S(1)}, bf16[4,2,128,256]{3,2,1,0:T(8,128)(2,1)S(1)}, f32[8,128]{1,0:T(8,128)}) custom-call(s32[2]{0:T(128)S(1)} %pad_add_fusion.refs_0_, f32[8,2,2,16,128]{4,3,2,1,0:T(8,128)S(1)} %get-tuple-element.77.refs_0_.refs_1_, ...), custom_call_target="tpu_custom_call" | custom-call | tf_op jit(solution)/shard_map/pallas_call | solution.py:447
  71.1 4.1 %collective-permute-start.18 = (bf16[64,1024]{1,0:T(8,128)(2,1)S(1)}, bf16[64,1024]{1,0:T(8,128)(2,1)S(1)}, u32[]{:S(2)}, u32[]{:S(2)}) collective-permute-start(bf16[64,1024]{1,0:T(8,128)(2,1)S(1)} %get-tuple-element.97.refs_1_), channel_id=1, source_target_pairs={{0,4},{1,5},{2,6},{3,7},{4,0},{5,1},{6,2},{7,3},{8,12},{9,13},{10,... | collective-permute-start | bytes 393224 | tf_op jit(solution)/shard_map/ppermute | solution.py:490
  75.3 2.0 %collective-permute-start.16 = (bf16[64,1024]{1,0:T(8,128)(2,1)S(1)}, bf16[64,1024]{1,0:T(8,128)(2,1)S(1)}, u32[]{:S(2)}, u32[]{:S(2)}) collective-permute-start(bf16[64,1024]{1,0:T(8,128)(2,1)S(1)} %get-tuple-element.97.refs_1_), channel_id=1, source_target_pairs={{0,2},{1,3},{2,4},{3,5},{4,6},{5,7},{6,0},{7,1},{8,10},{9,11},{10,... | collective-permute-start | bytes 393224 | tf_op jit(solution)/shard_map/ppermute | solution.py:490
  77.3 4.4 %collective-permute-done.18.refs_5_ = bf16[64,1024]{1,0:T(8,128)(2,1)S(1)} collective-permute-done((bf16[64,1024]{1,0:T(8,128)(2,1)S(1)}, bf16[64,1024]{1,0:T(8,128)(2,1)S(1)}, u32[]{:S(2)}, u32[]{:S(2)}) %collective-permute-start.18) | collective-permute-done | bytes 131104 | tf_op jit(solution)/shard_map/ppermute | solution.py:490
  84.5 2.2 %shard_map.91 = (bf16[128,512]{1,0:T(8,128)(2,1)S(1)}, bf16[128,512]{1,0:T(8,128)(2,1)S(1)}, f32[256,512]{1,0:T(8,128)S(1)}, bf16[256,512]{1,0:T(8,128)(2,1)}, f32[8,128]{1,0:T(8,128)}) custom-call(s32[3]{0:T(128)S(1)} %pad_add_fusion.1.refs_0_, bf16[64,1024]{1,0:T(8,128)(2,1)S(1)} %get-tuple-element.97.refs_1_, ...), custom_call_target="tpu_custom_call" | custom-call | tf_op jit(solution)/shard_map/pallas_call | solution.py:447
  89.5 2.9 %collective-permute-start.14 = (bf16[2,2,128,256]{3,2,1,0:T(8,128)(2,1)}, bf16[2,2,128,256]{3,2,1,0:T(8,128)(2,1)}, u32[]{:S(2)}, u32[]{:S(2)}) collective-permute-start(bf16[2,2,128,256]{3,2,1,0:T(8,128)(2,1)} %copy-done.18), channel_id=1, source_target_pairs={{0,6},{1,7},{2,0},{3,1},{4,2},{5,3},{6,4},{7,5},{8,14},{9,15},{10,... | collective-permute-start | bytes 786440 | tf_op jit(solution)/shard_map/ppermute | solution.py:490
  92.4 3.7 %collective-permute-done.22.refs_2_.refs_5_ = bf16[256,512]{1,0:T(8,128)(2,1)S(1)} collective-permute-done((bf16[256,512]{1,0:T(8,128)(2,1)}, bf16[256,512]{1,0:T(8,128)(2,1)S(1)}, u32[]{:S(2)}, u32[]{:S(2)}) %collective-permute-start.22) | collective-permute-done | bytes 262176 | tf_op jit(solution)/shard_map/ppermute | solution.py:486
  97.0 3.5 %shard_map.94 = (bf16[1,128,4096]{2,1,0:T(8,128)(2,1)}, bf16[128,1024]{1,0:T(8,128)(2,1)}, f32[8,128]{1,0:T(8,128)}) custom-call(s32[2]{0:T(128)S(1)} %pad_add_fusion.2.refs_0_, bf16[128,512]{1,0:T(8,128)(2,1)S(1)} %get-tuple-element.104.refs_1_, bf16[128,512]{1,0:T(8,128)(2,1)S(1)} %copy-done.16, bf16[2048,512]{1,0:T(8,128)(2,1)S(1)} %copy-done, ...), custom_call_target="tpu_custom_call" | custom-call | tf_op jit(solution)/shard_map/pallas_call | solution.py:447
  100.6 3.3 %collective-permute-start.25 = (bf16[128,512]{1,0:T(8,128)(2,1)S(1)}, bf16[128,512]{1,0:T(8,128)(2,1)S(1)}, u32[]{:S(2)}, u32[]{:S(2)}) collective-permute-start(bf16[128,512]{1,0:T(8,128)(2,1)S(1)} %get-tuple-element.112), channel_id=1, source_target_pairs={{0,8},{1,9},{2,10},{3,11},{4,12},{5,13},{6,14},{7,15},{8,0},{9,1},... | collective-permute-start | bytes 393224 | tf_op jit(solution)/shard_map/ppermute | solution.py:507
  103.9 2.1 %shard_map.93 = (bf16[1,128,2048]{2,1,0:T(8,128)(2,1)}, bf16[1,128,2048]{2,1,0:T(8,128)(2,1)}, f32[8,128]{1,0:T(8,128)S(1)}) custom-call(s32[1]{0:T(128)} %bitcast.refs_0_, bf16[2,2,128,256]{3,2,1,0:T(8,128)(2,1)S(1)} %get-tuple-element.93.refs_1_, bf16[2,2,128,256]{3,2,1,0:T(8,128)(2,1)S(1)} %collective-permute-done.12.refs_2_, ...), custom_call_target="tpu_custom_call" | custom-call | tf_op jit(solution)/shard_map/pallas_call | solution.py:447
  106.7 4.2 %collective-permute-done.25.refs_1_ = bf16[128,512]{1,0:T(8,128)(2,1)S(1)} collective-permute-done((bf16[128,512]{1,0:T(8,128)(2,1)S(1)}, bf16[128,512]{1,0:T(8,128)(2,1)S(1)}, u32[]{:S(2)}, u32[]{:S(2)}) %collective-permute-start.25) | collective-permute-done | bytes 131104 | tf_op jit(solution)/shard_map/ppermute | solution.py:507
  (97 shorter events, 36.5 us)
Async XLA Ops:
  10.9 11.0 %collective-permute-start.1 = (bf16[4,128,512]{2,1,0:T(8,128)(2,1)}, bf16[4,128,512]{2,1,0:T(8,128)(2,1)}, u32[]{:S(2)}, u32[]{:S(2)}) collective-permute-start(bf16[4,128,512]{2,1,0:T(8,128)(2,1)} %get-tuple-element.66), channel_id=1, source_target_pairs={{0,1},{1,0},{2,3},{3,2},{4,5},{5,4},{6,7},{7,6},{8,9},{9,8},{10,11... | collective-permute-start | bytes 1572872 | tf_op jit(solution)/shard_map/ppermute | solution.py:499
  11.4 17.7 %collective-permute-start = (bf16[128,2048]{1,0:T(8,128)(2,1)}, bf16[128,2048]{1,0:T(8,128)(2,1)S(1)}, u32[]{:S(2)}, u32[]{:S(2)}) collective-permute-start(bf16[128,2048]{1,0:T(8,128)(2,1)} %get-tuple-element.62), channel_id=1, source_target_pairs={{0,16},{16,0},{1,17},{17,1},{2,18},{18,2},{3,19},{19,3},{4,20},{20... | collective-permute-start | bytes 1572872 | tf_op jit(solution)/shard_map/ppermute | solution.py:486
  13.9 10.3 %collective-permute-start.2 = (bf16[2,2,128,256]{3,2,1,0:T(8,128)(2,1)}, bf16[2,2,128,256]{3,2,1,0:T(8,128)(2,1)S(1)}, u32[]{:S(2)}, u32[]{:S(2)}) collective-permute-start(bf16[2,2,128,256]{3,2,1,0:T(8,128)(2,1)} %get-tuple-element.69), channel_id=1, source_target_pairs={{0,2},{1,3},{2,4},{3,5},{4,6},{5,7},{6,0},{7,1},{8,10},{9,11},{10,... | collective-permute-start | bytes 786440 | tf_op jit(solution)/shard_map/ppermute | solution.py:490
  15.4 9.4 %collective-permute-start.3 = (bf16[2,2,128,256]{3,2,1,0:T(8,128)(2,1)}, bf16[2,2,128,256]{3,2,1,0:T(8,128)(2,1)S(1)}, u32[]{:S(2)}, u32[]{:S(2)}) collective-permute-start(bf16[2,2,128,256]{3,2,1,0:T(8,128)(2,1)} %get-tuple-element.70), channel_id=1, source_target_pairs={{0,4},{1,5},{2,6},{3,7},{4,0},{5,1},{6,2},{7,3},{8,12},{9,13},{10,... | collective-permute-start | bytes 786440 | tf_op jit(solution)/shard_map/ppermute | solution.py:490
  17.0 12.1 %collective-permute-start.4 = (bf16[2,2,128,256]{3,2,1,0:T(8,128)(2,1)}, bf16[2,2,128,256]{3,2,1,0:T(8,128)(2,1)S(1)}, u32[]{:S(2)}, u32[]{:S(2)}) collective-permute-start(bf16[2,2,128,256]{3,2,1,0:T(8,128)(2,1)} %get-tuple-element.71), channel_id=1, source_target_pairs={{0,6},{1,7},{2,0},{3,1},{4,2},{5,3},{6,4},{7,5},{8,14},{9,15},{10,... | collective-permute-start | bytes 786440 | tf_op jit(solution)/shard_map/ppermute | solution.py:490
  30.9 15.8 %all-to-all-start = ((f32[16,2,2,16,128]{4,3,2,1,0:T(8,128)}), f32[16,2,2,16,128]{4,3,2,1,0:T(8,128)}, u32[]{:S(2)}, u32[]{:S(2)}) async-start(f32[16,2,2,16,128]{4,3,2,1,0:T(8,128)} %bitcast.10), calls=%async_computation | async-start | bytes 1048576 | tf_op jit(solution)/shard_map/all_to_all | solution.py:601
  37.3 5.0 %collective-permute-start.5 = (bf16[4,2,128,256]{3,2,1,0:T(8,128)(2,1)S(1)}, bf16[4,2,128,256]{3,2,1,0:T(8,128)(2,1)S(1)}, u32[]{:S(2)}, u32[]{:S(2)}) collective-permute-start(bf16[4,2,128,256]{3,2,1,0:T(8,128)(2,1)S(1)} %get-tuple-element.75), channel_id=1, source_target_pairs={{0,1},{1,0},{2,3},{3,2},{4,5},{5,4},{6,7},{7,6},{8,9},{9,8},{10,11... | collective-permute-start | bytes 1572872 | tf_op jit(solution)/shard_map/ppermute | solution.py:499
  37.6 19.1 %collective-permute-start.7 = (bf16[2,128,512]{2,1,0:T(8,128)(2,1)}, bf16[2,128,512]{2,1,0:T(8,128)(2,1)S(1)}, u32[]{:S(2)}, u32[]{:S(2)}) collective-permute-start(bf16[2,128,512]{2,1,0:T(8,128)(2,1)} %get-tuple-element.80), channel_id=1, source_target_pairs={{0,2},{1,3},{2,4},{3,5},{4,6},{5,7},{6,0},{7,1},{8,10},{9,11},{10,... | collective-permute-start | bytes 786440 | tf_op jit(solution)/shard_map/ppermute | solution.py:490
  39.3 17.4 %collective-permute-start.8 = (bf16[2,128,512]{2,1,0:T(8,128)(2,1)}, bf16[2,128,512]{2,1,0:T(8,128)(2,1)}, u32[]{:S(2)}, u32[]{:S(2)}) collective-permute-start(bf16[2,128,512]{2,1,0:T(8,128)(2,1)} %get-tuple-element.81), channel_id=1, source_target_pairs={{0,4},{1,5},{2,6},{3,7},{4,0},{5,1},{6,2},{7,3},{8,12},{9,13},{10,... | collective-permute-start | bytes 786440 | tf_op jit(solution)/shard_map/ppermute | solution.py:490
  40.8 16.0 %collective-permute-start.9 = (bf16[2,128,512]{2,1,0:T(8,128)(2,1)}, bf16[2,128,512]{2,1,0:T(8,128)(2,1)}, u32[]{:S(2)}, u32[]{:S(2)}) collective-permute-start(bf16[2,128,512]{2,1,0:T(8,128)(2,1)} %get-tuple-element.82), channel_id=1, source_target_pairs={{0,6},{1,7},{2,0},{3,1},{4,2},{5,3},{6,4},{7,5},{8,14},{9,15},{10,... | collective-permute-start | bytes 786440 | tf_op jit(solution)/shard_map/ppermute | solution.py:490
  48.3 8.4 %collective-permute-start.6 = (bf16[2,176,128]{2,1,0:T(8,128)(2,1)S(1)}, bf16[2,176,128]{2,1,0:T(8,128)(2,1)S(1)}, u32[]{:S(2)}, u32[]{:S(2)}) collective-permute-start(bf16[2,176,128]{2,1,0:T(8,128)(2,1)S(1)} %get-tuple-element.79), channel_id=1, source_target_pairs={{0,8},{1,9},{2,10},{3,11},{4,12},{5,13},{6,14},{7,15},{16,24},{17,... | collective-permute-start | bytes 270344 | tf_op jit(solution)/shard_map/ppermute | solution.py:507
  52.8 39.6 %collective-permute-start.23 = (bf16[1024,512]{1,0:T(8,128)(2,1)}, bf16[1024,512]{1,0:T(8,128)(2,1)}, u32[]{:S(2)}, u32[]{:S(2)}) collective-permute-start(bf16[1024,512]{1,0:T(8,128)(2,1)} %copy-done.17), channel_id=1, source_target_pairs={{0,16},{16,0},{1,17},{17,1},{2,18},{18,2},{3,19},{19,3},{4,20},{20... | collective-permute-start | bytes 3145736 | tf_op jit(solution)/shard_map/ppermute | solution.py:486
  59.3 8.8 %collective-permute-start.10 = (bf16[2,176,128]{2,1,0:T(8,128)(2,1)S(1)}, bf16[2,176,128]{2,1,0:T(8,128)(2,1)S(1)}, u32[]{:S(2)}, u32[]{:S(2)}) collective-permute-start(bf16[2,176,128]{2,1,0:T(8,128)(2,1)S(1)} %get-tuple-element.87), channel_id=1, source_target_pairs={{8,0},{9,1},{10,2},{11,3},{12,4},{13,5},{14,6},{15,7},{24,16},{25,... | collective-permute-start | bytes 270344 | tf_op jit(solution)/shard_map/ppermute | solution.py:507
  70.5 12.5 %collective-permute-start.11 = (bf16[4,2,128,256]{3,2,1,0:T(8,128)(2,1)S(1)}, bf16[4,2,128,256]{3,2,1,0:T(8,128)(2,1)S(1)}, u32[]{:S(2)}, u32[]{:S(2)}) collective-permute-start(bf16[4,2,128,256]{3,2,1,0:T(8,128)(2,1)S(1)} %get-tuple-element.92), channel_id=1, source_target_pairs={{0,1},{1,0},{2,3},{3,2},{4,5},{5,4},{6,7},{7,6},{8,9},{9,8},{10,11... | collective-permute-start | bytes 1572872 | tf_op jit(solution)/shard_map/ppermute | solution.py:499
  70.5 6.9 %collective-permute-start.20 = (bf16[64,1024]{1,0:T(8,128)(2,1)S(1)}, bf16[64,1024]{1,0:T(8,128)(2,1)S(1)}, u32[]{:S(2)}, u32[]{:S(2)}) collective-permute-start(bf16[64,1024]{1,0:T(8,128)(2,1)S(1)} %get-tuple-element.97.refs_1_), channel_id=1, source_target_pairs={{0,6},{1,7},{2,0},{3,1},{4,2},{5,3},{6,4},{7,5},{8,14},{9,15},{10,... | collective-permute-start | bytes 393224 | tf_op jit(solution)/shard_map/ppermute | solution.py:490
  71.1 10.6 %collective-permute-start.18 = (bf16[64,1024]{1,0:T(8,128)(2,1)S(1)}, bf16[64,1024]{1,0:T(8,128)(2,1)S(1)}, u32[]{:S(2)}, u32[]{:S(2)}) collective-permute-start(bf16[64,1024]{1,0:T(8,128)(2,1)S(1)} %get-tuple-element.97.refs_1_), channel_id=1, source_target_pairs={{0,4},{1,5},{2,6},{3,7},{4,0},{5,1},{6,2},{7,3},{8,12},{9,13},{10,... | collective-permute-start | bytes 393224 | tf_op jit(solution)/shard_map/ppermute | solution.py:490
  75.3 7.6 %collective-permute-start.16 = (bf16[64,1024]{1,0:T(8,128)(2,1)S(1)}, bf16[64,1024]{1,0:T(8,128)(2,1)S(1)}, u32[]{:S(2)}, u32[]{:S(2)}) collective-permute-start(bf16[64,1024]{1,0:T(8,128)(2,1)S(1)} %get-tuple-element.97.refs_1_), channel_id=1, source_target_pairs={{0,2},{1,3},{2,4},{3,5},{4,6},{5,7},{6,0},{7,1},{8,10},{9,11},{10,... | collective-permute-start | bytes 393224 | tf_op jit(solution)/shard_map/ppermute | solution.py:490
  77.3 6.9 %collective-permute-start.15 = (bf16[64,1024]{1,0:T(8,128)(2,1)S(1)}, bf16[64,1024]{1,0:T(8,128)(2,1)S(1)}, u32[]{:S(2)}, u32[]{:S(2)}) collective-permute-start(bf16[64,1024]{1,0:T(8,128)(2,1)S(1)} %get-tuple-element.97.refs_1_), channel_id=1, source_target_pairs={{0,1},{1,0},{2,3},{3,2},{4,5},{5,4},{6,7},{7,6},{8,9},{9,8},{10,11... | collective-permute-start | bytes 393224 | tf_op jit(solution)/shard_map/ppermute | solution.py:499
  87.3 8.8 %collective-permute-start.22 = (bf16[256,512]{1,0:T(8,128)(2,1)}, bf16[256,512]{1,0:T(8,128)(2,1)S(1)}, u32[]{:S(2)}, u32[]{:S(2)}) collective-permute-start(bf16[256,512]{1,0:T(8,128)(2,1)} %get-tuple-element.101), channel_id=1, source_target_pairs={{0,16},{16,0},{1,17},{17,1},{2,18},{18,2},{3,19},{19,3},{4,20},{20... | collective-permute-start | bytes 786440 | tf_op jit(solution)/shard_map/ppermute | solution.py:486
  87.7 16.2 %collective-permute-start.12 = (bf16[2,2,128,256]{3,2,1,0:T(8,128)(2,1)}, bf16[2,2,128,256]{3,2,1,0:T(8,128)(2,1)S(1)}, u32[]{:S(2)}, u32[]{:S(2)}) collective-permute-start(bf16[2,2,128,256]{3,2,1,0:T(8,128)(2,1)} %copy-done.20), channel_id=1, source_target_pairs={{0,2},{1,3},{2,4},{3,5},{4,6},{5,7},{6,0},{7,1},{8,10},{9,11},{10,... | collective-permute-start | bytes 786440 | tf_op jit(solution)/shard_map/ppermute | solution.py:490
  88.0 15.9 %collective-permute-start.13 = (bf16[2,2,128,256]{3,2,1,0:T(8,128)(2,1)}, bf16[2,2,128,256]{3,2,1,0:T(8,128)(2,1)}, u32[]{:S(2)}, u32[]{:S(2)}) collective-permute-start(bf16[2,2,128,256]{3,2,1,0:T(8,128)(2,1)} %copy-done.19), channel_id=1, source_target_pairs={{0,4},{1,5},{2,6},{3,7},{4,0},{5,1},{6,2},{7,3},{8,12},{9,13},{10,... | collective-permute-start | bytes 786440 | tf_op jit(solution)/shard_map/ppermute | solution.py:490
  89.5 14.4 %collective-permute-start.14 = (bf16[2,2,128,256]{3,2,1,0:T(8,128)(2,1)}, bf16[2,2,128,256]{3,2,1,0:T(8,128)(2,1)}, u32[]{:S(2)}, u32[]{:S(2)}) collective-permute-start(bf16[2,2,128,256]{3,2,1,0:T(8,128)(2,1)} %copy-done.18), channel_id=1, source_target_pairs={{0,6},{1,7},{2,0},{3,1},{4,2},{5,3},{6,4},{7,5},{8,14},{9,15},{10,... | collective-permute-start | bytes 786440 | tf_op jit(solution)/shard_map/ppermute | solution.py:490
  100.4 5.5 %collective-permute-start.24 = (bf16[128,1024]{1,0:T(8,128)(2,1)}, bf16[128,1024]{1,0:T(8,128)(2,1)S(1)}, u32[]{:S(2)}, u32[]{:S(2)}) collective-permute-start(bf16[128,1024]{1,0:T(8,128)(2,1)} %get-tuple-element.108), channel_id=1, source_target_pairs={{0,1},{1,0},{2,3},{3,2},{4,5},{5,4},{6,7},{7,6},{8,9},{9,8},{10,11... | collective-permute-start | bytes 786440 | tf_op jit(solution)/shard_map/ppermute | solution.py:499
  100.6 10.3 %collective-permute-start.25 = (bf16[128,512]{1,0:T(8,128)(2,1)S(1)}, bf16[128,512]{1,0:T(8,128)(2,1)S(1)}, u32[]{:S(2)}, u32[]{:S(2)}) collective-permute-start(bf16[128,512]{1,0:T(8,128)(2,1)S(1)} %get-tuple-element.112), channel_id=1, source_target_pairs={{0,8},{1,9},{2,10},{3,11},{4,12},{5,13},{6,14},{7,15},{8,0},{9,1},... | collective-permute-start | bytes 393224 | tf_op jit(solution)/shard_map/ppermute | solution.py:507
  (24 other events, 69.7 us)

commit v14 on v13

--- a/solution.py
+++ b/solution.py
@@ -521,7 +521,7 @@
         copies=(dp_size - 1,),
     )
     arrived = [to_dp(part, shift) for shift, part in enumerate(parts, 1)]
-    parts, heads_token = call(
+    parts, token = call(
         pack_heads_kernel,
         [((2, 2, tok, heads * DH), bf16)] * chips,
         values,
@@ -556,19 +556,20 @@
     )
     part_shape = (tok, dp_size * runs * depth)
     if depth % 128 == 0:
-        (keep, send), _ = call(
+        (keep, send), pack_token = call(
             functools.partial(pack_tokens_kernel, depth),
             [((chips,) + part_shape, bf16)] * 2,
             tokens,
             scalars=(chip_at, core_at),
-            after=(heads_token,),
+            after_far=heads_parts[1:2],
         )
     else:
         blocks = tokens[0].reshape(tok, dp_size * runs, chips, 2, depth).transpose(2, 3, 0, 1, 4)
         blocks = blocks.reshape(chips, 2, *part_shape)
         blocks = jnp.stack([blocks[(chip_at + shift) % chips] for shift in range(chips)])
         keep, send = blocks[:, core_at], blocks[:, 1 - core_at]
-    token_parts, pair_token = call(
+        pack_token = token
+    token_parts, _ = call(
         pair_kernel,
         [((2,) + part_shape, bf16)] * chips,
         keep,
@@ -583,7 +584,7 @@
         [((piece, cols), bf16)],
         proj_weight,
         scalars=(parity,),
-        after=(heads_token,),
+        after_far=heads_parts[1:2],
         far_in=(0,),
         far_out=True,
         copies=(1,),
@@ -595,7 +596,7 @@
         proj_weight,
         *arrived,
         scalars=(dp_at,),
-        after=(token, pair_token, mine_token),
+        after=(token, pack_token, mine_token),
         after_far=heads_parts[1:],
     )
     qk_parts = lax.all_to_all(
@@ -691,7 +692,7 @@
         proj_weight,
         *fetched,
         scalars=[dp_at * share] + [base + parity * piece for base in bases],
-        after_far=parts,
+        after=(token,),
     )
     (grad_proj, *parts), token = call(
         functools.partial(run_sum_kernel, len(parts)),
@@ -699,6 +700,7 @@
         own,
         *parts,
         scalars=(run_at,),
+        after=(tokens_token,),
         scratch=[pltpu.VMEM((runs * depth, cols), f32)],
     )
     (attended, grad_values), token = call(

time: 112 us -> 105 us (0.938)
  local copies, waits for them, and re-layouts: 12.5 us -> 7.85 us
  starting transfers between devices: 38.5 us -> 36.8 us
    ppermute x12, waiting for transfers between devices: 10.6 us -> 20 us  [to_member(): return lax.ppermute(x, 'ctx', pairs)]
    unnamed x42 -> x28, local copies, waits for them, and re-layouts: 12.5 us -> 7.85 us
    ppermute x12, starting transfers between devices: 20.6 us -> 16.4 us  [to_member(): return lax.ppermute(x, 'ctx', pairs)]
    ppermute x3, waiting for transfers between devices: 3.71 us -> 0.01 us  [to_dp(): lax.ppermute(x, 'dp', [(i, (i + shift) % dp_size) for i in range(dp_size)])]
    all_to_all x1, waiting for transfers between devices: 3.31 us -> 0.01 us  [local(): lax.all_to_all(projected.reshape((dp_size * group,) + qk_shape[0][1:]), (...]
    ppermute x3, waiting for transfers between devices: 4.17 us -> 0.94 us  [to_run(): return lax.ppermute(x, 'ctx', pairs)]
    ppermute x3, starting transfers between devices: 3.04 us -> 5.42 us  [to_dp(): lax.ppermute(x, 'dp', [(i, (i + shift) % dp_size) for i in range(dp_size)])]
  transfers between devices with their start and end apart: 27 -> 27, of which waited for: 10 -> 8; matrix products, arithmetic and copies ran while one was open for 0% -> 0% of each run, Pallas kernels for 28% -> 33%
where the time goes in v14:
time: 105 us; the launch traced here: 104 us
  Pallas kernels  36.8 us (35%)
  starting transfers between devices  36.8 us (35%)
  waiting for transfers between devices  21 us (20%)
  local copies, waits for them, and re-layouts  7.85 us (7%)
    pallas_call x22, Pallas kernels, call(): pl.pallas_call(kernel, out_shape=[jax.ShapeDtypeStruct(shape, kind) for s...  36.8 us
    ppermute x12, waiting for transfers between devices, to_member(): return lax.ppermute(x, 'ctx', pairs)  20 us
    ppermute x12, starting transfers between devices, to_member(): return lax.ppermute(x, 'ctx', pairs)  16.4 us
    ppermute x3, starting transfers between devices, to_run(): return lax.ppermute(x, 'ctx', pairs)  9.55 us
    unnamed x28, local copies, waits for them, and re-layouts  7.85 us
    ppermute x3, starting transfers between devices, to_dp(): lax.ppermute(x, 'dp', [(i, (i + shift) % dp_size) for i in range(dp_size)])  5.42 us
    all_to_all x1, starting transfers between devices, local(): lax.all_to_all(projected.reshape((dp_size * group,) + qk_shape[0][1:]), (...  4.39 us
  transfers between devices with their start and end apart: 27, of which 8 were waited for; matrix products, arithmetic and copies ran while one was open for 0% of the time, Pallas kernels for 33%

profile of v14, /device:TPU:0, one launch (start us, length us, event | category | flops | bytes accessed | tf_op | source)
XLA Modules:
  0.0 103.5 jit_solution(13090138351798383691)
XLA Ops:
  2.8 3.0 %collective-permute-start = (bf16[128,2048]{1,0:T(8,128)(2,1)}, bf16[128,2048]{1,0:T(8,128)(2,1)S(1)}, u32[]{:S(2)}, u32[]{:S(2)}) collective-permute-start(bf16[128,2048]{1,0:T(8,128)(2,1)} %get-tuple-element.65), channel_id=1, source_target_pairs={{0,16},{16,0},{1,17},{17,1},{2,18},{18,2},{3,19},{19,3},{4,20},{20... | collective-permute-start | bytes 1572872 | tf_op jit(solution)/shard_map/ppermute | solution.py:486
  8.0 1.5 %shard_map.76 = (bf16[2,2,128,256]{3,2,1,0:T(8,128)(2,1)S(1)}, bf16[2,2,128,256]{3,2,1,0:T(8,128)(2,1)}, bf16[2,2,128,256]{3,2,1,0:T(8,128)(2,1)}, bf16[2,2,128,256]{3,2,1,0:T(8,128)(2,1)}, f32[8,128]{1,0:T(8,128)S(1)}) custom-call(s32[2]{0:T(128)S(1)} %pad_add_fusion.refs_0_, bf16[1,128,2048]{2,1,0:T(8,128)(2,1)S(1)} %copy-done.5, ...), custom_call_target="tpu_custom_call" | custom-call | tf_op jit(solution)/shard_map/pallas_call | solution.py:447
  10.2 1.5 %collective-permute-start.1 = (bf16[2,2,128,256]{3,2,1,0:T(8,128)(2,1)}, bf16[2,2,128,256]{3,2,1,0:T(8,128)(2,1)S(1)}, u32[]{:S(2)}, u32[]{:S(2)}) collective-permute-start(bf16[2,2,128,256]{3,2,1,0:T(8,128)(2,1)} %get-tuple-element.67), channel_id=1, source_target_pairs={{0,2},{1,3},{2,4},{3,5},{4,6},{5,7},{6,0},{7,1},{8,10},{9,11},{10,... | collective-permute-start | bytes 786440 | tf_op jit(solution)/shard_map/ppermute | solution.py:490
  11.8 1.6 %collective-permute-start.2 = (bf16[2,2,128,256]{3,2,1,0:T(8,128)(2,1)}, bf16[2,2,128,256]{3,2,1,0:T(8,128)(2,1)S(1)}, u32[]{:S(2)}, u32[]{:S(2)}) collective-permute-start(bf16[2,2,128,256]{3,2,1,0:T(8,128)(2,1)} %get-tuple-element.70), channel_id=1, source_target_pairs={{0,4},{1,5},{2,6},{3,7},{4,0},{5,1},{6,2},{7,3},{8,12},{9,13},{10,... | collective-permute-start | bytes 786440 | tf_op jit(solution)/shard_map/ppermute | solution.py:490
  16.6 4.1 %collective-permute-done.1.refs_2_.refs_7_ = bf16[2,2,128,256]{3,2,1,0:T(8,128)(2,1)S(1)} collective-permute-done((bf16[2,2,128,256]{3,2,1,0:T(8,128)(2,1)}, bf16[2,2,128,256]{3,2,1,0:T(8,128)(2,1)S(1)}, u32[]{:S(2)}, u32[]{:S(2)}) %collective-permute-start.1) | collective-permute-done | bytes 262176 | tf_op jit(solution)/shard_map/ppermute | solution.py:490
  22.6 2.2 %collective-permute-done.3.refs_9_.refs_4_ = bf16[2,2,128,256]{3,2,1,0:T(8,128)(2,1)S(1)} collective-permute-done((bf16[2,2,128,256]{3,2,1,0:T(8,128)(2,1)}, bf16[2,2,128,256]{3,2,1,0:T(8,128)(2,1)S(1)}, u32[]{:S(2)}, u32[]{:S(2)}) %collective-permute-start.3) | collective-permute-done | bytes 262176 | tf_op jit(solution)/shard_map/ppermute | solution.py:490
  26.6 4.4 %all-to-all-start = ((f32[16,2,2,16,128]{4,3,2,1,0:T(8,128)}), f32[16,2,2,16,128]{4,3,2,1,0:T(8,128)}, u32[]{:S(2)}, u32[]{:S(2)}) async-start(f32[16,2,2,16,128]{4,3,2,1,0:T(8,128)} %bitcast.10), calls=%async_computation | async-start | bytes 1048576 | tf_op jit(solution)/shard_map/all_to_all | solution.py:602
  35.8 1.8 %collective-permute-start.7 = (bf16[2,128,512]{2,1,0:T(8,128)(2,1)}, bf16[2,128,512]{2,1,0:T(8,128)(2,1)S(1)}, u32[]{:S(2)}, u32[]{:S(2)}) collective-permute-start(bf16[2,128,512]{2,1,0:T(8,128)(2,1)} %get-tuple-element.82), channel_id=1, source_target_pairs={{0,2},{1,3},{2,4},{3,5},{4,6},{5,7},{6,0},{7,1},{8,10},{9,11},{10,... | collective-permute-start | bytes 786440 | tf_op jit(solution)/shard_map/ppermute | solution.py:490
  43.2 1.6 %shard_map.83 = (f32[8,2,2,16,128]{4,3,2,1,0:T(8,128)S(1)}, bf16[2,176,128]{2,1,0:T(8,128)(2,1)S(1)}, f32[8,128]{1,0:T(8,128)}) custom-call(f32[2,8,2,2,16,128]{5,4,3,2,1,0:T(8,128)} %bitcast.5.refs_0_, bf16[8,2,128,256]{3,2,1,0:T(8,128)(2,1)S(1)} %get-tuple-element.76.refs_1_.refs_2_), custom_call_target="tpu_custom_call" | custom-call | tf_op jit(solution)/shard_map/pallas_call | solution.py:447
  44.8 4.5 %collective-permute-start.5 = (bf16[2,176,128]{2,1,0:T(8,128)(2,1)S(1)}, bf16[2,176,128]{2,1,0:T(8,128)(2,1)S(1)}, u32[]{:S(2)}, u32[]{:S(2)}) collective-permute-start(bf16[2,176,128]{2,1,0:T(8,128)(2,1)S(1)} %get-tuple-element.79), channel_id=1, source_target_pairs={{0,8},{1,9},{2,10},{3,11},{4,12},{5,13},{6,14},{7,15},{16,24},{17,... | collective-permute-start | bytes 270344 | tf_op jit(solution)/shard_map/ppermute | solution.py:507
  49.3 3.6 %shard_map.84 = (f32[1024,256]{1,0:T(8,128)S(1)}, f32[8,128]{1,0:T(8,128)}) custom-call(f32[8,2,2,16,128]{4,3,2,1,0:T(8,128)S(1)} %get-tuple-element.77.refs_0_.refs_1_, bf16[8,2,128,256]{3,2,1,0:T(8,128)(2,1)S(1)} %get-tuple-element.76.refs_1_.refs_2_), custom_call_target="tpu_custom_call" | custom-call | tf_op jit(solution)/shard_map/pallas_call | solution.py:447
  53.0 2.6 %shard_map.86 = (bf16[1024,256]{1,0:T(8,128)(2,1)S(1)}, f32[1024,256]{1,0:T(8,128)S(1)}, bf16[2,176,128]{2,1,0:T(8,128)(2,1)S(1)}, f32[8,128]{1,0:T(8,128)}) custom-call(f32[8,2,2,16,128]{4,3,2,1,0:T(8,128)S(1)} %get-tuple-element.77.refs_0_.refs_1_, bf16[8,2,128,256]{3,2,1,0:T(8,128)(2,1)S(1)} %get-tuple-element.76.refs_1_.refs_2_, ...), custom_call_target="tpu_custom_call" | custom-call | tf_op jit(solution)/shard_map/pallas_call | solution.py:447
  57.0 5.9 %shard_map.87 = (f32[2,2,16,1024]{3,2,1,0:T(8,128)S(1)}, f32[2,128,1024]{2,1,0:T(8,128)S(1)}, f32[8,128]{1,0:T(8,128)S(1)}) custom-call(f32[8,2,2,16,128]{4,3,2,1,0:T(8,128)S(1)} %get-tuple-element.77.refs_0_.refs_1_, bf16[8,2,128,256]{3,2,1,0:T(8,128)(2,1)S(1)} %get-tuple-element.76.refs_1_.refs_2_, f32[1024,256]{1,0:T(8,128)S(1)} %get-tuple-element.86.refs_2_, ...), custom_call_target="tpu_custom_call" | custom-call | tf_op jit(solution)/shard_map/pallas_call | solution.py:447
  64.4 2.3 %shard_map.89 = (bf16[64,1024]{1,0:T(8,128)(2,1)S(1)}, bf16[4,2,128,256]{3,2,1,0:T(8,128)(2,1)S(1)}, bf16[4,2,128,256]{3,2,1,0:T(8,128)(2,1)S(1)}, f32[8,128]{1,0:T(8,128)}) custom-call(s32[2]{0:T(128)S(1)} %pad_add_fusion.refs_0_, f32[8,2,2,16,128]{4,3,2,1,0:T(8,128)S(1)} %get-tuple-element.77.refs_0_.refs_1_, ...), custom_call_target="tpu_custom_call" | custom-call | tf_op jit(solution)/shard_map/pallas_call | solution.py:447
  66.7 2.0 %collective-permute-start.20 = (bf16[64,1024]{1,0:T(8,128)(2,1)S(1)}, bf16[64,1024]{1,0:T(8,128)(2,1)S(1)}, u32[]{:S(2)}, u32[]{:S(2)}) collective-permute-start(bf16[64,1024]{1,0:T(8,128)(2,1)S(1)} %get-tuple-element.99.refs_1_), channel_id=1, source_target_pairs={{0,6},{1,7},{2,0},{3,1},{4,2},{5,3},{6,4},{7,5},{8,14},{9,15},{10,... | collective-permute-start | bytes 393224 | tf_op jit(solution)/shard_map/ppermute | solution.py:490
  69.3 3.3 %collective-permute-done.20.refs_7_ = bf16[64,1024]{1,0:T(8,128)(2,1)S(1)} collective-permute-done((bf16[64,1024]{1,0:T(8,128)(2,1)S(1)}, bf16[64,1024]{1,0:T(8,128)(2,1)S(1)}, u32[]{:S(2)}, u32[]{:S(2)}) %collective-permute-start.20) | collective-permute-done | bytes 131104 | tf_op jit(solution)/shard_map/ppermute | solution.py:490
  72.6 2.9 %collective-permute-done.18.refs_5_ = bf16[64,1024]{1,0:T(8,128)(2,1)S(1)} collective-permute-done((bf16[64,1024]{1,0:T(8,128)(2,1)S(1)}, bf16[64,1024]{1,0:T(8,128)(2,1)S(1)}, u32[]{:S(2)}, u32[]{:S(2)}) %collective-permute-start.18) | collective-permute-done | bytes 131104 | tf_op jit(solution)/shard_map/ppermute | solution.py:490
  78.7 2.2 %shard_map.91 = (bf16[128,512]{1,0:T(8,128)(2,1)S(1)}, bf16[128,512]{1,0:T(8,128)(2,1)S(1)}, f32[256,512]{1,0:T(8,128)S(1)}, bf16[256,512]{1,0:T(8,128)(2,1)}, f32[8,128]{1,0:T(8,128)S(1)}) custom-call(s32[3]{0:T(128)S(1)} %pad_add_fusion.1.refs_0_, bf16[64,1024]{1,0:T(8,128)(2,1)S(1)} %get-tuple-element.99.refs_1_, ...), custom_call_target="tpu_custom_call" | custom-call | tf_op jit(solution)/shard_map/pallas_call | solution.py:447
  81.9 3.4 %shard_map.92 = (bf16[1,128,4096]{2,1,0:T(8,128)(2,1)}, bf16[128,1024]{1,0:T(8,128)(2,1)}, f32[8,128]{1,0:T(8,128)S(1)}) custom-call(s32[2]{0:T(128)S(1)} %pad_add_fusion.2.refs_0_, bf16[128,512]{1,0:T(8,128)(2,1)S(1)} %get-tuple-element.104.refs_1_, bf16[128,512]{1,0:T(8,128)(2,1)S(1)} %get-tuple-element.105.refs_2_, bf16[2048,512]{1,0:T(8,128)(2,1)S(1)} %copy-done, ...), custom_call_target="tpu_custom_call" | custom-call | tf_op jit(solution)/shard_map/pallas_call | solution.py:447
  85.8 2.4 %collective-permute-start.13 = (bf16[2,2,128,256]{3,2,1,0:T(8,128)(2,1)}, bf16[2,2,128,256]{3,2,1,0:T(8,128)(2,1)S(1)}, u32[]{:S(2)}, u32[]{:S(2)}) collective-permute-start(bf16[2,2,128,256]{3,2,1,0:T(8,128)(2,1)} %get-tuple-element.97), channel_id=1, source_target_pairs={{0,4},{1,5},{2,6},{3,7},{4,0},{5,1},{6,2},{7,3},{8,12},{9,13},{10,... | collective-permute-start | bytes 786440 | tf_op jit(solution)/shard_map/ppermute | solution.py:490
  88.2 1.7 %collective-permute-start.14 = (bf16[2,2,128,256]{3,2,1,0:T(8,128)(2,1)}, bf16[2,2,128,256]{3,2,1,0:T(8,128)(2,1)S(1)}, u32[]{:S(2)}, u32[]{:S(2)}) collective-permute-start(bf16[2,2,128,256]{3,2,1,0:T(8,128)(2,1)} %get-tuple-element.98), channel_id=1, source_target_pairs={{0,6},{1,7},{2,0},{3,1},{4,2},{5,3},{6,4},{7,5},{8,14},{9,15},{10,... | collective-permute-start | bytes 786440 | tf_op jit(solution)/shard_map/ppermute | solution.py:490
  90.1 3.6 %collective-permute-start.25 = (bf16[128,512]{1,0:T(8,128)(2,1)S(1)}, bf16[128,512]{1,0:T(8,128)(2,1)S(1)}, u32[]{:S(2)}, u32[]{:S(2)}) collective-permute-start(bf16[128,512]{1,0:T(8,128)(2,1)S(1)} %get-tuple-element.116), channel_id=1, source_target_pairs={{0,8},{1,9},{2,10},{3,11},{4,12},{5,13},{6,14},{7,15},{8,0},{9,1},... | collective-permute-start | bytes 393224 | tf_op jit(solution)/shard_map/ppermute | solution.py:507
  94.4 4.1 %collective-permute-done.12.refs_2_ = bf16[2,2,128,256]{3,2,1,0:T(8,128)(2,1)S(1)} collective-permute-done((bf16[2,2,128,256]{3,2,1,0:T(8,128)(2,1)}, bf16[2,2,128,256]{3,2,1,0:T(8,128)(2,1)S(1)}, u32[]{:S(2)}, u32[]{:S(2)}) %collective-permute-start.12) | collective-permute-done | bytes 262176 | tf_op jit(solution)/shard_map/ppermute | solution.py:490
  98.4 2.4 %collective-permute-done.14.refs_4_ = bf16[2,2,128,256]{3,2,1,0:T(8,128)(2,1)S(1)} collective-permute-done((bf16[2,2,128,256]{3,2,1,0:T(8,128)(2,1)}, bf16[2,2,128,256]{3,2,1,0:T(8,128)(2,1)S(1)}, u32[]{:S(2)}, u32[]{:S(2)}) %collective-permute-start.14) | collective-permute-done | bytes 262176 | tf_op jit(solution)/shard_map/ppermute | solution.py:490
  (83 shorter events, 33.8 us)
Async XLA Ops:
  2.8 21.9 %collective-permute-start = (bf16[128,2048]{1,0:T(8,128)(2,1)}, bf16[128,2048]{1,0:T(8,128)(2,1)S(1)}, u32[]{:S(2)}, u32[]{:S(2)}) collective-permute-start(bf16[128,2048]{1,0:T(8,128)(2,1)} %get-tuple-element.65), channel_id=1, source_target_pairs={{0,16},{16,0},{1,17},{17,1},{2,18},{18,2},{3,19},{19,3},{4,20},{20... | collective-permute-start | bytes 1572872 | tf_op jit(solution)/shard_map/ppermute | solution.py:486
  10.2 10.4 %collective-permute-start.1 = (bf16[2,2,128,256]{3,2,1,0:T(8,128)(2,1)}, bf16[2,2,128,256]{3,2,1,0:T(8,128)(2,1)S(1)}, u32[]{:S(2)}, u32[]{:S(2)}) collective-permute-start(bf16[2,2,128,256]{3,2,1,0:T(8,128)(2,1)} %get-tuple-element.67), channel_id=1, source_target_pairs={{0,2},{1,3},{2,4},{3,5},{4,6},{5,7},{6,0},{7,1},{8,10},{9,11},{10,... | collective-permute-start | bytes 786440 | tf_op jit(solution)/shard_map/ppermute | solution.py:490
  11.8 10.8 %collective-permute-start.2 = (bf16[2,2,128,256]{3,2,1,0:T(8,128)(2,1)}, bf16[2,2,128,256]{3,2,1,0:T(8,128)(2,1)S(1)}, u32[]{:S(2)}, u32[]{:S(2)}) collective-permute-start(bf16[2,2,128,256]{3,2,1,0:T(8,128)(2,1)} %get-tuple-element.70), channel_id=1, source_target_pairs={{0,4},{1,5},{2,6},{3,7},{4,0},{5,1},{6,2},{7,3},{8,12},{9,13},{10,... | collective-permute-start | bytes 786440 | tf_op jit(solution)/shard_map/ppermute | solution.py:490
  13.3 11.4 %collective-permute-start.3 = (bf16[2,2,128,256]{3,2,1,0:T(8,128)(2,1)}, bf16[2,2,128,256]{3,2,1,0:T(8,128)(2,1)S(1)}, u32[]{:S(2)}, u32[]{:S(2)}) collective-permute-start(bf16[2,2,128,256]{3,2,1,0:T(8,128)(2,1)} %get-tuple-element.71), channel_id=1, source_target_pairs={{0,6},{1,7},{2,0},{3,1},{4,2},{5,3},{6,4},{7,5},{8,14},{9,15},{10,... | collective-permute-start | bytes 786440 | tf_op jit(solution)/shard_map/ppermute | solution.py:490
  26.6 16.6 %all-to-all-start = ((f32[16,2,2,16,128]{4,3,2,1,0:T(8,128)}), f32[16,2,2,16,128]{4,3,2,1,0:T(8,128)}, u32[]{:S(2)}, u32[]{:S(2)}) async-start(f32[16,2,2,16,128]{4,3,2,1,0:T(8,128)} %bitcast.10), calls=%async_computation | async-start | bytes 1048576 | tf_op jit(solution)/shard_map/all_to_all | solution.py:602
  33.4 8.6 %collective-permute-start.4 = (bf16[4,2,128,256]{3,2,1,0:T(8,128)(2,1)S(1)}, bf16[4,2,128,256]{3,2,1,0:T(8,128)(2,1)S(1)}, u32[]{:S(2)}, u32[]{:S(2)}) collective-permute-start(bf16[4,2,128,256]{3,2,1,0:T(8,128)(2,1)S(1)} %get-tuple-element.75), channel_id=1, source_target_pairs={{0,1},{1,0},{2,3},{3,2},{4,5},{5,4},{6,7},{7,6},{8,9},{9,8},{10,11... | collective-permute-start | bytes 1572872 | tf_op jit(solution)/shard_map/ppermute | solution.py:499
  35.8 17.1 %collective-permute-start.7 = (bf16[2,128,512]{2,1,0:T(8,128)(2,1)}, bf16[2,128,512]{2,1,0:T(8,128)(2,1)S(1)}, u32[]{:S(2)}, u32[]{:S(2)}) collective-permute-start(bf16[2,128,512]{2,1,0:T(8,128)(2,1)} %get-tuple-element.82), channel_id=1, source_target_pairs={{0,2},{1,3},{2,4},{3,5},{4,6},{5,7},{6,0},{7,1},{8,10},{9,11},{10,... | collective-permute-start | bytes 786440 | tf_op jit(solution)/shard_map/ppermute | solution.py:490
  37.7 15.3 %collective-permute-start.8 = (bf16[2,128,512]{2,1,0:T(8,128)(2,1)}, bf16[2,128,512]{2,1,0:T(8,128)(2,1)}, u32[]{:S(2)}, u32[]{:S(2)}) collective-permute-start(bf16[2,128,512]{2,1,0:T(8,128)(2,1)} %get-tuple-element.83), channel_id=1, source_target_pairs={{0,4},{1,5},{2,6},{3,7},{4,0},{5,1},{6,2},{7,3},{8,12},{9,13},{10,... | collective-permute-start | bytes 786440 | tf_op jit(solution)/shard_map/ppermute | solution.py:490
  39.1 13.8 %collective-permute-start.9 = (bf16[2,128,512]{2,1,0:T(8,128)(2,1)}, bf16[2,128,512]{2,1,0:T(8,128)(2,1)}, u32[]{:S(2)}, u32[]{:S(2)}) collective-permute-start(bf16[2,128,512]{2,1,0:T(8,128)(2,1)} %get-tuple-element.84), channel_id=1, source_target_pairs={{0,6},{1,7},{2,0},{3,1},{4,2},{5,3},{6,4},{7,5},{8,14},{9,15},{10,... | collective-permute-start | bytes 786440 | tf_op jit(solution)/shard_map/ppermute | solution.py:490
  40.6 41.4 %collective-permute-start.23 = (bf16[1024,512]{1,0:T(8,128)(2,1)}, bf16[1024,512]{1,0:T(8,128)(2,1)}, u32[]{:S(2)}, u32[]{:S(2)}) collective-permute-start(bf16[1024,512]{1,0:T(8,128)(2,1)} %get-tuple-element.106), channel_id=1, source_target_pairs={{0,16},{16,0},{1,17},{17,1},{2,18},{18,2},{3,19},{19,3},{4,20},{20... | collective-permute-start | bytes 3145736 | tf_op jit(solution)/shard_map/ppermute | solution.py:486
  44.8 8.1 %collective-permute-start.5 = (bf16[2,176,128]{2,1,0:T(8,128)(2,1)S(1)}, bf16[2,176,128]{2,1,0:T(8,128)(2,1)S(1)}, u32[]{:S(2)}, u32[]{:S(2)}) collective-permute-start(bf16[2,176,128]{2,1,0:T(8,128)(2,1)S(1)} %get-tuple-element.79), channel_id=1, source_target_pairs={{0,8},{1,9},{2,10},{3,11},{4,12},{5,13},{6,14},{7,15},{16,24},{17,... | collective-permute-start | bytes 270344 | tf_op jit(solution)/shard_map/ppermute | solution.py:507
  55.6 8.8 %collective-permute-start.10 = (bf16[2,176,128]{2,1,0:T(8,128)(2,1)S(1)}, bf16[2,176,128]{2,1,0:T(8,128)(2,1)S(1)}, u32[]{:S(2)}, u32[]{:S(2)}) collective-permute-start(bf16[2,176,128]{2,1,0:T(8,128)(2,1)S(1)} %get-tuple-element.89), channel_id=1, source_target_pairs={{8,0},{9,1},{10,2},{11,3},{12,4},{13,5},{14,6},{15,7},{24,16},{25,... | collective-permute-start | bytes 270344 | tf_op jit(solution)/shard_map/ppermute | solution.py:507
  66.7 9.9 %collective-permute-start.11 = (bf16[4,2,128,256]{3,2,1,0:T(8,128)(2,1)S(1)}, bf16[4,2,128,256]{3,2,1,0:T(8,128)(2,1)S(1)}, u32[]{:S(2)}, u32[]{:S(2)}) collective-permute-start(bf16[4,2,128,256]{3,2,1,0:T(8,128)(2,1)S(1)} %get-tuple-element.94), channel_id=1, source_target_pairs={{0,1},{1,0},{2,3},{3,2},{4,5},{5,4},{6,7},{7,6},{8,9},{9,8},{10,11... | collective-permute-start | bytes 1572872 | tf_op jit(solution)/shard_map/ppermute | solution.py:499
  66.7 5.9 %collective-permute-start.20 = (bf16[64,1024]{1,0:T(8,128)(2,1)S(1)}, bf16[64,1024]{1,0:T(8,128)(2,1)S(1)}, u32[]{:S(2)}, u32[]{:S(2)}) collective-permute-start(bf16[64,1024]{1,0:T(8,128)(2,1)S(1)} %get-tuple-element.99.refs_1_), channel_id=1, source_target_pairs={{0,6},{1,7},{2,0},{3,1},{4,2},{5,3},{6,4},{7,5},{8,14},{9,15},{10,... | collective-permute-start | bytes 393224 | tf_op jit(solution)/shard_map/ppermute | solution.py:490
  68.7 6.8 %collective-permute-start.18 = (bf16[64,1024]{1,0:T(8,128)(2,1)S(1)}, bf16[64,1024]{1,0:T(8,128)(2,1)S(1)}, u32[]{:S(2)}, u32[]{:S(2)}) collective-permute-start(bf16[64,1024]{1,0:T(8,128)(2,1)S(1)} %get-tuple-element.99.refs_1_), channel_id=1, source_target_pairs={{0,4},{1,5},{2,6},{3,7},{4,0},{5,1},{6,2},{7,3},{8,12},{9,13},{10,... | collective-permute-start | bytes 393224 | tf_op jit(solution)/shard_map/ppermute | solution.py:490
  68.8 7.8 %collective-permute-start.16 = (bf16[64,1024]{1,0:T(8,128)(2,1)S(1)}, bf16[64,1024]{1,0:T(8,128)(2,1)S(1)}, u32[]{:S(2)}, u32[]{:S(2)}) collective-permute-start(bf16[64,1024]{1,0:T(8,128)(2,1)S(1)} %get-tuple-element.99.refs_1_), channel_id=1, source_target_pairs={{0,2},{1,3},{2,4},{3,5},{4,6},{5,7},{6,0},{7,1},{8,10},{9,11},{10,... | collective-permute-start | bytes 393224 | tf_op jit(solution)/shard_map/ppermute | solution.py:490
  72.6 6.1 %collective-permute-start.15 = (bf16[64,1024]{1,0:T(8,128)(2,1)S(1)}, bf16[64,1024]{1,0:T(8,128)(2,1)S(1)}, u32[]{:S(2)}, u32[]{:S(2)}) collective-permute-start(bf16[64,1024]{1,0:T(8,128)(2,1)S(1)} %get-tuple-element.99.refs_1_), channel_id=1, source_target_pairs={{0,1},{1,0},{2,3},{3,2},{4,5},{5,4},{6,7},{7,6},{8,9},{9,8},{10,11... | collective-permute-start | bytes 393224 | tf_op jit(solution)/shard_map/ppermute | solution.py:499
  75.5 3.1 %collective-permute-start.21 = (bf16[64,1024]{1,0:T(8,128)(2,1)S(1)}, bf16[64,1024]{1,0:T(8,128)(2,1)S(1)}, u32[]{:S(2)}, u32[]{:S(2)}) collective-permute-start(bf16[64,1024]{1,0:T(8,128)(2,1)S(1)} %collective-permute-done.20.refs_7_), channel_id=1, source_target_pairs={{0,1},{1,0},{2,3},{3,2},{4,5},{5,4},{6,7},{7,6},{8,9},{9,8},{10,11... | collective-permute-start | bytes 393224 | tf_op jit(solution)/shard_map/ppermute | solution.py:499
  80.9 9.0 %collective-permute-start.22 = (bf16[256,512]{1,0:T(8,128)(2,1)}, bf16[256,512]{1,0:T(8,128)(2,1)S(1)}, u32[]{:S(2)}, u32[]{:S(2)}) collective-permute-start(bf16[256,512]{1,0:T(8,128)(2,1)} %get-tuple-element.103), channel_id=1, source_target_pairs={{0,16},{16,0},{1,17},{17,1},{2,18},{18,2},{3,19},{19,3},{4,20},{20... | collective-permute-start | bytes 786440 | tf_op jit(solution)/shard_map/ppermute | solution.py:486
  85.4 8.3 %collective-permute-start.24 = (bf16[128,1024]{1,0:T(8,128)(2,1)}, bf16[128,1024]{1,0:T(8,128)(2,1)S(1)}, u32[]{:S(2)}, u32[]{:S(2)}) collective-permute-start(bf16[128,1024]{1,0:T(8,128)(2,1)} %get-tuple-element.112), channel_id=1, source_target_pairs={{0,1},{1,0},{2,3},{3,2},{4,5},{5,4},{6,7},{7,6},{8,9},{9,8},{10,11... | collective-permute-start | bytes 786440 | tf_op jit(solution)/shard_map/ppermute | solution.py:499
  85.4 13.1 %collective-permute-start.12 = (bf16[2,2,128,256]{3,2,1,0:T(8,128)(2,1)}, bf16[2,2,128,256]{3,2,1,0:T(8,128)(2,1)S(1)}, u32[]{:S(2)}, u32[]{:S(2)}) collective-permute-start(bf16[2,2,128,256]{3,2,1,0:T(8,128)(2,1)} %get-tuple-element.96), channel_id=1, source_target_pairs={{0,2},{1,3},{2,4},{3,5},{4,6},{5,7},{6,0},{7,1},{8,10},{9,11},{10,... | collective-permute-start | bytes 786440 | tf_op jit(solution)/shard_map/ppermute | solution.py:490
  85.8 12.7 %collective-permute-start.13 = (bf16[2,2,128,256]{3,2,1,0:T(8,128)(2,1)}, bf16[2,2,128,256]{3,2,1,0:T(8,128)(2,1)S(1)}, u32[]{:S(2)}, u32[]{:S(2)}) collective-permute-start(bf16[2,2,128,256]{3,2,1,0:T(8,128)(2,1)} %get-tuple-element.97), channel_id=1, source_target_pairs={{0,4},{1,5},{2,6},{3,7},{4,0},{5,1},{6,2},{7,3},{8,12},{9,13},{10,... | collective-permute-start | bytes 786440 | tf_op jit(solution)/shard_map/ppermute | solution.py:490
  88.2 12.6 %collective-permute-start.14 = (bf16[2,2,128,256]{3,2,1,0:T(8,128)(2,1)}, bf16[2,2,128,256]{3,2,1,0:T(8,128)(2,1)S(1)}, u32[]{:S(2)}, u32[]{:S(2)}) collective-permute-start(bf16[2,2,128,256]{3,2,1,0:T(8,128)(2,1)} %get-tuple-element.98), channel_id=1, source_target_pairs={{0,6},{1,7},{2,0},{3,1},{4,2},{5,3},{6,4},{7,5},{8,14},{9,15},{10,... | collective-permute-start | bytes 786440 | tf_op jit(solution)/shard_map/ppermute | solution.py:490
  90.1 12.7 %collective-permute-start.25 = (bf16[128,512]{1,0:T(8,128)(2,1)S(1)}, bf16[128,512]{1,0:T(8,128)(2,1)S(1)}, u32[]{:S(2)}, u32[]{:S(2)}) collective-permute-start(bf16[128,512]{1,0:T(8,128)(2,1)S(1)} %get-tuple-element.116), channel_id=1, source_target_pairs={{0,8},{1,9},{2,10},{3,11},{4,12},{5,13},{6,14},{7,15},{8,0},{9,1},... | collective-permute-start | bytes 393224 | tf_op jit(solution)/shard_map/ppermute | solution.py:507
  (17 other events, 59.2 us)

commit v15 on v14

--- a/solution.py
+++ b/solution.py
@@ -355,7 +355,7 @@
                 held_ref[rows, :] = part_ref[which * half : (which + 1) * half, :]
 
 
-def product_kernel(group, at_ref, *rest):
+def product_kernel(group, dp_size, at_ref, *rest):
     rows_refs, rest = rest[:group], rest[group:]
     tokens_ref, own_rows_ref, other_rows_ref, *part_refs, total_ref, held_ref = rest
     place_rows(at_ref[1], at_ref[2], rows_refs, held_ref)
@@ -363,27 +363,12 @@
     tok = own_rows_ref.shape[0]
     own_rows_ref[...] = held_ref[:, aligned(2 * at_ref[1] + at_ref[2], tok)].T
     other_rows_ref[...] = held_ref[:, aligned(2 * at_ref[1] + 1 - at_ref[2], tok)].T
-    count = len(part_refs)
     size = part_refs[0].shape[0]
-    for shift, part_ref in enumerate(part_refs):
-        owner = lax.rem(at_ref[0] + shift, count)
-        part = total_ref[pl.ds(pl.multiple_of(owner * size, size), size), :]
-        part_ref[...] = part.astype(part_ref.dtype)
-
-
-def run_sum_kernel(arrived, at_ref, *rest):
-    own_ref, *rest = rest
-    total_ref = rest[-1]
-    total = own_ref[...]
-    for ref in rest[:arrived]:
-        total = total + ref[...].astype(f32)
-    total_ref[...] = total
-    part_refs = rest[arrived:-1]
-    size = part_refs[0].shape[0]
-    for shift, part_ref in enumerate(part_refs):
-        owner = lax.rem(at_ref[0] + shift, len(part_refs))
-        part = total_ref[pl.ds(pl.multiple_of(owner * size, size), size), :]
-        part_ref[...] = part.astype(part_ref.dtype)
+    runs = total_ref.shape[0] // size // dp_size
+    for i, part_ref in enumerate(part_refs):
+        dp = lax.rem(at_ref[0] + i // runs, dp_size)
+        run = lax.rem(at_ref[3] + i % runs, runs)
+        part_ref[...] = total_ref[aligned(dp * runs + run, size), :].astype(part_ref.dtype)
 
 
 def grad_tokens_kernel(at_ref, rows_ref, other_rows_ref, weight_ref, *rest):
@@ -498,13 +483,24 @@
     def to_other_core(x):
         return lax.ppermute(x, "ctx", [(i, i ^ 1) for i in range(ctx_size)])
 
-    def to_run(x, shift, wrap):
+    def to_run(x, shift):
         pairs = [
-            (i, (i + shift * group) % ctx_size)
+            (i, i + shift * group)
             for i in range(ctx_size)
-            if wrap or 0 <= i + shift * group < ctx_size
+            if 0 <= i + shift * group < ctx_size
         ]
         return lax.ppermute(x, "ctx", pairs)
+
+    def to_share(x, dp_shift, run_shift):
+        pairs = [
+            (
+                dp * ctx_size + i,
+                (dp + dp_shift) % dp_size * ctx_size + (i + run_shift * group) % ctx_size,
+            )
+            for dp in range(dp_size)
+            for i in range(ctx_size)
+        ]
+        return lax.ppermute(x, ("dp", "ctx"), pairs)
 
     qk_shape = ((group, 2, heads, F, tok), f32)
     state_shape = ((heads, PSI, DH), bf16)
@@ -619,7 +615,7 @@
     )
     prefix, suffix = (), ()
     if with_state:
-        prefix = [to_run(state[0], shift, False) for shift in range(1, runs)]
+        prefix = [to_run(state[0], shift) for shift in range(1, runs)]
     (numerator,), token = call(numerator_kernel, [rows_shape], qk, vg)
     (attended, grad_num, *carried), token = call(
         functools.partial(normalize_kernel, with_state),
@@ -631,7 +627,7 @@
         after_far=token_parts[1:],
     )
     if with_state:
-        suffix = [to_run(carried[0], -shift, False) for shift in range(1, runs)]
+        suffix = [to_run(carried[0], -shift) for shift in range(1, runs)]
     (grad_qk, grad_v), token = call(
         functools.partial(backward_kernel, with_state),
         [((2, heads, F, length), f32), ((heads, DH, length), f32)],
@@ -673,17 +669,17 @@
     results = [to_chip(part, shift) for shift, part in enumerate(results)]
 
     held = pltpu.VMEM((cols, length), bf16)
+    shares = dp_size * runs
     (own_rows, other_rows, own, *parts), token = call(
-        functools.partial(product_kernel, 2 * chips),
-        [((tok, cols), bf16)] * 2
-        + [((runs * depth, cols), f32)] + [((runs * depth, cols), bf16)] * (dp_size - 1),
+        functools.partial(product_kernel, 2 * chips, dp_size),
+        [((tok, cols), bf16)] * 2 + [((depth, cols), f32)] + [((depth, cols), bf16)] * (shares - 1),
         *rows,
         token_cols,
-        scalars=(dp_at, chip_at, core_at),
+        scalars=(dp_at, chip_at, core_at, run_at),
         after=(token,),
-        scratch=[pltpu.VMEM((dp_size * runs * depth, cols), f32), held],
-    )
-    parts = [to_dp(part, shift) for shift, part in enumerate(parts, 1)]
+        scratch=[pltpu.VMEM((shares * depth, cols), f32), held],
+    )
+    parts = [to_share(part, shift // runs, shift % runs) for shift, part in enumerate(parts, 1)]
     (grad_tokens, *others), tokens_token = call(
         grad_tokens_kernel,
         [((1, tok, width), bf16)] + [((tok, piece), bf16)] * (dp_size - 1),
@@ -693,15 +689,6 @@
         *fetched,
         scalars=[dp_at * share] + [base + parity * piece for base in bases],
         after=(token,),
-    )
-    (grad_proj, *parts), token = call(
-        functools.partial(run_sum_kernel, len(parts)),
-        [((depth, cols), f32)] + [((depth, cols), bf16)] * (runs - 1),
-        own,
-        *parts,
-        scalars=(run_at,),
-        after=(tokens_token,),
-        scratch=[pltpu.VMEM((runs * depth, cols), f32)],
     )
     (attended, grad_values), token = call(
         unpack_heads_kernel,
@@ -722,11 +709,7 @@
         alias=True,
     )
     (grad_proj,), _ = call(
-        final_sum_kernel,
-        [((depth, cols), f32)],
-        grad_proj,
-        *[to_run(part, shift, True) for shift, part in enumerate(parts, 1)],
-        after=(token, tokens_token),
+        final_sum_kernel, [((depth, cols), f32)], own, *parts, after=(token, tokens_token)
     )
     return (attended, grad_tokens, grad_values, grad_proj)
 

time: 105 us -> 116 us (1.10)
  waiting for transfers between devices: 21 us -> 26.8 us
  local copies, waits for them, and re-layouts: 7.85 us -> 11.9 us
  starting transfers between devices: 36.8 us -> 38.1 us
    ppermute x0 -> x3, waiting for transfers between devices: none -> 9.11 us  [to_share(): return lax.ppermute(x, ('dp', 'ctx'), pairs)]
    ppermute x0 -> x3, starting transfers between devices: none -> 6.1 us  [to_share(): return lax.ppermute(x, ('dp', 'ctx'), pairs)]
    unnamed x28 -> x36, local copies, waits for them, and re-layouts: 7.85 us -> 11.9 us
    ppermute x3 -> x2, starting transfers between devices: 9.55 us -> 5.95 us  [to_run(): return lax.ppermute(x, 'ctx', pairs)]
    ppermute x12, waiting for transfers between devices: 20 us -> 17.7 us  [to_member(): return lax.ppermute(x, 'ctx', pairs)]
    ppermute x3 -> x2, starting transfers between devices: 5.42 us -> 4.47 us  [to_dp(): lax.ppermute(x, 'dp', [(i, (i + shift) % dp_size) for i in range(dp_size)])]
    pallas_call x22 -> x21, Pallas kernels: 36.8 us -> 37.3 us  [call(): pl.pallas_call(kernel, out_shape=[jax.ShapeDtypeStruct(shape, kind) for s...]
  transfers between devices with their start and end apart: 27 -> 28, of which waited for: 8 -> 9; matrix products, arithmetic and copies ran while one was open for 0% -> 0% of each run, Pallas kernels for 33% -> 27%
where the time goes in v15:
time: 116 us; the launch traced here: 115 us
  starting transfers between devices  38.1 us (33%)
  Pallas kernels  37.3 us (32%)
  waiting for transfers between devices  26.8 us (23%)
  local copies, waits for them, and re-layouts  11.9 us (10%)
    pallas_call x21, Pallas kernels, call(): pl.pallas_call(kernel, out_shape=[jax.ShapeDtypeStruct(shape, kind) for s...  37.3 us
    ppermute x12, waiting for transfers between devices, to_member(): return lax.ppermute(x, 'ctx', pairs)  17.7 us
    ppermute x12, starting transfers between devices, to_member(): return lax.ppermute(x, 'ctx', pairs)  16.1 us
    unnamed x36, local copies, waits for them, and re-layouts  11.9 us
    ppermute x3, waiting for transfers between devices, to_share(): return lax.ppermute(x, ('dp', 'ctx'), pairs)  9.11 us
    ppermute x3, starting transfers between devices, to_share(): return lax.ppermute(x, ('dp', 'ctx'), pairs)  6.1 us
    ppermute x2, starting transfers between devices, to_run(): return lax.ppermute(x, 'ctx', pairs)  5.95 us
    ppermute x2, starting transfers between devices, to_dp(): lax.ppermute(x, 'dp', [(i, (i + shift) % dp_size) for i in range(dp_size)])  4.47 us
  transfers between devices with their start and end apart: 28, of which 9 were waited for; matrix products, arithmetic and copies ran while one was open for 0% of the time, Pallas kernels for 27%

profile of v15, /device:TPU:0, one launch (start us, length us, event | category | flops | bytes accessed | tf_op | source)
XLA Modules:
  0.0 115.3 jit_solution(9204781333065127723)
XLA Ops:
  2.8 3.0 %collective-permute-start = (bf16[128,2048]{1,0:T(8,128)(2,1)}, bf16[128,2048]{1,0:T(8,128)(2,1)S(1)}, u32[]{:S(2)}, u32[]{:S(2)}) collective-permute-start(bf16[128,2048]{1,0:T(8,128)(2,1)} %get-tuple-element.63), channel_id=1, source_target_pairs={{0,16},{16,0},{1,17},{17,1},{2,18},{18,2},{3,19},{19,3},{4,20},{20... | collective-permute-start | bytes 1572872 | tf_op jit(solution)/shard_map/ppermute | solution.py:471
  8.0 1.5 %shard_map.76 = (bf16[2,2,128,256]{3,2,1,0:T(8,128)(2,1)S(1)}, bf16[2,2,128,256]{3,2,1,0:T(8,128)(2,1)}, bf16[2,2,128,256]{3,2,1,0:T(8,128)(2,1)}, bf16[2,2,128,256]{3,2,1,0:T(8,128)(2,1)}, f32[8,128]{1,0:T(8,128)S(1)}) custom-call(s32[2]{0:T(128)S(1)} %pad_add_fusion.refs_0_, bf16[1,128,2048]{2,1,0:T(8,128)(2,1)S(1)} %copy-done.7, ...), custom_call_target="tpu_custom_call" | custom-call | tf_op jit(solution)/shard_map/pallas_call | solution.py:432
  10.2 1.5 %collective-permute-start.1 = (bf16[2,2,128,256]{3,2,1,0:T(8,128)(2,1)}, bf16[2,2,128,256]{3,2,1,0:T(8,128)(2,1)S(1)}, u32[]{:S(2)}, u32[]{:S(2)}) collective-permute-start(bf16[2,2,128,256]{3,2,1,0:T(8,128)(2,1)} %get-tuple-element.65), channel_id=1, source_target_pairs={{0,2},{1,3},{2,4},{3,5},{4,6},{5,7},{6,0},{7,1},{8,10},{9,11},{10,... | collective-permute-start | bytes 786440 | tf_op jit(solution)/shard_map/ppermute | solution.py:475
  11.8 1.6 %collective-permute-start.2 = (bf16[2,2,128,256]{3,2,1,0:T(8,128)(2,1)}, bf16[2,2,128,256]{3,2,1,0:T(8,128)(2,1)S(1)}, u32[]{:S(2)}, u32[]{:S(2)}) collective-permute-start(bf16[2,2,128,256]{3,2,1,0:T(8,128)(2,1)} %get-tuple-element.68), channel_id=1, source_target_pairs={{0,4},{1,5},{2,6},{3,7},{4,0},{5,1},{6,2},{7,3},{8,12},{9,13},{10,... | collective-permute-start | bytes 786440 | tf_op jit(solution)/shard_map/ppermute | solution.py:475
  16.6 4.1 %collective-permute-done.1.refs_2_.refs_7_ = bf16[2,2,128,256]{3,2,1,0:T(8,128)(2,1)S(1)} collective-permute-done((bf16[2,2,128,256]{3,2,1,0:T(8,128)(2,1)}, bf16[2,2,128,256]{3,2,1,0:T(8,128)(2,1)S(1)}, u32[]{:S(2)}, u32[]{:S(2)}) %collective-permute-start.1) | collective-permute-done | bytes 262176 | tf_op jit(solution)/shard_map/ppermute | solution.py:475
  22.5 2.2 %collective-permute-done.3.refs_9_.refs_4_ = bf16[2,2,128,256]{3,2,1,0:T(8,128)(2,1)S(1)} collective-permute-done((bf16[2,2,128,256]{3,2,1,0:T(8,128)(2,1)}, bf16[2,2,128,256]{3,2,1,0:T(8,128)(2,1)S(1)}, u32[]{:S(2)}, u32[]{:S(2)}) %collective-permute-start.3) | collective-permute-done | bytes 262176 | tf_op jit(solution)/shard_map/ppermute | solution.py:475
  26.6 4.4 %all-to-all-start = ((f32[16,2,2,16,128]{4,3,2,1,0:T(8,128)}), f32[16,2,2,16,128]{4,3,2,1,0:T(8,128)}, u32[]{:S(2)}, u32[]{:S(2)}) async-start(f32[16,2,2,16,128]{4,3,2,1,0:T(8,128)} %bitcast.10), calls=%async_computation | async-start | bytes 1048576 | tf_op jit(solution)/shard_map/all_to_all | solution.py:598
  35.8 1.8 %collective-permute-start.7 = (bf16[2,128,512]{2,1,0:T(8,128)(2,1)}, bf16[2,128,512]{2,1,0:T(8,128)(2,1)S(1)}, u32[]{:S(2)}, u32[]{:S(2)}) collective-permute-start(bf16[2,128,512]{2,1,0:T(8,128)(2,1)} %get-tuple-element.80), channel_id=1, source_target_pairs={{0,2},{1,3},{2,4},{3,5},{4,6},{5,7},{6,0},{7,1},{8,10},{9,11},{10,... | collective-permute-start | bytes 786440 | tf_op jit(solution)/shard_map/ppermute | solution.py:475
  43.2 1.6 %shard_map.83 = (f32[8,2,2,16,128]{4,3,2,1,0:T(8,128)S(1)}, bf16[2,176,128]{2,1,0:T(8,128)(2,1)S(1)}, f32[8,128]{1,0:T(8,128)}) custom-call(f32[2,8,2,2,16,128]{5,4,3,2,1,0:T(8,128)} %bitcast.5.refs_0_, bf16[8,2,128,256]{3,2,1,0:T(8,128)(2,1)S(1)} %get-tuple-element.74.refs_1_.refs_2_), custom_call_target="tpu_custom_call" | custom-call | tf_op jit(solution)/shard_map/pallas_call | solution.py:432
  44.8 4.5 %collective-permute-start.5 = (bf16[2,176,128]{2,1,0:T(8,128)(2,1)S(1)}, bf16[2,176,128]{2,1,0:T(8,128)(2,1)S(1)}, u32[]{:S(2)}, u32[]{:S(2)}) collective-permute-start(bf16[2,176,128]{2,1,0:T(8,128)(2,1)S(1)} %get-tuple-element.77), channel_id=1, source_target_pairs={{0,8},{1,9},{2,10},{3,11},{4,12},{5,13},{6,14},{7,15},{16,24},{17,... | collective-permute-start | bytes 270344 | tf_op jit(solution)/shard_map/ppermute | solution.py:492
  49.3 3.6 %shard_map.84 = (f32[1024,256]{1,0:T(8,128)S(1)}, f32[8,128]{1,0:T(8,128)}) custom-call(f32[8,2,2,16,128]{4,3,2,1,0:T(8,128)S(1)} %get-tuple-element.75.refs_0_.refs_1_, bf16[8,2,128,256]{3,2,1,0:T(8,128)(2,1)S(1)} %get-tuple-element.74.refs_1_.refs_2_), custom_call_target="tpu_custom_call" | custom-call | tf_op jit(solution)/shard_map/pallas_call | solution.py:432
  53.0 2.6 %shard_map.86 = (bf16[1024,256]{1,0:T(8,128)(2,1)S(1)}, f32[1024,256]{1,0:T(8,128)S(1)}, bf16[2,176,128]{2,1,0:T(8,128)(2,1)S(1)}, f32[8,128]{1,0:T(8,128)}) custom-call(f32[8,2,2,16,128]{4,3,2,1,0:T(8,128)S(1)} %get-tuple-element.75.refs_0_.refs_1_, bf16[8,2,128,256]{3,2,1,0:T(8,128)(2,1)S(1)} %get-tuple-element.74.refs_1_.refs_2_, ...), custom_call_target="tpu_custom_call" | custom-call | tf_op jit(solution)/shard_map/pallas_call | solution.py:432
  57.0 6.0 %shard_map.87 = (f32[2,2,16,1024]{3,2,1,0:T(8,128)S(1)}, f32[2,128,1024]{2,1,0:T(8,128)S(1)}, f32[8,128]{1,0:T(8,128)S(1)}) custom-call(f32[8,2,2,16,128]{4,3,2,1,0:T(8,128)S(1)} %get-tuple-element.75.refs_0_.refs_1_, bf16[8,2,128,256]{3,2,1,0:T(8,128)(2,1)S(1)} %get-tuple-element.74.refs_1_.refs_2_, f32[1024,256]{1,0:T(8,128)S(1)} %get-tuple-element.84.refs_2_, ...), custom_call_target="tpu_custom_call" | custom-call | tf_op jit(solution)/shard_map/pallas_call | solution.py:432
  65.4 2.6 %shard_map.89 = (bf16[64,1024]{1,0:T(8,128)(2,1)S(1)}, bf16[4,2,128,256]{3,2,1,0:T(8,128)(2,1)S(1)}, bf16[4,2,128,256]{3,2,1,0:T(8,128)(2,1)}, f32[8,128]{1,0:T(8,128)}) custom-call(s32[2]{0:T(128)S(1)} %pad_add_fusion.refs_0_, f32[8,2,2,16,128]{4,3,2,1,0:T(8,128)S(1)} %get-tuple-element.75.refs_0_.refs_1_, ...), custom_call_target="tpu_custom_call" | custom-call | tf_op jit(solution)/shard_map/pallas_call | solution.py:432
  68.8 2.0 %collective-permute-start.20 = (bf16[64,1024]{1,0:T(8,128)(2,1)S(1)}, bf16[64,1024]{1,0:T(8,128)(2,1)S(1)}, u32[]{:S(2)}, u32[]{:S(2)}) collective-permute-start(bf16[64,1024]{1,0:T(8,128)(2,1)S(1)} %get-tuple-element.97.refs_1_), channel_id=1, source_target_pairs={{0,6},{1,7},{2,0},{3,1},{4,2},{5,3},{6,4},{7,5},{8,14},{9,15},{10,... | collective-permute-start | bytes 393224 | tf_op jit(solution)/shard_map/ppermute | solution.py:475
  71.4 3.3 %collective-permute-done.20.refs_7_ = bf16[64,1024]{1,0:T(8,128)(2,1)S(1)} collective-permute-done((bf16[64,1024]{1,0:T(8,128)(2,1)S(1)}, bf16[64,1024]{1,0:T(8,128)(2,1)S(1)}, u32[]{:S(2)}, u32[]{:S(2)}) %collective-permute-start.20) | collective-permute-done | bytes 131104 | tf_op jit(solution)/shard_map/ppermute | solution.py:475
  74.7 2.8 %collective-permute-done.18.refs_5_ = bf16[64,1024]{1,0:T(8,128)(2,1)S(1)} collective-permute-done((bf16[64,1024]{1,0:T(8,128)(2,1)S(1)}, bf16[64,1024]{1,0:T(8,128)(2,1)S(1)}, u32[]{:S(2)}, u32[]{:S(2)}) %collective-permute-start.18) | collective-permute-done | bytes 131104 | tf_op jit(solution)/shard_map/ppermute | solution.py:475
  83.0 2.7 %shard_map.91 = (bf16[128,512]{1,0:T(8,128)(2,1)S(1)}, bf16[128,512]{1,0:T(8,128)(2,1)S(1)}, f32[128,512]{1,0:T(8,128)S(1)}, bf16[128,512]{1,0:T(8,128)(2,1)}, b...) custom-call(s32[4]{0:T(128)S(1)} %pad_add_fusion.1.refs_0_, ...), custom_call_target="tpu_custom_call" | custom-call | tf_op jit(solution)/shard_map/pallas_call | solution.py:432
  85.7 3.4 %shard_map.93 = (bf16[1,128,4096]{2,1,0:T(8,128)(2,1)}, bf16[128,1024]{1,0:T(8,128)(2,1)S(1)}, f32[8,128]{1,0:T(8,128)}) custom-call(s32[2]{0:T(128)S(1)} %pad_add_fusion.2.refs_0_, bf16[128,512]{1,0:T(8,128)(2,1)S(1)} %get-tuple-element.102.refs_1_, bf16[128,512]{1,0:T(8,128)(2,1)S(1)} %get-tuple-element.103.refs_2_, bf16[2048,512]{1,0:T(8,128)(2,1)S(1)} %copy-done, ...), custom_call_target="tpu_custom_call" | custom-call | tf_op jit(solution)/shard_map/pallas_call | solution.py:432
  89.4 2.0 %collective-permute-start.13 = (bf16[2,2,128,256]{3,2,1,0:T(8,128)(2,1)}, bf16[2,2,128,256]{3,2,1,0:T(8,128)(2,1)S(1)}, u32[]{:S(2)}, u32[]{:S(2)}) collective-permute-start(bf16[2,2,128,256]{3,2,1,0:T(8,128)(2,1)} %get-tuple-element.95), channel_id=1, source_target_pairs={{0,4},{1,5},{2,6},{3,7},{4,0},{5,1},{6,2},{7,3},{8,12},{9,13},{10,... | collective-permute-start | bytes 786440 | tf_op jit(solution)/shard_map/ppermute | solution.py:475
  91.5 2.0 %collective-permute-start.14 = (bf16[2,2,128,256]{3,2,1,0:T(8,128)(2,1)}, bf16[2,2,128,256]{3,2,1,0:T(8,128)(2,1)S(1)}, u32[]{:S(2)}, u32[]{:S(2)}) collective-permute-start(bf16[2,2,128,256]{3,2,1,0:T(8,128)(2,1)} %get-tuple-element.96), channel_id=1, source_target_pairs={{0,6},{1,7},{2,0},{3,1},{4,2},{5,3},{6,4},{7,5},{8,14},{9,15},{10,... | collective-permute-start | bytes 786440 | tf_op jit(solution)/shard_map/ppermute | solution.py:475
  93.4 3.6 %collective-permute-start.24 = (bf16[128,512]{1,0:T(8,128)(2,1)}, bf16[128,512]{1,0:T(8,128)(2,1)S(1)}, u32[]{:S(2)}, u32[]{:S(2)}) collective-permute-start(bf16[128,512]{1,0:T(8,128)(2,1)} %get-tuple-element.110), channel_id=1, source_target_pairs={{0,8},{1,9},{2,10},{3,11},{4,12},{5,13},{6,14},{7,15},{8,0},{9,1},... | collective-permute-start | bytes 393224 | tf_op jit(solution)/shard_map/ppermute | solution.py:503
  98.5 3.6 %collective-permute-done.12.refs_2_ = bf16[2,2,128,256]{3,2,1,0:T(8,128)(2,1)S(1)} collective-permute-done((bf16[2,2,128,256]{3,2,1,0:T(8,128)(2,1)S(1)}, bf16[2,2,128,256]{3,2,1,0:T(8,128)(2,1)S(1)}, u32[]{:S(2)}, u32[]{:S(2)}) %collective-permute-start.12) | collective-permute-done | bytes 262176 | tf_op jit(solution)/shard_map/ppermute | solution.py:475
  106.9 7.6 %collective-permute-done.26.refs_3_ = bf16[128,512]{1,0:T(8,128)(2,1)S(1)} collective-permute-done((bf16[128,512]{1,0:T(8,128)(2,1)}, bf16[128,512]{1,0:T(8,128)(2,1)S(1)}, u32[]{:S(2)}, u32[]{:S(2)}) %collective-permute-start.26) | collective-permute-done | bytes 131104 | tf_op jit(solution)/shard_map/ppermute | solution.py:503
  (92 shorter events, 40.5 us)
Async XLA Ops:
  2.8 21.9 %collective-permute-start = (bf16[128,2048]{1,0:T(8,128)(2,1)}, bf16[128,2048]{1,0:T(8,128)(2,1)S(1)}, u32[]{:S(2)}, u32[]{:S(2)}) collective-permute-start(bf16[128,2048]{1,0:T(8,128)(2,1)} %get-tuple-element.63), channel_id=1, source_target_pairs={{0,16},{16,0},{1,17},{17,1},{2,18},{18,2},{3,19},{19,3},{4,20},{20... | collective-permute-start | bytes 1572872 | tf_op jit(solution)/shard_map/ppermute | solution.py:471
  10.2 10.4 %collective-permute-start.1 = (bf16[2,2,128,256]{3,2,1,0:T(8,128)(2,1)}, bf16[2,2,128,256]{3,2,1,0:T(8,128)(2,1)S(1)}, u32[]{:S(2)}, u32[]{:S(2)}) collective-permute-start(bf16[2,2,128,256]{3,2,1,0:T(8,128)(2,1)} %get-tuple-element.65), channel_id=1, source_target_pairs={{0,2},{1,3},{2,4},{3,5},{4,6},{5,7},{6,0},{7,1},{8,10},{9,11},{10,... | collective-permute-start | bytes 786440 | tf_op jit(solution)/shard_map/ppermute | solution.py:475
  11.8 10.8 %collective-permute-start.2 = (bf16[2,2,128,256]{3,2,1,0:T(8,128)(2,1)}, bf16[2,2,128,256]{3,2,1,0:T(8,128)(2,1)S(1)}, u32[]{:S(2)}, u32[]{:S(2)}) collective-permute-start(bf16[2,2,128,256]{3,2,1,0:T(8,128)(2,1)} %get-tuple-element.68), channel_id=1, source_target_pairs={{0,4},{1,5},{2,6},{3,7},{4,0},{5,1},{6,2},{7,3},{8,12},{9,13},{10,... | collective-permute-start | bytes 786440 | tf_op jit(solution)/shard_map/ppermute | solution.py:475
  13.3 11.4 %collective-permute-start.3 = (bf16[2,2,128,256]{3,2,1,0:T(8,128)(2,1)}, bf16[2,2,128,256]{3,2,1,0:T(8,128)(2,1)S(1)}, u32[]{:S(2)}, u32[]{:S(2)}) collective-permute-start(bf16[2,2,128,256]{3,2,1,0:T(8,128)(2,1)} %get-tuple-element.69), channel_id=1, source_target_pairs={{0,6},{1,7},{2,0},{3,1},{4,2},{5,3},{6,4},{7,5},{8,14},{9,15},{10,... | collective-permute-start | bytes 786440 | tf_op jit(solution)/shard_map/ppermute | solution.py:475
  26.6 16.6 %all-to-all-start = ((f32[16,2,2,16,128]{4,3,2,1,0:T(8,128)}), f32[16,2,2,16,128]{4,3,2,1,0:T(8,128)}, u32[]{:S(2)}, u32[]{:S(2)}) async-start(f32[16,2,2,16,128]{4,3,2,1,0:T(8,128)} %bitcast.10), calls=%async_computation | async-start | bytes 1048576 | tf_op jit(solution)/shard_map/all_to_all | solution.py:598
  33.4 8.6 %collective-permute-start.4 = (bf16[4,2,128,256]{3,2,1,0:T(8,128)(2,1)S(1)}, bf16[4,2,128,256]{3,2,1,0:T(8,128)(2,1)S(1)}, u32[]{:S(2)}, u32[]{:S(2)}) collective-permute-start(bf16[4,2,128,256]{3,2,1,0:T(8,128)(2,1)S(1)} %get-tuple-element.73), channel_id=1, source_target_pairs={{0,1},{1,0},{2,3},{3,2},{4,5},{5,4},{6,7},{7,6},{8,9},{9,8},{10,11... | collective-permute-start | bytes 1572872 | tf_op jit(solution)/shard_map/ppermute | solution.py:484
  35.8 17.1 %collective-permute-start.7 = (bf16[2,128,512]{2,1,0:T(8,128)(2,1)}, bf16[2,128,512]{2,1,0:T(8,128)(2,1)S(1)}, u32[]{:S(2)}, u32[]{:S(2)}) collective-permute-start(bf16[2,128,512]{2,1,0:T(8,128)(2,1)} %get-tuple-element.80), channel_id=1, source_target_pairs={{0,2},{1,3},{2,4},{3,5},{4,6},{5,7},{6,0},{7,1},{8,10},{9,11},{10,... | collective-permute-start | bytes 786440 | tf_op jit(solution)/shard_map/ppermute | solution.py:475
  37.6 15.3 %collective-permute-start.8 = (bf16[2,128,512]{2,1,0:T(8,128)(2,1)}, bf16[2,128,512]{2,1,0:T(8,128)(2,1)}, u32[]{:S(2)}, u32[]{:S(2)}) collective-permute-start(bf16[2,128,512]{2,1,0:T(8,128)(2,1)} %get-tuple-element.81), channel_id=1, source_target_pairs={{0,4},{1,5},{2,6},{3,7},{4,0},{5,1},{6,2},{7,3},{8,12},{9,13},{10,... | collective-permute-start | bytes 786440 | tf_op jit(solution)/shard_map/ppermute | solution.py:475
  39.1 13.8 %collective-permute-start.9 = (bf16[2,128,512]{2,1,0:T(8,128)(2,1)}, bf16[2,128,512]{2,1,0:T(8,128)(2,1)}, u32[]{:S(2)}, u32[]{:S(2)}) collective-permute-start(bf16[2,128,512]{2,1,0:T(8,128)(2,1)} %get-tuple-element.82), channel_id=1, source_target_pairs={{0,6},{1,7},{2,0},{3,1},{4,2},{5,3},{6,4},{7,5},{8,14},{9,15},{10,... | collective-permute-start | bytes 786440 | tf_op jit(solution)/shard_map/ppermute | solution.py:475
  40.6 45.2 %collective-permute-start.22 = (bf16[1024,512]{1,0:T(8,128)(2,1)}, bf16[1024,512]{1,0:T(8,128)(2,1)}, u32[]{:S(2)}, u32[]{:S(2)}) collective-permute-start(bf16[1024,512]{1,0:T(8,128)(2,1)} %get-tuple-element.104), channel_id=1, source_target_pairs={{0,16},{16,0},{1,17},{17,1},{2,18},{18,2},{3,19},{19,3},{4,20},{20... | collective-permute-start | bytes 3145736 | tf_op jit(solution)/shard_map/ppermute | solution.py:471
  44.8 8.1 %collective-permute-start.5 = (bf16[2,176,128]{2,1,0:T(8,128)(2,1)S(1)}, bf16[2,176,128]{2,1,0:T(8,128)(2,1)S(1)}, u32[]{:S(2)}, u32[]{:S(2)}) collective-permute-start(bf16[2,176,128]{2,1,0:T(8,128)(2,1)S(1)} %get-tuple-element.77), channel_id=1, source_target_pairs={{0,8},{1,9},{2,10},{3,11},{4,12},{5,13},{6,14},{7,15},{16,24},{17,... | collective-permute-start | bytes 270344 | tf_op jit(solution)/shard_map/ppermute | solution.py:492
  55.6 9.8 %collective-permute-start.10 = (bf16[2,176,128]{2,1,0:T(8,128)(2,1)S(1)}, bf16[2,176,128]{2,1,0:T(8,128)(2,1)S(1)}, u32[]{:S(2)}, u32[]{:S(2)}) collective-permute-start(bf16[2,176,128]{2,1,0:T(8,128)(2,1)S(1)} %get-tuple-element.87), channel_id=1, source_target_pairs={{8,0},{9,1},{10,2},{11,3},{12,4},{13,5},{14,6},{15,7},{24,16},{25,... | collective-permute-start | bytes 270344 | tf_op jit(solution)/shard_map/ppermute | solution.py:492
  68.8 9.9 %collective-permute-start.11 = (bf16[4,2,128,256]{3,2,1,0:T(8,128)(2,1)}, bf16[4,2,128,256]{3,2,1,0:T(8,128)(2,1)S(1)}, u32[]{:S(2)}, u32[]{:S(2)}) collective-permute-start(bf16[4,2,128,256]{3,2,1,0:T(8,128)(2,1)} %get-tuple-element.92), channel_id=1, source_target_pairs={{0,1},{1,0},{2,3},{3,2},{4,5},{5,4},{6,7},{7,6},{8,9},{9,8},{10,11... | collective-permute-start | bytes 1572872 | tf_op jit(solution)/shard_map/ppermute | solution.py:484
  68.8 5.9 %collective-permute-start.20 = (bf16[64,1024]{1,0:T(8,128)(2,1)S(1)}, bf16[64,1024]{1,0:T(8,128)(2,1)S(1)}, u32[]{:S(2)}, u32[]{:S(2)}) collective-permute-start(bf16[64,1024]{1,0:T(8,128)(2,1)S(1)} %get-tuple-element.97.refs_1_), channel_id=1, source_target_pairs={{0,6},{1,7},{2,0},{3,1},{4,2},{5,3},{6,4},{7,5},{8,14},{9,15},{10,... | collective-permute-start | bytes 393224 | tf_op jit(solution)/shard_map/ppermute | solution.py:475
  70.8 6.7 %collective-permute-start.18 = (bf16[64,1024]{1,0:T(8,128)(2,1)S(1)}, bf16[64,1024]{1,0:T(8,128)(2,1)S(1)}, u32[]{:S(2)}, u32[]{:S(2)}) collective-permute-start(bf16[64,1024]{1,0:T(8,128)(2,1)S(1)} %get-tuple-element.97.refs_1_), channel_id=1, source_target_pairs={{0,4},{1,5},{2,6},{3,7},{4,0},{5,1},{6,2},{7,3},{8,12},{9,13},{10,... | collective-permute-start | bytes 393224 | tf_op jit(solution)/shard_map/ppermute | solution.py:475
  70.8 7.9 %collective-permute-start.16 = (bf16[64,1024]{1,0:T(8,128)(2,1)S(1)}, bf16[64,1024]{1,0:T(8,128)(2,1)S(1)}, u32[]{:S(2)}, u32[]{:S(2)}) collective-permute-start(bf16[64,1024]{1,0:T(8,128)(2,1)S(1)} %get-tuple-element.97.refs_1_), channel_id=1, source_target_pairs={{0,2},{1,3},{2,4},{3,5},{4,6},{5,7},{6,0},{7,1},{8,10},{9,11},{10,... | collective-permute-start | bytes 393224 | tf_op jit(solution)/shard_map/ppermute | solution.py:475
  74.7 7.1 %collective-permute-start.15 = (bf16[64,1024]{1,0:T(8,128)(2,1)S(1)}, bf16[64,1024]{1,0:T(8,128)(2,1)S(1)}, u32[]{:S(2)}, u32[]{:S(2)}) collective-permute-start(bf16[64,1024]{1,0:T(8,128)(2,1)S(1)} %get-tuple-element.97.refs_1_), channel_id=1, source_target_pairs={{0,1},{1,0},{2,3},{3,2},{4,5},{5,4},{6,7},{7,6},{8,9},{9,8},{10,11... | collective-permute-start | bytes 393224 | tf_op jit(solution)/shard_map/ppermute | solution.py:484
  89.1 7.9 %collective-permute-start.23 = (bf16[128,1024]{1,0:T(8,128)(2,1)S(1)}, bf16[128,1024]{1,0:T(8,128)(2,1)S(1)}, u32[]{:S(2)}, u32[]{:S(2)}) collective-permute-start(bf16[128,1024]{1,0:T(8,128)(2,1)S(1)} %get-tuple-element.106), channel_id=1, source_target_pairs={{0,1},{1,0},{2,3},{3,2},{4,5},{5,4},{6,7},{7,6},{8,9},{9,8},{10,11... | collective-permute-start | bytes 786440 | tf_op jit(solution)/shard_map/ppermute | solution.py:484
  89.1 12.9 %collective-permute-start.12 = (bf16[2,2,128,256]{3,2,1,0:T(8,128)(2,1)S(1)}, bf16[2,2,128,256]{3,2,1,0:T(8,128)(2,1)S(1)}, u32[]{:S(2)}, u32[]{:S(2)}) collective-permute-start(bf16[2,2,128,256]{3,2,1,0:T(8,128)(2,1)S(1)} %get-tuple-element.94), channel_id=1, source_target_pairs={{0,2},{1,3},{2,4},{3,5},{4,6},{5,7},{6,0},{7,1},{8,10},{9,11},{10,... | collective-permute-start | bytes 786440 | tf_op jit(solution)/shard_map/ppermute | solution.py:475
  89.4 14.4 %collective-permute-start.13 = (bf16[2,2,128,256]{3,2,1,0:T(8,128)(2,1)}, bf16[2,2,128,256]{3,2,1,0:T(8,128)(2,1)S(1)}, u32[]{:S(2)}, u32[]{:S(2)}) collective-permute-start(bf16[2,2,128,256]{3,2,1,0:T(8,128)(2,1)} %get-tuple-element.95), channel_id=1, source_target_pairs={{0,4},{1,5},{2,6},{3,7},{4,0},{5,1},{6,2},{7,3},{8,12},{9,13},{10,... | collective-permute-start | bytes 786440 | tf_op jit(solution)/shard_map/ppermute | solution.py:475
  91.5 12.9 %collective-permute-start.14 = (bf16[2,2,128,256]{3,2,1,0:T(8,128)(2,1)}, bf16[2,2,128,256]{3,2,1,0:T(8,128)(2,1)S(1)}, u32[]{:S(2)}, u32[]{:S(2)}) collective-permute-start(bf16[2,2,128,256]{3,2,1,0:T(8,128)(2,1)} %get-tuple-element.96), channel_id=1, source_target_pairs={{0,6},{1,7},{2,0},{3,1},{4,2},{5,3},{6,4},{7,5},{8,14},{9,15},{10,... | collective-permute-start | bytes 786440 | tf_op jit(solution)/shard_map/ppermute | solution.py:475
  93.4 13.4 %collective-permute-start.24 = (bf16[128,512]{1,0:T(8,128)(2,1)}, bf16[128,512]{1,0:T(8,128)(2,1)S(1)}, u32[]{:S(2)}, u32[]{:S(2)}) collective-permute-start(bf16[128,512]{1,0:T(8,128)(2,1)} %get-tuple-element.110), channel_id=1, source_target_pairs={{0,8},{1,9},{2,10},{3,11},{4,12},{5,13},{6,14},{7,15},{8,0},{9,1},... | collective-permute-start | bytes 393224 | tf_op jit(solution)/shard_map/ppermute | solution.py:503
  97.0 9.9 %collective-permute-start.25 = (bf16[128,512]{1,0:T(8,128)(2,1)}, bf16[128,512]{1,0:T(8,128)(2,1)S(1)}, u32[]{:S(2)}, u32[]{:S(2)}) collective-permute-start(bf16[128,512]{1,0:T(8,128)(2,1)} %get-tuple-element.111), channel_id=1, source_target_pairs={{0,16},{1,17},{2,18},{3,19},{4,20},{5,21},{6,22},{7,23},{8,24},{9,... | collective-permute-start | bytes 393224 | tf_op jit(solution)/shard_map/ppermute | solution.py:503
  102.0 12.5 %collective-permute-start.26 = (bf16[128,512]{1,0:T(8,128)(2,1)}, bf16[128,512]{1,0:T(8,128)(2,1)S(1)}, u32[]{:S(2)}, u32[]{:S(2)}) collective-permute-start(bf16[128,512]{1,0:T(8,128)(2,1)} %get-tuple-element.112), channel_id=1, source_target_pairs={{0,24},{1,25},{2,26},{3,27},{4,28},{5,29},{6,30},{7,31},{8,16},{9,... | collective-permute-start | bytes 393224 | tf_op jit(solution)/shard_map/ppermute | solution.py:503
  (22 other events, 68.6 us)

commit v16 on v14

--- a/solution.py
+++ b/solution.py
@@ -700,7 +700,6 @@
         own,
         *parts,
         scalars=(run_at,),
-        after=(tokens_token,),
         scratch=[pltpu.VMEM((runs * depth, cols), f32)],
     )
     (attended, grad_values), token = call(

time: 105 us -> 105 us (level)
  no operation moved by 1% of the time
where the time goes in v16:
time: 105 us; the launch traced here: 104 us
  Pallas kernels  36.8 us (35%)
  starting transfers between devices  36.8 us (35%)
  waiting for transfers between devices  21 us (20%)
  local copies, waits for them, and re-layouts  7.85 us (7%)
    pallas_call x22, Pallas kernels, call(): pl.pallas_call(kernel, out_shape=[jax.ShapeDtypeStruct(shape, kind) for s...  36.8 us
    ppermute x12, waiting for transfers between devices, to_member(): return lax.ppermute(x, 'ctx', pairs)  20 us
    ppermute x12, starting transfers between devices, to_member(): return lax.ppermute(x, 'ctx', pairs)  16.4 us
    ppermute x3, starting transfers between devices, to_run(): return lax.ppermute(x, 'ctx', pairs)  9.55 us
    unnamed x28, local copies, waits for them, and re-layouts  7.85 us
    ppermute x3, starting transfers between devices, to_dp(): lax.ppermute(x, 'dp', [(i, (i + shift) % dp_size) for i in range(dp_size)])  5.42 us
    all_to_all x1, starting transfers between devices, local(): lax.all_to_all(projected.reshape((dp_size * group,) + qk_shape[0][1:]), (...  4.39 us
  transfers between devices with their start and end apart: 27, of which 8 were waited for; matrix products, arithmetic and copies ran while one was open for 0% of the time, Pallas kernels for 33%

profile of v16, /device:TPU:0, one launch (start us, length us, event | category | flops | bytes accessed | tf_op | source)
XLA Modules:
  0.0 103.5 jit_solution(375685053669961560)
XLA Ops:
  2.8 3.0 %collective-permute-start = (bf16[128,2048]{1,0:T(8,128)(2,1)}, bf16[128,2048]{1,0:T(8,128)(2,1)S(1)}, u32[]{:S(2)}, u32[]{:S(2)}) collective-permute-start(bf16[128,2048]{1,0:T(8,128)(2,1)} %get-tuple-element.64), channel_id=1, source_target_pairs={{0,16},{16,0},{1,17},{17,1},{2,18},{18,2},{3,19},{19,3},{4,20},{20... | collective-permute-start | bytes 1572872 | tf_op jit(solution)/shard_map/ppermute | solution.py:486
  8.0 1.5 %shard_map.76 = (bf16[2,2,128,256]{3,2,1,0:T(8,128)(2,1)S(1)}, bf16[2,2,128,256]{3,2,1,0:T(8,128)(2,1)}, bf16[2,2,128,256]{3,2,1,0:T(8,128)(2,1)}, bf16[2,2,128,256]{3,2,1,0:T(8,128)(2,1)}, f32[8,128]{1,0:T(8,128)S(1)}) custom-call(s32[2]{0:T(128)S(1)} %pad_add_fusion.refs_0_, bf16[1,128,2048]{2,1,0:T(8,128)(2,1)S(1)} %copy-done.5, ...), custom_call_target="tpu_custom_call" | custom-call | tf_op jit(solution)/shard_map/pallas_call | solution.py:447
  10.2 1.5 %collective-permute-start.1 = (bf16[2,2,128,256]{3,2,1,0:T(8,128)(2,1)}, bf16[2,2,128,256]{3,2,1,0:T(8,128)(2,1)S(1)}, u32[]{:S(2)}, u32[]{:S(2)}) collective-permute-start(bf16[2,2,128,256]{3,2,1,0:T(8,128)(2,1)} %get-tuple-element.66), channel_id=1, source_target_pairs={{0,2},{1,3},{2,4},{3,5},{4,6},{5,7},{6,0},{7,1},{8,10},{9,11},{10,... | collective-permute-start | bytes 786440 | tf_op jit(solution)/shard_map/ppermute | solution.py:490
  11.8 1.6 %collective-permute-start.2 = (bf16[2,2,128,256]{3,2,1,0:T(8,128)(2,1)}, bf16[2,2,128,256]{3,2,1,0:T(8,128)(2,1)S(1)}, u32[]{:S(2)}, u32[]{:S(2)}) collective-permute-start(bf16[2,2,128,256]{3,2,1,0:T(8,128)(2,1)} %get-tuple-element.69), channel_id=1, source_target_pairs={{0,4},{1,5},{2,6},{3,7},{4,0},{5,1},{6,2},{7,3},{8,12},{9,13},{10,... | collective-permute-start | bytes 786440 | tf_op jit(solution)/shard_map/ppermute | solution.py:490
  16.6 4.1 %collective-permute-done.1.refs_2_.refs_7_ = bf16[2,2,128,256]{3,2,1,0:T(8,128)(2,1)S(1)} collective-permute-done((bf16[2,2,128,256]{3,2,1,0:T(8,128)(2,1)}, bf16[2,2,128,256]{3,2,1,0:T(8,128)(2,1)S(1)}, u32[]{:S(2)}, u32[]{:S(2)}) %collective-permute-start.1) | collective-permute-done | bytes 262176 | tf_op jit(solution)/shard_map/ppermute | solution.py:490
  22.6 2.2 %collective-permute-done.3.refs_9_.refs_4_ = bf16[2,2,128,256]{3,2,1,0:T(8,128)(2,1)S(1)} collective-permute-done((bf16[2,2,128,256]{3,2,1,0:T(8,128)(2,1)}, bf16[2,2,128,256]{3,2,1,0:T(8,128)(2,1)S(1)}, u32[]{:S(2)}, u32[]{:S(2)}) %collective-permute-start.3) | collective-permute-done | bytes 262176 | tf_op jit(solution)/shard_map/ppermute | solution.py:490
  26.6 4.4 %all-to-all-start = ((f32[16,2,2,16,128]{4,3,2,1,0:T(8,128)}), f32[16,2,2,16,128]{4,3,2,1,0:T(8,128)}, u32[]{:S(2)}, u32[]{:S(2)}) async-start(f32[16,2,2,16,128]{4,3,2,1,0:T(8,128)} %bitcast.10), calls=%async_computation | async-start | bytes 1048576 | tf_op jit(solution)/shard_map/all_to_all | solution.py:602
  35.8 1.8 %collective-permute-start.7 = (bf16[2,128,512]{2,1,0:T(8,128)(2,1)}, bf16[2,128,512]{2,1,0:T(8,128)(2,1)S(1)}, u32[]{:S(2)}, u32[]{:S(2)}) collective-permute-start(bf16[2,128,512]{2,1,0:T(8,128)(2,1)} %get-tuple-element.81), channel_id=1, source_target_pairs={{0,2},{1,3},{2,4},{3,5},{4,6},{5,7},{6,0},{7,1},{8,10},{9,11},{10,... | collective-permute-start | bytes 786440 | tf_op jit(solution)/shard_map/ppermute | solution.py:490
  43.2 1.6 %shard_map.83 = (f32[8,2,2,16,128]{4,3,2,1,0:T(8,128)S(1)}, bf16[2,176,128]{2,1,0:T(8,128)(2,1)S(1)}, f32[8,128]{1,0:T(8,128)}) custom-call(f32[2,8,2,2,16,128]{5,4,3,2,1,0:T(8,128)} %bitcast.5.refs_0_, bf16[8,2,128,256]{3,2,1,0:T(8,128)(2,1)S(1)} %get-tuple-element.75.refs_1_.refs_2_), custom_call_target="tpu_custom_call" | custom-call | tf_op jit(solution)/shard_map/pallas_call | solution.py:447
  44.8 4.5 %collective-permute-start.5 = (bf16[2,176,128]{2,1,0:T(8,128)(2,1)S(1)}, bf16[2,176,128]{2,1,0:T(8,128)(2,1)S(1)}, u32[]{:S(2)}, u32[]{:S(2)}) collective-permute-start(bf16[2,176,128]{2,1,0:T(8,128)(2,1)S(1)} %get-tuple-element.78), channel_id=1, source_target_pairs={{0,8},{1,9},{2,10},{3,11},{4,12},{5,13},{6,14},{7,15},{16,24},{17,... | collective-permute-start | bytes 270344 | tf_op jit(solution)/shard_map/ppermute | solution.py:507
  49.3 3.6 %shard_map.84 = (f32[1024,256]{1,0:T(8,128)S(1)}, f32[8,128]{1,0:T(8,128)}) custom-call(f32[8,2,2,16,128]{4,3,2,1,0:T(8,128)S(1)} %get-tuple-element.76.refs_0_.refs_1_, bf16[8,2,128,256]{3,2,1,0:T(8,128)(2,1)S(1)} %get-tuple-element.75.refs_1_.refs_2_), custom_call_target="tpu_custom_call" | custom-call | tf_op jit(solution)/shard_map/pallas_call | solution.py:447
  53.0 2.6 %shard_map.86 = (bf16[1024,256]{1,0:T(8,128)(2,1)S(1)}, f32[1024,256]{1,0:T(8,128)S(1)}, bf16[2,176,128]{2,1,0:T(8,128)(2,1)S(1)}, f32[8,128]{1,0:T(8,128)}) custom-call(f32[8,2,2,16,128]{4,3,2,1,0:T(8,128)S(1)} %get-tuple-element.76.refs_0_.refs_1_, bf16[8,2,128,256]{3,2,1,0:T(8,128)(2,1)S(1)} %get-tuple-element.75.refs_1_.refs_2_, ...), custom_call_target="tpu_custom_call" | custom-call | tf_op jit(solution)/shard_map/pallas_call | solution.py:447
  57.0 5.9 %shard_map.87 = (f32[2,2,16,1024]{3,2,1,0:T(8,128)S(1)}, f32[2,128,1024]{2,1,0:T(8,128)S(1)}, f32[8,128]{1,0:T(8,128)S(1)}) custom-call(f32[8,2,2,16,128]{4,3,2,1,0:T(8,128)S(1)} %get-tuple-element.76.refs_0_.refs_1_, bf16[8,2,128,256]{3,2,1,0:T(8,128)(2,1)S(1)} %get-tuple-element.75.refs_1_.refs_2_, f32[1024,256]{1,0:T(8,128)S(1)} %get-tuple-element.85.refs_2_, ...), custom_call_target="tpu_custom_call" | custom-call | tf_op jit(solution)/shard_map/pallas_call | solution.py:447
  64.4 2.3 %shard_map.89 = (bf16[64,1024]{1,0:T(8,128)(2,1)S(1)}, bf16[4,2,128,256]{3,2,1,0:T(8,128)(2,1)S(1)}, bf16[4,2,128,256]{3,2,1,0:T(8,128)(2,1)S(1)}, f32[8,128]{1,0:T(8,128)}) custom-call(s32[2]{0:T(128)S(1)} %pad_add_fusion.refs_0_, f32[8,2,2,16,128]{4,3,2,1,0:T(8,128)S(1)} %get-tuple-element.76.refs_0_.refs_1_, ...), custom_call_target="tpu_custom_call" | custom-call | tf_op jit(solution)/shard_map/pallas_call | solution.py:447
  66.7 2.0 %collective-permute-start.20 = (bf16[64,1024]{1,0:T(8,128)(2,1)S(1)}, bf16[64,1024]{1,0:T(8,128)(2,1)S(1)}, u32[]{:S(2)}, u32[]{:S(2)}) collective-permute-start(bf16[64,1024]{1,0:T(8,128)(2,1)S(1)} %get-tuple-element.98.refs_1_), channel_id=1, source_target_pairs={{0,6},{1,7},{2,0},{3,1},{4,2},{5,3},{6,4},{7,5},{8,14},{9,15},{10,... | collective-permute-start | bytes 393224 | tf_op jit(solution)/shard_map/ppermute | solution.py:490
  69.3 3.3 %collective-permute-done.20.refs_7_ = bf16[64,1024]{1,0:T(8,128)(2,1)S(1)} collective-permute-done((bf16[64,1024]{1,0:T(8,128)(2,1)S(1)}, bf16[64,1024]{1,0:T(8,128)(2,1)S(1)}, u32[]{:S(2)}, u32[]{:S(2)}) %collective-permute-start.20) | collective-permute-done | bytes 131104 | tf_op jit(solution)/shard_map/ppermute | solution.py:490
  72.6 2.9 %collective-permute-done.18.refs_5_ = bf16[64,1024]{1,0:T(8,128)(2,1)S(1)} collective-permute-done((bf16[64,1024]{1,0:T(8,128)(2,1)S(1)}, bf16[64,1024]{1,0:T(8,128)(2,1)S(1)}, u32[]{:S(2)}, u32[]{:S(2)}) %collective-permute-start.18) | collective-permute-done | bytes 131104 | tf_op jit(solution)/shard_map/ppermute | solution.py:490
  78.7 2.2 %shard_map.91 = (bf16[128,512]{1,0:T(8,128)(2,1)S(1)}, bf16[128,512]{1,0:T(8,128)(2,1)S(1)}, f32[256,512]{1,0:T(8,128)S(1)}, bf16[256,512]{1,0:T(8,128)(2,1)}, f32[8,128]{1,0:T(8,128)S(1)}) custom-call(s32[3]{0:T(128)S(1)} %pad_add_fusion.1.refs_0_, bf16[64,1024]{1,0:T(8,128)(2,1)S(1)} %get-tuple-element.98.refs_1_, ...), custom_call_target="tpu_custom_call" | custom-call | tf_op jit(solution)/shard_map/pallas_call | solution.py:447
  81.9 3.4 %shard_map.94 = (bf16[1,128,4096]{2,1,0:T(8,128)(2,1)}, bf16[128,1024]{1,0:T(8,128)(2,1)}, f32[8,128]{1,0:T(8,128)}) custom-call(s32[2]{0:T(128)S(1)} %pad_add_fusion.2.refs_0_, bf16[128,512]{1,0:T(8,128)(2,1)S(1)} %get-tuple-element.105.refs_1_, bf16[128,512]{1,0:T(8,128)(2,1)S(1)} %get-tuple-element.106.refs_2_, bf16[2048,512]{1,0:T(8,128)(2,1)S(1)} %copy-done, ...), custom_call_target="tpu_custom_call" | custom-call | tf_op jit(solution)/shard_map/pallas_call | solution.py:447
  85.8 2.4 %collective-permute-start.13 = (bf16[2,2,128,256]{3,2,1,0:T(8,128)(2,1)}, bf16[2,2,128,256]{3,2,1,0:T(8,128)(2,1)S(1)}, u32[]{:S(2)}, u32[]{:S(2)}) collective-permute-start(bf16[2,2,128,256]{3,2,1,0:T(8,128)(2,1)} %get-tuple-element.96), channel_id=1, source_target_pairs={{0,4},{1,5},{2,6},{3,7},{4,0},{5,1},{6,2},{7,3},{8,12},{9,13},{10,... | collective-permute-start | bytes 786440 | tf_op jit(solution)/shard_map/ppermute | solution.py:490
  88.2 1.7 %collective-permute-start.14 = (bf16[2,2,128,256]{3,2,1,0:T(8,128)(2,1)}, bf16[2,2,128,256]{3,2,1,0:T(8,128)(2,1)S(1)}, u32[]{:S(2)}, u32[]{:S(2)}) collective-permute-start(bf16[2,2,128,256]{3,2,1,0:T(8,128)(2,1)} %get-tuple-element.97), channel_id=1, source_target_pairs={{0,6},{1,7},{2,0},{3,1},{4,2},{5,3},{6,4},{7,5},{8,14},{9,15},{10,... | collective-permute-start | bytes 786440 | tf_op jit(solution)/shard_map/ppermute | solution.py:490
  90.1 3.6 %collective-permute-start.25 = (bf16[128,512]{1,0:T(8,128)(2,1)S(1)}, bf16[128,512]{1,0:T(8,128)(2,1)S(1)}, u32[]{:S(2)}, u32[]{:S(2)}) collective-permute-start(bf16[128,512]{1,0:T(8,128)(2,1)S(1)} %get-tuple-element.114), channel_id=1, source_target_pairs={{0,8},{1,9},{2,10},{3,11},{4,12},{5,13},{6,14},{7,15},{8,0},{9,1},... | collective-permute-start | bytes 393224 | tf_op jit(solution)/shard_map/ppermute | solution.py:507
  94.4 4.1 %collective-permute-done.12.refs_2_ = bf16[2,2,128,256]{3,2,1,0:T(8,128)(2,1)S(1)} collective-permute-done((bf16[2,2,128,256]{3,2,1,0:T(8,128)(2,1)}, bf16[2,2,128,256]{3,2,1,0:T(8,128)(2,1)S(1)}, u32[]{:S(2)}, u32[]{:S(2)}) %collective-permute-start.12) | collective-permute-done | bytes 262176 | tf_op jit(solution)/shard_map/ppermute | solution.py:490
  98.4 2.4 %collective-permute-done.14.refs_4_ = bf16[2,2,128,256]{3,2,1,0:T(8,128)(2,1)S(1)} collective-permute-done((bf16[2,2,128,256]{3,2,1,0:T(8,128)(2,1)}, bf16[2,2,128,256]{3,2,1,0:T(8,128)(2,1)S(1)}, u32[]{:S(2)}, u32[]{:S(2)}) %collective-permute-start.14) | collective-permute-done | bytes 262176 | tf_op jit(solution)/shard_map/ppermute | solution.py:490
  (83 shorter events, 33.8 us)
Async XLA Ops:
  2.8 21.9 %collective-permute-start = (bf16[128,2048]{1,0:T(8,128)(2,1)}, bf16[128,2048]{1,0:T(8,128)(2,1)S(1)}, u32[]{:S(2)}, u32[]{:S(2)}) collective-permute-start(bf16[128,2048]{1,0:T(8,128)(2,1)} %get-tuple-element.64), channel_id=1, source_target_pairs={{0,16},{16,0},{1,17},{17,1},{2,18},{18,2},{3,19},{19,3},{4,20},{20... | collective-permute-start | bytes 1572872 | tf_op jit(solution)/shard_map/ppermute | solution.py:486
  10.2 10.4 %collective-permute-start.1 = (bf16[2,2,128,256]{3,2,1,0:T(8,128)(2,1)}, bf16[2,2,128,256]{3,2,1,0:T(8,128)(2,1)S(1)}, u32[]{:S(2)}, u32[]{:S(2)}) collective-permute-start(bf16[2,2,128,256]{3,2,1,0:T(8,128)(2,1)} %get-tuple-element.66), channel_id=1, source_target_pairs={{0,2},{1,3},{2,4},{3,5},{4,6},{5,7},{6,0},{7,1},{8,10},{9,11},{10,... | collective-permute-start | bytes 786440 | tf_op jit(solution)/shard_map/ppermute | solution.py:490
  11.8 10.8 %collective-permute-start.2 = (bf16[2,2,128,256]{3,2,1,0:T(8,128)(2,1)}, bf16[2,2,128,256]{3,2,1,0:T(8,128)(2,1)S(1)}, u32[]{:S(2)}, u32[]{:S(2)}) collective-permute-start(bf16[2,2,128,256]{3,2,1,0:T(8,128)(2,1)} %get-tuple-element.69), channel_id=1, source_target_pairs={{0,4},{1,5},{2,6},{3,7},{4,0},{5,1},{6,2},{7,3},{8,12},{9,13},{10,... | collective-permute-start | bytes 786440 | tf_op jit(solution)/shard_map/ppermute | solution.py:490
  13.3 11.4 %collective-permute-start.3 = (bf16[2,2,128,256]{3,2,1,0:T(8,128)(2,1)}, bf16[2,2,128,256]{3,2,1,0:T(8,128)(2,1)S(1)}, u32[]{:S(2)}, u32[]{:S(2)}) collective-permute-start(bf16[2,2,128,256]{3,2,1,0:T(8,128)(2,1)} %get-tuple-element.70), channel_id=1, source_target_pairs={{0,6},{1,7},{2,0},{3,1},{4,2},{5,3},{6,4},{7,5},{8,14},{9,15},{10,... | collective-permute-start | bytes 786440 | tf_op jit(solution)/shard_map/ppermute | solution.py:490
  26.6 16.6 %all-to-all-start = ((f32[16,2,2,16,128]{4,3,2,1,0:T(8,128)}), f32[16,2,2,16,128]{4,3,2,1,0:T(8,128)}, u32[]{:S(2)}, u32[]{:S(2)}) async-start(f32[16,2,2,16,128]{4,3,2,1,0:T(8,128)} %bitcast.10), calls=%async_computation | async-start | bytes 1048576 | tf_op jit(solution)/shard_map/all_to_all | solution.py:602
  33.4 8.6 %collective-permute-start.4 = (bf16[4,2,128,256]{3,2,1,0:T(8,128)(2,1)S(1)}, bf16[4,2,128,256]{3,2,1,0:T(8,128)(2,1)S(1)}, u32[]{:S(2)}, u32[]{:S(2)}) collective-permute-start(bf16[4,2,128,256]{3,2,1,0:T(8,128)(2,1)S(1)} %get-tuple-element.74), channel_id=1, source_target_pairs={{0,1},{1,0},{2,3},{3,2},{4,5},{5,4},{6,7},{7,6},{8,9},{9,8},{10,11... | collective-permute-start | bytes 1572872 | tf_op jit(solution)/shard_map/ppermute | solution.py:499
  35.8 17.1 %collective-permute-start.7 = (bf16[2,128,512]{2,1,0:T(8,128)(2,1)}, bf16[2,128,512]{2,1,0:T(8,128)(2,1)S(1)}, u32[]{:S(2)}, u32[]{:S(2)}) collective-permute-start(bf16[2,128,512]{2,1,0:T(8,128)(2,1)} %get-tuple-element.81), channel_id=1, source_target_pairs={{0,2},{1,3},{2,4},{3,5},{4,6},{5,7},{6,0},{7,1},{8,10},{9,11},{10,... | collective-permute-start | bytes 786440 | tf_op jit(solution)/shard_map/ppermute | solution.py:490
  37.7 15.3 %collective-permute-start.8 = (bf16[2,128,512]{2,1,0:T(8,128)(2,1)}, bf16[2,128,512]{2,1,0:T(8,128)(2,1)}, u32[]{:S(2)}, u32[]{:S(2)}) collective-permute-start(bf16[2,128,512]{2,1,0:T(8,128)(2,1)} %get-tuple-element.82), channel_id=1, source_target_pairs={{0,4},{1,5},{2,6},{3,7},{4,0},{5,1},{6,2},{7,3},{8,12},{9,13},{10,... | collective-permute-start | bytes 786440 | tf_op jit(solution)/shard_map/ppermute | solution.py:490
  39.1 13.8 %collective-permute-start.9 = (bf16[2,128,512]{2,1,0:T(8,128)(2,1)}, bf16[2,128,512]{2,1,0:T(8,128)(2,1)}, u32[]{:S(2)}, u32[]{:S(2)}) collective-permute-start(bf16[2,128,512]{2,1,0:T(8,128)(2,1)} %get-tuple-element.83), channel_id=1, source_target_pairs={{0,6},{1,7},{2,0},{3,1},{4,2},{5,3},{6,4},{7,5},{8,14},{9,15},{10,... | collective-permute-start | bytes 786440 | tf_op jit(solution)/shard_map/ppermute | solution.py:490
  40.6 41.4 %collective-permute-start.23 = (bf16[1024,512]{1,0:T(8,128)(2,1)}, bf16[1024,512]{1,0:T(8,128)(2,1)}, u32[]{:S(2)}, u32[]{:S(2)}) collective-permute-start(bf16[1024,512]{1,0:T(8,128)(2,1)} %get-tuple-element.107), channel_id=1, source_target_pairs={{0,16},{16,0},{1,17},{17,1},{2,18},{18,2},{3,19},{19,3},{4,20},{20... | collective-permute-start | bytes 3145736 | tf_op jit(solution)/shard_map/ppermute | solution.py:486
  44.8 8.1 %collective-permute-start.5 = (bf16[2,176,128]{2,1,0:T(8,128)(2,1)S(1)}, bf16[2,176,128]{2,1,0:T(8,128)(2,1)S(1)}, u32[]{:S(2)}, u32[]{:S(2)}) collective-permute-start(bf16[2,176,128]{2,1,0:T(8,128)(2,1)S(1)} %get-tuple-element.78), channel_id=1, source_target_pairs={{0,8},{1,9},{2,10},{3,11},{4,12},{5,13},{6,14},{7,15},{16,24},{17,... | collective-permute-start | bytes 270344 | tf_op jit(solution)/shard_map/ppermute | solution.py:507
  55.6 8.8 %collective-permute-start.10 = (bf16[2,176,128]{2,1,0:T(8,128)(2,1)S(1)}, bf16[2,176,128]{2,1,0:T(8,128)(2,1)S(1)}, u32[]{:S(2)}, u32[]{:S(2)}) collective-permute-start(bf16[2,176,128]{2,1,0:T(8,128)(2,1)S(1)} %get-tuple-element.88), channel_id=1, source_target_pairs={{8,0},{9,1},{10,2},{11,3},{12,4},{13,5},{14,6},{15,7},{24,16},{25,... | collective-permute-start | bytes 270344 | tf_op jit(solution)/shard_map/ppermute | solution.py:507
  66.7 9.9 %collective-permute-start.11 = (bf16[4,2,128,256]{3,2,1,0:T(8,128)(2,1)S(1)}, bf16[4,2,128,256]{3,2,1,0:T(8,128)(2,1)S(1)}, u32[]{:S(2)}, u32[]{:S(2)}) collective-permute-start(bf16[4,2,128,256]{3,2,1,0:T(8,128)(2,1)S(1)} %get-tuple-element.93), channel_id=1, source_target_pairs={{0,1},{1,0},{2,3},{3,2},{4,5},{5,4},{6,7},{7,6},{8,9},{9,8},{10,11... | collective-permute-start | bytes 1572872 | tf_op jit(solution)/shard_map/ppermute | solution.py:499
  66.7 5.9 %collective-permute-start.20 = (bf16[64,1024]{1,0:T(8,128)(2,1)S(1)}, bf16[64,1024]{1,0:T(8,128)(2,1)S(1)}, u32[]{:S(2)}, u32[]{:S(2)}) collective-permute-start(bf16[64,1024]{1,0:T(8,128)(2,1)S(1)} %get-tuple-element.98.refs_1_), channel_id=1, source_target_pairs={{0,6},{1,7},{2,0},{3,1},{4,2},{5,3},{6,4},{7,5},{8,14},{9,15},{10,... | collective-permute-start | bytes 393224 | tf_op jit(solution)/shard_map/ppermute | solution.py:490
  68.7 6.8 %collective-permute-start.18 = (bf16[64,1024]{1,0:T(8,128)(2,1)S(1)}, bf16[64,1024]{1,0:T(8,128)(2,1)S(1)}, u32[]{:S(2)}, u32[]{:S(2)}) collective-permute-start(bf16[64,1024]{1,0:T(8,128)(2,1)S(1)} %get-tuple-element.98.refs_1_), channel_id=1, source_target_pairs={{0,4},{1,5},{2,6},{3,7},{4,0},{5,1},{6,2},{7,3},{8,12},{9,13},{10,... | collective-permute-start | bytes 393224 | tf_op jit(solution)/shard_map/ppermute | solution.py:490
  68.8 7.8 %collective-permute-start.16 = (bf16[64,1024]{1,0:T(8,128)(2,1)S(1)}, bf16[64,1024]{1,0:T(8,128)(2,1)S(1)}, u32[]{:S(2)}, u32[]{:S(2)}) collective-permute-start(bf16[64,1024]{1,0:T(8,128)(2,1)S(1)} %get-tuple-element.98.refs_1_), channel_id=1, source_target_pairs={{0,2},{1,3},{2,4},{3,5},{4,6},{5,7},{6,0},{7,1},{8,10},{9,11},{10,... | collective-permute-start | bytes 393224 | tf_op jit(solution)/shard_map/ppermute | solution.py:490
  72.6 6.1 %collective-permute-start.15 = (bf16[64,1024]{1,0:T(8,128)(2,1)S(1)}, bf16[64,1024]{1,0:T(8,128)(2,1)S(1)}, u32[]{:S(2)}, u32[]{:S(2)}) collective-permute-start(bf16[64,1024]{1,0:T(8,128)(2,1)S(1)} %get-tuple-element.98.refs_1_), channel_id=1, source_target_pairs={{0,1},{1,0},{2,3},{3,2},{4,5},{5,4},{6,7},{7,6},{8,9},{9,8},{10,11... | collective-permute-start | bytes 393224 | tf_op jit(solution)/shard_map/ppermute | solution.py:499
  75.5 3.1 %collective-permute-start.21 = (bf16[64,1024]{1,0:T(8,128)(2,1)S(1)}, bf16[64,1024]{1,0:T(8,128)(2,1)S(1)}, u32[]{:S(2)}, u32[]{:S(2)}) collective-permute-start(bf16[64,1024]{1,0:T(8,128)(2,1)S(1)} %collective-permute-done.20.refs_7_), channel_id=1, source_target_pairs={{0,1},{1,0},{2,3},{3,2},{4,5},{5,4},{6,7},{7,6},{8,9},{9,8},{10,11... | collective-permute-start | bytes 393224 | tf_op jit(solution)/shard_map/ppermute | solution.py:499
  80.9 9.0 %collective-permute-start.22 = (bf16[256,512]{1,0:T(8,128)(2,1)}, bf16[256,512]{1,0:T(8,128)(2,1)S(1)}, u32[]{:S(2)}, u32[]{:S(2)}) collective-permute-start(bf16[256,512]{1,0:T(8,128)(2,1)} %get-tuple-element.102), channel_id=1, source_target_pairs={{0,16},{16,0},{1,17},{17,1},{2,18},{18,2},{3,19},{19,3},{4,20},{20... | collective-permute-start | bytes 786440 | tf_op jit(solution)/shard_map/ppermute | solution.py:486
  85.4 8.3 %collective-permute-start.24 = (bf16[128,1024]{1,0:T(8,128)(2,1)}, bf16[128,1024]{1,0:T(8,128)(2,1)S(1)}, u32[]{:S(2)}, u32[]{:S(2)}) collective-permute-start(bf16[128,1024]{1,0:T(8,128)(2,1)} %get-tuple-element.110), channel_id=1, source_target_pairs={{0,1},{1,0},{2,3},{3,2},{4,5},{5,4},{6,7},{7,6},{8,9},{9,8},{10,11... | collective-permute-start | bytes 786440 | tf_op jit(solution)/shard_map/ppermute | solution.py:499
  85.4 13.1 %collective-permute-start.12 = (bf16[2,2,128,256]{3,2,1,0:T(8,128)(2,1)}, bf16[2,2,128,256]{3,2,1,0:T(8,128)(2,1)S(1)}, u32[]{:S(2)}, u32[]{:S(2)}) collective-permute-start(bf16[2,2,128,256]{3,2,1,0:T(8,128)(2,1)} %get-tuple-element.95), channel_id=1, source_target_pairs={{0,2},{1,3},{2,4},{3,5},{4,6},{5,7},{6,0},{7,1},{8,10},{9,11},{10,... | collective-permute-start | bytes 786440 | tf_op jit(solution)/shard_map/ppermute | solution.py:490
  85.8 12.7 %collective-permute-start.13 = (bf16[2,2,128,256]{3,2,1,0:T(8,128)(2,1)}, bf16[2,2,128,256]{3,2,1,0:T(8,128)(2,1)S(1)}, u32[]{:S(2)}, u32[]{:S(2)}) collective-permute-start(bf16[2,2,128,256]{3,2,1,0:T(8,128)(2,1)} %get-tuple-element.96), channel_id=1, source_target_pairs={{0,4},{1,5},{2,6},{3,7},{4,0},{5,1},{6,2},{7,3},{8,12},{9,13},{10,... | collective-permute-start | bytes 786440 | tf_op jit(solution)/shard_map/ppermute | solution.py:490
  88.2 12.6 %collective-permute-start.14 = (bf16[2,2,128,256]{3,2,1,0:T(8,128)(2,1)}, bf16[2,2,128,256]{3,2,1,0:T(8,128)(2,1)S(1)}, u32[]{:S(2)}, u32[]{:S(2)}) collective-permute-start(bf16[2,2,128,256]{3,2,1,0:T(8,128)(2,1)} %get-tuple-element.97), channel_id=1, source_target_pairs={{0,6},{1,7},{2,0},{3,1},{4,2},{5,3},{6,4},{7,5},{8,14},{9,15},{10,... | collective-permute-start | bytes 786440 | tf_op jit(solution)/shard_map/ppermute | solution.py:490
  90.1 12.7 %collective-permute-start.25 = (bf16[128,512]{1,0:T(8,128)(2,1)S(1)}, bf16[128,512]{1,0:T(8,128)(2,1)S(1)}, u32[]{:S(2)}, u32[]{:S(2)}) collective-permute-start(bf16[128,512]{1,0:T(8,128)(2,1)S(1)} %get-tuple-element.114), channel_id=1, source_target_pairs={{0,8},{1,9},{2,10},{3,11},{4,12},{5,13},{6,14},{7,15},{8,0},{9,1},... | collective-permute-start | bytes 393224 | tf_op jit(solution)/shard_map/ppermute | solution.py:507
  (17 other events, 59.2 us)

commit v17 on v14

--- a/solution.py
+++ b/solution.py
@@ -13,7 +13,7 @@
 EPSILON = 1e-05
 GROUP = 8
 TILE = 256
-VMEM_LIMIT = 16 * 1024 * 1024
+VMEM_LIMIT = 12 * 1024 * 1024
 PSI = 9 * F + 2 * F
 PSI_SCALE = (0.5,) + (1.0,) * 7 + (0.5,)
 

time: 105 us -> 105 us (level)
  no operation moved by 1% of the time
where the time goes in v17:
time: 105 us; the launch traced here: 104 us
  Pallas kernels  36.8 us (35%)
  starting transfers between devices  36.8 us (35%)
  waiting for transfers between devices  21 us (20%)
  local copies, waits for them, and re-layouts  7.85 us (7%)
    pallas_call x22, Pallas kernels, call(): pl.pallas_call(kernel, out_shape=[jax.ShapeDtypeStruct(shape, kind) for s...  36.8 us
    ppermute x12, waiting for transfers between devices, to_member(): return lax.ppermute(x, 'ctx', pairs)  20 us
    ppermute x12, starting transfers between devices, to_member(): return lax.ppermute(x, 'ctx', pairs)  16.4 us
    ppermute x3, starting transfers between devices, to_run(): return lax.ppermute(x, 'ctx', pairs)  9.55 us
    unnamed x28, local copies, waits for them, and re-layouts  7.85 us
    ppermute x3, starting transfers between devices, to_dp(): lax.ppermute(x, 'dp', [(i, (i + shift) % dp_size) for i in range(dp_size)])  5.42 us
    all_to_all x1, starting transfers between devices, local(): lax.all_to_all(projected.reshape((dp_size * group,) + qk_shape[0][1:]), (...  4.39 us
  transfers between devices with their start and end apart: 27, of which 8 were waited for; matrix products, arithmetic and copies ran while one was open for 0% of the time, Pallas kernels for 33%

profile of v17, /device:TPU:0, one launch (start us, length us, event | category | flops | bytes accessed | tf_op | source)
XLA Modules:
  0.0 103.5 jit_solution(17467185822584113732)
XLA Ops:
  2.8 3.0 %collective-permute-start = (bf16[128,2048]{1,0:T(8,128)(2,1)}, bf16[128,2048]{1,0:T(8,128)(2,1)S(1)}, u32[]{:S(2)}, u32[]{:S(2)}) collective-permute-start(bf16[128,2048]{1,0:T(8,128)(2,1)} %get-tuple-element.65), channel_id=1, source_target_pairs={{0,16},{16,0},{1,17},{17,1},{2,18},{18,2},{3,19},{19,3},{4,20},{20... | collective-permute-start | bytes 1572872 | tf_op jit(solution)/shard_map/ppermute | solution.py:486
  8.0 1.5 %shard_map.76 = (bf16[2,2,128,256]{3,2,1,0:T(8,128)(2,1)S(1)}, bf16[2,2,128,256]{3,2,1,0:T(8,128)(2,1)}, bf16[2,2,128,256]{3,2,1,0:T(8,128)(2,1)}, bf16[2,2,128,256]{3,2,1,0:T(8,128)(2,1)}, f32[8,128]{1,0:T(8,128)S(1)}) custom-call(s32[2]{0:T(128)S(1)} %pad_add_fusion.refs_0_, bf16[1,128,2048]{2,1,0:T(8,128)(2,1)S(1)} %copy-done.5, ...), custom_call_target="tpu_custom_call" | custom-call | tf_op jit(solution)/shard_map/pallas_call | solution.py:447
  10.2 1.5 %collective-permute-start.1 = (bf16[2,2,128,256]{3,2,1,0:T(8,128)(2,1)}, bf16[2,2,128,256]{3,2,1,0:T(8,128)(2,1)S(1)}, u32[]{:S(2)}, u32[]{:S(2)}) collective-permute-start(bf16[2,2,128,256]{3,2,1,0:T(8,128)(2,1)} %get-tuple-element.67), channel_id=1, source_target_pairs={{0,2},{1,3},{2,4},{3,5},{4,6},{5,7},{6,0},{7,1},{8,10},{9,11},{10,... | collective-permute-start | bytes 786440 | tf_op jit(solution)/shard_map/ppermute | solution.py:490
  11.8 1.6 %collective-permute-start.2 = (bf16[2,2,128,256]{3,2,1,0:T(8,128)(2,1)}, bf16[2,2,128,256]{3,2,1,0:T(8,128)(2,1)S(1)}, u32[]{:S(2)}, u32[]{:S(2)}) collective-permute-start(bf16[2,2,128,256]{3,2,1,0:T(8,128)(2,1)} %get-tuple-element.70), channel_id=1, source_target_pairs={{0,4},{1,5},{2,6},{3,7},{4,0},{5,1},{6,2},{7,3},{8,12},{9,13},{10,... | collective-permute-start | bytes 786440 | tf_op jit(solution)/shard_map/ppermute | solution.py:490
  16.6 4.1 %collective-permute-done.1.refs_2_.refs_7_ = bf16[2,2,128,256]{3,2,1,0:T(8,128)(2,1)S(1)} collective-permute-done((bf16[2,2,128,256]{3,2,1,0:T(8,128)(2,1)}, bf16[2,2,128,256]{3,2,1,0:T(8,128)(2,1)S(1)}, u32[]{:S(2)}, u32[]{:S(2)}) %collective-permute-start.1) | collective-permute-done | bytes 262176 | tf_op jit(solution)/shard_map/ppermute | solution.py:490
  22.6 2.2 %collective-permute-done.3.refs_9_.refs_4_ = bf16[2,2,128,256]{3,2,1,0:T(8,128)(2,1)S(1)} collective-permute-done((bf16[2,2,128,256]{3,2,1,0:T(8,128)(2,1)}, bf16[2,2,128,256]{3,2,1,0:T(8,128)(2,1)S(1)}, u32[]{:S(2)}, u32[]{:S(2)}) %collective-permute-start.3) | collective-permute-done | bytes 262176 | tf_op jit(solution)/shard_map/ppermute | solution.py:490
  26.6 4.4 %all-to-all-start = ((f32[16,2,2,16,128]{4,3,2,1,0:T(8,128)}), f32[16,2,2,16,128]{4,3,2,1,0:T(8,128)}, u32[]{:S(2)}, u32[]{:S(2)}) async-start(f32[16,2,2,16,128]{4,3,2,1,0:T(8,128)} %bitcast.10), calls=%async_computation | async-start | bytes 1048576 | tf_op jit(solution)/shard_map/all_to_all | solution.py:602
  35.8 1.8 %collective-permute-start.7 = (bf16[2,128,512]{2,1,0:T(8,128)(2,1)}, bf16[2,128,512]{2,1,0:T(8,128)(2,1)S(1)}, u32[]{:S(2)}, u32[]{:S(2)}) collective-permute-start(bf16[2,128,512]{2,1,0:T(8,128)(2,1)} %get-tuple-element.82), channel_id=1, source_target_pairs={{0,2},{1,3},{2,4},{3,5},{4,6},{5,7},{6,0},{7,1},{8,10},{9,11},{10,... | collective-permute-start | bytes 786440 | tf_op jit(solution)/shard_map/ppermute | solution.py:490
  43.2 1.6 %shard_map.83 = (f32[8,2,2,16,128]{4,3,2,1,0:T(8,128)S(1)}, bf16[2,176,128]{2,1,0:T(8,128)(2,1)S(1)}, f32[8,128]{1,0:T(8,128)}) custom-call(f32[2,8,2,2,16,128]{5,4,3,2,1,0:T(8,128)} %bitcast.5.refs_0_, bf16[8,2,128,256]{3,2,1,0:T(8,128)(2,1)S(1)} %get-tuple-element.76.refs_1_.refs_2_), custom_call_target="tpu_custom_call" | custom-call | tf_op jit(solution)/shard_map/pallas_call | solution.py:447
  44.8 4.5 %collective-permute-start.5 = (bf16[2,176,128]{2,1,0:T(8,128)(2,1)S(1)}, bf16[2,176,128]{2,1,0:T(8,128)(2,1)S(1)}, u32[]{:S(2)}, u32[]{:S(2)}) collective-permute-start(bf16[2,176,128]{2,1,0:T(8,128)(2,1)S(1)} %get-tuple-element.79), channel_id=1, source_target_pairs={{0,8},{1,9},{2,10},{3,11},{4,12},{5,13},{6,14},{7,15},{16,24},{17,... | collective-permute-start | bytes 270344 | tf_op jit(solution)/shard_map/ppermute | solution.py:507
  49.3 3.6 %shard_map.84 = (f32[1024,256]{1,0:T(8,128)S(1)}, f32[8,128]{1,0:T(8,128)}) custom-call(f32[8,2,2,16,128]{4,3,2,1,0:T(8,128)S(1)} %get-tuple-element.77.refs_0_.refs_1_, bf16[8,2,128,256]{3,2,1,0:T(8,128)(2,1)S(1)} %get-tuple-element.76.refs_1_.refs_2_), custom_call_target="tpu_custom_call" | custom-call | tf_op jit(solution)/shard_map/pallas_call | solution.py:447
  53.0 2.6 %shard_map.86 = (bf16[1024,256]{1,0:T(8,128)(2,1)S(1)}, f32[1024,256]{1,0:T(8,128)S(1)}, bf16[2,176,128]{2,1,0:T(8,128)(2,1)S(1)}, f32[8,128]{1,0:T(8,128)}) custom-call(f32[8,2,2,16,128]{4,3,2,1,0:T(8,128)S(1)} %get-tuple-element.77.refs_0_.refs_1_, bf16[8,2,128,256]{3,2,1,0:T(8,128)(2,1)S(1)} %get-tuple-element.76.refs_1_.refs_2_, ...), custom_call_target="tpu_custom_call" | custom-call | tf_op jit(solution)/shard_map/pallas_call | solution.py:447
  57.0 5.9 %shard_map.87 = (f32[2,2,16,1024]{3,2,1,0:T(8,128)S(1)}, f32[2,128,1024]{2,1,0:T(8,128)S(1)}, f32[8,128]{1,0:T(8,128)S(1)}) custom-call(f32[8,2,2,16,128]{4,3,2,1,0:T(8,128)S(1)} %get-tuple-element.77.refs_0_.refs_1_, bf16[8,2,128,256]{3,2,1,0:T(8,128)(2,1)S(1)} %get-tuple-element.76.refs_1_.refs_2_, f32[1024,256]{1,0:T(8,128)S(1)} %get-tuple-element.86.refs_2_, ...), custom_call_target="tpu_custom_call" | custom-call | tf_op jit(solution)/shard_map/pallas_call | solution.py:447
  64.4 2.3 %shard_map.89 = (bf16[64,1024]{1,0:T(8,128)(2,1)S(1)}, bf16[4,2,128,256]{3,2,1,0:T(8,128)(2,1)S(1)}, bf16[4,2,128,256]{3,2,1,0:T(8,128)(2,1)S(1)}, f32[8,128]{1,0:T(8,128)}) custom-call(s32[2]{0:T(128)S(1)} %pad_add_fusion.refs_0_, f32[8,2,2,16,128]{4,3,2,1,0:T(8,128)S(1)} %get-tuple-element.77.refs_0_.refs_1_, ...), custom_call_target="tpu_custom_call" | custom-call | tf_op jit(solution)/shard_map/pallas_call | solution.py:447
  66.7 2.0 %collective-permute-start.20 = (bf16[64,1024]{1,0:T(8,128)(2,1)S(1)}, bf16[64,1024]{1,0:T(8,128)(2,1)S(1)}, u32[]{:S(2)}, u32[]{:S(2)}) collective-permute-start(bf16[64,1024]{1,0:T(8,128)(2,1)S(1)} %get-tuple-element.99.refs_1_), channel_id=1, source_target_pairs={{0,6},{1,7},{2,0},{3,1},{4,2},{5,3},{6,4},{7,5},{8,14},{9,15},{10,... | collective-permute-start | bytes 393224 | tf_op jit(solution)/shard_map/ppermute | solution.py:490
  69.3 3.3 %collective-permute-done.20.refs_7_ = bf16[64,1024]{1,0:T(8,128)(2,1)S(1)} collective-permute-done((bf16[64,1024]{1,0:T(8,128)(2,1)S(1)}, bf16[64,1024]{1,0:T(8,128)(2,1)S(1)}, u32[]{:S(2)}, u32[]{:S(2)}) %collective-permute-start.20) | collective-permute-done | bytes 131104 | tf_op jit(solution)/shard_map/ppermute | solution.py:490
  72.6 2.9 %collective-permute-done.18.refs_5_ = bf16[64,1024]{1,0:T(8,128)(2,1)S(1)} collective-permute-done((bf16[64,1024]{1,0:T(8,128)(2,1)S(1)}, bf16[64,1024]{1,0:T(8,128)(2,1)S(1)}, u32[]{:S(2)}, u32[]{:S(2)}) %collective-permute-start.18) | collective-permute-done | bytes 131104 | tf_op jit(solution)/shard_map/ppermute | solution.py:490
  78.7 2.2 %shard_map.91 = (bf16[128,512]{1,0:T(8,128)(2,1)S(1)}, bf16[128,512]{1,0:T(8,128)(2,1)S(1)}, f32[256,512]{1,0:T(8,128)S(1)}, bf16[256,512]{1,0:T(8,128)(2,1)}, f32[8,128]{1,0:T(8,128)S(1)}) custom-call(s32[3]{0:T(128)S(1)} %pad_add_fusion.1.refs_0_, bf16[64,1024]{1,0:T(8,128)(2,1)S(1)} %get-tuple-element.99.refs_1_, ...), custom_call_target="tpu_custom_call" | custom-call | tf_op jit(solution)/shard_map/pallas_call | solution.py:447
  81.9 3.4 %shard_map.92 = (bf16[1,128,4096]{2,1,0:T(8,128)(2,1)}, bf16[128,1024]{1,0:T(8,128)(2,1)}, f32[8,128]{1,0:T(8,128)S(1)}) custom-call(s32[2]{0:T(128)S(1)} %pad_add_fusion.2.refs_0_, bf16[128,512]{1,0:T(8,128)(2,1)S(1)} %get-tuple-element.104.refs_1_, bf16[128,512]{1,0:T(8,128)(2,1)S(1)} %get-tuple-element.105.refs_2_, bf16[2048,512]{1,0:T(8,128)(2,1)S(1)} %copy-done, ...), custom_call_target="tpu_custom_call" | custom-call | tf_op jit(solution)/shard_map/pallas_call | solution.py:447
  85.8 2.4 %collective-permute-start.13 = (bf16[2,2,128,256]{3,2,1,0:T(8,128)(2,1)}, bf16[2,2,128,256]{3,2,1,0:T(8,128)(2,1)S(1)}, u32[]{:S(2)}, u32[]{:S(2)}) collective-permute-start(bf16[2,2,128,256]{3,2,1,0:T(8,128)(2,1)} %get-tuple-element.97), channel_id=1, source_target_pairs={{0,4},{1,5},{2,6},{3,7},{4,0},{5,1},{6,2},{7,3},{8,12},{9,13},{10,... | collective-permute-start | bytes 786440 | tf_op jit(solution)/shard_map/ppermute | solution.py:490
  88.2 1.7 %collective-permute-start.14 = (bf16[2,2,128,256]{3,2,1,0:T(8,128)(2,1)}, bf16[2,2,128,256]{3,2,1,0:T(8,128)(2,1)S(1)}, u32[]{:S(2)}, u32[]{:S(2)}) collective-permute-start(bf16[2,2,128,256]{3,2,1,0:T(8,128)(2,1)} %get-tuple-element.98), channel_id=1, source_target_pairs={{0,6},{1,7},{2,0},{3,1},{4,2},{5,3},{6,4},{7,5},{8,14},{9,15},{10,... | collective-permute-start | bytes 786440 | tf_op jit(solution)/shard_map/ppermute | solution.py:490
  90.1 3.6 %collective-permute-start.25 = (bf16[128,512]{1,0:T(8,128)(2,1)S(1)}, bf16[128,512]{1,0:T(8,128)(2,1)S(1)}, u32[]{:S(2)}, u32[]{:S(2)}) collective-permute-start(bf16[128,512]{1,0:T(8,128)(2,1)S(1)} %get-tuple-element.116), channel_id=1, source_target_pairs={{0,8},{1,9},{2,10},{3,11},{4,12},{5,13},{6,14},{7,15},{8,0},{9,1},... | collective-permute-start | bytes 393224 | tf_op jit(solution)/shard_map/ppermute | solution.py:507
  94.4 4.1 %collective-permute-done.12.refs_2_ = bf16[2,2,128,256]{3,2,1,0:T(8,128)(2,1)S(1)} collective-permute-done((bf16[2,2,128,256]{3,2,1,0:T(8,128)(2,1)}, bf16[2,2,128,256]{3,2,1,0:T(8,128)(2,1)S(1)}, u32[]{:S(2)}, u32[]{:S(2)}) %collective-permute-start.12) | collective-permute-done | bytes 262176 | tf_op jit(solution)/shard_map/ppermute | solution.py:490
  98.4 2.4 %collective-permute-done.14.refs_4_ = bf16[2,2,128,256]{3,2,1,0:T(8,128)(2,1)S(1)} collective-permute-done((bf16[2,2,128,256]{3,2,1,0:T(8,128)(2,1)}, bf16[2,2,128,256]{3,2,1,0:T(8,128)(2,1)S(1)}, u32[]{:S(2)}, u32[]{:S(2)}) %collective-permute-start.14) | collective-permute-done | bytes 262176 | tf_op jit(solution)/shard_map/ppermute | solution.py:490
  (83 shorter events, 33.8 us)
Async XLA Ops:
  2.8 21.9 %collective-permute-start = (bf16[128,2048]{1,0:T(8,128)(2,1)}, bf16[128,2048]{1,0:T(8,128)(2,1)S(1)}, u32[]{:S(2)}, u32[]{:S(2)}) collective-permute-start(bf16[128,2048]{1,0:T(8,128)(2,1)} %get-tuple-element.65), channel_id=1, source_target_pairs={{0,16},{16,0},{1,17},{17,1},{2,18},{18,2},{3,19},{19,3},{4,20},{20... | collective-permute-start | bytes 1572872 | tf_op jit(solution)/shard_map/ppermute | solution.py:486
  10.2 10.4 %collective-permute-start.1 = (bf16[2,2,128,256]{3,2,1,0:T(8,128)(2,1)}, bf16[2,2,128,256]{3,2,1,0:T(8,128)(2,1)S(1)}, u32[]{:S(2)}, u32[]{:S(2)}) collective-permute-start(bf16[2,2,128,256]{3,2,1,0:T(8,128)(2,1)} %get-tuple-element.67), channel_id=1, source_target_pairs={{0,2},{1,3},{2,4},{3,5},{4,6},{5,7},{6,0},{7,1},{8,10},{9,11},{10,... | collective-permute-start | bytes 786440 | tf_op jit(solution)/shard_map/ppermute | solution.py:490
  11.8 10.8 %collective-permute-start.2 = (bf16[2,2,128,256]{3,2,1,0:T(8,128)(2,1)}, bf16[2,2,128,256]{3,2,1,0:T(8,128)(2,1)S(1)}, u32[]{:S(2)}, u32[]{:S(2)}) collective-permute-start(bf16[2,2,128,256]{3,2,1,0:T(8,128)(2,1)} %get-tuple-element.70), channel_id=1, source_target_pairs={{0,4},{1,5},{2,6},{3,7},{4,0},{5,1},{6,2},{7,3},{8,12},{9,13},{10,... | collective-permute-start | bytes 786440 | tf_op jit(solution)/shard_map/ppermute | solution.py:490
  13.3 11.4 %collective-permute-start.3 = (bf16[2,2,128,256]{3,2,1,0:T(8,128)(2,1)}, bf16[2,2,128,256]{3,2,1,0:T(8,128)(2,1)S(1)}, u32[]{:S(2)}, u32[]{:S(2)}) collective-permute-start(bf16[2,2,128,256]{3,2,1,0:T(8,128)(2,1)} %get-tuple-element.71), channel_id=1, source_target_pairs={{0,6},{1,7},{2,0},{3,1},{4,2},{5,3},{6,4},{7,5},{8,14},{9,15},{10,... | collective-permute-start | bytes 786440 | tf_op jit(solution)/shard_map/ppermute | solution.py:490
  26.6 16.6 %all-to-all-start = ((f32[16,2,2,16,128]{4,3,2,1,0:T(8,128)}), f32[16,2,2,16,128]{4,3,2,1,0:T(8,128)}, u32[]{:S(2)}, u32[]{:S(2)}) async-start(f32[16,2,2,16,128]{4,3,2,1,0:T(8,128)} %bitcast.10), calls=%async_computation | async-start | bytes 1048576 | tf_op jit(solution)/shard_map/all_to_all | solution.py:602
  33.4 8.6 %collective-permute-start.4 = (bf16[4,2,128,256]{3,2,1,0:T(8,128)(2,1)S(1)}, bf16[4,2,128,256]{3,2,1,0:T(8,128)(2,1)S(1)}, u32[]{:S(2)}, u32[]{:S(2)}) collective-permute-start(bf16[4,2,128,256]{3,2,1,0:T(8,128)(2,1)S(1)} %get-tuple-element.75), channel_id=1, source_target_pairs={{0,1},{1,0},{2,3},{3,2},{4,5},{5,4},{6,7},{7,6},{8,9},{9,8},{10,11... | collective-permute-start | bytes 1572872 | tf_op jit(solution)/shard_map/ppermute | solution.py:499
  35.8 17.1 %collective-permute-start.7 = (bf16[2,128,512]{2,1,0:T(8,128)(2,1)}, bf16[2,128,512]{2,1,0:T(8,128)(2,1)S(1)}, u32[]{:S(2)}, u32[]{:S(2)}) collective-permute-start(bf16[2,128,512]{2,1,0:T(8,128)(2,1)} %get-tuple-element.82), channel_id=1, source_target_pairs={{0,2},{1,3},{2,4},{3,5},{4,6},{5,7},{6,0},{7,1},{8,10},{9,11},{10,... | collective-permute-start | bytes 786440 | tf_op jit(solution)/shard_map/ppermute | solution.py:490
  37.7 15.3 %collective-permute-start.8 = (bf16[2,128,512]{2,1,0:T(8,128)(2,1)}, bf16[2,128,512]{2,1,0:T(8,128)(2,1)}, u32[]{:S(2)}, u32[]{:S(2)}) collective-permute-start(bf16[2,128,512]{2,1,0:T(8,128)(2,1)} %get-tuple-element.83), channel_id=1, source_target_pairs={{0,4},{1,5},{2,6},{3,7},{4,0},{5,1},{6,2},{7,3},{8,12},{9,13},{10,... | collective-permute-start | bytes 786440 | tf_op jit(solution)/shard_map/ppermute | solution.py:490
  39.1 13.8 %collective-permute-start.9 = (bf16[2,128,512]{2,1,0:T(8,128)(2,1)}, bf16[2,128,512]{2,1,0:T(8,128)(2,1)}, u32[]{:S(2)}, u32[]{:S(2)}) collective-permute-start(bf16[2,128,512]{2,1,0:T(8,128)(2,1)} %get-tuple-element.84), channel_id=1, source_target_pairs={{0,6},{1,7},{2,0},{3,1},{4,2},{5,3},{6,4},{7,5},{8,14},{9,15},{10,... | collective-permute-start | bytes 786440 | tf_op jit(solution)/shard_map/ppermute | solution.py:490
  40.6 41.4 %collective-permute-start.23 = (bf16[1024,512]{1,0:T(8,128)(2,1)}, bf16[1024,512]{1,0:T(8,128)(2,1)}, u32[]{:S(2)}, u32[]{:S(2)}) collective-permute-start(bf16[1024,512]{1,0:T(8,128)(2,1)} %get-tuple-element.106), channel_id=1, source_target_pairs={{0,16},{16,0},{1,17},{17,1},{2,18},{18,2},{3,19},{19,3},{4,20},{20... | collective-permute-start | bytes 3145736 | tf_op jit(solution)/shard_map/ppermute | solution.py:486
  44.8 8.1 %collective-permute-start.5 = (bf16[2,176,128]{2,1,0:T(8,128)(2,1)S(1)}, bf16[2,176,128]{2,1,0:T(8,128)(2,1)S(1)}, u32[]{:S(2)}, u32[]{:S(2)}) collective-permute-start(bf16[2,176,128]{2,1,0:T(8,128)(2,1)S(1)} %get-tuple-element.79), channel_id=1, source_target_pairs={{0,8},{1,9},{2,10},{3,11},{4,12},{5,13},{6,14},{7,15},{16,24},{17,... | collective-permute-start | bytes 270344 | tf_op jit(solution)/shard_map/ppermute | solution.py:507
  55.6 8.8 %collective-permute-start.10 = (bf16[2,176,128]{2,1,0:T(8,128)(2,1)S(1)}, bf16[2,176,128]{2,1,0:T(8,128)(2,1)S(1)}, u32[]{:S(2)}, u32[]{:S(2)}) collective-permute-start(bf16[2,176,128]{2,1,0:T(8,128)(2,1)S(1)} %get-tuple-element.89), channel_id=1, source_target_pairs={{8,0},{9,1},{10,2},{11,3},{12,4},{13,5},{14,6},{15,7},{24,16},{25,... | collective-permute-start | bytes 270344 | tf_op jit(solution)/shard_map/ppermute | solution.py:507
  66.7 9.9 %collective-permute-start.11 = (bf16[4,2,128,256]{3,2,1,0:T(8,128)(2,1)S(1)}, bf16[4,2,128,256]{3,2,1,0:T(8,128)(2,1)S(1)}, u32[]{:S(2)}, u32[]{:S(2)}) collective-permute-start(bf16[4,2,128,256]{3,2,1,0:T(8,128)(2,1)S(1)} %get-tuple-element.94), channel_id=1, source_target_pairs={{0,1},{1,0},{2,3},{3,2},{4,5},{5,4},{6,7},{7,6},{8,9},{9,8},{10,11... | collective-permute-start | bytes 1572872 | tf_op jit(solution)/shard_map/ppermute | solution.py:499
  66.7 5.9 %collective-permute-start.20 = (bf16[64,1024]{1,0:T(8,128)(2,1)S(1)}, bf16[64,1024]{1,0:T(8,128)(2,1)S(1)}, u32[]{:S(2)}, u32[]{:S(2)}) collective-permute-start(bf16[64,1024]{1,0:T(8,128)(2,1)S(1)} %get-tuple-element.99.refs_1_), channel_id=1, source_target_pairs={{0,6},{1,7},{2,0},{3,1},{4,2},{5,3},{6,4},{7,5},{8,14},{9,15},{10,... | collective-permute-start | bytes 393224 | tf_op jit(solution)/shard_map/ppermute | solution.py:490
  68.7 6.8 %collective-permute-start.18 = (bf16[64,1024]{1,0:T(8,128)(2,1)S(1)}, bf16[64,1024]{1,0:T(8,128)(2,1)S(1)}, u32[]{:S(2)}, u32[]{:S(2)}) collective-permute-start(bf16[64,1024]{1,0:T(8,128)(2,1)S(1)} %get-tuple-element.99.refs_1_), channel_id=1, source_target_pairs={{0,4},{1,5},{2,6},{3,7},{4,0},{5,1},{6,2},{7,3},{8,12},{9,13},{10,... | collective-permute-start | bytes 393224 | tf_op jit(solution)/shard_map/ppermute | solution.py:490
  68.8 7.8 %collective-permute-start.16 = (bf16[64,1024]{1,0:T(8,128)(2,1)S(1)}, bf16[64,1024]{1,0:T(8,128)(2,1)S(1)}, u32[]{:S(2)}, u32[]{:S(2)}) collective-permute-start(bf16[64,1024]{1,0:T(8,128)(2,1)S(1)} %get-tuple-element.99.refs_1_), channel_id=1, source_target_pairs={{0,2},{1,3},{2,4},{3,5},{4,6},{5,7},{6,0},{7,1},{8,10},{9,11},{10,... | collective-permute-start | bytes 393224 | tf_op jit(solution)/shard_map/ppermute | solution.py:490
  72.6 6.1 %collective-permute-start.15 = (bf16[64,1024]{1,0:T(8,128)(2,1)S(1)}, bf16[64,1024]{1,0:T(8,128)(2,1)S(1)}, u32[]{:S(2)}, u32[]{:S(2)}) collective-permute-start(bf16[64,1024]{1,0:T(8,128)(2,1)S(1)} %get-tuple-element.99.refs_1_), channel_id=1, source_target_pairs={{0,1},{1,0},{2,3},{3,2},{4,5},{5,4},{6,7},{7,6},{8,9},{9,8},{10,11... | collective-permute-start | bytes 393224 | tf_op jit(solution)/shard_map/ppermute | solution.py:499
  75.5 3.1 %collective-permute-start.21 = (bf16[64,1024]{1,0:T(8,128)(2,1)S(1)}, bf16[64,1024]{1,0:T(8,128)(2,1)S(1)}, u32[]{:S(2)}, u32[]{:S(2)}) collective-permute-start(bf16[64,1024]{1,0:T(8,128)(2,1)S(1)} %collective-permute-done.20.refs_7_), channel_id=1, source_target_pairs={{0,1},{1,0},{2,3},{3,2},{4,5},{5,4},{6,7},{7,6},{8,9},{9,8},{10,11... | collective-permute-start | bytes 393224 | tf_op jit(solution)/shard_map/ppermute | solution.py:499
  80.9 9.0 %collective-permute-start.22 = (bf16[256,512]{1,0:T(8,128)(2,1)}, bf16[256,512]{1,0:T(8,128)(2,1)S(1)}, u32[]{:S(2)}, u32[]{:S(2)}) collective-permute-start(bf16[256,512]{1,0:T(8,128)(2,1)} %get-tuple-element.103), channel_id=1, source_target_pairs={{0,16},{16,0},{1,17},{17,1},{2,18},{18,2},{3,19},{19,3},{4,20},{20... | collective-permute-start | bytes 786440 | tf_op jit(solution)/shard_map/ppermute | solution.py:486
  85.4 8.3 %collective-permute-start.24 = (bf16[128,1024]{1,0:T(8,128)(2,1)}, bf16[128,1024]{1,0:T(8,128)(2,1)S(1)}, u32[]{:S(2)}, u32[]{:S(2)}) collective-permute-start(bf16[128,1024]{1,0:T(8,128)(2,1)} %get-tuple-element.112), channel_id=1, source_target_pairs={{0,1},{1,0},{2,3},{3,2},{4,5},{5,4},{6,7},{7,6},{8,9},{9,8},{10,11... | collective-permute-start | bytes 786440 | tf_op jit(solution)/shard_map/ppermute | solution.py:499
  85.4 13.1 %collective-permute-start.12 = (bf16[2,2,128,256]{3,2,1,0:T(8,128)(2,1)}, bf16[2,2,128,256]{3,2,1,0:T(8,128)(2,1)S(1)}, u32[]{:S(2)}, u32[]{:S(2)}) collective-permute-start(bf16[2,2,128,256]{3,2,1,0:T(8,128)(2,1)} %get-tuple-element.96), channel_id=1, source_target_pairs={{0,2},{1,3},{2,4},{3,5},{4,6},{5,7},{6,0},{7,1},{8,10},{9,11},{10,... | collective-permute-start | bytes 786440 | tf_op jit(solution)/shard_map/ppermute | solution.py:490
  85.8 12.7 %collective-permute-start.13 = (bf16[2,2,128,256]{3,2,1,0:T(8,128)(2,1)}, bf16[2,2,128,256]{3,2,1,0:T(8,128)(2,1)S(1)}, u32[]{:S(2)}, u32[]{:S(2)}) collective-permute-start(bf16[2,2,128,256]{3,2,1,0:T(8,128)(2,1)} %get-tuple-element.97), channel_id=1, source_target_pairs={{0,4},{1,5},{2,6},{3,7},{4,0},{5,1},{6,2},{7,3},{8,12},{9,13},{10,... | collective-permute-start | bytes 786440 | tf_op jit(solution)/shard_map/ppermute | solution.py:490
  88.2 12.6 %collective-permute-start.14 = (bf16[2,2,128,256]{3,2,1,0:T(8,128)(2,1)}, bf16[2,2,128,256]{3,2,1,0:T(8,128)(2,1)S(1)}, u32[]{:S(2)}, u32[]{:S(2)}) collective-permute-start(bf16[2,2,128,256]{3,2,1,0:T(8,128)(2,1)} %get-tuple-element.98), channel_id=1, source_target_pairs={{0,6},{1,7},{2,0},{3,1},{4,2},{5,3},{6,4},{7,5},{8,14},{9,15},{10,... | collective-permute-start | bytes 786440 | tf_op jit(solution)/shard_map/ppermute | solution.py:490
  90.1 12.7 %collective-permute-start.25 = (bf16[128,512]{1,0:T(8,128)(2,1)S(1)}, bf16[128,512]{1,0:T(8,128)(2,1)S(1)}, u32[]{:S(2)}, u32[]{:S(2)}) collective-permute-start(bf16[128,512]{1,0:T(8,128)(2,1)S(1)} %get-tuple-element.116), channel_id=1, source_target_pairs={{0,8},{1,9},{2,10},{3,11},{4,12},{5,13},{6,14},{7,15},{8,0},{9,1},... | collective-permute-start | bytes 393224 | tf_op jit(solution)/shard_map/ppermute | solution.py:507
  (17 other events, 59.2 us)
